TPU v7x, 32 devices: a whole 2x2x4 slice. The times are simulated.
32 devices in a mesh: groups: 2 (over y), seq: 16 (over z, x, core).
Axes of the slice: x: 2, y: 2, z: 4, core: 2. Of those that a mesh axis runs over, the one named last changes fastest.
Arguments:
- queries: bfloat16 [4096, 1536], P(('groups', 'seq')), parts along dimension 0, may hold values from -6 to 6
- keys: bfloat16 [4096, 1536], P(('groups', 'seq')), parts along dimension 0, may hold values from -6 to 6
- values: bfloat16 [4096, 1536], P(('groups', 'seq')), parts along dimension 0, may hold values from -6 to 6
- w_out: bfloat16 [1536, 3072], replicated, may hold values from -0.15625 to 0.15625
- shift_mod: float32 [6144], P('groups'), parts along dimension 0, may hold values from -5 to 5
- scale_mod: float32 [6144], P('groups'), parts along dimension 0, may hold values from -3 to 3
- w_final: bfloat16 [3072, 64], replicated, may hold values from -0.109375 to 0.109375
- conv_weight: bfloat16 [432, 512], replicated, may hold values from -0.3125 to 0.3125
- conv_bias: float32 [512], replicated, may hold values from -3 to 3
Outputs:
- decoded: bfloat16 [8, 32, 64, 512], P('groups', 'seq'), parts along dimension 0
There are 2 independent parts, one for each index of `groups`. A program takes and returns all parts, laid end to end along the dimension named above; an argument that names none is the same for every part. Nothing has to cross between parts.
All inputs are finite; a program needn't handle non-finite values.
Results may differ from a plain program's by a relative error of at most 0.018.
Values may be sent and summed in bfloat16 or wider, within the bound.
No kernel may reach another device: no remote copies, remote signals or barrier semaphores. Data moves between devices by JAX's collectives and lax.ppermute only.
A program may use at most 192 MiB of HBM per device.

v0:
```python
import math

import jax
import jax.numpy as jnp
from jax import lax
from jax.sharding import PartitionSpec as P

HEADS = 12
HEAD_DIM = 128
HEAD_GROUPS = 4
LATENT_CH = 16
FRAMES = 4
ROWS = 32
COLS_DEV = 1


def with_halo(cells, sides, width):
    for axis, dim in sides:
        count = lax.axis_size(axis)
        ends = count - 1
        head = lax.slice_in_dim(cells, 0, width, axis=dim)
        tail = lax.slice_in_dim(cells, cells.shape[dim] - width, cells.shape[dim], axis=dim)
        cells = jnp.concatenate(
            [
                lax.ppermute(tail, axis, [(i, (i + 1) % count) for i in range(ends)]),
                cells,
                lax.ppermute(head, axis, [((i + 1) % count, i) for i in range(ends)]),
            ],
            axis=dim,
        )
    return cells


def to_pieces(source, blocks):
    piece_rows = source.shape[0] // blocks
    grouped = source.reshape(blocks, piece_rows, HEAD_GROUPS, source.shape[1] // HEAD_GROUPS)
    return jnp.transpose(grouped, (0, 2, 1, 3)).reshape(
        blocks * HEAD_GROUPS, piece_rows, source.shape[1] // HEAD_GROUPS
    )


def absorb(state, key_part, value_part, query_rows):
    key_count = key_part.shape[0]
    block_rows = min(key_count, max(128, 1048576 // query_rows.shape[0]))
    per_head = HEADS // HEAD_GROUPS
    key_blocks = key_part.reshape(key_count // block_rows, block_rows, per_head, HEAD_DIM)
    value_blocks = value_part.reshape(key_count // block_rows, block_rows, per_head, HEAD_DIM)
    inv_root = 1.0 / math.sqrt(HEAD_DIM)

    def one_block(state_in, kv_block):
        run_max, run_sum, accumulated = state_in
        key_block, value_block = kv_block
        scores = (
            jnp.einsum("qhd,khd->hqk", query_rows, key_block, preferred_element_type=jnp.float32)
            * inv_root
        )
        new_max = jnp.maximum(run_max, jnp.max(scores, axis=2))
        factor = jnp.exp(run_max - new_max)
        exp_scores = jnp.exp(scores - new_max[:, :, None])
        run_sum = run_sum * factor + jnp.sum(exp_scores, axis=2)
        update = jnp.einsum(
            "hqk,khd->hqd",
            exp_scores.astype(jnp.bfloat16),
            value_block,
            preferred_element_type=jnp.float32,
        )
        accumulated = accumulated * factor[:, :, None] + update
        return ((new_max, run_sum, accumulated), None)

    state, unused = lax.scan(one_block, state, (key_blocks, value_blocks))
    return state


def fresh_state(per_head, count):
    return (
        jnp.full((per_head, count), -1e30, jnp.float32),
        jnp.zeros((per_head, count), jnp.float32),
        jnp.zeros((per_head, count, HEAD_DIM), jnp.float32),
    )


def convolve(padded, conv_weight, conv_bias, frames, width, height):
    taps = []
    for shift_t in range(3):
        for shift_x in range(3):
            for shift_y in range(3):
                taps.append(
                    padded[
                        shift_t : shift_t + frames,
                        shift_x : shift_x + width,
                        shift_y : shift_y + height,
                        :,
                    ]
                )
    stacked = jnp.concatenate(taps, axis=3)
    flat = stacked.reshape(frames * width * height, stacked.shape[3])
    output = jnp.dot(flat, conv_weight, preferred_element_type=jnp.float32) + conv_bias
    return output.astype(jnp.bfloat16).reshape(frames, width, height, conv_weight.shape[1])


def shards(queries, keys, values, w_out, shift_mod, scale_mod, w_final, conv_weight, conv_bias):
    devices = lax.axis_size("seq")
    position = lax.axis_index("seq")
    tok_dev = queries.shape[0]
    blocks = devices // HEAD_GROUPS
    per_head = HEADS // HEAD_GROUPS
    group_width = per_head * HEAD_DIM
    query_count = tok_dev * HEAD_GROUPS
    got_queries = lax.all_to_all(
        to_pieces(queries, blocks), "seq", split_axis=0, concat_axis=1, tiled=True
    )
    query_rows = got_queries.reshape(query_count, per_head, HEAD_DIM)
    key_groups = jnp.transpose(keys.reshape(tok_dev, HEAD_GROUPS, group_width), (1, 0, 2))
    value_groups = jnp.transpose(values.reshape(tok_dev, HEAD_GROUPS, group_width), (1, 0, 2))
    key_copies = jnp.broadcast_to(
        key_groups[None], (blocks, HEAD_GROUPS, tok_dev, group_width)
    ).reshape(devices, tok_dev, group_width)
    value_copies = jnp.broadcast_to(
        value_groups[None], (blocks, HEAD_GROUPS, tok_dev, group_width)
    ).reshape(devices, tok_dev, group_width)
    all_keys, all_values = (
        lax.all_to_all(key_copies, "seq", split_axis=0, concat_axis=1, tiled=True),
        lax.all_to_all(value_copies, "seq", split_axis=0, concat_axis=1, tiled=True),
    )
    state = absorb(fresh_state(per_head, query_count), all_keys[0], all_values[0], query_rows)
    run_max, run_sum, accumulated = state
    result = (accumulated / run_sum[:, :, None]).astype(jnp.bfloat16)
    result = jnp.transpose(result, (1, 0, 2)).reshape(1, query_count, group_width)
    returned = lax.all_to_all(result, "seq", split_axis=1, concat_axis=0, tiled=True)
    piece_rows = tok_dev // blocks
    attended = jnp.transpose(
        returned.reshape(blocks, HEAD_GROUPS, piece_rows, group_width), (0, 2, 1, 3)
    ).reshape(tok_dev, HEADS * HEAD_DIM)
    projected = jnp.dot(attended, w_out, preferred_element_type=jnp.float32)
    centered = projected - jnp.mean(projected, axis=1, keepdims=True)
    variance = jnp.mean(centered * centered, axis=1, keepdims=True)
    normed = (centered * lax.rsqrt(variance + 1e-06) * (1.0 + scale_mod) + shift_mod).astype(
        jnp.bfloat16
    )
    patches = jnp.dot(normed, w_final, preferred_element_type=jnp.float32).astype(jnp.bfloat16)
    rows_dev = FRAMES * ROWS // devices
    columns = COLS_DEV * devices
    laid = patches.reshape(rows_dev, columns, 4 * LATENT_CH)
    tile = lax.all_to_all(laid, "seq", split_axis=1, concat_axis=0, tiled=True)
    latent = tile.reshape(FRAMES, ROWS, COLS_DEV, LATENT_CH, 2, 2).transpose(0, 2, 5, 1, 4, 3)
    latent = latent.reshape(FRAMES, 2 * COLS_DEV, 2 * ROWS, LATENT_CH)
    rimmed = with_halo(latent, (("seq", 1),), 1)
    left_rim = jnp.where(position == 0, latent[:, :1], rimmed[:, :1])
    right_rim = jnp.where(position == devices - 1, latent[:, -1:], rimmed[:, -1:])
    widened = jnp.concatenate([left_rim, latent, right_rim], axis=1)
    padded = jnp.pad(widened, ((2, 0), (0, 0), (1, 1), (0, 0)), mode="edge")
    return convolve(padded, conv_weight, conv_bias, FRAMES, 2 * COLS_DEV, 2 * ROWS)


def solution(mesh):
    placed = (
        P(("groups", "seq"), None),
        P(("groups", "seq"), None),
        P(("groups", "seq"), None),
        P(),
        P("groups"),
        P("groups"),
        P(),
        P(),
        P(),
    )
    return jax.shard_map(
        shards,
        mesh=mesh,
        in_specs=placed,
        out_specs=P("groups", "seq", None, None),
        check_vma=False,
    )
```

profile of v0, /device:TPU:1, one launch (start us, length us, event | category | flops | bytes accessed | tf_op | source)
XLA Modules:
  0.0 180.8 jit_solution(2948887893393950316)
XLA Ops:
  0.0 1.2 reshape.125
  1.2 0.8 copy.31
  2.0 7.3 %all-to-all-start = ((bf16[16,32,384]{2,1,0:T(8,128)(2,1)}), bf16[16,32,384]{2,1,0:T(8,128)(2,1)S(1)}, u32[]{:S(2)}, u32[]{:S(2)}) async-start(bf16[16,32,384]{2,1,0:T(8,128)(2,1)} %bitcast.1), calls=%async_computation | async-start | bytes 786432 | tf_op jit(solution)/shard_map/all_to_all | solution.py:109
  9.4 0.3 copy.32
  9.7 11.5 %all-to-all-done = bf16[16,32,384]{2,1,0:T(8,128)(2,1)S(1)} async-done(((bf16[16,32,384]{2,1,0:T(8,128)(2,1)}), bf16[16,32,384]{2,1,0:T(8,128)(2,1)S(1)}, u32[]{:S(2)}, u32[]{:S(2)}) %all-to-all-start) | async-done | bytes 393248 | tf_op jit(solution)/shard_map/all_to_all | solution.py:109
  21.2 1.5 broadcast_in_dim.15
  22.7 4.0 %all-to-all-start.1 = ((bf16[16,128,384]{1,2,0:T(8,128)(2,1)}), bf16[16,128,384]{1,2,0:T(8,128)(2,1)S(1)}, u32[]{:S(2)}, u32[]{:S(2)}) async-start(bf16[16,128,384]{1,2,0:T(8,128)(2,1)} %bitcast.87), calls=%async_computation.1 | async-start | bytes 3145728 | tf_op jit(solution)/shard_map/all_to_all | solution.py:122
  26.8 0.3 copy.36
  27.1 32.0 %all-to-all-done.1 = bf16[16,128,384]{1,2,0:T(8,128)(2,1)S(1)} async-done(((bf16[16,128,384]{1,2,0:T(8,128)(2,1)}), bf16[16,128,384]{1,2,0:T(8,128)(2,1)S(1)}, u32[]{:S(2)}, u32[]{:S(2)}) %all-to-all-start.1) | async-done | bytes 1572896 | tf_op jit(solution)/shard_map/all_to_all | solution.py:122
  59.1 1.7 broadcast_in_dim.16
  60.8 8.7 %all-to-all-start.2 = ((bf16[16,128,384]{1,2,0:T(8,128)(2,1)}), bf16[16,128,384]{1,2,0:T(8,128)(2,1)S(1)}, u32[]{:S(2)}, u32[]{:S(2)}) async-start(bf16[16,128,384]{1,2,0:T(8,128)(2,1)} %bitcast.86), calls=%async_computation.2 | async-start | bytes 3145728 | tf_op jit(solution)/shard_map/all_to_all | solution.py:123
  69.7 3.6 %copy.33 = bf16[16,128,384]{1,0,2:T(8,128)(2,1)} copy(bf16[16,128,384]{1,2,0:T(8,128)(2,1)} %copy-done.2) | data formatting | bytes 3145728 | tf_op jit(solution)/shard_map/all_to_all | solution.py:122
  73.2 3.7 %squeeze.9 = bf16[2048,3,128]{0,2,1:T(8,128)(2,1)} reshape(bf16[16,128,384]{1,0,2:T(8,128)(2,1)} %copy.33) | data formatting | bytes 3145728 | tf_op jit(solution)/shard_map/while/body/jit(dynamic_index_in_dim)/squeeze | solution.py:70
  77.0 3.3 %multiply_reduce_fusion = (f32[3,512]{1,0:T(4,128)S(1)}, f32[3,512,2048]{2,1,0:T(8,128)S(1)}) fusion(bf16[2048,3,128]{0,2,1:T(8,128)(2,1)} %squeeze.9, bf16[512,3,128]{2,1,0:T(4,128)(2,1)S(1)} %reshape.127), kind=kOutput, calls=%fused_computation.1 | convolution fusion | flops 811596288 | bytes 14555136 | tf_op jit(solution)/shard_map/while/body/eval_jaxpr/qhd,khd->hqk/dot_general | solution.py:54
  80.3 2.5 %fusion = f32[3,512]{1,0:T(4,128)S(1)} fusion(f32[3,512,2048]{2,1,0:T(8,128)S(1)} %get-tuple-element.63, f32[3,512]{1,0:T(4,128)S(1)} %get-tuple-element.61), kind=kLoop, calls=%fused_computation.2 | loop fusion | flops 9435648 | bytes 12595200 | tf_op jit(solution)/shard_map/while/body/eval_jaxpr/reduce_sum | solution.py:60
  82.7 2.0 %copy-done.1 = f32[3,512,2048]{2,1,0:T(8,128)} copy-done((f32[3,512,2048]{2,1,0:T(8,128)}, f32[3,512,2048]{2,1,0:T(8,128)S(1)}, u32[]{:S(2)}) %copy-start.1) | copy-done | bytes 12582936
  84.8 17.1 %all-to-all-done.2 = bf16[16,128,384]{1,2,0:T(8,128)(2,1)S(1)} async-done(((bf16[16,128,384]{1,2,0:T(8,128)(2,1)}), bf16[16,128,384]{1,2,0:T(8,128)(2,1)S(1)}, u32[]{:S(2)}, u32[]{:S(2)}) %all-to-all-start.2) | async-done | bytes 1572896 | tf_op jit(solution)/shard_map/all_to_all | solution.py:123
  101.9 2.2 %copy.37 = bf16[16,128,384]{1,0,2:T(8,128)(2,1)} copy(bf16[16,128,384]{1,2,0:T(8,128)(2,1)S(1)} %all-to-all-done.2) | data formatting | bytes 3145728 | tf_op jit(solution)/shard_map/all_to_all | solution.py:123
  104.1 2.5 %squeeze.10 = bf16[2048,3,128]{0,2,1:T(8,128)(2,1)S(1)} reshape(bf16[16,128,384]{1,0,2:T(8,128)(2,1)} %copy.37) | data formatting | bytes 3145728 | tf_op jit(solution)/shard_map/while/body/jit(dynamic_index_in_dim)/squeeze | solution.py:70
  106.6 7.1 %fusion.16 = bf16[512,3,128]{0,2,1:T(8,128)(2,1)S(1)} fusion(bf16[2048,3,128]{0,2,1:T(8,128)(2,1)S(1)} %squeeze.10, f32[3,512,2048]{2,1,0:T(8,128)} %copy-done.1, f32[3,512]{1,0:T(4,128)S(1)} %get-tuple-element.61, f32[512,3]{0,1:T(4,128)S(1)} %bitcast_add_fusion, f32[512,3]{0,1:T(4,128)S(1)} %get-tuple-element.60), kind=kOutput, calls=%fused_computation.15 | convolution fusion | flops 815333376 | bytes 14567424 | tf_op jit(solution)/shard_map/while/body/eval_jaxpr/hqk,khd->hqd/dot_general | solution.py:61
  113.8 1.1 copy.38
  114.9 0.5 broadcast.84
  115.4 3.0 %reduce = bf16[512,384]{1,0:T(8,128)(2,1)S(1)} reduce(bf16[512,1,384]{2,1,0:T(2,128)(2,1)S(1)} %bitcast.92, bf16[]{:T(256)} %broadcast.84), dimensions={1}, to_apply=%bitcast.71.reduce_sub_computation | reduce | bytes 786434
  118.4 0.8 reshape.140
  119.3 8.7 %all-to-all-start.3 = ((bf16[16,2,6144]{2,1,0:T(2,128)(2,1)}), bf16[16,2,6144]{2,1,0:T(2,128)(2,1)S(1)}, u32[]{:S(2)}, u32[]{:S(2)}) async-start(bf16[16,2,6144]{2,1,0:T(2,128)(2,1)} %reshape.140), calls=%async_computation.3 | async-start | bytes 786432 | tf_op jit(solution)/shard_map/all_to_all | solution.py:129
  128.0 11.9 %all-to-all-done.3 = bf16[16,2,6144]{2,1,0:T(2,128)(2,1)S(1)} async-done(((bf16[16,2,6144]{2,1,0:T(2,128)(2,1)}), bf16[16,2,6144]{2,1,0:T(2,128)(2,1)S(1)}, u32[]{:S(2)}, u32[]{:S(2)}) %all-to-all-start.3) | async-done | bytes 393248 | tf_op jit(solution)/shard_map/all_to_all | solution.py:129
  139.9 0.4 reshape.141
  140.4 0.2 copy.39
  140.6 5.3 %fusion.31 = (f32[128]{0:T(128)S(1)}, f32[128,3072]{1,0:T(8,128)S(1)}) fusion(bf16[128,1536]{1,0:T(8,128)(2,1)S(1)} %bitcast.94, bf16[1536,3072]{1,0:T(8,128)(2,1)} %param.12), kind=kOutput, calls=%fused_computation.43 | convolution fusion | flops 1208352640 | bytes 11403776 | tf_op jit(solution)/shard_map/dot_general | solution.py:134
  145.9 0.3 multiply_reduce_fusion.1
  146.3 0.7 copy-done.7
  146.9 0.5 convolution_convert_fusion
  147.6 9.5 %all_to_all.51 = bf16[16,2,256]{2,1,0:T(2,128)(2,1)S(1)} all-to-all(bf16[16,2,256]{2,1,0:T(2,128)(2,1)S(1)} %reshape.142), channel_id=1, replica_groups=mesh['groups'=2,'seq'=16] {'seq'}, dimensions={0} | all-to-all | bytes 32768 | tf_op jit(solution)/shard_map/all_to_all | solution.py:144
  157.2 0.2 copy.42
  157.5 0.2 reshape.136
  157.6 0.1 copy.43
  157.8 2.7 %collective-permute-start = (bf16[4,1,64,16]{3,2,1,0:T(8,128)(2,1)S(1)}, bf16[4,1,64,16]{3,2,1,0:T(8,128)(2,1)S(1)}, u32[]{:S(2)}, u32[]{:S(2)}) collective-permute-start(bf16[4,1,64,16]{3,2,1,0:T(8,128)(2,1)S(1)} %get-tuple-element.19), channel_id=1, source_target_pairs={{0,1},{1,2},{2,3},{3,4},{4,5},{5,6},{6,7},{7,8},{8,9},{9,10},{10,1... | collective-permute-start | bytes 24584 | tf_op jit(solution)/shard_map/ppermute | solution.py:25
  160.5 1.9 %collective-permute-start.1 = (bf16[4,1,64,16]{3,2,1,0:T(8,128)(2,1)S(1)}, bf16[4,1,64,16]{3,2,1,0:T(8,128)(2,1)S(1)}, u32[]{:S(2)}, u32[]{:S(2)}) collective-permute-start(bf16[4,1,64,16]{3,2,1,0:T(8,128)(2,1)S(1)} %get-tuple-element.20), channel_id=1, source_target_pairs={{1,0},{2,1},{3,2},{4,3},{5,4},{6,5},{7,6},{8,7},{9,8},{10,9},{11,1... | collective-permute-start | bytes 24584 | tf_op jit(solution)/shard_map/ppermute | solution.py:27
  162.6 3.5 %collective-permute-done.1 = bf16[4,1,64,16]{3,2,1,0:T(8,128)(2,1)S(1)} collective-permute-done((bf16[4,1,64,16]{3,2,1,0:T(8,128)(2,1)S(1)}, bf16[4,1,64,16]{3,2,1,0:T(8,128)(2,1)S(1)}, u32[]{:S(2)}, u32[]{:S(2)}) %collective-permute-start.1) | collective-permute-done | bytes 8224 | tf_op jit(solution)/shard_map/ppermute | solution.py:27
  166.5 0.7 fusion.29
  167.3 0.1 copy.76
  167.4 0.1 pad_maximum_fusion
  167.6 0.2 fusion.27
  167.9 0.1 copy.49
  168.1 0.1 copy.52
  168.3 0.1 copy.53
  168.4 0.1 copy.55
  168.5 0.1 copy.56
  168.7 0.1 copy.58
  168.8 0.1 copy.59
  168.9 0.1 copy.61
  169.0 0.1 copy.62
  169.2 0.1 copy.64
  169.4 0.1 copy.69
  169.6 0.1 copy.70
  169.8 0.1 copy.73
  170.0 0.1 copy.77
  170.2 0.9 copy.51
  171.1 1.5 copy.54
  172.6 0.8 copy.57
  173.4 0.8 copy.60
  174.2 0.8 copy.63
  174.9 3.6 %concatenate.128 = bf16[512,432]{1,0:T(8,128)(2,1)} concatenate(bf16[512,16]{1,0:T(8,128)(2,1)S(1)} %bitcast.102, bf16[512,16]{1,0:T(8,128)(2,1)S(1)} %bitcast.120, bf16[512,16]{1,0:T(8,128)(2,1)S(1)} %bitcast.103, bf16[512,16]{1,0:T(8,128)(2,1)S(1)} %bitcast.104, bf16[512,16]{1,0:T(8,128)(2,1)S(1)} %bitcast.121, bf16[512,16]{1,0:T(8,128)(2,1)S(1)} %bitcast.105, ...), dimensions={1} | concatenate | bytes 884736 | tf_op jit(solution)/shard_map/concatenate | solution.py:95
  178.5 2.3 %fusion.9 = bf16[512,512]{1,0:T(8,128)(2,1)} fusion(bf16[512,432]{1,0:T(8,128)(2,1)} %concatenate.128, bf16[432,512]{1,0:T(8,128)(2,1)S(1)} %copy-done, f32[512]{0:T(512)S(1)} %copy-done.9), kind=kOutput, calls=%fused_computation.11 | convolution fusion | flops 227016704 | bytes 1411072 | tf_op jit(solution)/shard_map/dot_general | solution.py:97
  (50 shorter events, 2.0 us)
Async XLA Ops:
  0.0 178.5 %copy-start = (bf16[432,512]{1,0:T(8,128)(2,1)S(1)}, bf16[432,512]{1,0:T(8,128)(2,1)}, u32[]{:S(2)}) copy-start(bf16[432,512]{1,0:T(8,128)(2,1)} %param.16) | copy-start | bytes 1327108
  0.0 9.3 %copy-start.3 = (bf16[128,1536]{1,0:T(8,128)(2,1)S(1)}, bf16[128,1536]{1,0:T(8,128)(2,1)}, u32[]{:S(2)}) copy-start(bf16[128,1536]{1,0:T(8,128)(2,1)} %param.10) | copy-start | bytes 1179652
  2.0 19.2 %all-to-all-start = ((bf16[16,32,384]{2,1,0:T(8,128)(2,1)}), bf16[16,32,384]{2,1,0:T(8,128)(2,1)S(1)}, u32[]{:S(2)}, u32[]{:S(2)}) async-start(bf16[16,32,384]{2,1,0:T(8,128)(2,1)} %bitcast.1), calls=%async_computation | async-start | bytes 786432 | tf_op jit(solution)/shard_map/all_to_all | solution.py:109
  22.7 4.0 %copy-start.4 = (bf16[128,1536]{1,0:T(8,128)(2,1)S(1)}, bf16[128,1536]{1,0:T(8,128)(2,1)}, u32[]{:S(2)}) copy-start(bf16[128,1536]{1,0:T(8,128)(2,1)} %param.11) | copy-start | bytes 1179652
  22.7 36.4 %all-to-all-start.1 = ((bf16[16,128,384]{1,2,0:T(8,128)(2,1)}), bf16[16,128,384]{1,2,0:T(8,128)(2,1)S(1)}, u32[]{:S(2)}, u32[]{:S(2)}) async-start(bf16[16,128,384]{1,2,0:T(8,128)(2,1)} %bitcast.87), calls=%async_computation.1 | async-start | bytes 3145728 | tf_op jit(solution)/shard_map/all_to_all | solution.py:122
  59.1 1.7 copy-start.2
  60.8 41.1 %all-to-all-start.2 = ((bf16[16,128,384]{1,2,0:T(8,128)(2,1)}), bf16[16,128,384]{1,2,0:T(8,128)(2,1)S(1)}, u32[]{:S(2)}, u32[]{:S(2)}) async-start(bf16[16,128,384]{1,2,0:T(8,128)(2,1)} %bitcast.86), calls=%async_computation.2 | async-start | bytes 3145728 | tf_op jit(solution)/shard_map/all_to_all | solution.py:123
  80.2 4.5 %copy-start.1 = (f32[3,512,2048]{2,1,0:T(8,128)}, f32[3,512,2048]{2,1,0:T(8,128)S(1)}, u32[]{:S(2)}) copy-start(f32[3,512,2048]{2,1,0:T(8,128)S(1)} %get-tuple-element.63) | copy-start | bytes 37748740
  114.9 13.1 %copy-start.6 = (f32[3072]{0:T(1024)S(1)}, f32[3072]{0:T(1024)}, u32[]{:S(2)}) copy-start(f32[3072]{0:T(1024)} %param.14) | copy-start | bytes 36868
  119.3 20.7 %all-to-all-start.3 = ((bf16[16,2,6144]{2,1,0:T(2,128)(2,1)}), bf16[16,2,6144]{2,1,0:T(2,128)(2,1)S(1)}, u32[]{:S(2)}, u32[]{:S(2)}) async-start(bf16[16,2,6144]{2,1,0:T(2,128)(2,1)} %reshape.140), calls=%async_computation.3 | async-start | bytes 786432 | tf_op jit(solution)/shard_map/all_to_all | solution.py:129
  145.9 1.0 copy-start.7
  145.9 1.0 copy-start.8
  157.8 4.8 %collective-permute-start = (bf16[4,1,64,16]{3,2,1,0:T(8,128)(2,1)S(1)}, bf16[4,1,64,16]{3,2,1,0:T(8,128)(2,1)S(1)}, u32[]{:S(2)}, u32[]{:S(2)}) collective-permute-start(bf16[4,1,64,16]{3,2,1,0:T(8,128)(2,1)S(1)} %get-tuple-element.19), channel_id=1, source_target_pairs={{0,1},{1,2},{2,3},{3,4},{4,5},{5,6},{6,7},{7,8},{8,9},{9,10},{10,1... | collective-permute-start | bytes 24584 | tf_op jit(solution)/shard_map/ppermute | solution.py:25
  160.5 5.6 %collective-permute-start.1 = (bf16[4,1,64,16]{3,2,1,0:T(8,128)(2,1)S(1)}, bf16[4,1,64,16]{3,2,1,0:T(8,128)(2,1)S(1)}, u32[]{:S(2)}, u32[]{:S(2)}) collective-permute-start(bf16[4,1,64,16]{3,2,1,0:T(8,128)(2,1)S(1)} %get-tuple-element.20), channel_id=1, source_target_pairs={{1,0},{2,1},{3,2},{4,3},{5,4},{6,5},{7,6},{8,7},{9,8},{10,9},{11,1... | collective-permute-start | bytes 24584 | tf_op jit(solution)/shard_map/ppermute | solution.py:27
  168.0 4.6 %copy-start.5 = (bf16[4,2,64,16]{2,3,1,0:T(8,128)(2,1)S(1)}, bf16[4,2,64,16]{2,3,1,0:T(8,128)(2,1)}, u32[]{:S(2)}) copy-start(bf16[4,2,64,16]{2,3,1,0:T(8,128)(2,1)} %get-tuple-element.49) | copy-start | bytes 49156
  174.9 3.6 %copy-start.9 = (f32[512]{0:T(512)S(1)}, f32[512]{0:T(512)}, u32[]{:S(2)}) copy-start(f32[512]{0:T(512)} %param.17) | copy-start | bytes 6148
where the time goes:
time: 182 us; the launch traced here: 181 us
  waiting for transfers between devices  76 us (42%)
  local copies, waits for them, and re-layouts  36.9 us (20%)
  starting transfers between devices  33.5 us (18%)
  matrix products  18.4 us (10%)
  blocking collectives  9.46 us (5%)
  other arithmetic  6.04 us (3%)
    all_to_all x1, waiting for transfers between devices, shards(): lax.all_to_all(key_copies, 'seq', split_axis=0, concat_axis=1, tiled=True)  32 us
    all_to_all x1, waiting for transfers between devices, shards(): lax.all_to_all(value_copies, 'seq', split_axis=0, concat_axis=1, tiled=True)  17.1 us
    all_to_all x1, waiting for transfers between devices, shards(): lax.all_to_all(result, 'seq', split_axis=1, concat_axis=0, tiled=True)  11.9 us
    all_to_all x1, waiting for transfers between devices, shards(): lax.all_to_all(to_pieces(queries, blocks), 'seq', split_axis=0, concat_ax...  11.5 us
    all_to_all x1, blocking collectives, shards(): tile = lax.all_to_all(laid, 'seq', split_axis=1, concat_axis=0, tiled=True)  9.46 us
    all_to_all x1, starting transfers between devices, shards(): lax.all_to_all(result, 'seq', split_axis=1, concat_axis=0, tiled=True)  8.75 us
    all_to_all x1, starting transfers between devices, shards(): lax.all_to_all(value_copies, 'seq', split_axis=0, concat_axis=1, tiled=True)  8.73 us
    slice x28, local copies, waits for them, and re-layouts, convolve(): padded[shift_t:shift_t + frames, shift_x:shift_x + width, shift_y:shift_y...  8.1 us
  transfers between devices with their start and end apart: 6, of which 5 were waited for; matrix products, arithmetic and copies ran while one was open for 8% of the time, Pallas kernels for 0%

commit v1 on v0

v1 whole, which is shorter than its diff:
```python
import functools
import math

import jax
import jax.numpy as jnp
from jax import lax
from jax.experimental import pallas as pl
from jax.experimental.pallas import tpu as pltpu
from jax.sharding import Mesh
from jax.sharding import PartitionSpec as P

HEAD_DIM = 128
HEAD_GROUPS = 4
LATENT_CH = 16
FRAMES = 4
ROWS = 32
VMEM_LIMIT = 48 * 1024 * 1024
EXP2_SCALE = math.log2(math.e) / math.sqrt(HEAD_DIM)


def attend_kernel(q_ref, kv_ref, o_ref, *, q_blocks, key_step):
    planes, sources, _, part, _ = kv_ref.shape
    steps = planes // key_step
    keys = key_step * sources * part
    per_block = q_ref.shape[0] // q_blocks
    rows = per_block * part

    def scores_of(query, step):
        key = kv_ref[pl.ds(step * key_step, key_step), :, 0].reshape(keys, HEAD_DIM)
        return lax.dot_general(
            query, key, (((1,), (1,)), ((), ())), preferred_element_type=jnp.float32
        )

    def weighted(weights, step):
        value = kv_ref[pl.ds(step * key_step, key_step), :, 1].reshape(keys, HEAD_DIM)
        return jnp.dot(weights.astype(jnp.bfloat16), value, preferred_element_type=jnp.float32)

    for block in range(q_blocks):
        span = slice(block * per_block, (block + 1) * per_block)
        query = q_ref[span, 0].reshape(rows, HEAD_DIM)
        if steps == 1:
            scores = scores_of(query, 0)
            peak = jnp.max(scores, axis=1, keepdims=True) * EXP2_SCALE
            weights = jnp.exp2(scores * EXP2_SCALE - peak)
            total = jnp.sum(weights, axis=1, keepdims=True)
            summed = weighted(weights, 0)
        else:

            def absorb(step, state):
                peak, total, summed = state
                scores = scores_of(query, step) * EXP2_SCALE
                new_peak = jnp.maximum(peak, jnp.max(scores, axis=1, keepdims=True))
                factor = jnp.exp2(peak - new_peak)
                weights = jnp.exp2(scores - new_peak)
                total = total * factor + jnp.sum(weights, axis=1, keepdims=True)
                return new_peak, total, summed * factor + weighted(weights, step)

            peak, total, summed = lax.fori_loop(
                0,
                steps,
                absorb,
                (
                    jnp.full((rows, 1), -1e30, jnp.float32),
                    jnp.zeros((rows, 1), jnp.float32),
                    jnp.zeros((rows, HEAD_DIM), jnp.float32),
                ),
            )
        out = (summed / total).astype(jnp.bfloat16)
        o_ref[span] = out.reshape(per_block, part, HEAD_DIM)


def attend(queries, keys_values):
    sources, _, part, width = queries.shape
    planes = keys_values.shape[0]
    key_step = math.gcd(planes, 4)
    return pl.pallas_call(
        functools.partial(attend_kernel, q_blocks=2, key_step=key_step),
        grid=(width // HEAD_DIM,),
        in_specs=[
            pl.BlockSpec((sources, 1, part, HEAD_DIM), lambda h: (0, 0, 0, h)),
            pl.BlockSpec((planes, sources, 2, part, HEAD_DIM), lambda h: (0, 0, 0, 0, h)),
        ],
        out_specs=pl.BlockSpec((sources, part, HEAD_DIM), lambda h: (0, 0, h)),
        out_shape=jax.ShapeDtypeStruct((sources, part, width), jnp.bfloat16),
        compiler_params=pltpu.CompilerParams(vmem_limit_bytes=VMEM_LIMIT),
    )(queries, keys_values)


def final_kernel(o_ref, w_ref, scale_ref, shift_ref, w_final_ref, out_ref, projected, *, columns):
    step = pl.program_id(0)
    groups, _, width = o_ref.shape
    tile = w_ref.shape[1]
    acc = None
    for group in range(groups):
        part = jnp.dot(
            o_ref[group],
            w_ref[group * width : (group + 1) * width, :],
            preferred_element_type=jnp.float32,
        )
        acc = part if acc is None else acc + part
    projected[step] = acc

    @pl.when(step == pl.num_programs(0) - 1)
    def _():
        steps = projected.shape[0]
        tokens = projected.shape[1]
        features = steps * tile
        total = projected[0]
        for i in range(1, steps):
            total = total + projected[i]
        mean = jnp.sum(total, axis=1, keepdims=True) * (1.0 / features)
        squares = None
        for i in range(steps):
            centered = projected[i] - mean
            squares = centered * centered if squares is None else squares + centered * centered
        variance = jnp.sum(squares, axis=1, keepdims=True) * (1.0 / features)
        inverse = lax.rsqrt(variance + 1e-06)
        patches = None
        for i in range(steps):
            lanes = slice(i * tile, (i + 1) * tile)
            normed = (projected[i] - mean) * inverse * (1.0 + scale_ref[:, lanes]) + shift_ref[:, lanes]
            part = jnp.dot(
                normed.astype(jnp.bfloat16), w_final_ref[lanes, :], preferred_element_type=jnp.float32
            )
            patches = part if patches is None else patches + part
        half = patches.shape[1] // 2
        own = patches[:, :half]
        edge = patches[:, half:]
        lane = lax.broadcasted_iota(jnp.int32, own.shape, 1)
        column = lax.broadcasted_iota(jnp.int32, own.shape, 0) % columns
        from_left = jnp.where(column == 0, edge, pltpu.roll(own, 1, 0))
        from_right = jnp.where(column == columns - 1, edge, pltpu.roll(own, tokens - 1, 0))
        cells = jnp.where(
            lane < half // 4, from_left, jnp.where(lane >= 3 * (half // 4), from_right, own)
        )
        out_ref[...] = cells.astype(jnp.bfloat16)


def final_layer(attended, w_out, scale_mod, shift_mod, w_final, columns):
    groups, tokens, width = attended.shape
    inner, features = w_out.shape
    tile = 512
    steps = features // tile
    by_cell = w_final.reshape(features, LATENT_CH, 2, 2).transpose(0, 3, 2, 1)
    by_cell = by_cell.reshape(features, 2, 2 * LATENT_CH)
    order = jnp.concatenate([by_cell[:, i] for i in (1, 0, 1, 0, 0, 0, 1, 1)], axis=1)
    lanes = order.shape[1]
    return pl.pallas_call(
        functools.partial(final_kernel, columns=columns),
        grid=(steps,),
        in_specs=[
            pl.BlockSpec((groups, tokens, width), lambda i: (0, 0, 0)),
            pl.BlockSpec((inner, tile), lambda i: (0, i)),
            pl.BlockSpec((1, features), lambda i: (0, 0)),
            pl.BlockSpec((1, features), lambda i: (0, 0)),
            pl.BlockSpec((features, lanes), lambda i: (0, 0)),
        ],
        out_specs=pl.BlockSpec((tokens, lanes // 2), lambda i: (0, 0)),
        out_shape=jax.ShapeDtypeStruct((tokens, lanes // 2), jnp.bfloat16),
        scratch_shapes=[pltpu.VMEM((steps, tokens, tile), jnp.float32)],
        compiler_params=pltpu.CompilerParams(vmem_limit_bytes=VMEM_LIMIT),
    )(attended, w_out, scale_mod[None], shift_mod[None], order)


def convolve_kernel(cells_ref, w_ref, bias_ref, out_ref, latent):
    frames, rows, _ = cells_ref.shape
    cols = latent.shape[1]
    height = 2 * rows
    ch = LATENT_CH
    for f in range(frames):
        cells = cells_ref[f].astype(jnp.float32)
        for x in range(cols):
            for p in range(2):
                lane = (2 * x + p) * ch
                latent[f, x, pl.ds(8 + p, rows, stride=2), :] = cells[:, lane : lane + ch]
            latent[f, x, 7:8, :] = cells[:1, 2 * x * ch : (2 * x + 1) * ch]
            latent[f, x, 8 + height : 9 + height, :] = cells[rows - 1 :, (2 * x + 1) * ch : (2 * x + 2) * ch]
    depth = 9 * ch
    for x in range(cols - 2):
        stacked = []
        for f in range(frames):
            taps = [latent[f, x + b, 7 + e : 7 + e + height, :] for b in range(3) for e in range(3)]
            stacked.append(jnp.concatenate(taps, axis=1).astype(jnp.bfloat16))
        stacked = [stacked[0]] * 2 + stacked
        acc = None
        for a in range(3):
            flat = jnp.concatenate(stacked[a : a + frames], axis=0)
            part = jnp.dot(
                flat, w_ref[a * depth : (a + 1) * depth, :], preferred_element_type=jnp.float32
            )
            acc = part if acc is None else acc + part
        acc = (acc + bias_ref[...]).astype(jnp.bfloat16)
        out_ref[:, x] = acc.reshape(frames, height, acc.shape[1])


def convolve(cells, conv_weight, conv_bias):
    frames, rows, lanes = cells.shape
    cols = lanes // (2 * LATENT_CH)
    channels = conv_weight.shape[1]
    return pl.pallas_call(
        convolve_kernel,
        out_shape=jax.ShapeDtypeStruct((frames, cols - 2, 2 * rows, channels), jnp.bfloat16),
        scratch_shapes=[pltpu.VMEM((frames, cols, 2 * rows + 16, LATENT_CH), jnp.float32)],
        compiler_params=pltpu.CompilerParams(vmem_limit_bytes=VMEM_LIMIT),
    )(cells, conv_weight, conv_bias[None])


def shards(queries, keys, values, w_out, shift_mod, scale_mod, w_final, conv_weight, conv_bias):
    heads = lax.axis_size("heads")
    devices = heads * lax.axis_size("plane")
    tokens, width = queries.shape
    group_width = width // heads
    columns = devices
    pieces = jnp.stack([queries, keys, values]).reshape(3, tokens, heads, group_width)
    pieces = pieces.transpose(2, 0, 1, 3)
    got = lax.all_to_all(pieces, "heads", split_axis=0, concat_axis=0, tiled=True)
    keys_values = lax.all_gather(got[:, 1:], "plane")
    result = attend(got[:, :1], keys_values)
    returned = lax.all_to_all(result, "heads", split_axis=0, concat_axis=0, tiled=True)
    cells = final_layer(returned, w_out, scale_mod, shift_mod, w_final, columns)
    rows_dev = tokens // columns
    laid = cells.reshape(rows_dev, columns, cells.shape[1])
    tile = lax.all_to_all(laid, ("heads", "plane"), split_axis=1, concat_axis=0, tiled=True)
    tile = tile.reshape(FRAMES, ROWS, cells.shape[1])
    return convolve(tile, conv_weight, conv_bias)


def solution(mesh):
    groups, seq = mesh.devices.shape
    split = Mesh(
        mesh.devices.reshape(groups, HEAD_GROUPS, seq // HEAD_GROUPS), ("groups", "heads", "plane")
    )
    by_token = P(("groups", "heads", "plane"), None)
    placed = (by_token, by_token, by_token, P(), P("groups"), P("groups"), P(), P(), P())
    return jax.shard_map(
        shards,
        mesh=split,
        in_specs=placed,
        out_specs=P("groups", ("heads", "plane"), None, None),
        check_vma=False,
    )
```

time: 182 us -> 124 us (0.68)
  waiting for transfers between devices: 76 us -> 32.5 us
  blocking collectives: 9.46 us -> 42.7 us
  starting transfers between devices: 33.5 us -> 4.33 us
  local copies, waits for them, and re-layouts: 36.9 us -> 13.6 us
  matrix products: 18.4 us -> 0 us
  Pallas kernels: 0 us -> 15.8 us
  between operations: 0.49 us -> 13.5 us
  other arithmetic: 6.04 us -> 0.16 us
    all_to_all x4 -> x1, waiting for transfers between devices: 72.5 us -> 3.49 us  [shards(): lax.all_to_all(result, 'heads', split_axis=0, concat_axis=0, tiled=True)]
    all_to_all x1 -> x2, blocking collectives: 9.46 us -> 42.7 us  [the longest x1 32.9 us: shards(): lax.all_to_all(pieces, 'heads', split_axis=0, concat_axis=0, tiled=True)]
    all_gather x0 -> x1, waiting for transfers between devices: none -> 29 us  [shards(): keys_values = lax.all_gather(got[:, 1:], 'plane')]
    all_to_all x4 -> x1, starting transfers between devices: 28.8 us -> 4.32 us  [shards(): lax.all_to_all(result, 'heads', split_axis=0, concat_axis=0, tiled=True)]
    dot_general x5 -> x0, matrix products: 18.4 us -> none  [the longest x1 7.13 us: one_block(): jnp.einsum('hqk,khd->hqd', exp_scores.astype(jnp.bfloat16), value_block,...]
    pallas_call x0 -> x3, Pallas kernels: none -> 15.8 us  [the longest x1 7.18 us: attend(): pl.pallas_call(functools.partial(attend_kernel, q_blocks=2, key_step=key_...]
    slice x30 -> x3, local copies, waits for them, and re-layouts: 8.21 us -> 1.06 us  [the longest x1 1 us: shards(): keys_values = lax.all_gather(got[:, 1:], 'plane')]
    squeeze x2 -> x0, local copies, waits for them, and re-layouts: 6.26 us -> none  [absorb(): state, unused = lax.scan(one_block, state, (key_blocks, value_blocks))]
  transfers between devices with their start and end apart: 6 -> 2, of which waited for: 5 -> 2; matrix products, arithmetic and copies ran while one was open for 8% -> 7% of each run, Pallas kernels for 0% -> 0%
where the time goes in v1:
time: 124 us; the launch traced here: 123 us
  blocking collectives  42.7 us (34%)
  waiting for transfers between devices  32.5 us (26%)
  Pallas kernels  15.8 us (13%)
  local copies, waits for them, and re-layouts  13.6 us (11%)
  between operations  13.5 us (11%)
  starting transfers between devices  4.33 us (3%)
    all_to_all x1, blocking collectives, shards(): lax.all_to_all(pieces, 'heads', split_axis=0, concat_axis=0, tiled=True)  32.9 us
    all_gather x1, waiting for transfers between devices, shards(): keys_values = lax.all_gather(got[:, 1:], 'plane')  29 us
    all_to_all x1, blocking collectives, shards(): lax.all_to_all(laid, ('heads', 'plane'), split_axis=1, concat_axis=0, til...  9.85 us
    pallas_call x1, Pallas kernels, attend(): pl.pallas_call(functools.partial(attend_kernel, q_blocks=2, key_step=key_...  7.18 us
    pallas_call x1, Pallas kernels, final_layer(): pl.pallas_call(functools.partial(final_kernel, columns=columns), grid=(st...  7.04 us
    concatenate x1, local copies, waits for them, and re-layouts, final_layer(): jnp.concatenate([by_cell[:, i] for i in (1, 0, 1, 0, 0, 0, 1, 1)], axis=1)  6.15 us
    unnamed x21, local copies, waits for them, and re-layouts  5.47 us
    all_to_all x1, starting transfers between devices, shards(): lax.all_to_all(result, 'heads', split_axis=0, concat_axis=0, tiled=True)  4.32 us
  transfers between devices with their start and end apart: 2, of which 2 were waited for; matrix products, arithmetic and copies ran while one was open for 7% of the time, Pallas kernels for 0%

profile of v1, /device:TPU:1, one launch (start us, length us, event | category | flops | bytes accessed | tf_op | source)
XLA Modules:
  0.0 122.7 jit_solution(5688838687306911983)
XLA Ops:
  6.5 0.0 copy-start.5
  6.5 0.0 all-gather.3.cloned.1.call-start
  6.5 1.3 %copy.31 = bf16[128,1536]{0,1:T(8,128)(2,1)S(1)} copy(bf16[128,1536]{1,0:T(8,128)(2,1)} %param.9) | data formatting | bytes 786432 | tf_op args[0]
  7.8 0.0 copy-start.6
  7.8 0.2 copy.34
  8.0 0.0 copy-done.5
  8.1 0.2 copy.32
  8.3 0.2 copy.35
  8.5 0.3 copy-done.6
  8.8 0.2 copy.33
  9.0 0.2 copy.36
  9.3 0.2 maximum_bitcast_fusion
  9.4 32.9 %all_to_all.25 = bf16[4,3,128,384]{3,2,1,0:T(8,128)(2,1)S(1)} all-to-all(bf16[4,3,128,384]{3,2,1,0:T(8,128)(2,1)S(1)} %maximum_bitcast_fusion), channel_id=1, replica_groups=mesh['groups'=2,'heads'=4,'plane'=4] {'heads'}, dimensions={0} | all-to-all | bytes 2359296 | tf_op jit(solution)/shard_map/all_to_all | solution.py:216
  42.3 0.0 copy-start.7
  42.3 1.0 slice.23
  43.3 0.0 all-gather.3.cloned.1.call-update
  43.4 0.0 copy-done.7
  43.4 0.1 reshape.20
  43.5 0.1 copy.37
  43.7 29.0 %all-gather.3.cloned.1.call-done = bf16[16,2,128,384]{3,2,1,0:T(8,128)(2,1)} async-done(((bf16[4,2,128,384]{3,2,1,0:T(8,128)(2,1)}), bf16[16,2,128,384]{3,2,1,0:T(8,128)(2,1)}) %all-gather.3.cloned.1.call-update) | async-done | bytes 3145744 | tf_op jit(solution)/shard_map/all_gather | solution.py:217
  72.7 0.0 copy-start
  72.7 1.9 %copy-done = bf16[16,2,128,384]{3,2,1,0:T(8,128)(2,1)S(1)} copy-done((bf16[16,2,128,384]{3,2,1,0:T(8,128)(2,1)S(1)}, bf16[16,2,128,384]{3,2,1,0:T(8,128)(2,1)}, u32[]{:S(2)}) %copy-start) | copy-done | bytes 3145752
  74.6 7.2 %shard_map.91 = bf16[4,128,384]{2,1,0:T(8,128)(2,1)} custom-call(bf16[4,1,128,384]{3,2,1,0:T(8,128)(2,1)S(1)} %slice.22.q_ref, bf16[4,4,2,128,384]{4,3,2,1,0:T(8,128)(2,1)S(1)} %bitcast.21), custom_call_target="tpu_custom_call" | custom-call | tf_op jit(solution)/shard_map/pallas_call | solution.py:76
  81.8 4.3 %all-to-all-start.1 = ((bf16[4,128,384]{2,1,0:T(8,128)(2,1)}), bf16[4,128,384]{2,1,0:T(8,128)(2,1)S(1)}, u32[]{:S(2)}, u32[]{:S(2)}) async-start(bf16[4,128,384]{2,1,0:T(8,128)(2,1)} %shard_map.91), calls=%async_computation.1 | async-start | bytes 786432 | tf_op jit(solution)/shard_map/all_to_all | solution.py:219
  86.1 0.4 copy.42
  86.5 1.2 copy.41
  87.7 0.0 copy-start.2
  87.7 0.0 copy-start.3
  87.7 6.2 %concatenate.4.w_final_ref = bf16[3072,256]{1,0:T(8,128)(2,1)S(1)} concatenate(bf16[3072,32]{1,0:T(8,128)(2,1)} %bitcast.31, bf16[3072,32]{1,0:T(8,128)(2,1)S(1)} %bitcast.27, bf16[3072,32]{1,0:T(8,128)(2,1)} %bitcast.32, bf16[3072,32]{1,0:T(8,128)(2,1)S(1)} %bitcast.28, bf16[3072,32]{1,0:T(8,128)(2,1)S(1)} %bitcast.29, bf16[3072,32]{1,0:T(8,128)(2,1)S(1)} %bitcast.30, ...), dimensions={1} | concatenate | bytes 3145728 | tf_op jit(solution)/shard_map/concatenate | solution.py:146
  93.8 3.5 %all-to-all-done.1.o_ref = bf16[4,128,384]{2,1,0:T(8,128)(2,1)S(1)} async-done(((bf16[4,128,384]{2,1,0:T(8,128)(2,1)}), bf16[4,128,384]{2,1,0:T(8,128)(2,1)S(1)}, u32[]{:S(2)}, u32[]{:S(2)}) %all-to-all-start.1) | async-done | bytes 393248 | tf_op jit(solution)/shard_map/all_to_all | solution.py:219
  97.3 0.0 copy-done.2
  97.3 0.0 copy-done.3
  97.3 0.0 copy-start.1
  97.3 0.0 copy-start.4
  97.3 7.0 %shard_map.92 = bf16[128,128]{1,0:T(8,128)(2,1)S(1)} custom-call(bf16[4,128,384]{2,1,0:T(8,128)(2,1)S(1)} %all-to-all-done.1.o_ref, bf16[1536,3072]{1,0:T(8,128)(2,1)} %w_ref.2, f32[1,3072]{1,0:T(1,128)S(1)} %bitcast.24, f32[1,3072]{1,0:T(1,128)S(1)} %bitcast.25, bf16[3072,256]{1,0:T(8,128)(2,1)S(1)} %concatenate.4.w_final_ref), custom_call_target="tpu_custom_call" | custom-call | tf_op jit(solution)/shard_map/pallas_call | solution.py:148
  104.4 9.8 %all_to_all.26 = bf16[8,16,128]{2,0,1:T(8,128)(2,1)S(1)} all-to-all(bf16[8,16,128]{2,0,1:T(8,128)(2,1)S(1)} %copy.40), channel_id=1, replica_groups=mesh['groups'=2,'heads'=4,'plane'=4] {'heads','plane'}, dimensions={1} | all-to-all | bytes 65536 | tf_op jit(solution)/shard_map/all_to_all | solution.py:223
  114.3 0.0 copy-done.1
  114.3 0.0 copy-done.4
  114.3 1.6 %shard_map.93 = bf16[4,2,64,512]{3,2,1,0:T(8,128)(2,1)} custom-call(bf16[4,32,128]{2,1,0:T(8,128)(2,1)S(1)} %bitcast.23, bf16[432,512]{1,0:T(8,128)(2,1)S(1)} %copy-done.1, f32[1,512]{1,0:T(1,128)S(1)} %bitcast.26), custom_call_target="tpu_custom_call" | custom-call | tf_op jit(solution)/shard_map/pallas_call | solution.py:200
  (3 shorter events, 0.1 us)
Async XLA Ops:
  6.5 1.5 %copy-start.5 = (bf16[128,1536]{1,0:T(8,128)(2,1)S(1)}, bf16[128,1536]{1,0:T(8,128)(2,1)}, u32[]{:S(2)}) copy-start(bf16[128,1536]{1,0:T(8,128)(2,1)} %param.10) | copy-start | bytes 1179652
  6.5 66.2 %all-gather.3.cloned.1.call-start = ((), (), s32[]{:S(2)}) async-start(), calls=%async_computation.3 | async-start | bytes 3932160 | tf_op jit(solution)/shard_map/all_gather | solution.py:217
  7.8 1.0 copy-start.6
  42.3 1.0 copy-start.7
  72.7 1.9 %copy-start = (bf16[16,2,128,384]{3,2,1,0:T(8,128)(2,1)S(1)}, bf16[16,2,128,384]{3,2,1,0:T(8,128)(2,1)}, u32[]{:S(2)}) copy-start(bf16[16,2,128,384]{3,2,1,0:T(8,128)(2,1)} %all-gather.3.cloned.1.call-done) | copy-start | bytes 9437188
  81.8 15.6 %all-to-all-start.1 = ((bf16[4,128,384]{2,1,0:T(8,128)(2,1)}), bf16[4,128,384]{2,1,0:T(8,128)(2,1)S(1)}, u32[]{:S(2)}, u32[]{:S(2)}) async-start(bf16[4,128,384]{2,1,0:T(8,128)(2,1)} %shard_map.91), calls=%async_computation.1 | async-start | bytes 786432 | tf_op jit(solution)/shard_map/all_to_all | solution.py:219
  87.7 9.7 %copy-start.2 = (f32[3072]{0:T(1024)S(1)}, f32[3072]{0:T(1024)}, u32[]{:S(2)}) copy-start(f32[3072]{0:T(1024)} %param.14) | copy-start | bytes 36868
  87.7 9.7 %copy-start.3 = (f32[3072]{0:T(1024)S(1)}, f32[3072]{0:T(1024)}, u32[]{:S(2)}) copy-start(f32[3072]{0:T(1024)} %param.13) | copy-start | bytes 36868
  97.3 16.9 %copy-start.1 = (bf16[432,512]{1,0:T(8,128)(2,1)S(1)}, bf16[432,512]{1,0:T(8,128)(2,1)}, u32[]{:S(2)}) copy-start(bf16[432,512]{1,0:T(8,128)(2,1)} %w_ref.3) | copy-start | bytes 1327108
  97.3 16.9 %copy-start.4 = (f32[512]{0:T(512)S(1)}, f32[512]{0:T(512)}, u32[]{:S(2)}) copy-start(f32[512]{0:T(512)} %param.17) | copy-start | bytes 6148
Sparse Core Ops, SparseCore 0:
  43.5 29.1 all-gather.2

commit v2 on v1

v2 whole, which is shorter than its diff:
```python
import functools
import math

import jax
import jax.numpy as jnp
from jax import lax
from jax.experimental import pallas as pl
from jax.experimental.pallas import tpu as pltpu
from jax.sharding import Mesh
from jax.sharding import PartitionSpec as P

HEAD_DIM = 128
HEAD_GROUPS = 4
LATENT_CH = 16
FRAMES = 4
VMEM_LIMIT = 56 * 1024 * 1024
EXP2_SCALE = math.log2(math.e) / math.sqrt(HEAD_DIM)
EARLY, LATE = (1, 0), (2, 3)


def swap(source, axis, distance):
    count = lax.axis_size(axis)
    return lax.ppermute(source, axis, [(i, i ^ distance) for i in range(count)])


def attend_kernel(*refs, sources, parts, targets, rows_step):
    q_refs = refs[:sources]
    kv_refs = refs[sources : sources + parts]
    o_refs = refs[sources + parts :]
    keys = [r[:, :, 0].reshape(-1, HEAD_DIM) for r in kv_refs]
    values = [r[:, :, 1].reshape(-1, HEAD_DIM) for r in kv_refs]
    rows = q_refs[0].shape[1]
    for first in range(0, len(targets), rows_step):
        block = range(first, min(first + rows_step, len(targets)))
        query = jnp.concatenate([q[targets[i]] for i in block for q in q_refs], axis=0)
        scores = [
            lax.dot_general(query, k, (((1,), (1,)), ((), ())), preferred_element_type=jnp.float32)
            for k in keys
        ]
        peak = functools.reduce(
            jnp.maximum, [jnp.max(s, axis=1, keepdims=True) for s in scores]
        )
        peak = peak * EXP2_SCALE
        total = summed = None
        for s, v in zip(scores, values):
            weights = jnp.exp2(s * EXP2_SCALE - peak)
            part_total = jnp.sum(weights, axis=1, keepdims=True)
            part = jnp.dot(weights.astype(jnp.bfloat16), v, preferred_element_type=jnp.float32)
            total = part_total if total is None else total + part_total
            summed = part if summed is None else summed + part
        out = (summed / total).astype(jnp.bfloat16)
        for n, i in enumerate(block):
            for r in range(sources):
                at = (n * sources + r) * rows
                o_refs[i][targets[i] ^ r] = out[at : at + rows]


def attend(queries, keys_values, targets):
    sources, rows, width = queries[0].shape
    key_count = sum(math.prod(kv.shape[:2]) * kv.shape[3] for kv in keys_values)
    result = jax.ShapeDtypeStruct((sources, rows, width), jnp.bfloat16)
    kv_block = keys_values[0].shape[:-1] + (HEAD_DIM,)
    return pl.pallas_call(
        functools.partial(
            attend_kernel,
            sources=sources,
            parts=len(keys_values),
            targets=targets,
            rows_step=2 if key_count <= 4096 else 1,
        ),
        grid=(width // HEAD_DIM,),
        in_specs=[pl.BlockSpec((sources, rows, HEAD_DIM), lambda h: (0, 0, h))] * sources
        + [pl.BlockSpec(kv_block, lambda h: (0, 0, 0, 0, h))] * len(keys_values),
        out_specs=[pl.BlockSpec((sources, rows, HEAD_DIM), lambda h: (0, 0, h))] * len(targets),
        out_shape=[result] * len(targets),
        compiler_params=pltpu.CompilerParams(vmem_limit_bytes=VMEM_LIMIT),
    )(*queries, *keys_values)


def final_kernel(where_ref, *refs, groups, planes, rows_dev):
    o_refs = refs[:groups]
    w_ref, scale_ref, shift_ref, w_final_ref, even_ref, odd_ref, projected = refs[groups:]
    step = pl.program_id(0)
    heads_at, plane_at = where_ref[0], where_ref[1]
    tokens = projected.shape[1]
    width = o_refs[0].shape[2]
    tile = w_ref.shape[1]
    acc = None
    for t in range(groups):
        rows = pl.ds(pl.multiple_of((heads_at ^ t) * width, 128), width)
        part = jnp.dot(
            o_refs[t][...].reshape(tokens, width), w_ref[rows, :], preferred_element_type=jnp.float32
        )
        acc = part if acc is None else acc + part
    projected[step] = acc

    @pl.when(step == pl.num_programs(0) - 1)
    def _():
        steps = projected.shape[0]
        features = steps * tile
        total = projected[0]
        for i in range(1, steps):
            total = total + projected[i]
        mean = jnp.sum(total, axis=1, keepdims=True) * (1.0 / features)
        squares = None
        for i in range(steps):
            centered = projected[i] - mean
            squares = centered * centered if squares is None else squares + centered * centered
        variance = jnp.sum(squares, axis=1, keepdims=True) * (1.0 / features)
        inverse = lax.rsqrt(variance + 1e-06)
        patches = None
        for i in range(steps):
            lanes = slice(i * tile, (i + 1) * tile)
            normed = (projected[i] - mean) * inverse * (1.0 + scale_ref[:, lanes]) + shift_ref[:, lanes]
            part = jnp.dot(
                normed.astype(jnp.bfloat16), w_final_ref[lanes, :], preferred_element_type=jnp.float32
            )
            patches = part if patches is None else patches + part
        patches = patches.astype(jnp.bfloat16)
        channels = patches.shape[1]
        half = channels // 2
        source = lax.broadcasted_iota(jnp.int32, (channels, channels), 0)
        target = lax.broadcasted_iota(jnp.int32, (channels, channels), 1)
        q, p, c = target // half, (target // LATENT_CH) % 2, target % LATENT_CH
        lane_order = (source == 4 * c + 2 * p + q).astype(jnp.bfloat16)
        to = lax.broadcasted_iota(jnp.int32, (tokens, tokens), 0)
        at = lax.broadcasted_iota(jnp.int32, (tokens, tokens), 1)
        share = planes * rows_dev
        place = ((to // share) ^ heads_at) * share
        place = place + (((to % share) // rows_dev) ^ plane_at) * rows_dev + to % rows_dev
        row_order = (at == place).astype(jnp.bfloat16)
        cells = jnp.dot(patches, lane_order, preferred_element_type=jnp.float32)
        cells = jnp.dot(row_order, cells.astype(jnp.bfloat16), preferred_element_type=jnp.float32)
        cells = cells.astype(jnp.bfloat16)
        even_ref[...] = cells[:, :half]
        odd_ref[...] = cells[:, half:]


def final_layer(where, attended, w_out, scale_mod, shift_mod, w_final, rows_dev, planes):
    groups = len(attended)
    sources, rows, width = attended[0].shape
    tokens = sources * rows
    inner, features = w_out.shape
    channels = w_final.shape[1]
    tile = 512
    steps = features // tile
    whole = lambda shape: pl.BlockSpec(shape, lambda i, *_: (0,) * len(shape))
    result = jax.ShapeDtypeStruct((tokens, channels // 2), jnp.bfloat16)
    return pl.pallas_call(
        functools.partial(final_kernel, groups=groups, planes=planes, rows_dev=rows_dev),
        grid_spec=pltpu.PrefetchScalarGridSpec(
            num_scalar_prefetch=1,
            grid=(steps,),
            in_specs=[whole((sources, rows, width))] * groups
            + [
                pl.BlockSpec((inner, tile), lambda i, *_: (0, i)),
                whole((1, features)),
                whole((1, features)),
                whole((features, channels)),
            ],
            out_specs=[whole((tokens, channels // 2))] * 2,
            scratch_shapes=[pltpu.VMEM((steps, tokens, tile), jnp.float32)],
        ),
        out_shape=[result] * 2,
        compiler_params=pltpu.CompilerParams(vmem_limit_bytes=VMEM_LIMIT),
    )(where, *attended, w_out, scale_mod[None], shift_mod[None], w_final)


def convolve_kernel(where_ref, even_ref, odd_ref, left_ref, right_ref, w_ref, bias_ref, out_ref, latent):
    frames, cols, _, ch = latent.shape
    rows = even_ref.shape[0] // frames
    height = 2 * rows
    even = even_ref[...].astype(jnp.float32)
    odd = odd_ref[...].astype(jnp.float32)
    left = jnp.where(where_ref[0] == 0, even, left_ref[...].astype(jnp.float32))
    right = jnp.where(where_ref[0] == where_ref[1] - 1, odd, right_ref[...].astype(jnp.float32))
    for x, cells in enumerate((left, even, odd, right)):
        for f in range(frames):
            own = cells[f * rows : (f + 1) * rows]
            for p in range(2):
                latent[f, x, pl.ds(8 + p, rows, stride=2), :] = own[:, p * ch : (p + 1) * ch]
            latent[f, x, 7:8, :] = own[:1, :ch]
            latent[f, x, 8 + height : 9 + height, :] = own[rows - 1 :, ch:]
    depth = 9 * ch
    for x in range(cols - 2):
        stacked = []
        for f in range(frames):
            taps = [latent[f, x + b, 7 + e : 7 + e + height, :] for b in range(3) for e in range(3)]
            stacked.append(jnp.concatenate(taps, axis=1).astype(jnp.bfloat16))
        stacked = [stacked[0]] * 2 + stacked
        acc = None
        for a in range(3):
            flat = jnp.concatenate(stacked[a : a + frames], axis=0)
            part = jnp.dot(
                flat, w_ref[a * depth : (a + 1) * depth, :], preferred_element_type=jnp.float32
            )
            acc = part if acc is None else acc + part
        acc = (acc + bias_ref[...]).astype(jnp.bfloat16)
        out_ref[:, x] = acc.reshape(frames, height, acc.shape[1])


def convolve(where, even, odd, left, right, conv_weight, conv_bias):
    rows = even.shape[0] // FRAMES
    channels = conv_weight.shape[1]
    smem = pl.BlockSpec(memory_space=pltpu.SMEM)
    vmem = pl.BlockSpec(memory_space=pltpu.VMEM)
    return pl.pallas_call(
        convolve_kernel,
        in_specs=[smem] + [vmem] * 6,
        out_specs=vmem,
        out_shape=jax.ShapeDtypeStruct((FRAMES, 2, 2 * rows, channels), jnp.bfloat16),
        scratch_shapes=[pltpu.VMEM((FRAMES, 4, 2 * rows + 16, LATENT_CH), jnp.float32)],
        compiler_params=pltpu.CompilerParams(vmem_limit_bytes=VMEM_LIMIT),
    )(where, even, odd, left, right, conv_weight, conv_bias[None])


def gather_plane(batch):
    planes = lax.axis_size("plane")
    same = [batch] + [swap(batch, "plane", d) for d in range(2, planes, 2)]
    same = jnp.concatenate(same, axis=0)
    return [same, swap(same, "plane", 1)]


def shards(queries, keys, values, w_out, shift_mod, scale_mod, w_final, conv_weight, conv_bias):
    groups = lax.axis_size("heads")
    planes = lax.axis_size("plane")
    heads_at = lax.axis_index("heads")
    plane_at = lax.axis_index("plane")
    devices = groups * planes
    tokens, width = queries.shape
    group_width = width // groups
    rows_dev = tokens // devices

    def group_of(source, r):
        return lax.dynamic_slice_in_dim(source, (heads_at ^ r) * group_width, group_width, axis=1)

    piece = [jnp.stack([group_of(keys, r), group_of(values, r)]) for r in range(groups)]
    got = [piece[0]] + [swap(piece[r], "heads", r) for r in range(1, groups)]

    to = lax.broadcasted_iota(jnp.int32, (tokens, tokens), 0)
    at = lax.broadcasted_iota(jnp.int32, (tokens, tokens), 1)
    j, u, row = to // (groups * rows_dev), (to // rows_dev) % groups, to % rows_dev
    place = row * devices + (u ^ heads_at) * planes + (j ^ plane_at)
    mixed = jnp.concatenate([group_of(queries, r) for r in range(groups)], axis=1)
    mixed = jnp.dot((at == place).astype(jnp.bfloat16), mixed, preferred_element_type=jnp.float32)
    mixed = mixed.astype(jnp.bfloat16).reshape(planes, groups, rows_dev, width)
    in_plane = jnp.stack([mixed[0]] + [swap(mixed[d], "plane", d) for d in range(1, planes)], axis=1)
    in_plane = in_plane.reshape(groups, planes * rows_dev, width)

    early = gather_plane(jnp.stack([got[r] for r in EARLY]))
    late = gather_plane(jnp.stack([got[r] for r in LATE]))
    keys_values = [kv.reshape((-1, 2) + kv.shape[1:]) for kv in early + late]

    asked = []
    for r in range(groups):
        lanes = slice(r * group_width, (r + 1) * group_width)
        own = jnp.stack([in_plane[r ^ t, :, lanes] for t in range(groups)])
        asked.append(own if r == 0 else swap(own, "heads", r))

    attended = [None] * groups
    for targets in (LATE, EARLY):
        for t, result in zip(targets, attend(asked, keys_values, targets)):
            attended[t] = result if t == 0 else swap(result, "heads", t)

    where = jnp.stack([heads_at, plane_at]).astype(jnp.int32)
    even, odd = final_layer(where, attended, w_out, scale_mod, shift_mod, w_final, rows_dev, planes)
    both = ("heads", "plane")
    left = lax.ppermute(odd, both, [(i, i + 1) for i in range(devices - 1)])
    right = lax.ppermute(even, both, [(i + 1, i) for i in range(devices - 1)])
    spot = jnp.stack([heads_at * planes + plane_at, jnp.int32(devices)]).astype(jnp.int32)
    return convolve(spot, even, odd, left, right, conv_weight, conv_bias)


def solution(mesh):
    groups, seq = mesh.devices.shape
    split = Mesh(
        mesh.devices.reshape(groups, HEAD_GROUPS, seq // HEAD_GROUPS), ("groups", "heads", "plane")
    )
    by_token = P(("groups", "heads", "plane"), None)
    placed = (by_token, by_token, by_token, P(), P("groups"), P("groups"), P(), P(), P())
    return jax.shard_map(
        shards,
        mesh=split,
        in_specs=placed,
        out_specs=P("groups", ("heads", "plane"), None, None),
        check_vma=False,
    )
```

time: 124 us -> 93.4 us (0.75)
  blocking collectives: 42.7 us -> 0 us
  starting transfers between devices: 4.33 us -> 33.1 us
  between operations: 13.5 us -> 0.19 us
  waiting for transfers between devices: 32.5 us -> 24.9 us
  Pallas kernels: 15.8 us -> 22.3 us
  local copies, waits for them, and re-layouts: 13.6 us -> 7.69 us
  other arithmetic: 0.16 us -> 3.63 us
    all_to_all x2 -> x0, blocking collectives: 42.7 us -> none  [the longest x1 32.9 us: shards(): lax.all_to_all(pieces, 'heads', split_axis=0, concat_axis=0, tiled=True)]
    ppermute x0 -> x18, starting transfers between devices: none -> 33.1 us  [the longest x16 26.9 us: swap(): return lax.ppermute(source, axis, [(i, i ^ distance) for i in range(count)])]
    all_gather x1 -> x0, waiting for transfers between devices: 29 us -> none  [shards(): keys_values = lax.all_gather(got[:, 1:], 'plane')]
    ppermute x0 -> x18, waiting for transfers between devices: none -> 24.9 us  [the longest x16 22 us: swap(): return lax.ppermute(source, axis, [(i, i ^ distance) for i in range(count)])]
    pallas_call x3 -> x4, Pallas kernels: 15.8 us -> 22.3 us  [the longest x2 10.6 us: attend(): pl.pallas_call(functools.partial(attend_kernel, sources=sources, parts=le...]
    concatenate x1 -> x0, local copies, waits for them, and re-layouts: 6.15 us -> none  [final_layer(): jnp.concatenate([by_cell[:, i] for i in (1, 0, 1, 0, 0, 0, 1, 1)], axis=1)]
    all_to_all x1 -> x0, starting transfers between devices: 4.32 us -> none  [shards(): lax.all_to_all(result, 'heads', split_axis=0, concat_axis=0, tiled=True)]
    all_to_all x1 -> x0, waiting for transfers between devices: 3.49 us -> none  [shards(): lax.all_to_all(result, 'heads', split_axis=0, concat_axis=0, tiled=True)]
  transfers between devices with their start and end apart: 2 -> 18, of which waited for: 2 -> 8; matrix products, arithmetic and copies ran while one was open for 7% -> 9% of each run, Pallas kernels for 0% -> 6%
where the time goes in v2:
time: 93.4 us; the launch traced here: 92.3 us
  starting transfers between devices  33.1 us (35%)
  waiting for transfers between devices  24.9 us (27%)
  Pallas kernels  22.3 us (24%)
  local copies, waits for them, and re-layouts  7.69 us (8%)
  other arithmetic  3.63 us (4%)
    ppermute x16, starting transfers between devices, swap(): return lax.ppermute(source, axis, [(i, i ^ distance) for i in range(count)])  26.9 us
    ppermute x16, waiting for transfers between devices, swap(): return lax.ppermute(source, axis, [(i, i ^ distance) for i in range(count)])  22 us
    pallas_call x2, Pallas kernels, attend(): pl.pallas_call(functools.partial(attend_kernel, sources=sources, parts=le...  10.6 us
    pallas_call x1, Pallas kernels, final_layer(): pl.pallas_call(functools.partial(final_kernel, groups=groups, planes=plan...  9.01 us
    unnamed x19, local copies, waits for them, and re-layouts  4.58 us
    ppermute x1, starting transfers between devices, shards(): left = lax.ppermute(odd, both, [(i, i + 1) for i in range(devices - 1)])  4.28 us
    ppermute x1, waiting for transfers between devices, shards(): right = lax.ppermute(even, both, [(i + 1, i) for i in range(devices - 1)])  2.92 us
    pallas_call x1, Pallas kernels, convolve(): pl.pallas_call(convolve_kernel, in_specs=[smem] + [vmem] * 6, out_specs=v...  2.72 us
  transfers between devices with their start and end apart: 18, of which 8 were waited for; matrix products, arithmetic and copies ran while one was open for 9% of the time, Pallas kernels for 6%

profile of v2, /device:TPU:1, one launch (start us, length us, event | category | flops | bytes accessed | tf_op | source)
XLA Modules:
  0.0 92.3 jit_solution(16808362994670084618)
XLA Ops:
  0.0 1.3 %dynamic-slice_bitcast_fusion.2 = (bf16[1,128,384]{2,1,0:T(8,128)(2,1)S(1)}, bf16[1,128,384]{2,1,0:T(8,128)(2,1)S(1)}, bf16[1,128,384]{2,1,0:T(8,128)(2,1)S(1)},...) fusion(bf16[128,1536]{1,0:T(8,128)(2,1)} %param.11, ...), kind=kLoop, calls=%fused_computation.29 | loop fusion | bytes 1572880 | tf_op jit(solution)/shard_map/stack | solution.py:237
  1.3 2.2 %collective-permute-start.6 = (bf16[2,128,384]{2,1,0:T(8,128)(2,1)S(1)}, bf16[2,128,384]{2,1,0:T(8,128)(2,1)S(1)}, u32[]{:S(2)}, u32[]{:S(2)}) collective-permute-start(bf16[2,128,384]{2,1,0:T(8,128)(2,1)S(1)} %pad_maximum_fusion.4), channel_id=1, source_target_pairs={{0,4},{4,0},{8,12},{12,8},{1,5},{5,1},{9,13},{13,9},{2,6},{6,2},{1... | collective-permute-start | bytes 589832 | tf_op jit(solution)/shard_map/ppermute | solution.py:23
  3.6 2.3 %collective-permute-start.10 = (bf16[2,128,384]{2,1,0:T(8,128)(2,1)S(1)}, bf16[2,128,384]{2,1,0:T(8,128)(2,1)S(1)}, u32[]{:S(2)}, u32[]{:S(2)}) collective-permute-start(bf16[2,128,384]{2,1,0:T(8,128)(2,1)S(1)} %pad_maximum_fusion.6), channel_id=1, source_target_pairs={{0,12},{4,8},{8,4},{12,0},{1,13},{5,9},{9,5},{13,1},{2,14},{6,10},... | collective-permute-start | bytes 589832 | tf_op jit(solution)/shard_map/ppermute | solution.py:23
  5.9 0.2 collective-permute-start.9
  6.1 1.1 %constant_dynamic-slice_fusion.3 = (bf16[128,384]{1,0:T(8,128)(2,1)S(1)}, bf16[128,384]{1,0:T(8,128)(2,1)S(1)}, bf16[128,384]{1,0:T(8,128)(2,1)S(1)}, bf16[128,384]{1,0:T(8,128)(2,1)S(1)}) fusion(bf16[128,1536]{1,0:T(8,128)(2,1)} %param.9, s32[]{:T(128)S(6)} %select_n.43, s32[]{:T(128)S(6)} %select_n.44, s32[]{:T(128)S(6)} %select_n.46, s32[]{:T(128)S(6)} %select_n.45), kind=kLoop, calls=%fused_computation.64 | loop fusion | bytes 786448 | tf_op jit(solution)/shard_map/dynamic_slice | solution.py:235
  7.2 0.4 convolution_convert_fusion
  7.6 0.5 collective-permute-done.6
  8.2 1.1 %collective-permute-start.7 = (bf16[2,2,128,384]{3,2,1,0:T(8,128)(2,1)S(1)}, bf16[2,2,128,384]{3,2,1,0:T(8,128)(2,1)S(1)}, u32[]{:S(2)}, u32[]{:S(2)}) collective-permute-start(bf16[2,2,128,384]{3,2,1,0:T(8,128)(2,1)S(1)} %pad_maximum_fusion.2), channel_id=1, source_target_pairs={{0,2},{1,3},{2,0},{3,1},{4,6},{5,7},{6,4},{7,5},{8,10},{9,11},{10,... | collective-permute-start | bytes 1179656 | tf_op jit(solution)/shard_map/ppermute | solution.py:23
  9.4 2.3 %collective-permute-start.2 = (bf16[4,8,1536]{2,1,0:T(8,128)(2,1)S(1)}, bf16[4,8,1536]{2,1,0:T(8,128)(2,1)S(1)}, u32[]{:S(2)}, u32[]{:S(2)}) collective-permute-start(bf16[4,8,1536]{2,1,0:T(8,128)(2,1)S(1)} %get-tuple-element.36), channel_id=1, source_target_pairs={{0,3},{1,2},{2,1},{3,0},{4,7},{5,6},{6,5},{7,4},{8,11},{9,10},{10,... | collective-permute-start | bytes 294920 | tf_op jit(solution)/shard_map/ppermute | solution.py:23
  11.6 1.2 %collective-permute-start.1 = (bf16[4,8,1536]{2,1,0:T(8,128)(2,1)S(1)}, bf16[4,8,1536]{2,1,0:T(8,128)(2,1)S(1)}, u32[]{:S(2)}, u32[]{:S(2)}) collective-permute-start(bf16[4,8,1536]{2,1,0:T(8,128)(2,1)S(1)} %get-tuple-element.37), channel_id=1, source_target_pairs={{0,2},{1,3},{2,0},{3,1},{4,6},{5,7},{6,4},{7,5},{8,10},{9,11},{10,... | collective-permute-start | bytes 294920 | tf_op jit(solution)/shard_map/ppermute | solution.py:23
  12.9 1.4 %collective-permute-done.10 = bf16[2,128,384]{2,1,0:T(8,128)(2,1)S(1)} collective-permute-done((bf16[2,128,384]{2,1,0:T(8,128)(2,1)S(1)}, bf16[2,128,384]{2,1,0:T(8,128)(2,1)S(1)}, u32[]{:S(2)}, u32[]{:S(2)}) %collective-permute-start.10) | collective-permute-done | bytes 196640 | tf_op jit(solution)/shard_map/ppermute | solution.py:23
  14.3 2.7 %collective-permute-start = (bf16[4,8,1536]{2,1,0:T(8,128)(2,1)S(1)}, bf16[4,8,1536]{2,1,0:T(8,128)(2,1)S(1)}, u32[]{:S(2)}, u32[]{:S(2)}) collective-permute-start(bf16[4,8,1536]{2,1,0:T(8,128)(2,1)S(1)} %get-tuple-element.38), channel_id=1, source_target_pairs={{0,1},{1,0},{2,3},{3,2},{4,5},{5,4},{6,7},{7,6},{8,9},{9,8},{10,11... | collective-permute-start | bytes 294920 | tf_op jit(solution)/shard_map/ppermute | solution.py:23
  17.0 5.8 %collective-permute-done.9 = bf16[2,128,384]{2,1,0:T(8,128)(2,1)S(1)} collective-permute-done((bf16[2,128,384]{2,1,0:T(8,128)(2,1)S(1)}, bf16[2,128,384]{2,1,0:T(8,128)(2,1)S(1)}, u32[]{:S(2)}, u32[]{:S(2)}) %collective-permute-start.9) | collective-permute-done | bytes 196640 | tf_op jit(solution)/shard_map/ppermute | solution.py:23
  22.9 1.3 %collective-permute-start.11 = (bf16[2,2,128,384]{3,2,1,0:T(8,128)(2,1)S(1)}, bf16[2,2,128,384]{3,2,1,0:T(8,128)(2,1)S(1)}, u32[]{:S(2)}, u32[]{:S(2)}) collective-permute-start(bf16[2,2,128,384]{3,2,1,0:T(8,128)(2,1)S(1)} %pad_maximum_fusion.3), channel_id=1, source_target_pairs={{0,2},{1,3},{2,0},{3,1},{4,6},{5,7},{6,4},{7,5},{8,10},{9,11},{10,... | collective-permute-start | bytes 1179656 | tf_op jit(solution)/shard_map/ppermute | solution.py:23
  24.2 0.0 collective-permute-done.2
  24.2 0.0 collective-permute-done.1
  24.2 0.0 collective-permute-done
  24.2 0.1 maximum_bitcast_fusion
  24.3 0.0 collective-permute-done.7
  24.3 0.1 pad_maximum_fusion
  24.4 0.0 copy-start
  24.4 1.9 %collective-permute-start.8 = (bf16[4,2,128,384]{3,2,1,0:T(8,128)(2,1)S(1)}, bf16[4,2,128,384]{3,2,1,0:T(8,128)(2,1)S(1)}, u32[]{:S(2)}, u32[]{:S(2)}) collective-permute-start(bf16[4,2,128,384]{3,2,1,0:T(8,128)(2,1)S(1)} %pad_maximum_fusion), channel_id=1, source_target_pairs={{0,1},{1,0},{2,3},{3,2},{4,5},{5,4},{6,7},{7,6},{8,9},{9,8},{10,11... | collective-permute-start | bytes 2359304 | tf_op jit(solution)/shard_map/ppermute | solution.py:23
  26.3 5.8 %collective-permute-done.11 = bf16[2,2,128,384]{3,2,1,0:T(8,128)(2,1)S(1)} collective-permute-done((bf16[2,2,128,384]{3,2,1,0:T(8,128)(2,1)S(1)}, bf16[2,2,128,384]{3,2,1,0:T(8,128)(2,1)S(1)}, u32[]{:S(2)}, u32[]{:S(2)}) %collective-permute-start.11) | collective-permute-done | bytes 393248 | tf_op jit(solution)/shard_map/ppermute | solution.py:23
  32.1 0.1 pad_maximum_fusion.1
  32.2 0.0 copy-start.1
  32.2 2.5 %collective-permute-start.12 = (bf16[4,2,128,384]{3,2,1,0:T(8,128)(2,1)S(1)}, bf16[4,2,128,384]{3,2,1,0:T(8,128)(2,1)S(1)}, u32[]{:S(2)}, u32[]{:S(2)}) collective-permute-start(bf16[4,2,128,384]{3,2,1,0:T(8,128)(2,1)S(1)} %pad_maximum_fusion.1), channel_id=1, source_target_pairs={{0,1},{1,0},{2,3},{3,2},{4,5},{5,4},{6,7},{7,6},{8,9},{9,8},{10,11... | collective-permute-start | bytes 2359304 | tf_op jit(solution)/shard_map/ppermute | solution.py:23
  34.7 0.7 pad_maximum_fusion.7
  35.4 0.0 collective-permute-start.3
  35.4 0.7 pad_maximum_fusion.8
  36.1 2.4 %collective-permute-start.4 = (bf16[4,32,384]{2,1,0:T(8,128)(2,1)}, bf16[4,32,384]{2,1,0:T(8,128)(2,1)}, u32[]{:S(2)}, u32[]{:S(2)}) collective-permute-start(bf16[4,32,384]{2,1,0:T(8,128)(2,1)} %pad_maximum_fusion.8), channel_id=1, source_target_pairs={{0,8},{4,12},{8,0},{12,4},{1,9},{5,13},{9,1},{13,5},{2,10},{6,14},... | collective-permute-start | bytes 294920 | tf_op jit(solution)/shard_map/ppermute | solution.py:23
  38.5 0.7 pad_maximum_fusion.9
  39.1 1.1 %collective-permute-start.5 = (bf16[4,32,384]{2,1,0:T(8,128)(2,1)}, bf16[4,32,384]{2,1,0:T(8,128)(2,1)}, u32[]{:S(2)}, u32[]{:S(2)}) collective-permute-start(bf16[4,32,384]{2,1,0:T(8,128)(2,1)} %pad_maximum_fusion.9), channel_id=1, source_target_pairs={{0,12},{4,8},{8,4},{12,0},{1,13},{5,9},{9,5},{13,1},{2,14},{6,10},... | collective-permute-start | bytes 294920 | tf_op jit(solution)/shard_map/ppermute | solution.py:23
  40.3 2.2 %copy.11.refs_7_ = bf16[3072,64]{1,0:T(8,128)(2,1)} copy(bf16[3072,64]{0,1:T(8,128)(2,1)} %param.15) | data formatting | bytes 786432 | tf_op args[6]
  42.4 0.7 slice.76.refs_0_
  43.1 0.0 collective-permute-done.3.refs_1_
  43.1 0.6 collective-permute-done.4.refs_2_
  43.7 1.1 %collective-permute-done.5.refs_3_ = bf16[4,32,384]{2,1,0:T(8,128)(2,1)} collective-permute-done((bf16[4,32,384]{2,1,0:T(8,128)(2,1)}, bf16[4,32,384]{2,1,0:T(8,128)(2,1)}, u32[]{:S(2)}, u32[]{:S(2)}) %collective-permute-start.5) | collective-permute-done | bytes 98336 | tf_op jit(solution)/shard_map/ppermute | solution.py:23
  44.8 0.0 collective-permute-done.8
  44.8 0.0 collective-permute-done.12
  44.8 0.0 copy-start.3
  44.8 0.0 copy-done
  44.9 0.0 copy-done.1
  44.9 0.9 copy-done.2
  45.7 0.3 copy-done.3
  46.0 5.3 %shard_map.91 = (bf16[4,32,384]{2,1,0:T(8,128)(2,1)}, bf16[4,32,384]{2,1,0:T(8,128)(2,1)}) custom-call(bf16[4,32,384]{2,1,0:T(8,128)(2,1)} %slice.76.refs_0_, bf16[4,32,384]{2,1,0:T(8,128)(2,1)} %collective-permute-done.3.refs_1_, bf16[4,32,384]{2,1,0:T(8,128)(2,1)} %collective-permute-done.4.refs_2_, bf16[4,32,384]{2,1,0:T(8,128)(2,1)} %collective-permute-done.5.refs_3_, ...), custom_call_target="tpu_custom_call" | custom-call | tf_op jit(solution)/shard_map/pallas_call | solution.py:63
  51.3 3.5 %collective-permute-start.13 = (bf16[4,32,384]{2,1,0:T(8,128)(2,1)}, bf16[4,32,384]{2,1,0:T(8,128)(2,1)S(1)}, u32[]{:S(2)}, u32[]{:S(2)}) collective-permute-start(bf16[4,32,384]{2,1,0:T(8,128)(2,1)} %get-tuple-element.12), channel_id=1, source_target_pairs={{0,4},{4,0},{8,12},{12,8},{1,5},{5,1},{9,13},{13,9},{2,6},{6,2},{1... | collective-permute-start | bytes 294920 | tf_op jit(solution)/shard_map/ppermute | solution.py:23
  54.7 5.3 %shard_map.92 = (bf16[4,32,384]{2,1,0:T(8,128)(2,1)}, bf16[4,32,384]{2,1,0:T(8,128)(2,1)}) custom-call(bf16[4,32,384]{2,1,0:T(8,128)(2,1)} %slice.76.refs_0_, bf16[4,32,384]{2,1,0:T(8,128)(2,1)} %collective-permute-done.3.refs_1_, bf16[4,32,384]{2,1,0:T(8,128)(2,1)} %collective-permute-done.4.refs_2_, bf16[4,32,384]{2,1,0:T(8,128)(2,1)} %collective-permute-done.5.refs_3_, ...), custom_call_target="tpu_custom_call" | custom-call | tf_op jit(solution)/shard_map/pallas_call | solution.py:63
  60.0 1.0 %collective-permute-start.14 = (bf16[4,32,384]{2,1,0:T(8,128)(2,1)}, bf16[4,32,384]{2,1,0:T(8,128)(2,1)S(1)}, u32[]{:S(2)}, u32[]{:S(2)}) collective-permute-start(bf16[4,32,384]{2,1,0:T(8,128)(2,1)} %get-tuple-element.13), channel_id=1, source_target_pairs={{0,8},{4,12},{8,0},{12,4},{1,9},{5,13},{9,1},{13,5},{2,10},{6,14},... | collective-permute-start | bytes 294920 | tf_op jit(solution)/shard_map/ppermute | solution.py:23
  61.0 1.2 %collective-permute-start.15 = (bf16[4,32,384]{2,1,0:T(8,128)(2,1)}, bf16[4,32,384]{2,1,0:T(8,128)(2,1)S(1)}, u32[]{:S(2)}, u32[]{:S(2)}) collective-permute-start(bf16[4,32,384]{2,1,0:T(8,128)(2,1)} %get-tuple-element.14), channel_id=1, source_target_pairs={{0,12},{4,8},{8,4},{12,0},{1,13},{5,9},{9,5},{13,1},{2,14},{6,10},... | collective-permute-start | bytes 294920 | tf_op jit(solution)/shard_map/ppermute | solution.py:23
  62.2 0.6 pad_add_fusion.1.where_ref
  62.8 0.0 collective-permute-done.13.refs_1_
  62.8 6.7 %collective-permute-done.14.refs_2_ = bf16[4,32,384]{2,1,0:T(8,128)(2,1)S(1)} collective-permute-done((bf16[4,32,384]{2,1,0:T(8,128)(2,1)}, bf16[4,32,384]{2,1,0:T(8,128)(2,1)S(1)}, u32[]{:S(2)}, u32[]{:S(2)}) %collective-permute-start.14) | collective-permute-done | bytes 98336 | tf_op jit(solution)/shard_map/ppermute | solution.py:23
  69.5 0.0 collective-permute-done.15.refs_3_
  69.5 0.0 copy-done.4
  69.5 0.6 copy-done.5
  70.2 0.1 copy-done.6
  70.2 9.0 %shard_map.93 = (bf16[128,32]{1,0:T(8,128)(2,1)}, bf16[128,32]{1,0:T(8,128)(2,1)}) custom-call(s32[2]{0:T(128)} %pad_add_fusion.1.where_ref, bf16[4,32,384]{2,1,0:T(8,128)(2,1)} %get-tuple-element.11.refs_0_, bf16[4,32,384]{2,1,0:T(8,128)(2,1)} %copy-done.4, bf16[4,32,384]{2,1,0:T(8,128)(2,1)} %copy-done.5, bf16[4,32,384]{2,1,0:T(8,128)(2,1)} %copy-done.6, ...), custom_call_target="tpu_custom_call" | custom-call | tf_op jit(solution)/shard_map/pallas_call | solution.py:149
  79.2 4.3 %collective-permute-start.16 = (bf16[128,32]{1,0:T(8,128)(2,1)}, bf16[128,32]{1,0:T(8,128)(2,1)S(1)}, u32[]{:S(2)}, u32[]{:S(2)}) collective-permute-start(bf16[128,32]{1,0:T(8,128)(2,1)} %get-tuple-element.16.odd_ref), channel_id=1, source_target_pairs={{0,1},{1,2},{2,3},{3,4},{4,5},{5,6},{6,7},{7,8},{8,9},{9,10},{10,1... | collective-permute-start | bytes 24584 | tf_op jit(solution)/shard_map/ppermute | solution.py:268
  83.5 1.9 %collective-permute-start.17 = (bf16[128,32]{1,0:T(8,128)(2,1)}, bf16[128,32]{1,0:T(8,128)(2,1)S(1)}, u32[]{:S(2)}, u32[]{:S(2)}) collective-permute-start(bf16[128,32]{1,0:T(8,128)(2,1)} %get-tuple-element.15.even_ref), channel_id=1, source_target_pairs={{1,0},{2,1},{3,2},{4,3},{5,4},{6,5},{7,6},{8,7},{9,8},{10,9},{11,1... | collective-permute-start | bytes 24584 | tf_op jit(solution)/shard_map/ppermute | solution.py:269
  85.4 0.6 pad_add_fusion.where_ref
  86.0 0.0 collective-permute-done.16.left_ref
  86.0 2.9 %collective-permute-done.17.right_ref = bf16[128,32]{1,0:T(8,128)(2,1)S(1)} collective-permute-done((bf16[128,32]{1,0:T(8,128)(2,1)}, bf16[128,32]{1,0:T(8,128)(2,1)S(1)}, u32[]{:S(2)}, u32[]{:S(2)}) %collective-permute-start.17) | collective-permute-done | bytes 8224 | tf_op jit(solution)/shard_map/ppermute | solution.py:269
  89.0 0.6 copy-done.8
  89.6 2.7 %shard_map.94 = bf16[4,2,64,512]{3,2,1,0:T(8,128)(2,1)} custom-call(s32[2]{0:T(128)} %pad_add_fusion.where_ref, bf16[128,32]{1,0:T(8,128)(2,1)} %get-tuple-element.15.even_ref, bf16[128,32]{1,0:T(8,128)(2,1)} %get-tuple-element.16.odd_ref, bf16[128,32]{1,0:T(8,128)(2,1)} %copy-done.7, bf16[128,32]{1,0:T(8,128)(2,1)} %copy-done.8, bf16[432,512]{1,0:T(8,128)(2,1)} %w_ref.1, ...), custom_call_target="tpu_custom_call" | custom-call | tf_op jit(solution)/shard_map/pallas_call | solution.py:207
  (21 shorter events, 0.3 us)
Async XLA Ops:
  1.3 6.8 %collective-permute-start.6 = (bf16[2,128,384]{2,1,0:T(8,128)(2,1)S(1)}, bf16[2,128,384]{2,1,0:T(8,128)(2,1)S(1)}, u32[]{:S(2)}, u32[]{:S(2)}) collective-permute-start(bf16[2,128,384]{2,1,0:T(8,128)(2,1)S(1)} %pad_maximum_fusion.4), channel_id=1, source_target_pairs={{0,4},{4,0},{8,12},{12,8},{1,5},{5,1},{9,13},{13,9},{2,6},{6,2},{1... | collective-permute-start | bytes 589832 | tf_op jit(solution)/shard_map/ppermute | solution.py:23
  3.6 10.7 %collective-permute-start.10 = (bf16[2,128,384]{2,1,0:T(8,128)(2,1)S(1)}, bf16[2,128,384]{2,1,0:T(8,128)(2,1)S(1)}, u32[]{:S(2)}, u32[]{:S(2)}) collective-permute-start(bf16[2,128,384]{2,1,0:T(8,128)(2,1)S(1)} %pad_maximum_fusion.6), channel_id=1, source_target_pairs={{0,12},{4,8},{8,4},{12,0},{1,13},{5,9},{9,5},{13,1},{2,14},{6,10},... | collective-permute-start | bytes 589832 | tf_op jit(solution)/shard_map/ppermute | solution.py:23
  5.9 17.0 %collective-permute-start.9 = (bf16[2,128,384]{2,1,0:T(8,128)(2,1)S(1)}, bf16[2,128,384]{2,1,0:T(8,128)(2,1)S(1)}, u32[]{:S(2)}, u32[]{:S(2)}) collective-permute-start(bf16[2,128,384]{2,1,0:T(8,128)(2,1)S(1)} %pad_maximum_fusion.5), channel_id=1, source_target_pairs={{0,8},{4,12},{8,0},{12,4},{1,9},{5,13},{9,1},{13,5},{2,10},{6,14},... | collective-permute-start | bytes 589832 | tf_op jit(solution)/shard_map/ppermute | solution.py:23
  8.2 16.1 %collective-permute-start.7 = (bf16[2,2,128,384]{3,2,1,0:T(8,128)(2,1)S(1)}, bf16[2,2,128,384]{3,2,1,0:T(8,128)(2,1)S(1)}, u32[]{:S(2)}, u32[]{:S(2)}) collective-permute-start(bf16[2,2,128,384]{3,2,1,0:T(8,128)(2,1)S(1)} %pad_maximum_fusion.2), channel_id=1, source_target_pairs={{0,2},{1,3},{2,0},{3,1},{4,6},{5,7},{6,4},{7,5},{8,10},{9,11},{10,... | collective-permute-start | bytes 1179656 | tf_op jit(solution)/shard_map/ppermute | solution.py:23
  9.4 14.9 %collective-permute-start.2 = (bf16[4,8,1536]{2,1,0:T(8,128)(2,1)S(1)}, bf16[4,8,1536]{2,1,0:T(8,128)(2,1)S(1)}, u32[]{:S(2)}, u32[]{:S(2)}) collective-permute-start(bf16[4,8,1536]{2,1,0:T(8,128)(2,1)S(1)} %get-tuple-element.36), channel_id=1, source_target_pairs={{0,3},{1,2},{2,1},{3,0},{4,7},{5,6},{6,5},{7,4},{8,11},{9,10},{10,... | collective-permute-start | bytes 294920 | tf_op jit(solution)/shard_map/ppermute | solution.py:23
  11.6 12.6 %collective-permute-start.1 = (bf16[4,8,1536]{2,1,0:T(8,128)(2,1)S(1)}, bf16[4,8,1536]{2,1,0:T(8,128)(2,1)S(1)}, u32[]{:S(2)}, u32[]{:S(2)}) collective-permute-start(bf16[4,8,1536]{2,1,0:T(8,128)(2,1)S(1)} %get-tuple-element.37), channel_id=1, source_target_pairs={{0,2},{1,3},{2,0},{3,1},{4,6},{5,7},{6,4},{7,5},{8,10},{9,11},{10,... | collective-permute-start | bytes 294920 | tf_op jit(solution)/shard_map/ppermute | solution.py:23
  14.3 9.9 %collective-permute-start = (bf16[4,8,1536]{2,1,0:T(8,128)(2,1)S(1)}, bf16[4,8,1536]{2,1,0:T(8,128)(2,1)S(1)}, u32[]{:S(2)}, u32[]{:S(2)}) collective-permute-start(bf16[4,8,1536]{2,1,0:T(8,128)(2,1)S(1)} %get-tuple-element.38), channel_id=1, source_target_pairs={{0,1},{1,0},{2,3},{3,2},{4,5},{5,4},{6,7},{7,6},{8,9},{9,8},{10,11... | collective-permute-start | bytes 294920 | tf_op jit(solution)/shard_map/ppermute | solution.py:23
  22.9 9.1 %collective-permute-start.11 = (bf16[2,2,128,384]{3,2,1,0:T(8,128)(2,1)S(1)}, bf16[2,2,128,384]{3,2,1,0:T(8,128)(2,1)S(1)}, u32[]{:S(2)}, u32[]{:S(2)}) collective-permute-start(bf16[2,2,128,384]{3,2,1,0:T(8,128)(2,1)S(1)} %pad_maximum_fusion.3), channel_id=1, source_target_pairs={{0,2},{1,3},{2,0},{3,1},{4,6},{5,7},{6,4},{7,5},{8,10},{9,11},{10,... | collective-permute-start | bytes 1179656 | tf_op jit(solution)/shard_map/ppermute | solution.py:23
  24.4 20.4 %copy-start = (bf16[4,2,128,384]{3,2,1,0:T(8,128)(2,1)}, bf16[4,2,128,384]{3,2,1,0:T(8,128)(2,1)S(1)}, u32[]{:S(2)}) copy-start(bf16[4,2,128,384]{3,2,1,0:T(8,128)(2,1)S(1)} %pad_maximum_fusion) | copy-start | bytes 2359300
  24.4 20.4 %collective-permute-start.8 = (bf16[4,2,128,384]{3,2,1,0:T(8,128)(2,1)S(1)}, bf16[4,2,128,384]{3,2,1,0:T(8,128)(2,1)S(1)}, u32[]{:S(2)}, u32[]{:S(2)}) collective-permute-start(bf16[4,2,128,384]{3,2,1,0:T(8,128)(2,1)S(1)} %pad_maximum_fusion), channel_id=1, source_target_pairs={{0,1},{1,0},{2,3},{3,2},{4,5},{5,4},{6,7},{7,6},{8,9},{9,8},{10,11... | collective-permute-start | bytes 2359304 | tf_op jit(solution)/shard_map/ppermute | solution.py:23
  32.2 12.7 %copy-start.1 = (bf16[4,2,128,384]{3,2,1,0:T(8,128)(2,1)}, bf16[4,2,128,384]{3,2,1,0:T(8,128)(2,1)S(1)}, u32[]{:S(2)}) copy-start(bf16[4,2,128,384]{3,2,1,0:T(8,128)(2,1)S(1)} %pad_maximum_fusion.1) | copy-start | bytes 2359300
  32.2 12.7 %collective-permute-start.12 = (bf16[4,2,128,384]{3,2,1,0:T(8,128)(2,1)S(1)}, bf16[4,2,128,384]{3,2,1,0:T(8,128)(2,1)S(1)}, u32[]{:S(2)}, u32[]{:S(2)}) collective-permute-start(bf16[4,2,128,384]{3,2,1,0:T(8,128)(2,1)S(1)} %pad_maximum_fusion.1), channel_id=1, source_target_pairs={{0,1},{1,0},{2,3},{3,2},{4,5},{5,4},{6,7},{7,6},{8,9},{9,8},{10,11... | collective-permute-start | bytes 2359304 | tf_op jit(solution)/shard_map/ppermute | solution.py:23
  35.4 7.7 %collective-permute-start.3 = (bf16[4,32,384]{2,1,0:T(8,128)(2,1)}, bf16[4,32,384]{2,1,0:T(8,128)(2,1)}, u32[]{:S(2)}, u32[]{:S(2)}) collective-permute-start(bf16[4,32,384]{2,1,0:T(8,128)(2,1)} %pad_maximum_fusion.7), channel_id=1, source_target_pairs={{0,4},{4,0},{8,12},{12,8},{1,5},{5,1},{9,13},{13,9},{2,6},{6,2},{1... | collective-permute-start | bytes 294920 | tf_op jit(solution)/shard_map/ppermute | solution.py:23
  36.1 7.7 %collective-permute-start.4 = (bf16[4,32,384]{2,1,0:T(8,128)(2,1)}, bf16[4,32,384]{2,1,0:T(8,128)(2,1)}, u32[]{:S(2)}, u32[]{:S(2)}) collective-permute-start(bf16[4,32,384]{2,1,0:T(8,128)(2,1)} %pad_maximum_fusion.8), channel_id=1, source_target_pairs={{0,8},{4,12},{8,0},{12,4},{1,9},{5,13},{9,1},{13,5},{2,10},{6,14},... | collective-permute-start | bytes 294920 | tf_op jit(solution)/shard_map/ppermute | solution.py:23
  39.1 5.7 %collective-permute-start.5 = (bf16[4,32,384]{2,1,0:T(8,128)(2,1)}, bf16[4,32,384]{2,1,0:T(8,128)(2,1)}, u32[]{:S(2)}, u32[]{:S(2)}) collective-permute-start(bf16[4,32,384]{2,1,0:T(8,128)(2,1)} %pad_maximum_fusion.9), channel_id=1, source_target_pairs={{0,12},{4,8},{8,4},{12,0},{1,13},{5,9},{9,5},{13,1},{2,14},{6,10},... | collective-permute-start | bytes 294920 | tf_op jit(solution)/shard_map/ppermute | solution.py:23
  44.8 0.9 copy-start.2
  44.8 1.1 %copy-start.3 = (bf16[4,2,128,384]{3,2,1,0:T(8,128)(2,1)}, bf16[4,2,128,384]{3,2,1,0:T(8,128)(2,1)S(1)}, u32[]{:S(2)}) copy-start(bf16[4,2,128,384]{3,2,1,0:T(8,128)(2,1)S(1)} %collective-permute-done.12) | copy-start | bytes 2359300
  51.3 11.5 %collective-permute-start.13 = (bf16[4,32,384]{2,1,0:T(8,128)(2,1)}, bf16[4,32,384]{2,1,0:T(8,128)(2,1)S(1)}, u32[]{:S(2)}, u32[]{:S(2)}) collective-permute-start(bf16[4,32,384]{2,1,0:T(8,128)(2,1)} %get-tuple-element.12), channel_id=1, source_target_pairs={{0,4},{4,0},{8,12},{12,8},{1,5},{5,1},{9,13},{13,9},{2,6},{6,2},{1... | collective-permute-start | bytes 294920 | tf_op jit(solution)/shard_map/ppermute | solution.py:23
  60.0 9.5 %collective-permute-start.14 = (bf16[4,32,384]{2,1,0:T(8,128)(2,1)}, bf16[4,32,384]{2,1,0:T(8,128)(2,1)S(1)}, u32[]{:S(2)}, u32[]{:S(2)}) collective-permute-start(bf16[4,32,384]{2,1,0:T(8,128)(2,1)} %get-tuple-element.13), channel_id=1, source_target_pairs={{0,8},{4,12},{8,0},{12,4},{1,9},{5,13},{9,1},{13,5},{2,10},{6,14},... | collective-permute-start | bytes 294920 | tf_op jit(solution)/shard_map/ppermute | solution.py:23
  61.0 8.5 %collective-permute-start.15 = (bf16[4,32,384]{2,1,0:T(8,128)(2,1)}, bf16[4,32,384]{2,1,0:T(8,128)(2,1)S(1)}, u32[]{:S(2)}, u32[]{:S(2)}) collective-permute-start(bf16[4,32,384]{2,1,0:T(8,128)(2,1)} %get-tuple-element.14), channel_id=1, source_target_pairs={{0,12},{4,8},{8,4},{12,0},{1,13},{5,9},{9,5},{13,1},{2,14},{6,10},... | collective-permute-start | bytes 294920 | tf_op jit(solution)/shard_map/ppermute | solution.py:23
  62.8 6.7 %copy-start.4 = (bf16[4,32,384]{2,1,0:T(8,128)(2,1)}, bf16[4,32,384]{2,1,0:T(8,128)(2,1)S(1)}, u32[]{:S(2)}) copy-start(bf16[4,32,384]{2,1,0:T(8,128)(2,1)S(1)} %collective-permute-done.13.refs_1_) | copy-start | bytes 294916
  69.5 0.7 copy-start.5
  69.5 0.7 copy-start.6
  79.2 6.8 %collective-permute-start.16 = (bf16[128,32]{1,0:T(8,128)(2,1)}, bf16[128,32]{1,0:T(8,128)(2,1)S(1)}, u32[]{:S(2)}, u32[]{:S(2)}) collective-permute-start(bf16[128,32]{1,0:T(8,128)(2,1)} %get-tuple-element.16.odd_ref), channel_id=1, source_target_pairs={{0,1},{1,2},{2,3},{3,4},{4,5},{5,6},{6,7},{7,8},{8,9},{9,10},{10,1... | collective-permute-start | bytes 24584 | tf_op jit(solution)/shard_map/ppermute | solution.py:268
  83.5 5.4 %collective-permute-start.17 = (bf16[128,32]{1,0:T(8,128)(2,1)}, bf16[128,32]{1,0:T(8,128)(2,1)S(1)}, u32[]{:S(2)}, u32[]{:S(2)}) collective-permute-start(bf16[128,32]{1,0:T(8,128)(2,1)} %get-tuple-element.15.even_ref), channel_id=1, source_target_pairs={{1,0},{2,1},{3,2},{4,3},{5,4},{6,5},{7,6},{8,7},{9,8},{10,9},{11,1... | collective-permute-start | bytes 24584 | tf_op jit(solution)/shard_map/ppermute | solution.py:269
  86.0 2.9 %copy-start.7 = (bf16[128,32]{1,0:T(8,128)(2,1)}, bf16[128,32]{1,0:T(8,128)(2,1)S(1)}, u32[]{:S(2)}) copy-start(bf16[128,32]{1,0:T(8,128)(2,1)S(1)} %collective-permute-done.16.left_ref) | copy-start | bytes 24580
  88.9 0.6 copy-start.8

commit v3 on v2

v3 whole, which is shorter than its diff:
```python
import functools
import math

import jax
import jax.numpy as jnp
from jax import lax
from jax.experimental import pallas as pl
from jax.experimental.pallas import tpu as pltpu
from jax.sharding import Mesh
from jax.sharding import PartitionSpec as P

HEAD_DIM = 128
HEAD_GROUPS = 4
LATENT_CH = 16
FRAMES = 4
VMEM_LIMIT = 16 * 1024 * 1024
EXP2_SCALE = math.log2(math.e) / math.sqrt(HEAD_DIM)


def swap(source, axis, distance):
    count = lax.axis_size(axis)
    return lax.ppermute(source, axis, [(i, i ^ distance) for i in range(count)])


def attend_kernel(*refs, sources, parts, targets, rows_step):
    q_refs = refs[:sources]
    kv_refs = refs[sources : sources + parts]
    o_refs = refs[sources + parts :]
    rows, width = q_refs[0].shape[1:]
    key_rows = [r.shape[0] * r.shape[2] for r in kv_refs]
    works = [
        (h, range(first, min(first + rows_step, len(targets))))
        for h in range(width // HEAD_DIM)
        for first in range(0, len(targets), rows_step)
    ]

    def lanes(h):
        return slice(h * HEAD_DIM, (h + 1) * HEAD_DIM)

    def scores_of(work):
        h, block = work
        query = jnp.concatenate([q[targets[i], :, lanes(h)] for i in block for q in q_refs], axis=0)
        return [
            lax.dot_general(
                query,
                kv[:, 0, :, lanes(h)].reshape(count, HEAD_DIM),
                (((1,), (1,)), ((), ())),
                preferred_element_type=jnp.float32,
            )
            for kv, count in zip(kv_refs, key_rows)
        ]

    def finish(work, scores):
        h, block = work
        peak = functools.reduce(jnp.maximum, [jnp.max(s, axis=1, keepdims=True) for s in scores])
        peak = peak * EXP2_SCALE
        summed = None
        for s, kv, count in zip(scores, kv_refs, key_rows):
            weights = jnp.exp2(s * EXP2_SCALE - peak).astype(jnp.bfloat16)
            value = kv[:, 1, :, lanes(h)].reshape(count, HEAD_DIM)
            value = jnp.concatenate([value, jnp.ones_like(value)], axis=1)
            part = jnp.dot(weights, value, preferred_element_type=jnp.float32)
            summed = part if summed is None else summed + part
        out = (summed[:, :HEAD_DIM] / summed[:, HEAD_DIM:]).astype(jnp.bfloat16)
        for n, i in enumerate(block):
            for r in range(sources):
                at = (n * sources + r) * rows
                o_refs[i][targets[i] ^ r, :, lanes(h)] = out[at : at + rows]

    scores = scores_of(works[0])
    for n, work in enumerate(works):
        following = scores_of(works[n + 1]) if n + 1 < len(works) else None
        finish(work, scores)
        scores = following


def attend(queries, keys_values, targets):
    sources, rows, width = queries[0].shape
    key_count = sum(kv.shape[0] * kv.shape[2] for kv in keys_values)
    small = key_count <= 4096
    rows_step, step_width = (2, width) if small else (1, HEAD_DIM)
    score_bytes = rows_step * sources * rows * key_count * 4
    limit = 8 * key_count * step_width + 3 * score_bytes + 6 * 1024 * 1024
    q_spec = pl.BlockSpec((sources, rows, step_width), lambda h: (0, 0, h))
    return pl.pallas_call(
        functools.partial(
            attend_kernel,
            sources=sources,
            parts=len(keys_values),
            targets=targets,
            rows_step=rows_step,
        ),
        grid=(width // step_width,),
        in_specs=[q_spec] * sources
        + [
            pl.BlockSpec(kv.shape[:-1] + (step_width,), lambda h: (0, 0, 0, h))
            for kv in keys_values
        ],
        out_specs=[q_spec] * len(targets),
        out_shape=[jax.ShapeDtypeStruct((sources, rows, width), jnp.bfloat16)] * len(targets),
        compiler_params=pltpu.CompilerParams(vmem_limit_bytes=min(limit, 60 * 1024 * 1024)),
    )(*queries, *keys_values)


def project_kernel(where_ref, *refs, targets):
    o_refs = refs[: len(targets)]
    w_ref, out_ref, lined = refs[len(targets) :]
    width = o_refs[0].shape[2]
    tokens = lined.shape[0]
    for n in range(len(targets)):
        lined[:, n * width : (n + 1) * width] = o_refs[n][...].reshape(tokens, width)
    rows = [pl.ds(pl.multiple_of((where_ref[0] ^ t) * width, 128), width) for t in targets]
    weights = jnp.concatenate([w_ref[r, :] for r in rows], axis=0)
    out_ref[...] = jnp.dot(lined[...], weights, preferred_element_type=jnp.float32)


def project(where, attended, targets, w_out, tile):
    sources, rows, width = attended[0].shape
    tokens = sources * rows
    inner, features = w_out.shape
    return pl.pallas_call(
        functools.partial(project_kernel, targets=targets),
        grid_spec=pltpu.PrefetchScalarGridSpec(
            num_scalar_prefetch=1,
            grid=(features // tile,),
            in_specs=[pl.BlockSpec((sources, rows, width), lambda i, *_: (0, 0, 0))] * len(targets)
            + [pl.BlockSpec((inner, tile), lambda i, *_: (0, i))],
            out_specs=pl.BlockSpec((None, tokens, tile), lambda i, *_: (i, 0, 0)),
            scratch_shapes=[pltpu.VMEM((tokens, len(targets) * width), jnp.bfloat16)],
        ),
        out_shape=jax.ShapeDtypeStruct((features // tile, tokens, tile), jnp.float32),
        compiler_params=pltpu.CompilerParams(vmem_limit_bytes=VMEM_LIMIT),
    )(where, *attended, w_out)


def final_kernel(where_ref, *refs, targets, planes, rows_dev):
    o_refs = refs[: len(targets)]
    partial_ref, w_ref, scale_ref, shift_ref, w_final_ref, even_ref, odd_ref, lined, projected = refs[
        len(targets) :
    ]
    step = pl.program_id(0)
    heads_at, plane_at = where_ref[0], where_ref[1]
    tokens = lined.shape[0]
    width = o_refs[0].shape[2]
    tile = w_ref.shape[1]
    for n in range(len(targets)):
        lined[:, n * width : (n + 1) * width] = o_refs[n][...].reshape(tokens, width)
    rows = [pl.ds(pl.multiple_of((heads_at ^ t) * width, 128), width) for t in targets]
    weights = jnp.concatenate([w_ref[r, :] for r in rows], axis=0)
    projected[step] = partial_ref[...] + jnp.dot(
        lined[...], weights, preferred_element_type=jnp.float32
    )

    @pl.when(step == pl.num_programs(0) - 1)
    def _():
        steps = projected.shape[0]
        features = steps * tile
        total = projected[0]
        for i in range(1, steps):
            total = total + projected[i]
        mean = jnp.sum(total, axis=1, keepdims=True) * (1.0 / features)
        squares = None
        for i in range(steps):
            centered = projected[i] - mean
            squares = centered * centered if squares is None else squares + centered * centered
        variance = jnp.sum(squares, axis=1, keepdims=True) * (1.0 / features)
        inverse = lax.rsqrt(variance + 1e-06)
        patches = None
        for i in range(steps):
            lanes = slice(i * tile, (i + 1) * tile)
            normed = (projected[i] - mean) * inverse * (1.0 + scale_ref[:, lanes]) + shift_ref[:, lanes]
            part = lax.dot_general(
                normed.astype(jnp.bfloat16),
                w_final_ref[:, lanes],
                (((1,), (1,)), ((), ())),
                preferred_element_type=jnp.float32,
            )
            patches = part if patches is None else patches + part
        patches = patches.astype(jnp.bfloat16)
        channels = patches.shape[1]
        half = channels // 2
        source = lax.broadcasted_iota(jnp.int32, (channels, channels), 0)
        target = lax.broadcasted_iota(jnp.int32, (channels, channels), 1)
        q, p, c = target // half, (target // LATENT_CH) % 2, target % LATENT_CH
        lane_order = (source == 4 * c + 2 * p + q).astype(jnp.bfloat16)
        to = lax.broadcasted_iota(jnp.int32, (tokens, tokens), 0)
        at = lax.broadcasted_iota(jnp.int32, (tokens, tokens), 1)
        share = planes * rows_dev
        place = ((to // share) ^ heads_at) * share
        place = place + (((to % share) // rows_dev) ^ plane_at) * rows_dev + to % rows_dev
        row_order = (at == place).astype(jnp.bfloat16)
        cells = jnp.dot(patches, lane_order, preferred_element_type=jnp.float32)
        cells = jnp.dot(row_order, cells.astype(jnp.bfloat16), preferred_element_type=jnp.float32)
        cells = cells.astype(jnp.bfloat16)
        even_ref[...] = cells[:, :half]
        odd_ref[...] = cells[:, half:]


def final_layer(where, attended, targets, partial, w_out, scale_mod, shift_mod, w_final, rows_dev, planes):
    sources, rows, width = attended[0].shape
    inner, features = w_out.shape
    steps, tokens, tile = partial.shape
    channels = w_final.shape[1]
    whole = lambda shape: pl.BlockSpec(shape, lambda i, *_: (0,) * len(shape))
    result = jax.ShapeDtypeStruct((tokens, channels // 2), jnp.bfloat16)
    return pl.pallas_call(
        functools.partial(final_kernel, targets=targets, planes=planes, rows_dev=rows_dev),
        grid_spec=pltpu.PrefetchScalarGridSpec(
            num_scalar_prefetch=1,
            grid=(steps,),
            in_specs=[whole((sources, rows, width))] * len(targets)
            + [
                pl.BlockSpec((None, tokens, tile), lambda i, *_: (i, 0, 0)),
                pl.BlockSpec((inner, tile), lambda i, *_: (0, i)),
                whole((1, features)),
                whole((1, features)),
                whole((channels, features)),
            ],
            out_specs=[whole((tokens, channels // 2))] * 2,
            scratch_shapes=[
                pltpu.VMEM((tokens, len(targets) * width), jnp.bfloat16),
                pltpu.VMEM((steps, tokens, tile), jnp.float32),
            ],
        ),
        out_shape=[result] * 2,
        compiler_params=pltpu.CompilerParams(vmem_limit_bytes=VMEM_LIMIT),
    )(where, *attended, partial, w_out, scale_mod[None], shift_mod[None], w_final.T)


def convolve_kernel(where_ref, even_ref, odd_ref, left_ref, right_ref, w_ref, bias_ref, out_ref, latent):
    frames, cols, _, ch = latent.shape
    rows = even_ref.shape[0] // frames
    height = 2 * rows
    even = even_ref[...].astype(jnp.float32)
    odd = odd_ref[...].astype(jnp.float32)
    left = jnp.where(where_ref[2] == 0, even, left_ref[...].astype(jnp.float32))
    right = jnp.where(where_ref[2] == where_ref[3] - 1, odd, right_ref[...].astype(jnp.float32))
    for x, cells in enumerate((left, even, odd, right)):
        for f in range(frames):
            own = cells[f * rows : (f + 1) * rows]
            for p in range(2):
                latent[f, x, pl.ds(8 + p, rows, stride=2), :] = own[:, p * ch : (p + 1) * ch]
            latent[f, x, 7:8, :] = own[:1, :ch]
            latent[f, x, 8 + height : 9 + height, :] = own[rows - 1 :, ch:]
    depth = 9 * ch
    for x in range(cols - 2):
        stacked = []
        for f in range(frames):
            taps = [latent[f, x + b, 7 + e : 7 + e + height, :] for b in range(3) for e in range(3)]
            stacked.append(jnp.concatenate(taps, axis=1).astype(jnp.bfloat16))
        stacked = [stacked[0]] * 2 + stacked
        acc = None
        for a in range(3):
            flat = jnp.concatenate(stacked[a : a + frames], axis=0)
            part = jnp.dot(
                flat, w_ref[a * depth : (a + 1) * depth, :], preferred_element_type=jnp.float32
            )
            acc = part if acc is None else acc + part
        acc = (acc + bias_ref[...]).astype(jnp.bfloat16)
        out_ref[:, x] = acc.reshape(frames, height, acc.shape[1])


def convolve(where, even, odd, left, right, conv_weight, conv_bias):
    rows = even.shape[0] // FRAMES
    channels = conv_weight.shape[1]
    smem = pl.BlockSpec(memory_space=pltpu.SMEM)
    vmem = pl.BlockSpec(memory_space=pltpu.VMEM)
    return pl.pallas_call(
        convolve_kernel,
        in_specs=[smem] + [vmem] * 6,
        out_specs=vmem,
        out_shape=jax.ShapeDtypeStruct((FRAMES, 2, 2 * rows, channels), jnp.bfloat16),
        scratch_shapes=[pltpu.VMEM((FRAMES, 4, 2 * rows + 16, LATENT_CH), jnp.float32)],
        compiler_params=pltpu.CompilerParams(vmem_limit_bytes=VMEM_LIMIT),
    )(where, even, odd, left, right, conv_weight, conv_bias[None])


def gather_cores(pieces):
    same = jnp.concatenate(pieces, axis=0) if len(pieces) > 1 else pieces[0]
    return [same, swap(same, "plane", 1)]


def after(value, *others):
    return lax.optimization_barrier((value,) + others)[0]


def shards(queries, keys, values, w_out, shift_mod, scale_mod, w_final, conv_weight, conv_bias):
    groups = lax.axis_size("heads")
    planes = lax.axis_size("plane")
    heads_at = lax.axis_index("heads")
    plane_at = lax.axis_index("plane")
    devices = groups * planes
    tokens, width = queries.shape
    group_width = width // groups
    rows_dev = tokens // devices
    where = jnp.stack(
        [heads_at, plane_at, heads_at * planes + plane_at, jnp.int32(devices)]
    ).astype(jnp.int32)

    def group_of(source, r):
        return lax.dynamic_slice_in_dim(source, (heads_at ^ r) * group_width, group_width, axis=1)

    def across(piece):
        return [piece] + [swap(piece, "plane", d) for d in range(2, planes, 2)]

    piece = [jnp.stack([group_of(keys, r), group_of(values, r)])[None] for r in range(groups)]
    got = [piece[0], swap(piece[1], "heads", 1), swap(piece[2], "heads", 2)]
    got.append(swap(after(piece[3], got[2]), "heads", 3))

    queries = after(queries, *piece)
    to = lax.broadcasted_iota(jnp.int32, (tokens, tokens), 0)
    at = lax.broadcasted_iota(jnp.int32, (tokens, tokens), 1)
    j, t, row = to // (groups * rows_dev), (to // rows_dev) % groups, to % rows_dev
    mixed = []
    for r in range(groups):
        place = row * devices + (t ^ (r ^ heads_at)) * planes + (j ^ plane_at)
        part = jnp.dot(
            (at == place).astype(jnp.bfloat16), group_of(queries, r), preferred_element_type=jnp.float32
        )
        mixed.append(part.astype(jnp.bfloat16).reshape(planes, groups, rows_dev, group_width))
    mixed = jnp.stack(mixed, axis=1)
    in_plane = [mixed[0]] + [swap(mixed[d], "plane", d) for d in range(1, planes)]
    asked = []
    for r in range(groups):
        own = jnp.stack([part[r] for part in in_plane], axis=1)
        own = own.reshape(groups, planes * rows_dev, group_width)
        asked.append(own if r == 0 else swap(after(own, got[3]), "heads", r))

    crossed = [across(p) for p in got]
    keys_values = gather_cores(crossed[0] + crossed[1])
    for r in range(2, groups):
        keys_values += gather_cores(crossed[r])

    near, far = (0, 1), (3, 2)
    sent = [swap(o, "heads", t) for t, o in zip(far, attend(asked, keys_values, far))]
    kept = [o if t == 0 else swap(o, "heads", t) for t, o in zip(near, attend(asked, keys_values, near))]
    partial = project(where, kept, near, w_out, 512)
    even, odd = final_layer(
        where, sent, far, partial, w_out, scale_mod, shift_mod, w_final, rows_dev, planes
    )
    both = ("heads", "plane")
    left = lax.ppermute(odd, both, [(i, i + 1) for i in range(devices - 1)])
    right = lax.ppermute(even, both, [(i + 1, i) for i in range(devices - 1)])
    return convolve(where, even, odd, left, right, conv_weight, conv_bias)


def solution(mesh):
    groups, seq = mesh.devices.shape
    split = Mesh(
        mesh.devices.reshape(groups, HEAD_GROUPS, seq // HEAD_GROUPS), ("groups", "heads", "plane")
    )
    by_token = P(("groups", "heads", "plane"), None)
    placed = (by_token, by_token, by_token, P(), P("groups"), P("groups"), P(), P(), P())
    return jax.shard_map(
        shards,
        mesh=split,
        in_specs=placed,
        out_specs=P("groups", ("heads", "plane"), None, None),
        check_vma=False,
    )
```

time: 93.4 us -> 77.5 us (0.83); the launches traced: 92.3 us -> 77.3 us
  Pallas kernels: 22.3 us -> 13.1 us
  local copies, waits for them, and re-layouts: 7.69 us -> 1.53 us
  other arithmetic: 3.63 us -> 0.45 us
  waiting for transfers between devices: 24.9 us -> 26.4 us
  starting transfers between devices: 33.1 us -> 34.2 us
  matrix products: 0.41 us -> 1.35 us
    pallas_call x2, Pallas kernels: 10.6 us -> 4.11 us  [attend(): pl.pallas_call(functools.partial(attend_kernel, sources=sources, parts=le...]
    unnamed x19 -> x16, local copies, waits for them, and re-layouts: 4.58 us -> 0.08 us
    another operation x11 -> x1, other arithmetic: 3.35 us -> 0.08 us  [shards(): jnp.stack([heads_at, plane_at, heads_at * planes + plane_at, jnp.int32(de...]
    ppermute x1, starting transfers between devices: 4.28 us -> 6.49 us  [shards(): left = lax.ppermute(odd, both, [(i, i + 1) for i in range(devices - 1)])]
    pallas_call x1 -> x2, Pallas kernels: 9.01 us -> 6.85 us  [the longest x1 3.95 us: final_layer(): pl.pallas_call(functools.partial(final_kernel, targets=targets, planes=pl...]
    ppermute x16 -> x19, starting transfers between devices: 26.9 us -> 25.8 us  [swap(): return lax.ppermute(source, axis, [(i, i ^ distance) for i in range(count)])]
    dynamic_slice x1 -> x0, local copies, waits for them, and re-layouts: 1.09 us -> none  [group_of(): lax.dynamic_slice_in_dim(source, (heads_at ^ r) * group_width, group_widt...]
    ppermute x16 -> x19, waiting for transfers between devices: 22 us -> 23.1 us  [swap(): return lax.ppermute(source, axis, [(i, i ^ distance) for i in range(count)])]
  transfers between devices with their start and end apart: 18 -> 21, of which waited for: 8 -> 10; matrix products, arithmetic and copies ran while one was open for 9% -> 2% of each run, Pallas kernels for 6% -> 6%
where the time goes in v3:
time: 77.5 us; the launch traced here: 77.3 us
  starting transfers between devices  34.2 us (44%)
  waiting for transfers between devices  26.4 us (34%)
  Pallas kernels  13.1 us (17%)
  local copies, waits for them, and re-layouts  1.53 us (2%)
  matrix products  1.35 us (2%)
    ppermute x19, starting transfers between devices, swap(): return lax.ppermute(source, axis, [(i, i ^ distance) for i in range(count)])  25.8 us
    ppermute x19, waiting for transfers between devices, swap(): return lax.ppermute(source, axis, [(i, i ^ distance) for i in range(count)])  23.1 us
    ppermute x1, starting transfers between devices, shards(): left = lax.ppermute(odd, both, [(i, i + 1) for i in range(devices - 1)])  6.49 us
    pallas_call x2, Pallas kernels, attend(): pl.pallas_call(functools.partial(attend_kernel, sources=sources, parts=le...  4.11 us
    pallas_call x1, Pallas kernels, final_layer(): pl.pallas_call(functools.partial(final_kernel, targets=targets, planes=pl...  3.95 us
    ppermute x1, waiting for transfers between devices, shards(): right = lax.ppermute(even, both, [(i + 1, i) for i in range(devices - 1)])  3.29 us
    pallas_call x1, Pallas kernels, project(): pl.pallas_call(functools.partial(project_kernel, targets=targets), grid_s...  2.9 us
    pallas_call x1, Pallas kernels, convolve(): pl.pallas_call(convolve_kernel, in_specs=[smem] + [vmem] * 6, out_specs=v...  2.16 us
  transfers between devices with their start and end apart: 21, of which 10 were waited for; matrix products, arithmetic and copies ran while one was open for 2% of the time, Pallas kernels for 6%

profile of v3, /device:TPU:1, one launch (start us, length us, event | category | flops | bytes accessed | tf_op | source)
XLA Modules:
  0.0 77.3 jit_solution(12802645463030036114)
XLA Ops:
  0.0 0.0 copy-start
  0.0 1.3 %dynamic-slice_bitcast_fusion = (bf16[1,128,384]{2,1,0:T(8,128)(2,1)S(1)}, bf16[1,128,384]{2,1,0:T(8,128)(2,1)S(1)}, bf16[1,128,384]{2,1,0:T(8,128)(2,1)S(1)}, b...) fusion(bf16[128,1536]{1,0:T(8,128)(2,1)} %param.11, ...), kind=kLoop, calls=%fused_computation.29 | loop fusion | bytes 1572880 | tf_op jit(solution)/shard_map/stack | solution.py:306
  1.4 3.2 %collective-permute-start.3 = (bf16[1,2,128,384]{3,2,1,0:T(8,128)(2,1)S(1)}, bf16[1,2,128,384]{3,2,1,0:T(8,128)(2,1)S(1)}, u32[]{:S(2)}, u32[]{:S(2)}) collective-permute-start(bf16[1,2,128,384]{3,2,1,0:T(8,128)(2,1)S(1)} %maximum_bitcast_fusion.2), channel_id=1, source_target_pairs={{0,8},{4,12},{8,0},{12,4},{1,9},{5,13},{9,1},{13,5},{2,10},{6,14},... | collective-permute-start | bytes 589832 | tf_op jit(solution)/shard_map/ppermute | solution.py:22
  4.6 1.4 %collective-permute-start.9 = (bf16[1,2,128,384]{3,2,1,0:T(8,128)(2,1)S(1)}, bf16[1,2,128,384]{3,2,1,0:T(8,128)(2,1)S(1)}, u32[]{:S(2)}, u32[]{:S(2)}) collective-permute-start(bf16[1,2,128,384]{3,2,1,0:T(8,128)(2,1)S(1)} %maximum_bitcast_fusion.1), channel_id=1, source_target_pairs={{0,4},{4,0},{8,12},{12,8},{1,5},{5,1},{9,13},{13,9},{2,6},{6,2},{1... | collective-permute-start | bytes 589832 | tf_op jit(solution)/shard_map/ppermute | solution.py:22
  6.0 1.3 %collective-permute-start.8 = (bf16[1,2,128,384]{3,2,1,0:T(8,128)(2,1)S(1)}, bf16[1,2,128,384]{3,2,1,0:T(8,128)(2,1)S(1)}, u32[]{:S(2)}, u32[]{:S(2)}) collective-permute-start(bf16[1,2,128,384]{3,2,1,0:T(8,128)(2,1)S(1)} %maximum_bitcast_fusion), channel_id=1, source_target_pairs={{0,2},{1,3},{2,0},{3,1},{4,6},{5,7},{6,4},{7,5},{8,10},{9,11},{10,... | collective-permute-start | bytes 589832 | tf_op jit(solution)/shard_map/ppermute | solution.py:22
  7.4 0.3 convolution_convert_fusion
  7.7 0.3 convolution_convert_fusion.1
  8.1 0.3 convolution_convert_fusion.2
  8.4 0.3 convolution_convert_fusion.3
  8.7 0.1 maximum_bitcast_fusion.5
  8.8 1.7 %collective-permute-start.2 = (bf16[4,4,8,384]{3,2,1,0:T(8,128)(2,1)S(1)}, bf16[4,4,8,384]{3,2,1,0:T(8,128)(2,1)S(1)}, u32[]{:S(2)}, u32[]{:S(2)}) collective-permute-start(bf16[4,4,8,384]{3,2,1,0:T(8,128)(2,1)S(1)} %get-tuple-element.29), channel_id=1, source_target_pairs={{0,3},{1,2},{2,1},{3,0},{4,7},{5,6},{6,5},{7,4},{8,11},{9,10},{10,... | collective-permute-start | bytes 294920 | tf_op jit(solution)/shard_map/ppermute | solution.py:22
  10.5 1.2 %collective-permute-start.1 = (bf16[4,4,8,384]{3,2,1,0:T(8,128)(2,1)S(1)}, bf16[4,4,8,384]{3,2,1,0:T(8,128)(2,1)S(1)}, u32[]{:S(2)}, u32[]{:S(2)}) collective-permute-start(bf16[4,4,8,384]{3,2,1,0:T(8,128)(2,1)S(1)} %get-tuple-element.28), channel_id=1, source_target_pairs={{0,2},{1,3},{2,0},{3,1},{4,6},{5,7},{6,4},{7,5},{8,10},{9,11},{10,... | collective-permute-start | bytes 294920 | tf_op jit(solution)/shard_map/ppermute | solution.py:22
  11.8 0.0 copy-start.1
  11.8 3.3 %collective-permute-done.2 = bf16[4,4,8,384]{3,2,1,0:T(8,128)(2,1)S(1)} collective-permute-done((bf16[4,4,8,384]{3,2,1,0:T(8,128)(2,1)S(1)}, bf16[4,4,8,384]{3,2,1,0:T(8,128)(2,1)S(1)}, u32[]{:S(2)}, u32[]{:S(2)}) %collective-permute-start.2) | collective-permute-done | bytes 98336 | tf_op jit(solution)/shard_map/ppermute | solution.py:22
  15.1 0.5 collective-permute-start
  15.6 1.6 %collective-permute-done.1 = bf16[4,4,8,384]{3,2,1,0:T(8,128)(2,1)S(1)} collective-permute-done((bf16[4,4,8,384]{3,2,1,0:T(8,128)(2,1)S(1)}, bf16[4,4,8,384]{3,2,1,0:T(8,128)(2,1)S(1)}, u32[]{:S(2)}, u32[]{:S(2)}) %collective-permute-start.1) | collective-permute-done | bytes 98336 | tf_op jit(solution)/shard_map/ppermute | solution.py:22
  17.2 0.0 collective-permute-done.9
  17.2 0.4 collective-permute-start.10
  17.6 0.0 collective-permute-done
  17.6 0.0 collective-permute-done.3
  17.6 0.1 collective-permute-start.4
  17.7 1.2 %collective-permute-start.12 = (bf16[1,2,128,384]{3,2,1,0:T(8,128)(2,1)S(1)}, bf16[1,2,128,384]{3,2,1,0:T(8,128)(2,1)S(1)}, u32[]{:S(2)}, u32[]{:S(2)}) collective-permute-start(bf16[1,2,128,384]{3,2,1,0:T(8,128)(2,1)S(1)} %collective-permute-done.3), channel_id=1, source_target_pairs={{0,2},{1,3},{2,0},{3,1},{4,6},{5,7},{6,4},{7,5},{8,10},{9,11},{10,... | collective-permute-start | bytes 589832 | tf_op jit(solution)/shard_map/ppermute | solution.py:22
  18.9 0.0 collective-permute-done.8
  18.9 4.4 %collective-permute-done.10 = bf16[1,2,128,384]{3,2,1,0:T(8,128)(2,1)S(1)} collective-permute-done((bf16[1,2,128,384]{3,2,1,0:T(8,128)(2,1)S(1)}, bf16[1,2,128,384]{3,2,1,0:T(8,128)(2,1)S(1)}, u32[]{:S(2)}, u32[]{:S(2)}) %collective-permute-start.10) | collective-permute-done | bytes 196640 | tf_op jit(solution)/shard_map/ppermute | solution.py:22
  23.4 0.1 pad_maximum_fusion.refs_4_
  23.5 2.1 %collective-permute-start.11 = (bf16[4,2,128,384]{3,2,1,0:T(8,128)(2,1)S(1)}, bf16[4,2,128,384]{3,2,1,0:T(8,128)(2,1)S(1)}, u32[]{:S(2)}, u32[]{:S(2)}) collective-permute-start(bf16[4,2,128,384]{3,2,1,0:T(8,128)(2,1)S(1)} %pad_maximum_fusion.refs_4_), channel_id=1, source_target_pairs={{0,1},{1,0},{2,3},{3,2},{4,5},{5,4},{6,7},{7,6},{8,9},{9,8},{10,11... | collective-permute-start | bytes 2359304 | tf_op jit(solution)/shard_map/ppermute | solution.py:22
  25.6 0.0 collective-permute-done.4
  25.6 1.3 %collective-permute-start.14 = (bf16[1,2,128,384]{3,2,1,0:T(8,128)(2,1)S(1)}, bf16[1,2,128,384]{3,2,1,0:T(8,128)(2,1)S(1)}, u32[]{:S(2)}, u32[]{:S(2)}) collective-permute-start(bf16[1,2,128,384]{3,2,1,0:T(8,128)(2,1)S(1)} %collective-permute-done.4), channel_id=1, source_target_pairs={{0,2},{1,3},{2,0},{3,1},{4,6},{5,7},{6,4},{7,5},{8,10},{9,11},{10,... | collective-permute-start | bytes 589832 | tf_op jit(solution)/shard_map/ppermute | solution.py:22
  26.9 0.6 collective-permute-done.12
  27.6 1.3 %collective-permute-start.13 = (bf16[2,2,128,384]{3,2,1,0:T(8,128)(2,1)S(1)}, bf16[2,2,128,384]{3,2,1,0:T(8,128)(2,1)S(1)}, u32[]{:S(2)}, u32[]{:S(2)}) collective-permute-start(bf16[2,2,128,384]{3,2,1,0:T(8,128)(2,1)S(1)} %constant_dynamic-update-slice_fusion.refs_6_), channel_id=1, source_target_pairs={{0,1},{1,0},{2,3},{3,2},{4,5},{5,4},{6,7},{7,6},{8,9},{9,8},{10,11... | collective-permute-start | bytes 1179656 | tf_op jit(solution)/shard_map/ppermute | solution.py:22
  28.9 1.9 %collective-permute-done.14 = bf16[1,2,128,384]{3,2,1,0:T(8,128)(2,1)S(1)} collective-permute-done((bf16[1,2,128,384]{3,2,1,0:T(8,128)(2,1)S(1)}, bf16[1,2,128,384]{3,2,1,0:T(8,128)(2,1)S(1)}, u32[]{:S(2)}, u32[]{:S(2)}) %collective-permute-start.14) | collective-permute-done | bytes 196640 | tf_op jit(solution)/shard_map/ppermute | solution.py:22
  30.9 2.2 %collective-permute-start.15 = (bf16[2,2,128,384]{3,2,1,0:T(8,128)(2,1)S(1)}, bf16[2,2,128,384]{3,2,1,0:T(8,128)(2,1)S(1)}, u32[]{:S(2)}, u32[]{:S(2)}) collective-permute-start(bf16[2,2,128,384]{3,2,1,0:T(8,128)(2,1)S(1)} %constant_dynamic-update-slice_fusion.2.refs_8_), channel_id=1, source_target_pairs={{0,1},{1,0},{2,3},{3,2},{4,5},{5,4},{6,7},{7,6},{8,9},{9,8},{10,11... | collective-permute-start | bytes 1179656 | tf_op jit(solution)/shard_map/ppermute | solution.py:22
  33.1 0.0 copy-start.3
  33.1 0.0 copy-start.4
  33.2 0.0 copy-start.5
  33.2 2.1 %collective-permute-start.5 = (bf16[4,32,384]{2,1,0:T(8,128)(2,1)S(1)}, bf16[4,32,384]{2,1,0:T(8,128)(2,1)S(1)}, u32[]{:S(2)}, u32[]{:S(2)}) collective-permute-start(bf16[4,32,384]{2,1,0:T(8,128)(2,1)S(1)} %copy_bitcast_fusion.1), channel_id=1, source_target_pairs={{0,4},{4,0},{8,12},{12,8},{1,5},{5,1},{9,13},{13,9},{2,6},{6,2},{1... | collective-permute-start | bytes 294920 | tf_op jit(solution)/shard_map/ppermute | solution.py:22
  35.3 0.2 collective-permute-start.6
  35.5 2.9 %collective-permute-done.5.refs_1_ = bf16[4,32,384]{2,1,0:T(8,128)(2,1)S(1)} collective-permute-done((bf16[4,32,384]{2,1,0:T(8,128)(2,1)S(1)}, bf16[4,32,384]{2,1,0:T(8,128)(2,1)S(1)}, u32[]{:S(2)}, u32[]{:S(2)}) %collective-permute-start.5) | collective-permute-done | bytes 98336 | tf_op jit(solution)/shard_map/ppermute | solution.py:22
  38.4 1.3 %collective-permute-start.7 = (bf16[4,32,384]{2,1,0:T(8,128)(2,1)S(1)}, bf16[4,32,384]{2,1,0:T(8,128)(2,1)S(1)}, u32[]{:S(2)}, u32[]{:S(2)}) collective-permute-start(bf16[4,32,384]{2,1,0:T(8,128)(2,1)S(1)} %maximum_bitcast_fusion.6), channel_id=1, source_target_pairs={{0,12},{4,8},{8,4},{12,0},{1,13},{5,9},{9,5},{13,1},{2,14},{6,10},... | collective-permute-start | bytes 294920 | tf_op jit(solution)/shard_map/ppermute | solution.py:22
  39.8 2.8 %collective-permute-done.6.refs_2_ = bf16[4,32,384]{2,1,0:T(8,128)(2,1)S(1)} collective-permute-done((bf16[4,32,384]{2,1,0:T(8,128)(2,1)S(1)}, bf16[4,32,384]{2,1,0:T(8,128)(2,1)S(1)}, u32[]{:S(2)}, u32[]{:S(2)}) %collective-permute-start.6) | collective-permute-done | bytes 98336 | tf_op jit(solution)/shard_map/ppermute | solution.py:22
  42.6 1.5 %collective-permute-done.7.refs_3_ = bf16[4,32,384]{2,1,0:T(8,128)(2,1)S(1)} collective-permute-done((bf16[4,32,384]{2,1,0:T(8,128)(2,1)S(1)}, bf16[4,32,384]{2,1,0:T(8,128)(2,1)S(1)}, u32[]{:S(2)}, u32[]{:S(2)}) %collective-permute-start.7) | collective-permute-done | bytes 98336 | tf_op jit(solution)/shard_map/ppermute | solution.py:22
  44.1 0.0 collective-permute-done.13.refs_7_
  44.1 0.0 collective-permute-done.15.refs_9_
  44.1 0.0 collective-permute-done.11.refs_5_
  44.1 2.1 %shard_map.91 = (bf16[4,32,384]{2,1,0:T(8,128)(2,1)S(1)}, bf16[4,32,384]{2,1,0:T(8,128)(2,1)S(1)}) custom-call(bf16[4,32,384]{2,1,0:T(8,128)(2,1)S(1)} %copy_bitcast_fusion.2.refs_0_, bf16[4,32,384]{2,1,0:T(8,128)(2,1)S(1)} %collective-permute-done.5.refs_1_, bf16[4,32,384]{2,1,0:T(8,128)(2,1)S(1)} %collective-permute-done.6.refs_2_, ...), custom_call_target="tpu_custom_call" | custom-call | tf_op jit(solution)/shard_map/pallas_call | solution.py:85
  46.2 1.0 %collective-permute-start.16 = (bf16[4,32,384]{2,1,0:T(8,128)(2,1)S(1)}, bf16[4,32,384]{2,1,0:T(8,128)(2,1)S(1)}, u32[]{:S(2)}, u32[]{:S(2)}) collective-permute-start(bf16[4,32,384]{2,1,0:T(8,128)(2,1)S(1)} %get-tuple-element.21), channel_id=1, source_target_pairs={{0,12},{4,8},{8,4},{12,0},{1,13},{5,9},{9,5},{13,1},{2,14},{6,10},... | collective-permute-start | bytes 294920 | tf_op jit(solution)/shard_map/ppermute | solution.py:22
  47.2 3.2 %collective-permute-start.17 = (bf16[4,32,384]{2,1,0:T(8,128)(2,1)S(1)}, bf16[4,32,384]{2,1,0:T(8,128)(2,1)S(1)}, u32[]{:S(2)}, u32[]{:S(2)}) collective-permute-start(bf16[4,32,384]{2,1,0:T(8,128)(2,1)S(1)} %get-tuple-element.22), channel_id=1, source_target_pairs={{0,8},{4,12},{8,0},{12,4},{1,9},{5,13},{9,1},{13,5},{2,10},{6,14},... | collective-permute-start | bytes 294920 | tf_op jit(solution)/shard_map/ppermute | solution.py:22
  50.4 2.1 %shard_map.92 = (bf16[4,32,384]{2,1,0:T(8,128)(2,1)S(1)}, bf16[4,32,384]{2,1,0:T(8,128)(2,1)S(1)}) custom-call(bf16[4,32,384]{2,1,0:T(8,128)(2,1)S(1)} %copy_bitcast_fusion.2.refs_0_, bf16[4,32,384]{2,1,0:T(8,128)(2,1)S(1)} %collective-permute-done.5.refs_1_, bf16[4,32,384]{2,1,0:T(8,128)(2,1)S(1)} %collective-permute-done.6.refs_2_, ...), custom_call_target="tpu_custom_call" | custom-call | tf_op jit(solution)/shard_map/pallas_call | solution.py:85
  52.5 0.1 collective-permute-start.18
  52.5 0.1 pad_add_fusion.where_ref
  52.6 3.9 %collective-permute-done.18.refs_1_ = bf16[4,32,384]{2,1,0:T(8,128)(2,1)S(1)} collective-permute-done((bf16[4,32,384]{2,1,0:T(8,128)(2,1)S(1)}, bf16[4,32,384]{2,1,0:T(8,128)(2,1)S(1)}, u32[]{:S(2)}, u32[]{:S(2)}) %collective-permute-start.18) | collective-permute-done | bytes 98336 | tf_op jit(solution)/shard_map/ppermute | solution.py:22
  56.5 2.9 %shard_map.93.refs_2_ = f32[6,128,512]{2,1,0:T(8,128)S(1)} custom-call(s32[4]{0:T(128)S(1)} %pad_add_fusion.where_ref, bf16[4,32,384]{2,1,0:T(8,128)(2,1)S(1)} %get-tuple-element.23.refs_0_, bf16[4,32,384]{2,1,0:T(8,128)(2,1)S(1)} %collective-permute-done.18.refs_1_, bf16[1536,3072]{1,0:T(8,128)(2,1)S(1)} %copy-done.1), custom_call_target="tpu_custom_call" | custom-call | tf_op jit(solution)/shard_map/pallas_call | solution.py:121
  59.4 0.0 collective-permute-done.16.refs_0_
  59.4 0.0 collective-permute-done.17.refs_1_
  59.5 0.0 copy-done.3
  59.5 0.0 copy-done.4
  59.5 0.0 copy-done.5
  59.5 4.0 %shard_map.94 = (bf16[128,32]{1,0:T(8,128)(2,1)S(1)}, bf16[128,32]{1,0:T(8,128)(2,1)S(1)}) custom-call(s32[4]{0:T(128)S(1)} %pad_add_fusion.where_ref, bf16[4,32,384]{2,1,0:T(8,128)(2,1)S(1)} %collective-permute-done.16.refs_0_, bf16[4,32,384]{2,1,0:T(8,128)(2,1)S(1)} %collective-permute-done.17.refs_1_, f32[6,128,512]{2,1,0:T(8,128)S(1)} %shard_map.93.refs_2_, ...), custom_call_target="tpu_custom_call" | custom-call | tf_op jit(solution)/shard_map/pallas_call | solution.py:206
  63.4 6.5 %collective-permute-start.19 = (bf16[128,32]{1,0:T(8,128)(2,1)S(1)}, bf16[128,32]{1,0:T(8,128)(2,1)S(1)}, u32[]{:S(2)}, u32[]{:S(2)}) collective-permute-start(bf16[128,32]{1,0:T(8,128)(2,1)S(1)} %get-tuple-element.26.odd_ref), channel_id=1, source_target_pairs={{0,1},{1,2},{2,3},{3,4},{4,5},{5,6},{6,7},{7,8},{8,9},{9,10},{10,1... | collective-permute-start | bytes 24584 | tf_op jit(solution)/shard_map/ppermute | solution.py:342
  69.9 1.9 %collective-permute-start.20 = (bf16[128,32]{1,0:T(8,128)(2,1)S(1)}, bf16[128,32]{1,0:T(8,128)(2,1)S(1)}, u32[]{:S(2)}, u32[]{:S(2)}) collective-permute-start(bf16[128,32]{1,0:T(8,128)(2,1)S(1)} %get-tuple-element.25.even_ref), channel_id=1, source_target_pairs={{1,0},{2,1},{3,2},{4,3},{5,4},{6,5},{7,6},{8,7},{9,8},{10,9},{11,1... | collective-permute-start | bytes 24584 | tf_op jit(solution)/shard_map/ppermute | solution.py:343
  71.9 0.0 collective-permute-done.19.left_ref
  71.9 3.3 %collective-permute-done.20.right_ref = bf16[128,32]{1,0:T(8,128)(2,1)S(1)} collective-permute-done((bf16[128,32]{1,0:T(8,128)(2,1)S(1)}, bf16[128,32]{1,0:T(8,128)(2,1)S(1)}, u32[]{:S(2)}, u32[]{:S(2)}) %collective-permute-start.20) | collective-permute-done | bytes 8224 | tf_op jit(solution)/shard_map/ppermute | solution.py:343
  75.2 0.0 copy-done.2
  75.2 2.2 %shard_map.95 = bf16[4,2,64,512]{3,2,1,0:T(8,128)(2,1)} custom-call(s32[4]{0:T(128)S(1)} %pad_add_fusion.where_ref, bf16[128,32]{1,0:T(8,128)(2,1)S(1)} %get-tuple-element.25.even_ref, bf16[128,32]{1,0:T(8,128)(2,1)S(1)} %get-tuple-element.26.odd_ref, bf16[128,32]{1,0:T(8,128)(2,1)S(1)} %collective-permute-done.19.left_ref, ...), custom_call_target="tpu_custom_call" | custom-call | tf_op jit(solution)/shard_map/pallas_call | solution.py:268
  (29 shorter events, 0.3 us)
Async XLA Ops:
  0.0 7.4 %copy-start = (bf16[128,1536]{1,0:T(8,128)(2,1)S(1)}, bf16[128,1536]{1,0:T(8,128)(2,1)}, u32[]{:S(2)}) copy-start(bf16[128,1536]{1,0:T(8,128)(2,1)} %param.9) | copy-start | bytes 1179652
  1.4 16.2 %collective-permute-start.3 = (bf16[1,2,128,384]{3,2,1,0:T(8,128)(2,1)S(1)}, bf16[1,2,128,384]{3,2,1,0:T(8,128)(2,1)S(1)}, u32[]{:S(2)}, u32[]{:S(2)}) collective-permute-start(bf16[1,2,128,384]{3,2,1,0:T(8,128)(2,1)S(1)} %maximum_bitcast_fusion.2), channel_id=1, source_target_pairs={{0,8},{4,12},{8,0},{12,4},{1,9},{5,13},{9,1},{13,5},{2,10},{6,14},... | collective-permute-start | bytes 589832 | tf_op jit(solution)/shard_map/ppermute | solution.py:22
  4.6 12.6 %collective-permute-start.9 = (bf16[1,2,128,384]{3,2,1,0:T(8,128)(2,1)S(1)}, bf16[1,2,128,384]{3,2,1,0:T(8,128)(2,1)S(1)}, u32[]{:S(2)}, u32[]{:S(2)}) collective-permute-start(bf16[1,2,128,384]{3,2,1,0:T(8,128)(2,1)S(1)} %maximum_bitcast_fusion.1), channel_id=1, source_target_pairs={{0,4},{4,0},{8,12},{12,8},{1,5},{5,1},{9,13},{13,9},{2,6},{6,2},{1... | collective-permute-start | bytes 589832 | tf_op jit(solution)/shard_map/ppermute | solution.py:22
  6.0 12.9 %collective-permute-start.8 = (bf16[1,2,128,384]{3,2,1,0:T(8,128)(2,1)S(1)}, bf16[1,2,128,384]{3,2,1,0:T(8,128)(2,1)S(1)}, u32[]{:S(2)}, u32[]{:S(2)}) collective-permute-start(bf16[1,2,128,384]{3,2,1,0:T(8,128)(2,1)S(1)} %maximum_bitcast_fusion), channel_id=1, source_target_pairs={{0,2},{1,3},{2,0},{3,1},{4,6},{5,7},{6,4},{7,5},{8,10},{9,11},{10,... | collective-permute-start | bytes 589832 | tf_op jit(solution)/shard_map/ppermute | solution.py:22
  8.8 6.3 %collective-permute-start.2 = (bf16[4,4,8,384]{3,2,1,0:T(8,128)(2,1)S(1)}, bf16[4,4,8,384]{3,2,1,0:T(8,128)(2,1)S(1)}, u32[]{:S(2)}, u32[]{:S(2)}) collective-permute-start(bf16[4,4,8,384]{3,2,1,0:T(8,128)(2,1)S(1)} %get-tuple-element.29), channel_id=1, source_target_pairs={{0,3},{1,2},{2,1},{3,0},{4,7},{5,6},{6,5},{7,4},{8,11},{9,10},{10,... | collective-permute-start | bytes 294920 | tf_op jit(solution)/shard_map/ppermute | solution.py:22
  10.5 6.7 %collective-permute-start.1 = (bf16[4,4,8,384]{3,2,1,0:T(8,128)(2,1)S(1)}, bf16[4,4,8,384]{3,2,1,0:T(8,128)(2,1)S(1)}, u32[]{:S(2)}, u32[]{:S(2)}) collective-permute-start(bf16[4,4,8,384]{3,2,1,0:T(8,128)(2,1)S(1)} %get-tuple-element.28), channel_id=1, source_target_pairs={{0,2},{1,3},{2,0},{3,1},{4,6},{5,7},{6,4},{7,5},{8,10},{9,11},{10,... | collective-permute-start | bytes 294920 | tf_op jit(solution)/shard_map/ppermute | solution.py:22
  11.8 44.8 %copy-start.1 = (bf16[1536,3072]{1,0:T(8,128)(2,1)S(1)}, bf16[1536,3072]{1,0:T(8,128)(2,1)}, u32[]{:S(2)}) copy-start(bf16[1536,3072]{1,0:T(8,128)(2,1)} %refs_3_.1) | copy-start | bytes 28311556
  15.1 2.5 %collective-permute-start = (bf16[4,4,8,384]{3,2,1,0:T(8,128)(2,1)S(1)}, bf16[4,4,8,384]{3,2,1,0:T(8,128)(2,1)S(1)}, u32[]{:S(2)}, u32[]{:S(2)}) collective-permute-start(bf16[4,4,8,384]{3,2,1,0:T(8,128)(2,1)S(1)} %get-tuple-element.27), channel_id=1, source_target_pairs={{0,1},{1,0},{2,3},{3,2},{4,5},{5,4},{6,7},{7,6},{8,9},{9,8},{10,11... | collective-permute-start | bytes 294920 | tf_op jit(solution)/shard_map/ppermute | solution.py:22
  17.2 6.2 %collective-permute-start.10 = (bf16[1,2,128,384]{3,2,1,0:T(8,128)(2,1)S(1)}, bf16[1,2,128,384]{3,2,1,0:T(8,128)(2,1)S(1)}, u32[]{:S(2)}, u32[]{:S(2)}) collective-permute-start(bf16[1,2,128,384]{3,2,1,0:T(8,128)(2,1)S(1)} %collective-permute-done.9), channel_id=1, source_target_pairs={{0,2},{1,3},{2,0},{3,1},{4,6},{5,7},{6,4},{7,5},{8,10},{9,11},{10,... | collective-permute-start | bytes 589832 | tf_op jit(solution)/shard_map/ppermute | solution.py:22
  17.6 8.0 %collective-permute-start.4 = (bf16[1,2,128,384]{3,2,1,0:T(8,128)(2,1)S(1)}, bf16[1,2,128,384]{3,2,1,0:T(8,128)(2,1)S(1)}, u32[]{:S(2)}, u32[]{:S(2)}) collective-permute-start(bf16[1,2,128,384]{3,2,1,0:T(8,128)(2,1)S(1)} %maximum_bitcast_fusion.3), channel_id=1, source_target_pairs={{0,12},{4,8},{8,4},{12,0},{1,13},{5,9},{9,5},{13,1},{2,14},{6,10},... | collective-permute-start | bytes 589832 | tf_op jit(solution)/shard_map/ppermute | solution.py:22
  17.7 9.9 %collective-permute-start.12 = (bf16[1,2,128,384]{3,2,1,0:T(8,128)(2,1)S(1)}, bf16[1,2,128,384]{3,2,1,0:T(8,128)(2,1)S(1)}, u32[]{:S(2)}, u32[]{:S(2)}) collective-permute-start(bf16[1,2,128,384]{3,2,1,0:T(8,128)(2,1)S(1)} %collective-permute-done.3), channel_id=1, source_target_pairs={{0,2},{1,3},{2,0},{3,1},{4,6},{5,7},{6,4},{7,5},{8,10},{9,11},{10,... | collective-permute-start | bytes 589832 | tf_op jit(solution)/shard_map/ppermute | solution.py:22
  23.5 20.6 %collective-permute-start.11 = (bf16[4,2,128,384]{3,2,1,0:T(8,128)(2,1)S(1)}, bf16[4,2,128,384]{3,2,1,0:T(8,128)(2,1)S(1)}, u32[]{:S(2)}, u32[]{:S(2)}) collective-permute-start(bf16[4,2,128,384]{3,2,1,0:T(8,128)(2,1)S(1)} %pad_maximum_fusion.refs_4_), channel_id=1, source_target_pairs={{0,1},{1,0},{2,3},{3,2},{4,5},{5,4},{6,7},{7,6},{8,9},{9,8},{10,11... | collective-permute-start | bytes 2359304 | tf_op jit(solution)/shard_map/ppermute | solution.py:22
  25.6 5.3 %collective-permute-start.14 = (bf16[1,2,128,384]{3,2,1,0:T(8,128)(2,1)S(1)}, bf16[1,2,128,384]{3,2,1,0:T(8,128)(2,1)S(1)}, u32[]{:S(2)}, u32[]{:S(2)}) collective-permute-start(bf16[1,2,128,384]{3,2,1,0:T(8,128)(2,1)S(1)} %collective-permute-done.4), channel_id=1, source_target_pairs={{0,2},{1,3},{2,0},{3,1},{4,6},{5,7},{6,4},{7,5},{8,10},{9,11},{10,... | collective-permute-start | bytes 589832 | tf_op jit(solution)/shard_map/ppermute | solution.py:22
  27.6 16.5 %collective-permute-start.13 = (bf16[2,2,128,384]{3,2,1,0:T(8,128)(2,1)S(1)}, bf16[2,2,128,384]{3,2,1,0:T(8,128)(2,1)S(1)}, u32[]{:S(2)}, u32[]{:S(2)}) collective-permute-start(bf16[2,2,128,384]{3,2,1,0:T(8,128)(2,1)S(1)} %constant_dynamic-update-slice_fusion.refs_6_), channel_id=1, source_target_pairs={{0,1},{1,0},{2,3},{3,2},{4,5},{5,4},{6,7},{7,6},{8,9},{9,8},{10,11... | collective-permute-start | bytes 1179656 | tf_op jit(solution)/shard_map/ppermute | solution.py:22
  30.9 13.2 %collective-permute-start.15 = (bf16[2,2,128,384]{3,2,1,0:T(8,128)(2,1)S(1)}, bf16[2,2,128,384]{3,2,1,0:T(8,128)(2,1)S(1)}, u32[]{:S(2)}, u32[]{:S(2)}) collective-permute-start(bf16[2,2,128,384]{3,2,1,0:T(8,128)(2,1)S(1)} %constant_dynamic-update-slice_fusion.2.refs_8_), channel_id=1, source_target_pairs={{0,1},{1,0},{2,3},{3,2},{4,5},{5,4},{6,7},{7,6},{8,9},{9,8},{10,11... | collective-permute-start | bytes 1179656 | tf_op jit(solution)/shard_map/ppermute | solution.py:22
  33.1 26.3 %copy-start.3 = (bf16[3072,64]{0,1:T(8,128)(2,1)S(1)}, bf16[3072,64]{0,1:T(8,128)(2,1)}, u32[]{:S(2)}) copy-start(bf16[3072,64]{0,1:T(8,128)(2,1)} %param.15) | copy-start | bytes 1179652
  33.1 26.3 %copy-start.4 = (f32[3072]{0:T(1024)S(1)}, f32[3072]{0:T(1024)}, u32[]{:S(2)}) copy-start(f32[3072]{0:T(1024)} %param.14) | copy-start | bytes 36868
  33.2 26.3 %copy-start.5 = (f32[3072]{0:T(1024)S(1)}, f32[3072]{0:T(1024)}, u32[]{:S(2)}) copy-start(f32[3072]{0:T(1024)} %param.13) | copy-start | bytes 36868
  33.2 5.3 %collective-permute-start.5 = (bf16[4,32,384]{2,1,0:T(8,128)(2,1)S(1)}, bf16[4,32,384]{2,1,0:T(8,128)(2,1)S(1)}, u32[]{:S(2)}, u32[]{:S(2)}) collective-permute-start(bf16[4,32,384]{2,1,0:T(8,128)(2,1)S(1)} %copy_bitcast_fusion.1), channel_id=1, source_target_pairs={{0,4},{4,0},{8,12},{12,8},{1,5},{5,1},{9,13},{13,9},{2,6},{6,2},{1... | collective-permute-start | bytes 294920 | tf_op jit(solution)/shard_map/ppermute | solution.py:22
  35.3 7.3 %collective-permute-start.6 = (bf16[4,32,384]{2,1,0:T(8,128)(2,1)S(1)}, bf16[4,32,384]{2,1,0:T(8,128)(2,1)S(1)}, u32[]{:S(2)}, u32[]{:S(2)}) collective-permute-start(bf16[4,32,384]{2,1,0:T(8,128)(2,1)S(1)} %copy_bitcast_fusion), channel_id=1, source_target_pairs={{0,8},{4,12},{8,0},{12,4},{1,9},{5,13},{9,1},{13,5},{2,10},{6,14},... | collective-permute-start | bytes 294920 | tf_op jit(solution)/shard_map/ppermute | solution.py:22
  38.4 5.6 %collective-permute-start.7 = (bf16[4,32,384]{2,1,0:T(8,128)(2,1)S(1)}, bf16[4,32,384]{2,1,0:T(8,128)(2,1)S(1)}, u32[]{:S(2)}, u32[]{:S(2)}) collective-permute-start(bf16[4,32,384]{2,1,0:T(8,128)(2,1)S(1)} %maximum_bitcast_fusion.6), channel_id=1, source_target_pairs={{0,12},{4,8},{8,4},{12,0},{1,13},{5,9},{9,5},{13,1},{2,14},{6,10},... | collective-permute-start | bytes 294920 | tf_op jit(solution)/shard_map/ppermute | solution.py:22
  46.2 13.3 %collective-permute-start.16 = (bf16[4,32,384]{2,1,0:T(8,128)(2,1)S(1)}, bf16[4,32,384]{2,1,0:T(8,128)(2,1)S(1)}, u32[]{:S(2)}, u32[]{:S(2)}) collective-permute-start(bf16[4,32,384]{2,1,0:T(8,128)(2,1)S(1)} %get-tuple-element.21), channel_id=1, source_target_pairs={{0,12},{4,8},{8,4},{12,0},{1,13},{5,9},{9,5},{13,1},{2,14},{6,10},... | collective-permute-start | bytes 294920 | tf_op jit(solution)/shard_map/ppermute | solution.py:22
  47.2 12.3 %collective-permute-start.17 = (bf16[4,32,384]{2,1,0:T(8,128)(2,1)S(1)}, bf16[4,32,384]{2,1,0:T(8,128)(2,1)S(1)}, u32[]{:S(2)}, u32[]{:S(2)}) collective-permute-start(bf16[4,32,384]{2,1,0:T(8,128)(2,1)S(1)} %get-tuple-element.22), channel_id=1, source_target_pairs={{0,8},{4,12},{8,0},{12,4},{1,9},{5,13},{9,1},{13,5},{2,10},{6,14},... | collective-permute-start | bytes 294920 | tf_op jit(solution)/shard_map/ppermute | solution.py:22
  52.5 4.1 %collective-permute-start.18 = (bf16[4,32,384]{2,1,0:T(8,128)(2,1)S(1)}, bf16[4,32,384]{2,1,0:T(8,128)(2,1)S(1)}, u32[]{:S(2)}, u32[]{:S(2)}) collective-permute-start(bf16[4,32,384]{2,1,0:T(8,128)(2,1)S(1)} %get-tuple-element.24), channel_id=1, source_target_pairs={{0,4},{4,0},{8,12},{12,8},{1,5},{5,1},{9,13},{13,9},{2,6},{6,2},{1... | collective-permute-start | bytes 294920 | tf_op jit(solution)/shard_map/ppermute | solution.py:22
  56.5 18.7 %copy-start.2 = (bf16[432,512]{1,0:T(8,128)(2,1)S(1)}, bf16[432,512]{1,0:T(8,128)(2,1)}, u32[]{:S(2)}) copy-start(bf16[432,512]{1,0:T(8,128)(2,1)} %w_ref.1) | copy-start | bytes 1327108
  56.5 18.7 %copy-start.6 = (f32[512]{0:T(512)S(1)}, f32[512]{0:T(512)}, u32[]{:S(2)}) copy-start(f32[512]{0:T(512)} %param.17) | copy-start | bytes 6148
  63.4 8.4 %collective-permute-start.19 = (bf16[128,32]{1,0:T(8,128)(2,1)S(1)}, bf16[128,32]{1,0:T(8,128)(2,1)S(1)}, u32[]{:S(2)}, u32[]{:S(2)}) collective-permute-start(bf16[128,32]{1,0:T(8,128)(2,1)S(1)} %get-tuple-element.26.odd_ref), channel_id=1, source_target_pairs={{0,1},{1,2},{2,3},{3,4},{4,5},{5,6},{6,7},{7,8},{8,9},{9,10},{10,1... | collective-permute-start | bytes 24584 | tf_op jit(solution)/shard_map/ppermute | solution.py:342
  69.9 5.2 %collective-permute-start.20 = (bf16[128,32]{1,0:T(8,128)(2,1)S(1)}, bf16[128,32]{1,0:T(8,128)(2,1)S(1)}, u32[]{:S(2)}, u32[]{:S(2)}) collective-permute-start(bf16[128,32]{1,0:T(8,128)(2,1)S(1)} %get-tuple-element.25.even_ref), channel_id=1, source_target_pairs={{1,0},{2,1},{3,2},{4,3},{5,4},{6,5},{7,6},{8,7},{9,8},{10,9},{11,1... | collective-permute-start | bytes 24584 | tf_op jit(solution)/shard_map/ppermute | solution.py:343

commit v4 on v3

--- a/solution.py
+++ b/solution.py
@@ -22,32 +22,76 @@
     return lax.ppermute(source, axis, [(i, i ^ distance) for i in range(count)])
 
 
-def attend_kernel(*refs, sources, parts, targets, rows_step):
+def bundle_kernel(where_ref, q_ref, k_ref, v_ref, *out_refs, groups, planes, distances):
+    tokens, width = q_ref.shape
+    group_width = width // groups
+    rows_dev = tokens // (groups * planes)
+    to = lax.broadcasted_iota(jnp.int32, (tokens, tokens), 0)
+    at = lax.broadcasted_iota(jnp.int32, (tokens, tokens), 1)
+    j, t, row = to // (groups * rows_dev), (to // rows_dev) % groups, to % rows_dev
+    for r, out_ref in zip(distances, out_refs):
+        group = where_ref[0] ^ r
+        lanes = pl.ds(pl.multiple_of(group * group_width, 128), group_width)
+        place = row * (groups * planes) + (t ^ group) * planes + (j ^ where_ref[1])
+        order = (at == place).astype(jnp.bfloat16)
+        out_ref[:tokens] = k_ref[:, lanes]
+        out_ref[tokens : 2 * tokens] = v_ref[:, lanes]
+        mixed = jnp.dot(order, q_ref[:, lanes], preferred_element_type=jnp.float32)
+        out_ref[2 * tokens :] = mixed.astype(jnp.bfloat16)
+
+
+def bundles(where, queries, keys, values, groups, planes, distances):
+    tokens, width = queries.shape
+    vmem = pl.BlockSpec(memory_space=pltpu.VMEM)
+    result = jax.ShapeDtypeStruct((3 * tokens, width // groups), jnp.bfloat16)
+    return pl.pallas_call(
+        functools.partial(bundle_kernel, groups=groups, planes=planes, distances=distances),
+        in_specs=[pl.BlockSpec(memory_space=pltpu.SMEM)] + [vmem] * 3,
+        out_specs=[vmem] * len(distances),
+        out_shape=[result] * len(distances),
+        compiler_params=pltpu.CompilerParams(vmem_limit_bytes=VMEM_LIMIT),
+    )(where, queries, keys, values)
+
+
+def attend_kernel(*refs, sources, planes, blocks, part, targets, rows_step):
     q_refs = refs[:sources]
-    kv_refs = refs[sources : sources + parts]
-    o_refs = refs[sources + parts :]
-    rows, width = q_refs[0].shape[1:]
-    key_rows = [r.shape[0] * r.shape[2] for r in kv_refs]
+    kv_refs = refs[sources : sources + len(blocks)]
+    o_refs = refs[sources + len(blocks) :]
+    tokens, width = q_refs[0].shape
+    rows = tokens // sources
+    rows_dev = rows // planes
+    to = lax.broadcasted_iota(jnp.int32, (tokens, tokens), 0)
+    at = lax.broadcasted_iota(jnp.int32, (tokens, tokens), 1)
+    t, j, row = to // rows, (to // rows_dev) % planes, to % rows_dev
+    place = ((j % 2) * (planes // 2) + j // 2) * rows + t * rows_dev + row
+    order = (at == place).astype(jnp.bfloat16)
+    asked = [
+        jnp.dot(order, q[...], preferred_element_type=jnp.float32).astype(jnp.bfloat16) for q in q_refs
+    ]
     works = [
         (h, range(first, min(first + rows_step, len(targets))))
         for h in range(width // HEAD_DIM)
         for first in range(0, len(targets), rows_step)
     ]
 
-    def lanes(h):
-        return slice(h * HEAD_DIM, (h + 1) * HEAD_DIM)
+    def taken(ref, count, h, which):
+        cut = ref[: count * 2 * part, h * HEAD_DIM : (h + 1) * HEAD_DIM]
+        return cut.reshape(count, 2, part, HEAD_DIM)[:, which].reshape(count * part, HEAD_DIM)
 
     def scores_of(work):
         h, block = work
-        query = jnp.concatenate([q[targets[i], :, lanes(h)] for i in block for q in q_refs], axis=0)
+        lanes = slice(h * HEAD_DIM, (h + 1) * HEAD_DIM)
+        query = jnp.concatenate(
+            [q[targets[i] * rows : (targets[i] + 1) * rows, lanes] for i in block for q in asked], axis=0
+        )
         return [
             lax.dot_general(
                 query,
-                kv[:, 0, :, lanes(h)].reshape(count, HEAD_DIM),
+                taken(kv, count, h, 0),
                 (((1,), (1,)), ((), ())),
                 preferred_element_type=jnp.float32,
             )
-            for kv, count in zip(kv_refs, key_rows)
+            for kv, count in zip(kv_refs, blocks)
         ]
 
     def finish(work, scores):
@@ -55,17 +99,17 @@
         peak = functools.reduce(jnp.maximum, [jnp.max(s, axis=1, keepdims=True) for s in scores])
         peak = peak * EXP2_SCALE
         summed = None
-        for s, kv, count in zip(scores, kv_refs, key_rows):
+        for s, kv, count in zip(scores, kv_refs, blocks):
             weights = jnp.exp2(s * EXP2_SCALE - peak).astype(jnp.bfloat16)
-            value = kv[:, 1, :, lanes(h)].reshape(count, HEAD_DIM)
+            value = taken(kv, count, h, 1)
             value = jnp.concatenate([value, jnp.ones_like(value)], axis=1)
-            part = jnp.dot(weights, value, preferred_element_type=jnp.float32)
-            summed = part if summed is None else summed + part
+            product = jnp.dot(weights, value, preferred_element_type=jnp.float32)
+            summed = product if summed is None else summed + product
         out = (summed[:, :HEAD_DIM] / summed[:, HEAD_DIM:]).astype(jnp.bfloat16)
         for n, i in enumerate(block):
             for r in range(sources):
-                at = (n * sources + r) * rows
-                o_refs[i][targets[i] ^ r, :, lanes(h)] = out[at : at + rows]
+                first = (n * sources + r) * rows
+                o_refs[i][targets[i] ^ r, :, h * HEAD_DIM : (h + 1) * HEAD_DIM] = out[first : first + rows]
 
     scores = scores_of(works[0])
     for n, work in enumerate(works):
@@ -74,29 +118,30 @@
         scores = following
 
 
-def attend(queries, keys_values, targets):
-    sources, rows, width = queries[0].shape
-    key_count = sum(kv.shape[0] * kv.shape[2] for kv in keys_values)
+def attend(queries, keys_values, targets, planes):
+    sources = len(queries)
+    tokens, width = queries[0].shape
+    rows = tokens // sources
+    blocks = [kv.shape[0] // (2 * tokens) for kv in keys_values]
+    key_count = sum(blocks) * tokens
     small = key_count <= 4096
     rows_step, step_width = (2, width) if small else (1, HEAD_DIM)
-    score_bytes = rows_step * sources * rows * key_count * 4
+    score_bytes = rows_step * tokens * key_count * 4
     limit = 8 * key_count * step_width + 3 * score_bytes + 6 * 1024 * 1024
-    q_spec = pl.BlockSpec((sources, rows, step_width), lambda h: (0, 0, h))
     return pl.pallas_call(
         functools.partial(
             attend_kernel,
             sources=sources,
-            parts=len(keys_values),
+            planes=planes,
+            blocks=blocks,
+            part=tokens,
             targets=targets,
             rows_step=rows_step,
         ),
         grid=(width // step_width,),
-        in_specs=[q_spec] * sources
-        + [
-            pl.BlockSpec(kv.shape[:-1] + (step_width,), lambda h: (0, 0, 0, h))
-            for kv in keys_values
-        ],
-        out_specs=[q_spec] * len(targets),
+        in_specs=[pl.BlockSpec((tokens, step_width), lambda h: (0, h))] * sources
+        + [pl.BlockSpec((kv.shape[0], step_width), lambda h: (0, h)) for kv in keys_values],
+        out_specs=[pl.BlockSpec((sources, rows, step_width), lambda h: (0, 0, h))] * len(targets),
         out_shape=[jax.ShapeDtypeStruct((sources, rows, width), jnp.bfloat16)] * len(targets),
         compiler_params=pltpu.CompilerParams(vmem_limit_bytes=min(limit, 60 * 1024 * 1024)),
     )(*queries, *keys_values)
@@ -275,66 +320,54 @@
     )(where, even, odd, left, right, conv_weight, conv_bias[None])
 
 
-def gather_cores(pieces):
-    same = jnp.concatenate(pieces, axis=0) if len(pieces) > 1 else pieces[0]
-    return [same, swap(same, "plane", 1)]
-
-
-def after(value, *others):
-    return lax.optimization_barrier((value,) + others)[0]
-
-
 def shards(queries, keys, values, w_out, shift_mod, scale_mod, w_final, conv_weight, conv_bias):
     groups = lax.axis_size("heads")
     planes = lax.axis_size("plane")
     heads_at = lax.axis_index("heads")
     plane_at = lax.axis_index("plane")
     devices = groups * planes
-    tokens, width = queries.shape
-    group_width = width // groups
+    tokens = queries.shape[0]
     rows_dev = tokens // devices
     where = jnp.stack(
         [heads_at, plane_at, heads_at * planes + plane_at, jnp.int32(devices)]
     ).astype(jnp.int32)
 
-    def group_of(source, r):
-        return lax.dynamic_slice_in_dim(source, (heads_at ^ r) * group_width, group_width, axis=1)
-
-    def across(piece):
-        return [piece] + [swap(piece, "plane", d) for d in range(2, planes, 2)]
-
-    piece = [jnp.stack([group_of(keys, r), group_of(values, r)])[None] for r in range(groups)]
-    got = [piece[0], swap(piece[1], "heads", 1), swap(piece[2], "heads", 2)]
-    got.append(swap(after(piece[3], got[2]), "heads", 3))
-
-    queries = after(queries, *piece)
-    to = lax.broadcasted_iota(jnp.int32, (tokens, tokens), 0)
-    at = lax.broadcasted_iota(jnp.int32, (tokens, tokens), 1)
-    j, t, row = to // (groups * rows_dev), (to // rows_dev) % groups, to % rows_dev
-    mixed = []
-    for r in range(groups):
-        place = row * devices + (t ^ (r ^ heads_at)) * planes + (j ^ plane_at)
-        part = jnp.dot(
-            (at == place).astype(jnp.bfloat16), group_of(queries, r), preferred_element_type=jnp.float32
-        )
-        mixed.append(part.astype(jnp.bfloat16).reshape(planes, groups, rows_dev, group_width))
-    mixed = jnp.stack(mixed, axis=1)
-    in_plane = [mixed[0]] + [swap(mixed[d], "plane", d) for d in range(1, planes)]
-    asked = []
-    for r in range(groups):
-        own = jnp.stack([part[r] for part in in_plane], axis=1)
-        own = own.reshape(groups, planes * rows_dev, group_width)
-        asked.append(own if r == 0 else swap(after(own, got[3]), "heads", r))
-
-    crossed = [across(p) for p in got]
-    keys_values = gather_cores(crossed[0] + crossed[1])
-    for r in range(2, groups):
-        keys_values += gather_cores(crossed[r])
-
+    made = bundles(where, queries, keys, values, groups, planes, range(groups))
+    got = {r: swap(made[r], "heads", r) if r else made[r] for r in range(groups)}
+
+    both_parts, share = 2 * tokens, tokens // planes
+    held = {r: [got[r]] for r in range(groups)}
+    for r in (0, 1, 2, 3):
+        for d in range(2, planes, 2):
+            asked = got[r][both_parts + d * share : both_parts + (d + 2) * share]
+            held[r].append(swap(jnp.concatenate([got[r][:both_parts], asked], axis=0), "plane", d))
+
+    keys_values, asked = [], {}
+    for distances in ((0, 1), (2,), (3,)):
+        passed = [h[:both_parts] for r in distances for h in held[r]]
+        passed += [h[both_parts + share : both_parts + 2 * share] for r in distances for h in held[r]]
+        mine = jnp.concatenate(passed, axis=0)
+        other = swap(mine, "plane", 1)
+        keys_values += [mine, other]
+        half = planes // 2
+        first = both_parts * half * len(distances)
+        for n, r in enumerate(distances):
+            start = first + n * half * share
+            asked[r] = jnp.concatenate(
+                [h[both_parts : both_parts + share] for h in held[r]]
+                + [other[start : start + half * share]],
+                axis=0,
+            )
+    asked = [asked[r] for r in range(groups)]
+
+    first, second = (1, 3), (2, 0)
     near, far = (0, 1), (3, 2)
-    sent = [swap(o, "heads", t) for t, o in zip(far, attend(asked, keys_values, far))]
-    kept = [o if t == 0 else swap(o, "heads", t) for t, o in zip(near, attend(asked, keys_values, near))]
-    partial = project(where, kept, near, w_out, 512)
+    results = {}
+    for targets in (first, second):
+        for t, o in zip(targets, attend(asked, keys_values, targets, planes)):
+            results[t] = o if t == 0 else swap(o, "heads", t)
+    partial = project(where, [results[t] for t in near], near, w_out, 512)
+    sent = [results[t] for t in far]
     even, odd = final_layer(
         where, sent, far, partial, w_out, scale_mod, shift_mod, w_final, rows_dev, planes
     )

time: 77.5 us -> 74.1 us (0.956)
  starting transfers between devices: 34.2 us -> 28.9 us
  local copies, waits for them, and re-layouts: 1.53 us -> 4.14 us
  matrix products: 1.35 us -> 0 us
  Pallas kernels: 13.1 us -> 14.4 us
    ppermute x1, starting transfers between devices: 6.49 us -> 2.54 us  [shards(): left = lax.ppermute(odd, both, [(i, i + 1) for i in range(devices - 1)])]
    unnamed x16 -> x20, local copies, waits for them, and re-layouts: 0.08 us -> 3.84 us
    another operation x8 -> x0, local copies, waits for them, and re-layouts: 1.39 us -> none  [the longest x1 1.35 us: shards(): jnp.stack([group_of(keys, r), group_of(values, r)])[None]]
    ppermute x19 -> x13, starting transfers between devices: 25.8 us -> 24.4 us  [swap(): return lax.ppermute(source, axis, [(i, i ^ distance) for i in range(count)])]
    dot_general x4 -> x0, matrix products: 1.35 us -> none  [shards(): jnp.dot((at == place).astype(jnp.bfloat16), group_of(queries, r), preferr...]
    pallas_call x2 -> x3, Pallas kernels: 4.11 us -> 5.34 us  [the longest x2 4.51 us: attend(): pl.pallas_call(functools.partial(attend_kernel, sources=sources, planes=p...]
    ppermute x19 -> x13, waiting for transfers between devices: 23.1 us -> 22.5 us  [swap(): return lax.ppermute(source, axis, [(i, i ^ distance) for i in range(count)])]
  transfers between devices with their start and end apart: 21 -> 15, of which waited for: 10 -> 6; matrix products, arithmetic and copies ran while one was open for 2% -> 1% of each run, Pallas kernels for 6% -> 7%
where the time goes in v4:
time: 74.1 us; the launch traced here: 73.9 us
  starting transfers between devices  28.9 us (39%)
  waiting for transfers between devices  25.8 us (35%)
  Pallas kernels  14.4 us (19%)
  local copies, waits for them, and re-layouts  4.14 us (6%)
    ppermute x13, starting transfers between devices, swap(): return lax.ppermute(source, axis, [(i, i ^ distance) for i in range(count)])  24.4 us
    ppermute x13, waiting for transfers between devices, swap(): return lax.ppermute(source, axis, [(i, i ^ distance) for i in range(count)])  22.5 us
    pallas_call x2, Pallas kernels, attend(): pl.pallas_call(functools.partial(attend_kernel, sources=sources, planes=p...  4.51 us
    pallas_call x1, Pallas kernels, final_layer(): pl.pallas_call(functools.partial(final_kernel, targets=targets, planes=pl...  3.98 us
    unnamed x20, local copies, waits for them, and re-layouts  3.84 us
    ppermute x1, waiting for transfers between devices, shards(): right = lax.ppermute(even, both, [(i + 1, i) for i in range(devices - 1)])  3.29 us
    pallas_call x1, Pallas kernels, project(): pl.pallas_call(functools.partial(project_kernel, targets=targets), grid_s...  2.9 us
    ppermute x1, starting transfers between devices, shards(): left = lax.ppermute(odd, both, [(i, i + 1) for i in range(devices - 1)])  2.54 us
  transfers between devices with their start and end apart: 15, of which 6 were waited for; matrix products, arithmetic and copies ran while one was open for 1% of the time, Pallas kernels for 7%

profile of v4, /device:TPU:1, one launch (start us, length us, event | category | flops | bytes accessed | tf_op | source)
XLA Modules:
  0.0 73.9 jit_solution(8419984425840785169)
XLA Ops:
  0.0 0.0 copy-start
  0.0 0.1 pad_add_fusion.where_ref
  0.1 0.0 copy-start.3
  0.1 1.1 %copy-done.3 = bf16[128,1536]{1,0:T(8,128)(2,1)S(1)} copy-done((bf16[128,1536]{1,0:T(8,128)(2,1)S(1)}, bf16[128,1536]{1,0:T(8,128)(2,1)}, u32[]{:S(2)}) %copy-start.3) | copy-done | bytes 393240
  1.2 0.0 copy-start.4
  1.2 1.2 %copy-done.4 = bf16[128,1536]{1,0:T(8,128)(2,1)S(1)} copy-done((bf16[128,1536]{1,0:T(8,128)(2,1)S(1)}, bf16[128,1536]{1,0:T(8,128)(2,1)}, u32[]{:S(2)}) %copy-start.4) | copy-done | bytes 393240
  2.5 0.0 copy-start.5
  2.5 1.4 %copy-done.5 = bf16[128,1536]{1,0:T(8,128)(2,1)S(1)} copy-done((bf16[128,1536]{1,0:T(8,128)(2,1)S(1)}, bf16[128,1536]{1,0:T(8,128)(2,1)}, u32[]{:S(2)}) %copy-start.5) | copy-done | bytes 393240
  3.8 0.8 %shard_map.91 = (bf16[384,384]{1,0:T(8,128)(2,1)S(1)}, bf16[384,384]{1,0:T(8,128)(2,1)S(1)}, bf16[384,384]{1,0:T(8,128)(2,1)S(1)}, bf16[384,384]{1,0:T(8,128)(2,1)S(1)}) custom-call(s32[4]{0:T(128)S(1)} %pad_add_fusion.where_ref, bf16[128,1536]{1,0:T(8,128)(2,1)S(1)} %copy-done.3, bf16[128,1536]{1,0:T(8,128)(2,1)S(1)} %copy-done.4, ...), custom_call_target="tpu_custom_call" | custom-call | tf_op jit(solution)/shard_map/pallas_call | solution.py:47
  4.8 2.1 %collective-permute-start = (bf16[320,384]{1,0:T(8,128)(2,1)S(1)}, bf16[320,384]{1,0:T(8,128)(2,1)S(1)}, u32[]{:S(2)}, u32[]{:S(2)}) collective-permute-start(bf16[320,384]{1,0:T(8,128)(2,1)S(1)} %pad_maximum_fusion.2), channel_id=1, source_target_pairs={{0,2},{1,3},{2,0},{3,1},{4,6},{5,7},{6,4},{7,5},{8,10},{9,11},{10,... | collective-permute-start | bytes 737288 | tf_op jit(solution)/shard_map/ppermute | solution.py:22
  6.9 1.3 %collective-permute-start.1 = (bf16[384,384]{1,0:T(8,128)(2,1)S(1)}, bf16[384,384]{1,0:T(8,128)(2,1)S(1)}, u32[]{:S(2)}, u32[]{:S(2)}) collective-permute-start(bf16[384,384]{1,0:T(8,128)(2,1)S(1)} %get-tuple-element.16), channel_id=1, source_target_pairs={{0,4},{4,0},{8,12},{12,8},{1,5},{5,1},{9,13},{13,9},{2,6},{6,2},{1... | collective-permute-start | bytes 884744 | tf_op jit(solution)/shard_map/ppermute | solution.py:22
  8.2 2.3 %collective-permute-start.4 = (bf16[384,384]{1,0:T(8,128)(2,1)S(1)}, bf16[384,384]{1,0:T(8,128)(2,1)S(1)}, u32[]{:S(2)}, u32[]{:S(2)}) collective-permute-start(bf16[384,384]{1,0:T(8,128)(2,1)S(1)} %get-tuple-element.17), channel_id=1, source_target_pairs={{0,8},{4,12},{8,0},{12,4},{1,9},{5,13},{9,1},{13,5},{2,10},{6,14},... | collective-permute-start | bytes 884744 | tf_op jit(solution)/shard_map/ppermute | solution.py:22
  10.5 0.0 collective-permute-start.7
  10.5 2.1 %collective-permute-done = bf16[320,384]{1,0:T(8,128)(2,1)S(1)} collective-permute-done((bf16[320,384]{1,0:T(8,128)(2,1)S(1)}, bf16[320,384]{1,0:T(8,128)(2,1)S(1)}, u32[]{:S(2)}, u32[]{:S(2)}) %collective-permute-start) | collective-permute-done | bytes 245792 | tf_op jit(solution)/shard_map/ppermute | solution.py:22
  12.6 7.2 %collective-permute-done.1 = bf16[384,384]{1,0:T(8,128)(2,1)S(1)} collective-permute-done((bf16[384,384]{1,0:T(8,128)(2,1)S(1)}, bf16[384,384]{1,0:T(8,128)(2,1)S(1)}, u32[]{:S(2)}, u32[]{:S(2)}) %collective-permute-start.1) | collective-permute-done | bytes 294944 | tf_op jit(solution)/shard_map/ppermute | solution.py:22
  19.8 0.1 fusion.5
  19.9 0.5 collective-permute-start.2
  20.4 0.0 collective-permute-done.4
  20.5 1.1 %collective-permute-start.5 = (bf16[320,384]{1,0:T(8,128)(2,1)S(1)}, bf16[320,384]{1,0:T(8,128)(2,1)S(1)}, u32[]{:S(2)}, u32[]{:S(2)}) collective-permute-start(bf16[320,384]{1,0:T(8,128)(2,1)S(1)} %pad_maximum_fusion.4), channel_id=1, source_target_pairs={{0,2},{1,3},{2,0},{3,1},{4,6},{5,7},{6,4},{7,5},{8,10},{9,11},{10,... | collective-permute-start | bytes 737288 | tf_op jit(solution)/shard_map/ppermute | solution.py:22
  21.6 7.5 %collective-permute-done.7 = bf16[384,384]{1,0:T(8,128)(2,1)S(1)} collective-permute-done((bf16[384,384]{1,0:T(8,128)(2,1)S(1)}, bf16[384,384]{1,0:T(8,128)(2,1)S(1)}, u32[]{:S(2)}, u32[]{:S(2)}) %collective-permute-start.7) | collective-permute-done | bytes 294944 | tf_op jit(solution)/shard_map/ppermute | solution.py:22
  29.2 0.3 collective-permute-start.8
  29.5 0.0 collective-permute-done.2
  29.7 5.7 %collective-permute-start.3 = (bf16[1152,384]{1,0:T(8,128)(2,1)S(1)}, bf16[1152,384]{1,0:T(8,128)(2,1)S(1)}, u32[]{:S(2)}, u32[]{:S(2)}) collective-permute-start(bf16[1152,384]{1,0:T(8,128)(2,1)S(1)} %get-tuple-element.44.refs_4_), channel_id=1, source_target_pairs={{0,1},{1,0},{2,3},{3,2},{4,5},{5,4},{6,7},{7,6},{8,9},{9,8},{10,11... | collective-permute-start | bytes 2654216 | tf_op jit(solution)/shard_map/ppermute | solution.py:22
  35.4 0.0 collective-permute-done.5
  35.5 3.9 %collective-permute-start.6 = (bf16[576,384]{1,0:T(8,128)(2,1)S(1)}, bf16[576,384]{1,0:T(8,128)(2,1)S(1)}, u32[]{:S(2)}, u32[]{:S(2)}) collective-permute-start(bf16[576,384]{1,0:T(8,128)(2,1)S(1)} %pad_maximum_fusion.refs_6_), channel_id=1, source_target_pairs={{0,1},{1,0},{2,3},{3,2},{4,5},{5,4},{6,7},{7,6},{8,9},{9,8},{10,11... | collective-permute-start | bytes 1327112 | tf_op jit(solution)/shard_map/ppermute | solution.py:22
  39.4 0.0 collective-permute-done.8
  39.5 2.5 %collective-permute-start.9 = (bf16[576,384]{1,0:T(8,128)(2,1)S(1)}, bf16[576,384]{1,0:T(8,128)(2,1)S(1)}, u32[]{:S(2)}, u32[]{:S(2)}) collective-permute-start(bf16[576,384]{1,0:T(8,128)(2,1)S(1)} %pad_maximum_fusion.1.refs_8_), channel_id=1, source_target_pairs={{0,1},{1,0},{2,3},{3,2},{4,5},{5,4},{6,7},{7,6},{8,9},{9,8},{10,11... | collective-permute-start | bytes 1327112 | tf_op jit(solution)/shard_map/ppermute | solution.py:22
  42.0 0.0 collective-permute-done.6.refs_7_
  42.0 1.4 %collective-permute-done.9.refs_9_ = bf16[576,384]{1,0:T(8,128)(2,1)S(1)} collective-permute-done((bf16[576,384]{1,0:T(8,128)(2,1)S(1)}, bf16[576,384]{1,0:T(8,128)(2,1)S(1)}, u32[]{:S(2)}, u32[]{:S(2)}) %collective-permute-start.9) | collective-permute-done | bytes 442400 | tf_op jit(solution)/shard_map/ppermute | solution.py:22
  43.4 0.0 collective-permute-done.3.refs_5_
  43.5 0.0 copy-start.2
  43.5 0.0 copy-start.6
  43.5 0.0 copy-start.7
  43.5 2.2 %shard_map.92 = (bf16[4,32,384]{2,1,0:T(8,128)(2,1)S(1)}, bf16[4,32,384]{2,1,0:T(8,128)(2,1)S(1)}) custom-call(bf16[128,384]{1,0:T(8,128)(2,1)S(1)} %get-tuple-element.47.refs_0_, bf16[128,384]{1,0:T(8,128)(2,1)S(1)} %get-tuple-element.48.refs_1_, bf16[128,384]{1,0:T(8,128)(2,1)S(1)} %pad_maximum_fusion.8.refs_2_, ...), custom_call_target="tpu_custom_call" | custom-call | tf_op jit(solution)/shard_map/pallas_call | solution.py:131
  45.8 2.4 %collective-permute-start.12 = (bf16[4,32,384]{2,1,0:T(8,128)(2,1)S(1)}, bf16[4,32,384]{2,1,0:T(8,128)(2,1)S(1)}, u32[]{:S(2)}, u32[]{:S(2)}) collective-permute-start(bf16[4,32,384]{2,1,0:T(8,128)(2,1)S(1)} %get-tuple-element.22), channel_id=1, source_target_pairs={{0,4},{4,0},{8,12},{12,8},{1,5},{5,1},{9,13},{13,9},{2,6},{6,2},{1... | collective-permute-start | bytes 294920 | tf_op jit(solution)/shard_map/ppermute | solution.py:22
  48.2 2.2 %collective-permute-start.10 = (bf16[4,32,384]{2,1,0:T(8,128)(2,1)S(1)}, bf16[4,32,384]{2,1,0:T(8,128)(2,1)S(1)}, u32[]{:S(2)}, u32[]{:S(2)}) collective-permute-start(bf16[4,32,384]{2,1,0:T(8,128)(2,1)S(1)} %get-tuple-element.19), channel_id=1, source_target_pairs={{0,12},{4,8},{8,4},{12,0},{1,13},{5,9},{9,5},{13,1},{2,14},{6,10},... | collective-permute-start | bytes 294920 | tf_op jit(solution)/shard_map/ppermute | solution.py:22
  50.4 2.3 %shard_map.93 = (bf16[4,32,384]{2,1,0:T(8,128)(2,1)S(1)}, bf16[4,32,384]{2,1,0:T(8,128)(2,1)S(1)}) custom-call(bf16[128,384]{1,0:T(8,128)(2,1)S(1)} %get-tuple-element.47.refs_0_, bf16[128,384]{1,0:T(8,128)(2,1)S(1)} %get-tuple-element.48.refs_1_, bf16[128,384]{1,0:T(8,128)(2,1)S(1)} %pad_maximum_fusion.8.refs_2_, ...), custom_call_target="tpu_custom_call" | custom-call | tf_op jit(solution)/shard_map/pallas_call | solution.py:131
  52.7 0.1 collective-permute-start.11
  52.7 0.0 collective-permute-done.12.refs_1_
  52.7 0.0 copy-done
  52.8 0.0 copy-start.1
  52.8 0.0 copy-start.8
  52.8 2.9 %shard_map.94.refs_2_ = f32[6,128,512]{2,1,0:T(8,128)S(1)} custom-call(s32[4]{0:T(128)S(1)} %pad_add_fusion.where_ref, bf16[4,32,384]{2,1,0:T(8,128)(2,1)S(1)} %get-tuple-element.21.refs_0_, bf16[4,32,384]{2,1,0:T(8,128)(2,1)S(1)} %collective-permute-done.12.refs_1_, bf16[1536,3072]{1,0:T(8,128)(2,1)S(1)} %copy-done), custom_call_target="tpu_custom_call" | custom-call | tf_op jit(solution)/shard_map/pallas_call | solution.py:166
  55.7 0.0 collective-permute-done.10.refs_0_
  55.7 4.3 %collective-permute-done.11.refs_1_ = bf16[4,32,384]{2,1,0:T(8,128)(2,1)S(1)} collective-permute-done((bf16[4,32,384]{2,1,0:T(8,128)(2,1)S(1)}, bf16[4,32,384]{2,1,0:T(8,128)(2,1)S(1)}, u32[]{:S(2)}, u32[]{:S(2)}) %collective-permute-start.11) | collective-permute-done | bytes 98336 | tf_op jit(solution)/shard_map/ppermute | solution.py:22
  60.0 0.0 copy-done.2
  60.0 0.0 copy-done.6
  60.0 0.0 copy-done.7
  60.0 4.0 %shard_map.95 = (bf16[128,32]{1,0:T(8,128)(2,1)S(1)}, bf16[128,32]{1,0:T(8,128)(2,1)S(1)}) custom-call(s32[4]{0:T(128)S(1)} %pad_add_fusion.where_ref, bf16[4,32,384]{2,1,0:T(8,128)(2,1)S(1)} %collective-permute-done.10.refs_0_, bf16[4,32,384]{2,1,0:T(8,128)(2,1)S(1)} %collective-permute-done.11.refs_1_, f32[6,128,512]{2,1,0:T(8,128)S(1)} %shard_map.94.refs_2_, ...), custom_call_target="tpu_custom_call" | custom-call | tf_op jit(solution)/shard_map/pallas_call | solution.py:251
  64.0 2.5 %collective-permute-start.13 = (bf16[128,32]{1,0:T(8,128)(2,1)S(1)}, bf16[128,32]{1,0:T(8,128)(2,1)S(1)}, u32[]{:S(2)}, u32[]{:S(2)}) collective-permute-start(bf16[128,32]{1,0:T(8,128)(2,1)S(1)} %get-tuple-element.24.odd_ref), channel_id=1, source_target_pairs={{0,1},{1,2},{2,3},{3,4},{4,5},{5,6},{6,7},{7,8},{8,9},{9,10},{10,1... | collective-permute-start | bytes 24584 | tf_op jit(solution)/shard_map/ppermute | solution.py:375
  66.5 1.9 %collective-permute-start.14 = (bf16[128,32]{1,0:T(8,128)(2,1)S(1)}, bf16[128,32]{1,0:T(8,128)(2,1)S(1)}, u32[]{:S(2)}, u32[]{:S(2)}) collective-permute-start(bf16[128,32]{1,0:T(8,128)(2,1)S(1)} %get-tuple-element.23.even_ref), channel_id=1, source_target_pairs={{1,0},{2,1},{3,2},{4,3},{5,4},{6,5},{7,6},{8,7},{9,8},{10,9},{11,1... | collective-permute-start | bytes 24584 | tf_op jit(solution)/shard_map/ppermute | solution.py:376
  68.4 0.0 collective-permute-done.13.left_ref
  68.4 3.3 %collective-permute-done.14.right_ref = bf16[128,32]{1,0:T(8,128)(2,1)S(1)} collective-permute-done((bf16[128,32]{1,0:T(8,128)(2,1)S(1)}, bf16[128,32]{1,0:T(8,128)(2,1)S(1)}, u32[]{:S(2)}, u32[]{:S(2)}) %collective-permute-start.14) | collective-permute-done | bytes 8224 | tf_op jit(solution)/shard_map/ppermute | solution.py:376
  71.7 0.0 copy-done.1
  71.7 0.0 copy-done.8
  71.7 2.2 %shard_map.96 = bf16[4,2,64,512]{3,2,1,0:T(8,128)(2,1)} custom-call(s32[4]{0:T(128)S(1)} %pad_add_fusion.where_ref, bf16[128,32]{1,0:T(8,128)(2,1)S(1)} %get-tuple-element.23.even_ref, bf16[128,32]{1,0:T(8,128)(2,1)S(1)} %get-tuple-element.24.odd_ref, bf16[128,32]{1,0:T(8,128)(2,1)S(1)} %collective-permute-done.13.left_ref, ...), custom_call_target="tpu_custom_call" | custom-call | tf_op jit(solution)/shard_map/pallas_call | solution.py:313
  (31 shorter events, 0.6 us)
Async XLA Ops:
  0.0 52.7 %copy-start = (bf16[1536,3072]{1,0:T(8,128)(2,1)S(1)}, bf16[1536,3072]{1,0:T(8,128)(2,1)}, u32[]{:S(2)}) copy-start(bf16[1536,3072]{1,0:T(8,128)(2,1)} %refs_3_.1) | copy-start | bytes 28311556
  0.1 1.1 %copy-start.3 = (bf16[128,1536]{1,0:T(8,128)(2,1)S(1)}, bf16[128,1536]{1,0:T(8,128)(2,1)}, u32[]{:S(2)}) copy-start(bf16[128,1536]{1,0:T(8,128)(2,1)} %q_ref.1) | copy-start | bytes 1179652
  1.2 1.2 %copy-start.4 = (bf16[128,1536]{1,0:T(8,128)(2,1)S(1)}, bf16[128,1536]{1,0:T(8,128)(2,1)}, u32[]{:S(2)}) copy-start(bf16[128,1536]{1,0:T(8,128)(2,1)} %k_ref.1) | copy-start | bytes 1179652
  2.5 1.4 %copy-start.5 = (bf16[128,1536]{1,0:T(8,128)(2,1)S(1)}, bf16[128,1536]{1,0:T(8,128)(2,1)}, u32[]{:S(2)}) copy-start(bf16[128,1536]{1,0:T(8,128)(2,1)} %v_ref.1) | copy-start | bytes 1179652
  4.8 7.8 %collective-permute-start = (bf16[320,384]{1,0:T(8,128)(2,1)S(1)}, bf16[320,384]{1,0:T(8,128)(2,1)S(1)}, u32[]{:S(2)}, u32[]{:S(2)}) collective-permute-start(bf16[320,384]{1,0:T(8,128)(2,1)S(1)} %pad_maximum_fusion.2), channel_id=1, source_target_pairs={{0,2},{1,3},{2,0},{3,1},{4,6},{5,7},{6,4},{7,5},{8,10},{9,11},{10,... | collective-permute-start | bytes 737288 | tf_op jit(solution)/shard_map/ppermute | solution.py:22
  6.9 13.0 %collective-permute-start.1 = (bf16[384,384]{1,0:T(8,128)(2,1)S(1)}, bf16[384,384]{1,0:T(8,128)(2,1)S(1)}, u32[]{:S(2)}, u32[]{:S(2)}) collective-permute-start(bf16[384,384]{1,0:T(8,128)(2,1)S(1)} %get-tuple-element.16), channel_id=1, source_target_pairs={{0,4},{4,0},{8,12},{12,8},{1,5},{5,1},{9,13},{13,9},{2,6},{6,2},{1... | collective-permute-start | bytes 884744 | tf_op jit(solution)/shard_map/ppermute | solution.py:22
  8.2 12.2 %collective-permute-start.4 = (bf16[384,384]{1,0:T(8,128)(2,1)S(1)}, bf16[384,384]{1,0:T(8,128)(2,1)S(1)}, u32[]{:S(2)}, u32[]{:S(2)}) collective-permute-start(bf16[384,384]{1,0:T(8,128)(2,1)S(1)} %get-tuple-element.17), channel_id=1, source_target_pairs={{0,8},{4,12},{8,0},{12,4},{1,9},{5,13},{9,1},{13,5},{2,10},{6,14},... | collective-permute-start | bytes 884744 | tf_op jit(solution)/shard_map/ppermute | solution.py:22
  10.5 18.7 %collective-permute-start.7 = (bf16[384,384]{1,0:T(8,128)(2,1)S(1)}, bf16[384,384]{1,0:T(8,128)(2,1)S(1)}, u32[]{:S(2)}, u32[]{:S(2)}) collective-permute-start(bf16[384,384]{1,0:T(8,128)(2,1)S(1)} %get-tuple-element.18), channel_id=1, source_target_pairs={{0,12},{4,8},{8,4},{12,0},{1,13},{5,9},{9,5},{13,1},{2,14},{6,10},... | collective-permute-start | bytes 884744 | tf_op jit(solution)/shard_map/ppermute | solution.py:22
  19.9 9.6 %collective-permute-start.2 = (bf16[320,384]{1,0:T(8,128)(2,1)S(1)}, bf16[320,384]{1,0:T(8,128)(2,1)S(1)}, u32[]{:S(2)}, u32[]{:S(2)}) collective-permute-start(bf16[320,384]{1,0:T(8,128)(2,1)S(1)} %pad_maximum_fusion.3), channel_id=1, source_target_pairs={{0,2},{1,3},{2,0},{3,1},{4,6},{5,7},{6,4},{7,5},{8,10},{9,11},{10,... | collective-permute-start | bytes 737288 | tf_op jit(solution)/shard_map/ppermute | solution.py:22
  20.5 14.9 %collective-permute-start.5 = (bf16[320,384]{1,0:T(8,128)(2,1)S(1)}, bf16[320,384]{1,0:T(8,128)(2,1)S(1)}, u32[]{:S(2)}, u32[]{:S(2)}) collective-permute-start(bf16[320,384]{1,0:T(8,128)(2,1)S(1)} %pad_maximum_fusion.4), channel_id=1, source_target_pairs={{0,2},{1,3},{2,0},{3,1},{4,6},{5,7},{6,4},{7,5},{8,10},{9,11},{10,... | collective-permute-start | bytes 737288 | tf_op jit(solution)/shard_map/ppermute | solution.py:22
  29.2 10.2 %collective-permute-start.8 = (bf16[320,384]{1,0:T(8,128)(2,1)S(1)}, bf16[320,384]{1,0:T(8,128)(2,1)S(1)}, u32[]{:S(2)}, u32[]{:S(2)}) collective-permute-start(bf16[320,384]{1,0:T(8,128)(2,1)S(1)} %pad_maximum_fusion.5), channel_id=1, source_target_pairs={{0,2},{1,3},{2,0},{3,1},{4,6},{5,7},{6,4},{7,5},{8,10},{9,11},{10,... | collective-permute-start | bytes 737288 | tf_op jit(solution)/shard_map/ppermute | solution.py:22
  29.7 13.8 %collective-permute-start.3 = (bf16[1152,384]{1,0:T(8,128)(2,1)S(1)}, bf16[1152,384]{1,0:T(8,128)(2,1)S(1)}, u32[]{:S(2)}, u32[]{:S(2)}) collective-permute-start(bf16[1152,384]{1,0:T(8,128)(2,1)S(1)} %get-tuple-element.44.refs_4_), channel_id=1, source_target_pairs={{0,1},{1,0},{2,3},{3,2},{4,5},{5,4},{6,7},{7,6},{8,9},{9,8},{10,11... | collective-permute-start | bytes 2654216 | tf_op jit(solution)/shard_map/ppermute | solution.py:22
  35.5 6.5 %collective-permute-start.6 = (bf16[576,384]{1,0:T(8,128)(2,1)S(1)}, bf16[576,384]{1,0:T(8,128)(2,1)S(1)}, u32[]{:S(2)}, u32[]{:S(2)}) collective-permute-start(bf16[576,384]{1,0:T(8,128)(2,1)S(1)} %pad_maximum_fusion.refs_6_), channel_id=1, source_target_pairs={{0,1},{1,0},{2,3},{3,2},{4,5},{5,4},{6,7},{7,6},{8,9},{9,8},{10,11... | collective-permute-start | bytes 1327112 | tf_op jit(solution)/shard_map/ppermute | solution.py:22
  39.5 3.9 %collective-permute-start.9 = (bf16[576,384]{1,0:T(8,128)(2,1)S(1)}, bf16[576,384]{1,0:T(8,128)(2,1)S(1)}, u32[]{:S(2)}, u32[]{:S(2)}) collective-permute-start(bf16[576,384]{1,0:T(8,128)(2,1)S(1)} %pad_maximum_fusion.1.refs_8_), channel_id=1, source_target_pairs={{0,1},{1,0},{2,3},{3,2},{4,5},{5,4},{6,7},{7,6},{8,9},{9,8},{10,11... | collective-permute-start | bytes 1327112 | tf_op jit(solution)/shard_map/ppermute | solution.py:22
  43.5 16.5 %copy-start.2 = (bf16[3072,64]{0,1:T(8,128)(2,1)S(1)}, bf16[3072,64]{0,1:T(8,128)(2,1)}, u32[]{:S(2)}) copy-start(bf16[3072,64]{0,1:T(8,128)(2,1)} %param.15) | copy-start | bytes 1179652
  43.5 16.4 %copy-start.6 = (f32[3072]{0:T(1024)S(1)}, f32[3072]{0:T(1024)}, u32[]{:S(2)}) copy-start(f32[3072]{0:T(1024)} %param.14) | copy-start | bytes 36868
  43.5 16.4 %copy-start.7 = (f32[3072]{0:T(1024)S(1)}, f32[3072]{0:T(1024)}, u32[]{:S(2)}) copy-start(f32[3072]{0:T(1024)} %param.13) | copy-start | bytes 36868
  45.8 6.9 %collective-permute-start.12 = (bf16[4,32,384]{2,1,0:T(8,128)(2,1)S(1)}, bf16[4,32,384]{2,1,0:T(8,128)(2,1)S(1)}, u32[]{:S(2)}, u32[]{:S(2)}) collective-permute-start(bf16[4,32,384]{2,1,0:T(8,128)(2,1)S(1)} %get-tuple-element.22), channel_id=1, source_target_pairs={{0,4},{4,0},{8,12},{12,8},{1,5},{5,1},{9,13},{13,9},{2,6},{6,2},{1... | collective-permute-start | bytes 294920 | tf_op jit(solution)/shard_map/ppermute | solution.py:22
  48.2 7.5 %collective-permute-start.10 = (bf16[4,32,384]{2,1,0:T(8,128)(2,1)S(1)}, bf16[4,32,384]{2,1,0:T(8,128)(2,1)S(1)}, u32[]{:S(2)}, u32[]{:S(2)}) collective-permute-start(bf16[4,32,384]{2,1,0:T(8,128)(2,1)S(1)} %get-tuple-element.19), channel_id=1, source_target_pairs={{0,12},{4,8},{8,4},{12,0},{1,13},{5,9},{9,5},{13,1},{2,14},{6,10},... | collective-permute-start | bytes 294920 | tf_op jit(solution)/shard_map/ppermute | solution.py:22
  52.7 7.3 %collective-permute-start.11 = (bf16[4,32,384]{2,1,0:T(8,128)(2,1)S(1)}, bf16[4,32,384]{2,1,0:T(8,128)(2,1)S(1)}, u32[]{:S(2)}, u32[]{:S(2)}) collective-permute-start(bf16[4,32,384]{2,1,0:T(8,128)(2,1)S(1)} %get-tuple-element.20), channel_id=1, source_target_pairs={{0,8},{4,12},{8,0},{12,4},{1,9},{5,13},{9,1},{13,5},{2,10},{6,14},... | collective-permute-start | bytes 294920 | tf_op jit(solution)/shard_map/ppermute | solution.py:22
  52.8 19.0 %copy-start.1 = (bf16[432,512]{1,0:T(8,128)(2,1)S(1)}, bf16[432,512]{1,0:T(8,128)(2,1)}, u32[]{:S(2)}) copy-start(bf16[432,512]{1,0:T(8,128)(2,1)} %w_ref.1) | copy-start | bytes 1327108
  52.8 19.0 %copy-start.8 = (f32[512]{0:T(512)S(1)}, f32[512]{0:T(512)}, u32[]{:S(2)}) copy-start(f32[512]{0:T(512)} %param.17) | copy-start | bytes 6148
  64.0 4.5 %collective-permute-start.13 = (bf16[128,32]{1,0:T(8,128)(2,1)S(1)}, bf16[128,32]{1,0:T(8,128)(2,1)S(1)}, u32[]{:S(2)}, u32[]{:S(2)}) collective-permute-start(bf16[128,32]{1,0:T(8,128)(2,1)S(1)} %get-tuple-element.24.odd_ref), channel_id=1, source_target_pairs={{0,1},{1,2},{2,3},{3,4},{4,5},{5,6},{6,7},{7,8},{8,9},{9,10},{10,1... | collective-permute-start | bytes 24584 | tf_op jit(solution)/shard_map/ppermute | solution.py:375
  66.5 5.2 %collective-permute-start.14 = (bf16[128,32]{1,0:T(8,128)(2,1)S(1)}, bf16[128,32]{1,0:T(8,128)(2,1)S(1)}, u32[]{:S(2)}, u32[]{:S(2)}) collective-permute-start(bf16[128,32]{1,0:T(8,128)(2,1)S(1)} %get-tuple-element.23.even_ref), channel_id=1, source_target_pairs={{1,0},{2,1},{3,2},{4,3},{5,4},{6,5},{7,6},{8,7},{9,8},{10,9},{11,1... | collective-permute-start | bytes 24584 | tf_op jit(solution)/shard_map/ppermute | solution.py:376

commit v5 on v4

--- a/solution.py
+++ b/solution.py
@@ -14,6 +14,7 @@
 LATENT_CH = 16
 FRAMES = 4
 VMEM_LIMIT = 16 * 1024 * 1024
+VMEM_WHOLE = 63 * 1024 * 1024
 EXP2_SCALE = math.log2(math.e) / math.sqrt(HEAD_DIM)
 
 
@@ -22,35 +23,73 @@
     return lax.ppermute(source, axis, [(i, i ^ distance) for i in range(count)])
 
 
-def bundle_kernel(where_ref, q_ref, k_ref, v_ref, *out_refs, groups, planes, distances):
-    tokens, width = q_ref.shape
-    group_width = width // groups
+def run_copies(copies, semaphores, first=0):
+    started = [
+        pltpu.make_async_copy(source, target, semaphores.at[first + n])
+        for n, (source, target) in enumerate(copies)
+    ]
+    for copy in started:
+        copy.start()
+    return started
+
+
+def group_lanes(ref, r, groups):
+    width = ref.shape[1] // groups
+    return pl.ds(pl.multiple_of((lax.axis_index("heads") ^ r) * width, 128), width)
+
+
+def bundle_kernel(q_ref, k_ref, v_ref, *refs, groups, planes, parts):
+    out_refs, (mixed, semaphores) = refs[-2 - len(parts) : -2], refs[-2:]
+    tokens = q_ref.shape[0]
     rows_dev = tokens // (groups * planes)
+    copies = []
+    for (r, with_kv, _), out_ref in zip(parts, out_refs):
+        if with_kv:
+            lanes = group_lanes(k_ref, r, groups)
+            copies += [
+                (source.at[:, lanes], out_ref.at[pl.ds(n * tokens, tokens)])
+                for n, source in enumerate((k_ref, v_ref))
+            ]
+    waiting = run_copies(copies, semaphores)
+    heads_at, plane_at = lax.axis_index("heads"), lax.axis_index("plane")
     to = lax.broadcasted_iota(jnp.int32, (tokens, tokens), 0)
     at = lax.broadcasted_iota(jnp.int32, (tokens, tokens), 1)
     j, t, row = to // (groups * rows_dev), (to // rows_dev) % groups, to % rows_dev
-    for r, out_ref in zip(distances, out_refs):
-        group = where_ref[0] ^ r
-        lanes = pl.ds(pl.multiple_of(group * group_width, 128), group_width)
-        place = row * (groups * planes) + (t ^ group) * planes + (j ^ where_ref[1])
-        order = (at == place).astype(jnp.bfloat16)
-        out_ref[:tokens] = k_ref[:, lanes]
-        out_ref[tokens : 2 * tokens] = v_ref[:, lanes]
-        mixed = jnp.dot(order, q_ref[:, lanes], preferred_element_type=jnp.float32)
-        out_ref[2 * tokens :] = mixed.astype(jnp.bfloat16)
-
-
-def bundles(where, queries, keys, values, groups, planes, distances):
+    copies = []
+    for (r, with_kv, with_q), out_ref in zip(parts, out_refs):
+        if with_q:
+            place = row * (groups * planes) + (t ^ (heads_at ^ r)) * planes + (j ^ plane_at)
+            order = (at == place).astype(jnp.bfloat16)
+            query = jnp.dot(
+                order, q_ref[:, group_lanes(q_ref, r, groups)], preferred_element_type=jnp.float32
+            )
+            mixed[r] = query.astype(jnp.bfloat16)
+            first = 2 * tokens if with_kv else 0
+            copies.append((mixed.at[r], out_ref.at[pl.ds(first, tokens)]))
+    waiting += run_copies(copies, semaphores, len(waiting))
+    for copy in waiting:
+        copy.wait()
+
+
+def bundles(queries, keys, values, groups, planes, parts, *tokens_before):
     tokens, width = queries.shape
-    vmem = pl.BlockSpec(memory_space=pltpu.VMEM)
-    result = jax.ShapeDtypeStruct((3 * tokens, width // groups), jnp.bfloat16)
+    group_width = width // groups
+    anywhere = pl.BlockSpec(memory_space=pl.ANY)
+    copies = sum(2 * kv + q for _, kv, q in parts)
     return pl.pallas_call(
-        functools.partial(bundle_kernel, groups=groups, planes=planes, distances=distances),
-        in_specs=[pl.BlockSpec(memory_space=pltpu.SMEM)] + [vmem] * 3,
-        out_specs=[vmem] * len(distances),
-        out_shape=[result] * len(distances),
-        compiler_params=pltpu.CompilerParams(vmem_limit_bytes=VMEM_LIMIT),
-    )(where, queries, keys, values)
+        functools.partial(bundle_kernel, groups=groups, planes=planes, parts=parts),
+        in_specs=[pl.BlockSpec(memory_space=pltpu.VMEM)] + [anywhere] * (2 + len(tokens_before)),
+        out_specs=[anywhere] * len(parts),
+        out_shape=[
+            jax.ShapeDtypeStruct(((2 * kv + q) * tokens, group_width), jnp.bfloat16)
+            for _, kv, q in parts
+        ],
+        scratch_shapes=[
+            pltpu.VMEM((groups, tokens, group_width), jnp.bfloat16),
+            pltpu.SemaphoreType.DMA((copies,)),
+        ],
+        compiler_params=pltpu.CompilerParams(vmem_limit_bytes=VMEM_WHOLE),
+    )(queries, keys, values, *tokens_before)
 
 
 def attend_kernel(*refs, sources, planes, blocks, part, targets, rows_step):
@@ -147,54 +186,54 @@
     )(*queries, *keys_values)
 
 
+def projection_of(o_refs, w_refs, lined):
+    tokens, width = lined.shape[0], o_refs[0].shape[2]
+    for n, o_ref in enumerate(o_refs):
+        lined[:, n * width : (n + 1) * width] = o_ref[...].reshape(tokens, width)
+    weights = jnp.concatenate([w[...] for w in w_refs], axis=0)
+    return jnp.dot(lined[...], weights, preferred_element_type=jnp.float32)
+
+
+def projection_specs(attended, targets, tile):
+    o_spec = pl.BlockSpec(attended[0].shape, lambda i, *_: (0, 0, 0))
+    width = attended[0].shape[2]
+    return [o_spec] * len(targets) + [
+        pl.BlockSpec((width, tile), lambda i, where, t=t: (where[0] ^ t, i)) for t in targets
+    ]
+
+
 def project_kernel(where_ref, *refs, targets):
-    o_refs = refs[: len(targets)]
-    w_ref, out_ref, lined = refs[len(targets) :]
-    width = o_refs[0].shape[2]
-    tokens = lined.shape[0]
-    for n in range(len(targets)):
-        lined[:, n * width : (n + 1) * width] = o_refs[n][...].reshape(tokens, width)
-    rows = [pl.ds(pl.multiple_of((where_ref[0] ^ t) * width, 128), width) for t in targets]
-    weights = jnp.concatenate([w_ref[r, :] for r in rows], axis=0)
-    out_ref[...] = jnp.dot(lined[...], weights, preferred_element_type=jnp.float32)
+    count = len(targets)
+    out_ref, lined = refs[2 * count :]
+    out_ref[...] = projection_of(refs[:count], refs[count : 2 * count], lined)
 
 
 def project(where, attended, targets, w_out, tile):
     sources, rows, width = attended[0].shape
     tokens = sources * rows
-    inner, features = w_out.shape
+    features = w_out.shape[1]
     return pl.pallas_call(
         functools.partial(project_kernel, targets=targets),
         grid_spec=pltpu.PrefetchScalarGridSpec(
             num_scalar_prefetch=1,
             grid=(features // tile,),
-            in_specs=[pl.BlockSpec((sources, rows, width), lambda i, *_: (0, 0, 0))] * len(targets)
-            + [pl.BlockSpec((inner, tile), lambda i, *_: (0, i))],
+            in_specs=projection_specs(attended, targets, tile),
             out_specs=pl.BlockSpec((None, tokens, tile), lambda i, *_: (i, 0, 0)),
             scratch_shapes=[pltpu.VMEM((tokens, len(targets) * width), jnp.bfloat16)],
         ),
         out_shape=jax.ShapeDtypeStruct((features // tile, tokens, tile), jnp.float32),
         compiler_params=pltpu.CompilerParams(vmem_limit_bytes=VMEM_LIMIT),
-    )(where, *attended, w_out)
+    )(where, *attended, *[w_out] * len(targets))
 
 
 def final_kernel(where_ref, *refs, targets, planes, rows_dev):
-    o_refs = refs[: len(targets)]
-    partial_ref, w_ref, scale_ref, shift_ref, w_final_ref, even_ref, odd_ref, lined, projected = refs[
-        len(targets) :
-    ]
+    count = len(targets)
+    partial_ref, scale_ref, shift_ref, w_final_ref, even_ref, odd_ref, lined, projected = refs[2 * count :]
     step = pl.program_id(0)
     heads_at, plane_at = where_ref[0], where_ref[1]
     tokens = lined.shape[0]
-    width = o_refs[0].shape[2]
-    tile = w_ref.shape[1]
-    for n in range(len(targets)):
-        lined[:, n * width : (n + 1) * width] = o_refs[n][...].reshape(tokens, width)
-    rows = [pl.ds(pl.multiple_of((heads_at ^ t) * width, 128), width) for t in targets]
-    weights = jnp.concatenate([w_ref[r, :] for r in rows], axis=0)
-    projected[step] = partial_ref[...] + jnp.dot(
-        lined[...], weights, preferred_element_type=jnp.float32
-    )
+    tile = partial_ref.shape[1]
+    projected[step] = partial_ref[...] + projection_of(refs[:count], refs[count : 2 * count], lined)
 
     @pl.when(step == pl.num_programs(0) - 1)
     def _():
@@ -243,7 +282,7 @@
 
 def final_layer(where, attended, targets, partial, w_out, scale_mod, shift_mod, w_final, rows_dev, planes):
     sources, rows, width = attended[0].shape
-    inner, features = w_out.shape
+    features = w_out.shape[1]
     steps, tokens, tile = partial.shape
     channels = w_final.shape[1]
     whole = lambda shape: pl.BlockSpec(shape, lambda i, *_: (0,) * len(shape))
@@ -253,10 +292,9 @@
         grid_spec=pltpu.PrefetchScalarGridSpec(
             num_scalar_prefetch=1,
             grid=(steps,),
-            in_specs=[whole((sources, rows, width))] * len(targets)
+            in_specs=projection_specs(attended, targets, tile)
             + [
                 pl.BlockSpec((None, tokens, tile), lambda i, *_: (i, 0, 0)),
-                pl.BlockSpec((inner, tile), lambda i, *_: (0, i)),
                 whole((1, features)),
                 whole((1, features)),
                 whole((channels, features)),
@@ -269,7 +307,7 @@
         ),
         out_shape=[result] * 2,
         compiler_params=pltpu.CompilerParams(vmem_limit_bytes=VMEM_LIMIT),
-    )(where, *attended, partial, w_out, scale_mod[None], shift_mod[None], w_final.T)
+    )(where, *attended, *[w_out] * len(targets), partial, scale_mod[None], shift_mod[None], w_final.T)
 
 
 def convolve_kernel(where_ref, even_ref, odd_ref, left_ref, right_ref, w_ref, bias_ref, out_ref, latent):
@@ -320,6 +358,10 @@
     )(where, even, odd, left, right, conv_weight, conv_bias[None])
 
 
+def after(value, *others):
+    return lax.optimization_barrier((value,) + others)[0]
+
+
 def shards(queries, keys, values, w_out, shift_mod, scale_mod, w_final, conv_weight, conv_bias):
     groups = lax.axis_size("heads")
     planes = lax.axis_size("plane")
@@ -332,36 +374,49 @@
         [heads_at, plane_at, heads_at * planes + plane_at, jnp.int32(devices)]
     ).astype(jnp.int32)
 
-    made = bundles(where, queries, keys, values, groups, planes, range(groups))
-    got = {r: swap(made[r], "heads", r) if r else made[r] for r in range(groups)}
-
     both_parts, share = 2 * tokens, tokens // planes
-    held = {r: [got[r]] for r in range(groups)}
-    for r in (0, 1, 2, 3):
+    got = {2: bundles(queries, keys, values, groups, planes, ((2, 1, 1),))[0]}
+    parts = ((1, 1, 1), (3, 1, 0), (0, 1, 1), (3, 0, 1))
+    got[1], got[3], got[0], q_3 = bundles(queries, keys, values, groups, planes, parts, got[2])
+    got = {r: swap(got[r], "heads", r) if r else got[r] for r in (2, 3, 1, 0)}
+
+    held = {}
+    for r in range(groups):
+        held[r] = [got[r]]
         for d in range(2, planes, 2):
-            asked = got[r][both_parts + d * share : both_parts + (d + 2) * share]
-            held[r].append(swap(jnp.concatenate([got[r][:both_parts], asked], axis=0), "plane", d))
+            sent = got[r]
+            if sent.shape[0] > both_parts:
+                asked = sent[both_parts + d * share : both_parts + (d + 2) * share]
+                sent = jnp.concatenate([sent[:both_parts], asked], axis=0)
+            held[r].append(swap(after(sent, got[1]) if r == 0 else sent, "plane", d))
+    q_3 = swap(after(q_3, *held[1][1:], *held[2][1:]), "heads", 3)
 
     keys_values, asked = [], {}
+    half = planes // 2
     for distances in ((0, 1), (2,), (3,)):
         passed = [h[:both_parts] for r in distances for h in held[r]]
-        passed += [h[both_parts + share : both_parts + 2 * share] for r in distances for h in held[r]]
+        passed += [
+            h[both_parts + share : both_parts + 2 * share]
+            for r in distances
+            for h in held[r]
+            if h.shape[0] > both_parts
+        ]
         mine = jnp.concatenate(passed, axis=0)
         other = swap(mine, "plane", 1)
         keys_values += [mine, other]
-        half = planes // 2
         first = both_parts * half * len(distances)
         for n, r in enumerate(distances):
             start = first + n * half * share
-            asked[r] = jnp.concatenate(
-                [h[both_parts : both_parts + share] for h in held[r]]
-                + [other[start : start + half * share]],
-                axis=0,
-            )
-    asked = [asked[r] for r in range(groups)]
-
-    first, second = (1, 3), (2, 0)
-    near, far = (0, 1), (3, 2)
+            if start < mine.shape[0]:
+                asked[r] = [h[both_parts : both_parts + share] for h in held[r]]
+                asked[r].append(other[start : start + half * share])
+    arrival = list(range(0, planes, 2)) + list(range(1, planes, 2))
+    pieces = [q_3[d * share : (d + 1) * share] for d in arrival]
+    asked[3] = [swap(piece, "plane", d) if d else piece for d, piece in zip(arrival, pieces)]
+    asked = [jnp.concatenate(asked[r], axis=0) for r in range(groups)]
+
+    first, second = (3, 2), (1, 0)
+    near, far = (0, 3), (2, 1)
     results = {}
     for targets in (first, second):
         for t, o in zip(targets, attend(asked, keys_values, targets, planes)):

time: 74.1 us -> 103 us (1.39)
  Pallas kernels: 14.4 us -> 41.3 us
  waiting for transfers between devices: 25.8 us -> 30.7 us
  starting transfers between devices: 28.9 us -> 27.3 us
  local copies, waits for them, and re-layouts: 4.14 us -> 2.87 us
    pallas_call x1 -> x2, Pallas kernels: 0.83 us -> 28.1 us  [bundles(): pl.pallas_call(functools.partial(bundle_kernel, groups=groups, planes=pla...]
    ppermute x13 -> x17, waiting for transfers between devices: 22.5 us -> 27.4 us  [swap(): return lax.ppermute(source, axis, [(i, i ^ distance) for i in range(count)])]
    unnamed x20 -> x15, local copies, waits for them, and re-layouts: 3.84 us -> 0.12 us
    ppermute x13 -> x17, starting transfers between devices: 24.4 us -> 21.4 us  [swap(): return lax.ppermute(source, axis, [(i, i ^ distance) for i in range(count)])]
    slice x18 -> x14, local copies, waits for them, and re-layouts: 0.2 us -> 2.65 us  [the longest x2 0.98 us: shards(): sent = jnp.concatenate([sent[:both_parts], asked], axis=0)]
    ppermute x1, starting transfers between devices: 2.54 us -> 3.93 us  [shards(): left = lax.ppermute(odd, both, [(i, i + 1) for i in range(devices - 1)])]
  transfers between devices with their start and end apart: 15 -> 19, of which waited for: 6 -> 12; matrix products, arithmetic and copies ran while one was open for 1% -> 3% of each run, Pallas kernels for 7% -> 24%
where the time goes in v5:
time: 103 us
  Pallas kernels  41.3 us (40%)
  waiting for transfers between devices  30.7 us (30%)
  starting transfers between devices  27.3 us (27%)
  local copies, waits for them, and re-layouts  2.87 us (3%)
    pallas_call x2, Pallas kernels, bundles(): pl.pallas_call(functools.partial(bundle_kernel, groups=groups, planes=pla...  28.1 us
    ppermute x17, waiting for transfers between devices, swap(): return lax.ppermute(source, axis, [(i, i ^ distance) for i in range(count)])  27.4 us
    ppermute x17, starting transfers between devices, swap(): return lax.ppermute(source, axis, [(i, i ^ distance) for i in range(count)])  21.4 us
    pallas_call x2, Pallas kernels, attend(): pl.pallas_call(functools.partial(attend_kernel, sources=sources, planes=p...  4.53 us
    ppermute x1, starting transfers between devices, shards(): left = lax.ppermute(odd, both, [(i, i + 1) for i in range(devices - 1)])  3.93 us
    pallas_call x1, Pallas kernels, final_layer(): pl.pallas_call(functools.partial(final_kernel, targets=targets, planes=pl...  3.8 us
    ppermute x1, waiting for transfers between devices, shards(): right = lax.ppermute(even, both, [(i + 1, i) for i in range(devices - 1)])  3.29 us
    pallas_call x1, Pallas kernels, project(): pl.pallas_call(functools.partial(project_kernel, targets=targets), grid_s...  2.66 us
  transfers between devices with their start and end apart: 19, of which 12 were waited for; matrix products, arithmetic and copies ran while one was open for 3% of the time, Pallas kernels for 24%

profile of v5, /device:TPU:1, one launch (start us, length us, event | category | flops | bytes accessed | tf_op | source)
XLA Modules:
  0.0 102.6 jit_solution(14896331799658301942)
XLA Ops:
  0.0 8.1 %shard_map.91.refs_0_ = bf16[384,384]{1,0:T(8,128)(2,1)} custom-call(bf16[128,1536]{1,0:T(8,128)(2,1)} %q_ref.3, bf16[128,1536]{1,0:T(8,128)(2,1)} %k_ref.3, bf16[128,1536]{1,0:T(8,128)(2,1)} %v_ref.3), custom_call_target="tpu_custom_call" | custom-call | tf_op jit(solution)/shard_map/pallas_call | solution.py:79
  8.1 3.2 %collective-permute-start.4 = (bf16[384,384]{1,0:T(8,128)(2,1)}, bf16[384,384]{1,0:T(8,128)(2,1)S(1)}, u32[]{:S(2)}, u32[]{:S(2)}) collective-permute-start(bf16[384,384]{1,0:T(8,128)(2,1)} %shard_map.91.refs_0_), channel_id=1, source_target_pairs={{0,8},{4,12},{8,0},{12,4},{1,9},{5,13},{9,1},{13,5},{2,10},{6,14},... | collective-permute-start | bytes 884744 | tf_op jit(solution)/shard_map/ppermute | solution.py:23
  11.3 20.1 %shard_map.92 = (bf16[384,384]{1,0:T(8,128)(2,1)}, bf16[256,384]{1,0:T(8,128)(2,1)}, bf16[384,384]{1,0:T(8,128)(2,1)}, bf16[128,384]{1,0:T(8,128)(2,1)}) custom-call(bf16[128,1536]{1,0:T(8,128)(2,1)} %q_ref.3, bf16[128,1536]{1,0:T(8,128)(2,1)} %k_ref.3, bf16[128,1536]{1,0:T(8,128)(2,1)} %v_ref.3, bf16[384,384]{1,0:T(8,128)(2,1)} %shard_map.91.refs_0_), custom_call_target="tpu_custom_call" | custom-call | tf_op jit(solution)/shard_map/pallas_call | solution.py:79
  31.4 1.4 %collective-permute-start = (bf16[384,384]{1,0:T(8,128)(2,1)}, bf16[384,384]{1,0:T(8,128)(2,1)S(1)}, u32[]{:S(2)}, u32[]{:S(2)}) collective-permute-start(bf16[384,384]{1,0:T(8,128)(2,1)} %get-tuple-element.18), channel_id=1, source_target_pairs={{0,4},{4,0},{8,12},{12,8},{1,5},{5,1},{9,13},{13,9},{2,6},{6,2},{1... | collective-permute-start | bytes 884744 | tf_op jit(solution)/shard_map/ppermute | solution.py:23
  32.7 1.0 fusion.5
  33.7 0.8 slice.89
  34.5 4.7 %collective-permute-done = bf16[384,384]{1,0:T(8,128)(2,1)S(1)} collective-permute-done((bf16[384,384]{1,0:T(8,128)(2,1)}, bf16[384,384]{1,0:T(8,128)(2,1)S(1)}, u32[]{:S(2)}, u32[]{:S(2)}) %collective-permute-start) | collective-permute-done | bytes 294944 | tf_op jit(solution)/shard_map/ppermute | solution.py:23
  39.2 1.2 %collective-permute-start.1 = (bf16[320,384]{1,0:T(8,128)(2,1)S(1)}, bf16[320,384]{1,0:T(8,128)(2,1)S(1)}, u32[]{:S(2)}, u32[]{:S(2)}) collective-permute-start(bf16[320,384]{1,0:T(8,128)(2,1)S(1)} %pad_maximum_fusion.1), channel_id=1, source_target_pairs={{0,2},{1,3},{2,0},{3,1},{4,6},{5,7},{6,4},{7,5},{8,10},{9,11},{10,... | collective-permute-start | bytes 737288 | tf_op jit(solution)/shard_map/ppermute | solution.py:23
  40.4 1.1 %collective-permute-start.11 = (bf16[256,384]{1,0:T(8,128)(2,1)}, bf16[256,384]{1,0:T(8,128)(2,1)S(1)}, u32[]{:S(2)}, u32[]{:S(2)}) collective-permute-start(bf16[256,384]{1,0:T(8,128)(2,1)} %get-tuple-element.22), channel_id=1, source_target_pairs={{0,12},{4,8},{8,4},{12,0},{1,13},{5,9},{9,5},{13,1},{2,14},{6,10},... | collective-permute-start | bytes 589832 | tf_op jit(solution)/shard_map/ppermute | solution.py:23
  41.5 0.0 copy-start
  41.5 0.0 collective-permute-done.4
  41.6 0.3 collective-permute-start.5
  41.9 2.9 %collective-permute-done.1 = bf16[320,384]{1,0:T(8,128)(2,1)S(1)} collective-permute-done((bf16[320,384]{1,0:T(8,128)(2,1)S(1)}, bf16[320,384]{1,0:T(8,128)(2,1)S(1)}, u32[]{:S(2)}, u32[]{:S(2)}) %collective-permute-start.1) | collective-permute-done | bytes 245792 | tf_op jit(solution)/shard_map/ppermute | solution.py:23
  44.8 0.1 fusion.4
  44.9 1.3 %collective-permute-start.2 = (bf16[320,384]{1,0:T(8,128)(2,1)S(1)}, bf16[320,384]{1,0:T(8,128)(2,1)S(1)}, u32[]{:S(2)}, u32[]{:S(2)}) collective-permute-start(bf16[320,384]{1,0:T(8,128)(2,1)S(1)} %pad_maximum_fusion.2), channel_id=1, source_target_pairs={{0,2},{1,3},{2,0},{3,1},{4,6},{5,7},{6,4},{7,5},{8,10},{9,11},{10,... | collective-permute-start | bytes 737288 | tf_op jit(solution)/shard_map/ppermute | solution.py:23
  46.2 0.9 collective-permute-done.11
  47.1 0.3 collective-permute-start.12
  47.4 2.6 %collective-permute-done.5 = bf16[320,384]{1,0:T(8,128)(2,1)S(1)} collective-permute-done((bf16[320,384]{1,0:T(8,128)(2,1)S(1)}, bf16[320,384]{1,0:T(8,128)(2,1)S(1)}, u32[]{:S(2)}, u32[]{:S(2)}) %collective-permute-start.5) | collective-permute-done | bytes 245792 | tf_op jit(solution)/shard_map/ppermute | solution.py:23
  50.1 5.2 %collective-permute-done.2 = bf16[320,384]{1,0:T(8,128)(2,1)S(1)} collective-permute-done((bf16[320,384]{1,0:T(8,128)(2,1)S(1)}, bf16[320,384]{1,0:T(8,128)(2,1)S(1)}, u32[]{:S(2)}, u32[]{:S(2)}) %collective-permute-start.2) | collective-permute-done | bytes 245792 | tf_op jit(solution)/shard_map/ppermute | solution.py:23
  55.4 0.8 fusion.3
  56.2 5.0 %collective-permute-start.3 = (bf16[1152,384]{1,0:T(8,128)(2,1)S(1)}, bf16[1152,384]{1,0:T(8,128)(2,1)S(1)}, u32[]{:S(2)}, u32[]{:S(2)}) collective-permute-start(bf16[1152,384]{1,0:T(8,128)(2,1)S(1)} %get-tuple-element.44.refs_4_), channel_id=1, source_target_pairs={{0,1},{1,0},{2,3},{3,2},{4,5},{5,4},{6,7},{7,6},{8,9},{9,8},{10,11... | collective-permute-start | bytes 2654216 | tf_op jit(solution)/shard_map/ppermute | solution.py:23
  61.1 0.7 collective-permute-start.7
  61.9 0.4 collective-permute-start.6
  62.3 5.3 %collective-permute-done.7 = bf16[128,384]{1,0:T(8,128)(2,1)S(1)} collective-permute-done((bf16[128,384]{1,0:T(8,128)(2,1)}, bf16[128,384]{1,0:T(8,128)(2,1)S(1)}, u32[]{:S(2)}, u32[]{:S(2)}) %collective-permute-start.7) | collective-permute-done | bytes 98336 | tf_op jit(solution)/shard_map/ppermute | solution.py:23
  67.6 2.1 %collective-permute-start.10 = (bf16[32,384]{1,0:T(8,128)(2,1)S(1)}, bf16[32,384]{1,0:T(8,128)(2,1)S(1)}, u32[]{:S(2)}, u32[]{:S(2)}) collective-permute-start(bf16[32,384]{1,0:T(8,128)(2,1)S(1)} %get-tuple-element.48), channel_id=1, source_target_pairs={{0,3},{1,2},{2,1},{3,0},{4,7},{5,6},{6,5},{7,4},{8,11},{9,10},{10,... | collective-permute-start | bytes 73736 | tf_op jit(solution)/shard_map/ppermute | solution.py:23
  69.7 0.3 collective-permute-start.8
  69.9 0.0 collective-permute-done.12
  69.9 0.2 collective-permute-start.9
  70.2 1.5 %collective-permute-done.10 = bf16[32,384]{1,0:T(8,128)(2,1)S(1)} collective-permute-done((bf16[32,384]{1,0:T(8,128)(2,1)S(1)}, bf16[32,384]{1,0:T(8,128)(2,1)S(1)}, u32[]{:S(2)}, u32[]{:S(2)}) %collective-permute-start.10) | collective-permute-done | bytes 24608 | tf_op jit(solution)/shard_map/ppermute | solution.py:23
  71.6 0.4 collective-permute-start.13
  72.0 0.8 collective-permute-done.8
  72.9 0.0 collective-permute-done.9
  72.9 0.0 collective-permute-done.6.refs_7_
  72.9 0.0 collective-permute-done.3.refs_5_
  73.0 0.4 collective-permute-done.13.refs_9_
  73.4 2.3 %shard_map.93 = (bf16[4,32,384]{2,1,0:T(8,128)(2,1)S(1)}, bf16[4,32,384]{2,1,0:T(8,128)(2,1)S(1)}) custom-call(bf16[128,384]{1,0:T(8,128)(2,1)S(1)} %get-tuple-element.51.refs_0_, bf16[128,384]{1,0:T(8,128)(2,1)S(1)} %get-tuple-element.52.refs_1_, bf16[128,384]{1,0:T(8,128)(2,1)S(1)} %pad_maximum_fusion.6.refs_2_, ...), custom_call_target="tpu_custom_call" | custom-call | tf_op jit(solution)/shard_map/pallas_call | solution.py:170
  75.7 0.7 collective-permute-start.16
  76.4 2.3 %shard_map.94 = (bf16[4,32,384]{2,1,0:T(8,128)(2,1)S(1)}, bf16[4,32,384]{2,1,0:T(8,128)(2,1)S(1)}) custom-call(bf16[128,384]{1,0:T(8,128)(2,1)S(1)} %get-tuple-element.51.refs_0_, bf16[128,384]{1,0:T(8,128)(2,1)S(1)} %get-tuple-element.52.refs_1_, bf16[128,384]{1,0:T(8,128)(2,1)S(1)} %pad_maximum_fusion.6.refs_2_, ...), custom_call_target="tpu_custom_call" | custom-call | tf_op jit(solution)/shard_map/pallas_call | solution.py:170
  78.7 0.9 collective-permute-start.15
  79.6 2.0 %collective-permute-start.14 = (bf16[4,32,384]{2,1,0:T(8,128)(2,1)S(1)}, bf16[4,32,384]{2,1,0:T(8,128)(2,1)S(1)}, u32[]{:S(2)}, u32[]{:S(2)}) collective-permute-start(bf16[4,32,384]{2,1,0:T(8,128)(2,1)S(1)} %get-tuple-element.23), channel_id=1, source_target_pairs={{0,8},{4,12},{8,0},{12,4},{1,9},{5,13},{9,1},{13,5},{2,10},{6,14},... | collective-permute-start | bytes 294920 | tf_op jit(solution)/shard_map/ppermute | solution.py:23
  81.6 0.1 pad_add_fusion.where_ref
  81.7 0.0 collective-permute-done.16.refs_1_
  81.7 0.0 copy-done
  81.7 0.0 copy-start.2
  81.7 0.0 copy-start.3
  81.7 0.0 copy-start.4
  81.7 2.7 %shard_map.95.refs_4_ = f32[6,128,512]{2,1,0:T(8,128)S(1)} custom-call(s32[4]{0:T(128)S(1)} %pad_add_fusion.where_ref, bf16[4,32,384]{2,1,0:T(8,128)(2,1)S(1)} %get-tuple-element.25.refs_0_, bf16[4,32,384]{2,1,0:T(8,128)(2,1)S(1)} %collective-permute-done.16.refs_1_, bf16[1536,3072]{1,0:T(8,128)(2,1)S(1)} %copy-done, bf16[1536,3072]{1,0:T(8,128)(2,1)S(1)} %copy-done), custom_call_target="tpu_custom_call" | custom-call | tf_op jit(solution)/shard_map/pallas_call | solution.py:215
  84.4 0.8 collective-permute-done.15.refs_1_
  85.2 2.3 %collective-permute-done.14.refs_0_ = bf16[4,32,384]{2,1,0:T(8,128)(2,1)S(1)} collective-permute-done((bf16[4,32,384]{2,1,0:T(8,128)(2,1)S(1)}, bf16[4,32,384]{2,1,0:T(8,128)(2,1)S(1)}, u32[]{:S(2)}, u32[]{:S(2)}) %collective-permute-start.14) | collective-permute-done | bytes 98336 | tf_op jit(solution)/shard_map/ppermute | solution.py:23
  87.4 0.0 copy-done.2
  87.4 0.0 copy-done.3
  87.4 0.0 copy-done.4
  87.4 0.0 copy-start.1
  87.4 0.0 copy-start.5
  87.5 3.8 %shard_map.96 = (bf16[128,32]{1,0:T(8,128)(2,1)S(1)}, bf16[128,32]{1,0:T(8,128)(2,1)S(1)}) custom-call(s32[4]{0:T(128)S(1)} %pad_add_fusion.where_ref, bf16[4,32,384]{2,1,0:T(8,128)(2,1)S(1)} %collective-permute-done.14.refs_0_, bf16[4,32,384]{2,1,0:T(8,128)(2,1)S(1)} %collective-permute-done.15.refs_1_, bf16[1536,3072]{1,0:T(8,128)(2,1)S(1)} %copy-done, ...), custom_call_target="tpu_custom_call" | custom-call | tf_op jit(solution)/shard_map/pallas_call | solution.py:290
  91.3 3.9 %collective-permute-start.17 = (bf16[128,32]{1,0:T(8,128)(2,1)S(1)}, bf16[128,32]{1,0:T(8,128)(2,1)S(1)}, u32[]{:S(2)}, u32[]{:S(2)}) collective-permute-start(bf16[128,32]{1,0:T(8,128)(2,1)S(1)} %get-tuple-element.28.odd_ref), channel_id=1, source_target_pairs={{0,1},{1,2},{2,3},{3,4},{4,5},{5,6},{6,7},{7,8},{8,9},{9,10},{10,1... | collective-permute-start | bytes 24584 | tf_op jit(solution)/shard_map/ppermute | solution.py:430
  95.2 1.9 %collective-permute-start.18 = (bf16[128,32]{1,0:T(8,128)(2,1)S(1)}, bf16[128,32]{1,0:T(8,128)(2,1)S(1)}, u32[]{:S(2)}, u32[]{:S(2)}) collective-permute-start(bf16[128,32]{1,0:T(8,128)(2,1)S(1)} %get-tuple-element.27.even_ref), channel_id=1, source_target_pairs={{1,0},{2,1},{3,2},{4,3},{5,4},{6,5},{7,6},{8,7},{9,8},{10,9},{11,1... | collective-permute-start | bytes 24584 | tf_op jit(solution)/shard_map/ppermute | solution.py:431
  97.1 0.0 collective-permute-done.17.left_ref
  97.1 3.3 %collective-permute-done.18.right_ref = bf16[128,32]{1,0:T(8,128)(2,1)S(1)} collective-permute-done((bf16[128,32]{1,0:T(8,128)(2,1)S(1)}, bf16[128,32]{1,0:T(8,128)(2,1)S(1)}, u32[]{:S(2)}, u32[]{:S(2)}) %collective-permute-start.18) | collective-permute-done | bytes 8224 | tf_op jit(solution)/shard_map/ppermute | solution.py:431
  100.4 0.0 copy-done.1
  100.4 0.0 copy-done.5
  100.4 2.2 %shard_map.97 = bf16[4,2,64,512]{3,2,1,0:T(8,128)(2,1)} custom-call(s32[4]{0:T(128)S(1)} %pad_add_fusion.where_ref, bf16[128,32]{1,0:T(8,128)(2,1)S(1)} %get-tuple-element.27.even_ref, bf16[128,32]{1,0:T(8,128)(2,1)S(1)} %get-tuple-element.28.odd_ref, bf16[128,32]{1,0:T(8,128)(2,1)S(1)} %collective-permute-done.17.left_ref, ...), custom_call_target="tpu_custom_call" | custom-call | tf_op jit(solution)/shard_map/pallas_call | solution.py:351
  (23 shorter events, 0.4 us)
Async XLA Ops:
  8.1 33.4 %collective-permute-start.4 = (bf16[384,384]{1,0:T(8,128)(2,1)}, bf16[384,384]{1,0:T(8,128)(2,1)S(1)}, u32[]{:S(2)}, u32[]{:S(2)}) collective-permute-start(bf16[384,384]{1,0:T(8,128)(2,1)} %shard_map.91.refs_0_), channel_id=1, source_target_pairs={{0,8},{4,12},{8,0},{12,4},{1,9},{5,13},{9,1},{13,5},{2,10},{6,14},... | collective-permute-start | bytes 884744 | tf_op jit(solution)/shard_map/ppermute | solution.py:23
  31.4 7.8 %collective-permute-start = (bf16[384,384]{1,0:T(8,128)(2,1)}, bf16[384,384]{1,0:T(8,128)(2,1)S(1)}, u32[]{:S(2)}, u32[]{:S(2)}) collective-permute-start(bf16[384,384]{1,0:T(8,128)(2,1)} %get-tuple-element.18), channel_id=1, source_target_pairs={{0,4},{4,0},{8,12},{12,8},{1,5},{5,1},{9,13},{13,9},{2,6},{6,2},{1... | collective-permute-start | bytes 884744 | tf_op jit(solution)/shard_map/ppermute | solution.py:23
  39.2 5.6 %collective-permute-start.1 = (bf16[320,384]{1,0:T(8,128)(2,1)S(1)}, bf16[320,384]{1,0:T(8,128)(2,1)S(1)}, u32[]{:S(2)}, u32[]{:S(2)}) collective-permute-start(bf16[320,384]{1,0:T(8,128)(2,1)S(1)} %pad_maximum_fusion.1), channel_id=1, source_target_pairs={{0,2},{1,3},{2,0},{3,1},{4,6},{5,7},{6,4},{7,5},{8,10},{9,11},{10,... | collective-permute-start | bytes 737288 | tf_op jit(solution)/shard_map/ppermute | solution.py:23
  40.4 6.6 %collective-permute-start.11 = (bf16[256,384]{1,0:T(8,128)(2,1)}, bf16[256,384]{1,0:T(8,128)(2,1)S(1)}, u32[]{:S(2)}, u32[]{:S(2)}) collective-permute-start(bf16[256,384]{1,0:T(8,128)(2,1)} %get-tuple-element.22), channel_id=1, source_target_pairs={{0,12},{4,8},{8,4},{12,0},{1,13},{5,9},{9,5},{13,1},{2,14},{6,10},... | collective-permute-start | bytes 589832 | tf_op jit(solution)/shard_map/ppermute | solution.py:23
  41.5 40.2 %copy-start = (bf16[1536,3072]{1,0:T(8,128)(2,1)S(1)}, bf16[1536,3072]{1,0:T(8,128)(2,1)}, u32[]{:S(2)}) copy-start(bf16[1536,3072]{1,0:T(8,128)(2,1)} %refs_3_.3) | copy-start | bytes 28311556
  41.6 8.5 %collective-permute-start.5 = (bf16[320,384]{1,0:T(8,128)(2,1)S(1)}, bf16[320,384]{1,0:T(8,128)(2,1)S(1)}, u32[]{:S(2)}, u32[]{:S(2)}) collective-permute-start(bf16[320,384]{1,0:T(8,128)(2,1)S(1)} %pad_maximum_fusion.3), channel_id=1, source_target_pairs={{0,2},{1,3},{2,0},{3,1},{4,6},{5,7},{6,4},{7,5},{8,10},{9,11},{10,... | collective-permute-start | bytes 737288 | tf_op jit(solution)/shard_map/ppermute | solution.py:23
  44.9 10.4 %collective-permute-start.2 = (bf16[320,384]{1,0:T(8,128)(2,1)S(1)}, bf16[320,384]{1,0:T(8,128)(2,1)S(1)}, u32[]{:S(2)}, u32[]{:S(2)}) collective-permute-start(bf16[320,384]{1,0:T(8,128)(2,1)S(1)} %pad_maximum_fusion.2), channel_id=1, source_target_pairs={{0,2},{1,3},{2,0},{3,1},{4,6},{5,7},{6,4},{7,5},{8,10},{9,11},{10,... | collective-permute-start | bytes 737288 | tf_op jit(solution)/shard_map/ppermute | solution.py:23
  47.1 22.8 %collective-permute-start.12 = (bf16[256,384]{1,0:T(8,128)(2,1)S(1)}, bf16[256,384]{1,0:T(8,128)(2,1)S(1)}, u32[]{:S(2)}, u32[]{:S(2)}) collective-permute-start(bf16[256,384]{1,0:T(8,128)(2,1)S(1)} %collective-permute-done.11), channel_id=1, source_target_pairs={{0,2},{1,3},{2,0},{3,1},{4,6},{5,7},{6,4},{7,5},{8,10},{9,11},{10,... | collective-permute-start | bytes 589832 | tf_op jit(solution)/shard_map/ppermute | solution.py:23
  56.2 16.7 %collective-permute-start.3 = (bf16[1152,384]{1,0:T(8,128)(2,1)S(1)}, bf16[1152,384]{1,0:T(8,128)(2,1)S(1)}, u32[]{:S(2)}, u32[]{:S(2)}) collective-permute-start(bf16[1152,384]{1,0:T(8,128)(2,1)S(1)} %get-tuple-element.44.refs_4_), channel_id=1, source_target_pairs={{0,1},{1,0},{2,3},{3,2},{4,5},{5,4},{6,7},{7,6},{8,9},{9,8},{10,11... | collective-permute-start | bytes 2654216 | tf_op jit(solution)/shard_map/ppermute | solution.py:23
  61.1 6.4 %collective-permute-start.7 = (bf16[128,384]{1,0:T(8,128)(2,1)}, bf16[128,384]{1,0:T(8,128)(2,1)S(1)}, u32[]{:S(2)}, u32[]{:S(2)}) collective-permute-start(bf16[128,384]{1,0:T(8,128)(2,1)} %get-tuple-element.21), channel_id=1, source_target_pairs={{0,12},{4,8},{8,4},{12,0},{1,13},{5,9},{9,5},{13,1},{2,14},{6,10},... | collective-permute-start | bytes 294920 | tf_op jit(solution)/shard_map/ppermute | solution.py:23
  61.9 11.0 %collective-permute-start.6 = (bf16[576,384]{1,0:T(8,128)(2,1)S(1)}, bf16[576,384]{1,0:T(8,128)(2,1)S(1)}, u32[]{:S(2)}, u32[]{:S(2)}) collective-permute-start(bf16[576,384]{1,0:T(8,128)(2,1)S(1)} %pad_maximum_fusion.refs_6_), channel_id=1, source_target_pairs={{0,1},{1,0},{2,3},{3,2},{4,5},{5,4},{6,7},{7,6},{8,9},{9,8},{10,11... | collective-permute-start | bytes 1327112 | tf_op jit(solution)/shard_map/ppermute | solution.py:23
  67.6 4.1 %collective-permute-start.10 = (bf16[32,384]{1,0:T(8,128)(2,1)S(1)}, bf16[32,384]{1,0:T(8,128)(2,1)S(1)}, u32[]{:S(2)}, u32[]{:S(2)}) collective-permute-start(bf16[32,384]{1,0:T(8,128)(2,1)S(1)} %get-tuple-element.48), channel_id=1, source_target_pairs={{0,3},{1,2},{2,1},{3,0},{4,7},{5,6},{6,5},{7,4},{8,11},{9,10},{10,... | collective-permute-start | bytes 73736 | tf_op jit(solution)/shard_map/ppermute | solution.py:23
  69.7 3.2 %collective-permute-start.8 = (bf16[32,384]{1,0:T(8,128)(2,1)S(1)}, bf16[32,384]{1,0:T(8,128)(2,1)S(1)}, u32[]{:S(2)}, u32[]{:S(2)}) collective-permute-start(bf16[32,384]{1,0:T(8,128)(2,1)S(1)} %get-tuple-element.50), channel_id=1, source_target_pairs={{0,2},{1,3},{2,0},{3,1},{4,6},{5,7},{6,4},{7,5},{8,10},{9,11},{10,... | collective-permute-start | bytes 73736 | tf_op jit(solution)/shard_map/ppermute | solution.py:23
  69.9 2.9 %collective-permute-start.9 = (bf16[32,384]{1,0:T(8,128)(2,1)S(1)}, bf16[32,384]{1,0:T(8,128)(2,1)S(1)}, u32[]{:S(2)}, u32[]{:S(2)}) collective-permute-start(bf16[32,384]{1,0:T(8,128)(2,1)S(1)} %get-tuple-element.49), channel_id=1, source_target_pairs={{0,1},{1,0},{2,3},{3,2},{4,5},{5,4},{6,7},{7,6},{8,9},{9,8},{10,11... | collective-permute-start | bytes 73736 | tf_op jit(solution)/shard_map/ppermute | solution.py:23
  71.6 1.7 %collective-permute-start.13 = (bf16[512,384]{1,0:T(8,128)(2,1)S(1)}, bf16[512,384]{1,0:T(8,128)(2,1)S(1)}, u32[]{:S(2)}, u32[]{:S(2)}) collective-permute-start(bf16[512,384]{1,0:T(8,128)(2,1)S(1)} %constant_dynamic-update-slice_fusion.2.refs_8_), channel_id=1, source_target_pairs={{0,1},{1,0},{2,3},{3,2},{4,5},{5,4},{6,7},{7,6},{8,9},{9,8},{10,11... | collective-permute-start | bytes 1179656 | tf_op jit(solution)/shard_map/ppermute | solution.py:23
  75.7 6.0 %collective-permute-start.16 = (bf16[4,32,384]{2,1,0:T(8,128)(2,1)S(1)}, bf16[4,32,384]{2,1,0:T(8,128)(2,1)S(1)}, u32[]{:S(2)}, u32[]{:S(2)}) collective-permute-start(bf16[4,32,384]{2,1,0:T(8,128)(2,1)S(1)} %get-tuple-element.26), channel_id=1, source_target_pairs={{0,12},{4,8},{8,4},{12,0},{1,13},{5,9},{9,5},{13,1},{2,14},{6,10},... | collective-permute-start | bytes 294920 | tf_op jit(solution)/shard_map/ppermute | solution.py:23
  78.7 6.5 %collective-permute-start.15 = (bf16[4,32,384]{2,1,0:T(8,128)(2,1)S(1)}, bf16[4,32,384]{2,1,0:T(8,128)(2,1)S(1)}, u32[]{:S(2)}, u32[]{:S(2)}) collective-permute-start(bf16[4,32,384]{2,1,0:T(8,128)(2,1)S(1)} %get-tuple-element.24), channel_id=1, source_target_pairs={{0,4},{4,0},{8,12},{12,8},{1,5},{5,1},{9,13},{13,9},{2,6},{6,2},{1... | collective-permute-start | bytes 294920 | tf_op jit(solution)/shard_map/ppermute | solution.py:23
  79.6 7.8 %collective-permute-start.14 = (bf16[4,32,384]{2,1,0:T(8,128)(2,1)S(1)}, bf16[4,32,384]{2,1,0:T(8,128)(2,1)S(1)}, u32[]{:S(2)}, u32[]{:S(2)}) collective-permute-start(bf16[4,32,384]{2,1,0:T(8,128)(2,1)S(1)} %get-tuple-element.23), channel_id=1, source_target_pairs={{0,8},{4,12},{8,0},{12,4},{1,9},{5,13},{9,1},{13,5},{2,10},{6,14},... | collective-permute-start | bytes 294920 | tf_op jit(solution)/shard_map/ppermute | solution.py:23
  81.7 5.7 %copy-start.2 = (bf16[3072,64]{0,1:T(8,128)(2,1)S(1)}, bf16[3072,64]{0,1:T(8,128)(2,1)}, u32[]{:S(2)}) copy-start(bf16[3072,64]{0,1:T(8,128)(2,1)} %param.15) | copy-start | bytes 1179652
  81.7 5.7 %copy-start.3 = (f32[3072]{0:T(1024)S(1)}, f32[3072]{0:T(1024)}, u32[]{:S(2)}) copy-start(f32[3072]{0:T(1024)} %param.14) | copy-start | bytes 36868
  81.7 5.7 %copy-start.4 = (f32[3072]{0:T(1024)S(1)}, f32[3072]{0:T(1024)}, u32[]{:S(2)}) copy-start(f32[3072]{0:T(1024)} %param.13) | copy-start | bytes 36868
  87.4 13.0 %copy-start.1 = (bf16[432,512]{1,0:T(8,128)(2,1)S(1)}, bf16[432,512]{1,0:T(8,128)(2,1)}, u32[]{:S(2)}) copy-start(bf16[432,512]{1,0:T(8,128)(2,1)} %w_ref.1) | copy-start | bytes 1327108
  87.4 13.0 %copy-start.5 = (f32[512]{0:T(512)S(1)}, f32[512]{0:T(512)}, u32[]{:S(2)}) copy-start(f32[512]{0:T(512)} %param.17) | copy-start | bytes 6148
  91.3 5.9 %collective-permute-start.17 = (bf16[128,32]{1,0:T(8,128)(2,1)S(1)}, bf16[128,32]{1,0:T(8,128)(2,1)S(1)}, u32[]{:S(2)}, u32[]{:S(2)}) collective-permute-start(bf16[128,32]{1,0:T(8,128)(2,1)S(1)} %get-tuple-element.28.odd_ref), channel_id=1, source_target_pairs={{0,1},{1,2},{2,3},{3,4},{4,5},{5,6},{6,7},{7,8},{8,9},{9,10},{10,1... | collective-permute-start | bytes 24584 | tf_op jit(solution)/shard_map/ppermute | solution.py:430
  95.2 5.2 %collective-permute-start.18 = (bf16[128,32]{1,0:T(8,128)(2,1)S(1)}, bf16[128,32]{1,0:T(8,128)(2,1)S(1)}, u32[]{:S(2)}, u32[]{:S(2)}) collective-permute-start(bf16[128,32]{1,0:T(8,128)(2,1)S(1)} %get-tuple-element.27.even_ref), channel_id=1, source_target_pairs={{1,0},{2,1},{3,2},{4,3},{5,4},{6,5},{7,6},{8,7},{9,8},{10,9},{11,1... | collective-permute-start | bytes 24584 | tf_op jit(solution)/shard_map/ppermute | solution.py:431

commit v6 on v4

--- a/solution.py
+++ b/solution.py
@@ -14,6 +14,9 @@
 LATENT_CH = 16
 FRAMES = 4
 VMEM_LIMIT = 16 * 1024 * 1024
+VMEM_WHOLE = 63 * 1024 * 1024
+CHUNKS = ((0, 3),)
+VMEM_WHOLE = 63 * 1024 * 1024
 EXP2_SCALE = math.log2(math.e) / math.sqrt(HEAD_DIM)
 
 
@@ -22,17 +25,19 @@
     return lax.ppermute(source, axis, [(i, i ^ distance) for i in range(count)])
 
 
-def bundle_kernel(where_ref, q_ref, k_ref, v_ref, *out_refs, groups, planes, distances):
+def bundle_kernel(q_ref, k_ref, v_ref, *out_refs, groups, planes, cuts):
     tokens, width = q_ref.shape
     group_width = width // groups
     rows_dev = tokens // (groups * planes)
+    heads_at, plane_at = lax.axis_index("heads"), lax.axis_index("plane")
     to = lax.broadcasted_iota(jnp.int32, (tokens, tokens), 0)
     at = lax.broadcasted_iota(jnp.int32, (tokens, tokens), 1)
     j, t, row = to // (groups * rows_dev), (to // rows_dev) % groups, to % rows_dev
-    for r, out_ref in zip(distances, out_refs):
-        group = where_ref[0] ^ r
-        lanes = pl.ds(pl.multiple_of(group * group_width, 128), group_width)
-        place = row * (groups * planes) + (t ^ group) * planes + (j ^ where_ref[1])
+    for (r, low, high), out_ref in zip(cuts, out_refs):
+        group = heads_at ^ r
+        first = pl.multiple_of(group * group_width + low * HEAD_DIM, HEAD_DIM)
+        lanes = pl.ds(first, (high - low) * HEAD_DIM)
+        place = row * (groups * planes) + (t ^ group) * planes + (j ^ plane_at)
         order = (at == place).astype(jnp.bfloat16)
         out_ref[:tokens] = k_ref[:, lanes]
         out_ref[tokens : 2 * tokens] = v_ref[:, lanes]
@@ -40,17 +45,19 @@
         out_ref[2 * tokens :] = mixed.astype(jnp.bfloat16)
 
 
-def bundles(where, queries, keys, values, groups, planes, distances):
-    tokens, width = queries.shape
+def bundles(queries, keys, values, groups, planes, cuts):
+    tokens = queries.shape[0]
     vmem = pl.BlockSpec(memory_space=pltpu.VMEM)
-    result = jax.ShapeDtypeStruct((3 * tokens, width // groups), jnp.bfloat16)
     return pl.pallas_call(
-        functools.partial(bundle_kernel, groups=groups, planes=planes, distances=distances),
-        in_specs=[pl.BlockSpec(memory_space=pltpu.SMEM)] + [vmem] * 3,
-        out_specs=[vmem] * len(distances),
-        out_shape=[result] * len(distances),
-        compiler_params=pltpu.CompilerParams(vmem_limit_bytes=VMEM_LIMIT),
-    )(where, queries, keys, values)
+        functools.partial(bundle_kernel, groups=groups, planes=planes, cuts=cuts),
+        in_specs=[vmem] * 3,
+        out_specs=[vmem] * len(cuts),
+        out_shape=[
+            jax.ShapeDtypeStruct((3 * tokens, (high - low) * HEAD_DIM), jnp.bfloat16)
+            for _, low, high in cuts
+        ],
+        compiler_params=pltpu.CompilerParams(vmem_limit_bytes=VMEM_WHOLE),
+    )(queries, keys, values)
 
 
 def attend_kernel(*refs, sources, planes, blocks, part, targets, rows_step):
@@ -147,54 +154,59 @@
     )(*queries, *keys_values)
 
 
-def project_kernel(where_ref, *refs, targets):
-    o_refs = refs[: len(targets)]
-    w_ref, out_ref, lined = refs[len(targets) :]
-    width = o_refs[0].shape[2]
+def projection_of(o_refs, w_refs, lined):
     tokens = lined.shape[0]
-    for n in range(len(targets)):
-        lined[:, n * width : (n + 1) * width] = o_refs[n][...].reshape(tokens, width)
-    rows = [pl.ds(pl.multiple_of((where_ref[0] ^ t) * width, 128), width) for t in targets]
-    weights = jnp.concatenate([w_ref[r, :] for r in rows], axis=0)
-    out_ref[...] = jnp.dot(lined[...], weights, preferred_element_type=jnp.float32)
-
-
-def project(where, attended, targets, w_out, tile):
-    sources, rows, width = attended[0].shape
+    first = 0
+    for o_ref in o_refs:
+        width = o_ref.shape[2]
+        lined[:, first : first + width] = o_ref[...].reshape(tokens, width)
+        first += width
+    weights = jnp.concatenate([w[...] for w in w_refs], axis=0)
+    return jnp.dot(lined[...], weights, preferred_element_type=jnp.float32)
+
+
+def projection_specs(taken, tile, group_heads):
+    whole = [pl.BlockSpec(o.shape, lambda i, *_: (0, 0, 0)) for _, _, o in taken]
+    heads = [(t, low + n) for t, low, o in taken for n in range(o.shape[2] // HEAD_DIM)]
+    return whole + [
+        pl.BlockSpec(
+            (HEAD_DIM, tile), lambda i, where, t=t, h=h: ((where[0] ^ t) * group_heads + h, i)
+        )
+        for t, h in heads
+    ]
+
+
+def project_kernel(where_ref, *refs, count):
+    out_ref, lined = refs[-2:]
+    out_ref[...] = projection_of(refs[:count], refs[count:-2], lined)
+
+
+def project(where, taken, w_out, tile):
+    sources, rows, _ = taken[0][2].shape
     tokens = sources * rows
+    depth = sum(o.shape[2] for _, _, o in taken)
     inner, features = w_out.shape
     return pl.pallas_call(
-        functools.partial(project_kernel, targets=targets),
+        functools.partial(project_kernel, count=len(taken)),
         grid_spec=pltpu.PrefetchScalarGridSpec(
             num_scalar_prefetch=1,
             grid=(features // tile,),
-            in_specs=[pl.BlockSpec((sources, rows, width), lambda i, *_: (0, 0, 0))] * len(targets)
-            + [pl.BlockSpec((inner, tile), lambda i, *_: (0, i))],
+            in_specs=projection_specs(taken, tile, inner // HEAD_DIM // HEAD_GROUPS),
             out_specs=pl.BlockSpec((None, tokens, tile), lambda i, *_: (i, 0, 0)),
-            scratch_shapes=[pltpu.VMEM((tokens, len(targets) * width), jnp.bfloat16)],
+            scratch_shapes=[pltpu.VMEM((tokens, depth), jnp.bfloat16)],
         ),
         out_shape=jax.ShapeDtypeStruct((features // tile, tokens, tile), jnp.float32),
         compiler_params=pltpu.CompilerParams(vmem_limit_bytes=VMEM_LIMIT),
-    )(where, *attended, w_out)
-
-
-def final_kernel(where_ref, *refs, targets, planes, rows_dev):
-    o_refs = refs[: len(targets)]
-    partial_ref, w_ref, scale_ref, shift_ref, w_final_ref, even_ref, odd_ref, lined, projected = refs[
-        len(targets) :
-    ]
+    )(where, *[o for _, _, o in taken], *[w_out] * (depth // HEAD_DIM))
+
+
+def final_kernel(where_ref, *refs, count, planes, rows_dev):
+    partial_ref, scale_ref, shift_ref, w_final_ref, even_ref, odd_ref, lined, projected = refs[-8:]
     step = pl.program_id(0)
     heads_at, plane_at = where_ref[0], where_ref[1]
     tokens = lined.shape[0]
-    width = o_refs[0].shape[2]
-    tile = w_ref.shape[1]
-    for n in range(len(targets)):
-        lined[:, n * width : (n + 1) * width] = o_refs[n][...].reshape(tokens, width)
-    rows = [pl.ds(pl.multiple_of((heads_at ^ t) * width, 128), width) for t in targets]
-    weights = jnp.concatenate([w_ref[r, :] for r in rows], axis=0)
-    projected[step] = partial_ref[...] + jnp.dot(
-        lined[...], weights, preferred_element_type=jnp.float32
-    )
+    tile = partial_ref.shape[1]
+    projected[step] = partial_ref[...] + projection_of(refs[:count], refs[count:-8], lined)
 
     @pl.when(step == pl.num_programs(0) - 1)
     def _():
@@ -241,35 +253,42 @@
         odd_ref[...] = cells[:, half:]
 
 
-def final_layer(where, attended, targets, partial, w_out, scale_mod, shift_mod, w_final, rows_dev, planes):
-    sources, rows, width = attended[0].shape
+def final_layer(where, taken, partial, w_out, scale_mod, shift_mod, w_final, rows_dev, planes):
+    depth = sum(o.shape[2] for _, _, o in taken)
     inner, features = w_out.shape
     steps, tokens, tile = partial.shape
     channels = w_final.shape[1]
     whole = lambda shape: pl.BlockSpec(shape, lambda i, *_: (0,) * len(shape))
     result = jax.ShapeDtypeStruct((tokens, channels // 2), jnp.bfloat16)
     return pl.pallas_call(
-        functools.partial(final_kernel, targets=targets, planes=planes, rows_dev=rows_dev),
+        functools.partial(final_kernel, count=len(taken), planes=planes, rows_dev=rows_dev),
         grid_spec=pltpu.PrefetchScalarGridSpec(
             num_scalar_prefetch=1,
             grid=(steps,),
-            in_specs=[whole((sources, rows, width))] * len(targets)
+            in_specs=projection_specs(taken, tile, inner // HEAD_DIM // HEAD_GROUPS)
             + [
                 pl.BlockSpec((None, tokens, tile), lambda i, *_: (i, 0, 0)),
-                pl.BlockSpec((inner, tile), lambda i, *_: (0, i)),
                 whole((1, features)),
                 whole((1, features)),
                 whole((channels, features)),
             ],
             out_specs=[whole((tokens, channels // 2))] * 2,
             scratch_shapes=[
-                pltpu.VMEM((tokens, len(targets) * width), jnp.bfloat16),
+                pltpu.VMEM((tokens, depth), jnp.bfloat16),
                 pltpu.VMEM((steps, tokens, tile), jnp.float32),
             ],
         ),
         out_shape=[result] * 2,
         compiler_params=pltpu.CompilerParams(vmem_limit_bytes=VMEM_LIMIT),
-    )(where, *attended, partial, w_out, scale_mod[None], shift_mod[None], w_final.T)
+    )(
+        where,
+        *[o for _, _, o in taken],
+        *[w_out] * (depth // HEAD_DIM),
+        partial,
+        scale_mod[None],
+        shift_mod[None],
+        w_final.T,
+    )
 
 
 def convolve_kernel(where_ref, even_ref, odd_ref, left_ref, right_ref, w_ref, bias_ref, out_ref, latent):
@@ -320,6 +339,40 @@
     )(where, even, odd, left, right, conv_weight, conv_bias[None])
 
 
+def after(value, *others):
+    return lax.optimization_barrier((value,) + others)[0]
+
+
+def gather_plane(got, batch, both_parts, share):
+    planes = lax.axis_size("plane")
+    half, count = planes // 2, len(batch)
+    kv_rows = both_parts * count
+    crossed = []
+    for d in range(2, planes, 2):
+        sent = [got[r][:both_parts] for r in batch]
+        sent += [got[r][both_parts + d * share : both_parts + (d + 2) * share] for r in batch]
+        crossed.append(swap(jnp.concatenate(sent, axis=0), "plane", d))
+    near = [[got[r][both_parts : both_parts + share] for r in batch]]
+    far = [[got[r][both_parts + share : both_parts + 2 * share] for r in batch]]
+    for x in crossed:
+        firsts = [kv_rows + 2 * n * share for n in range(count)]
+        near.append([x[first : first + share] for first in firsts])
+        far.append([x[first + share : first + 2 * share] for first in firsts])
+    mine = [got[r][:both_parts] for r in batch] + [x[:kv_rows] for x in crossed]
+    mine = jnp.concatenate(mine + [q for pieces in far for q in pieces], axis=0)
+    other = swap(mine, "plane", 1)
+    asked = []
+    for n in range(count):
+        firsts = [kv_rows * half + (k * count + n) * share for k in range(half)]
+        asked.append(
+            jnp.concatenate(
+                [pieces[n] for pieces in near] + [other[first : first + share] for first in firsts],
+                axis=0,
+            )
+        )
+    return [mine, other], asked
+
+
 def shards(queries, keys, values, w_out, shift_mod, scale_mod, w_final, conv_weight, conv_bias):
     groups = lax.axis_size("heads")
     planes = lax.axis_size("plane")
@@ -328,48 +381,36 @@
     devices = groups * planes
     tokens = queries.shape[0]
     rows_dev = tokens // devices
+    both_parts, share = 2 * tokens, tokens // planes
     where = jnp.stack(
         [heads_at, plane_at, heads_at * planes + plane_at, jnp.int32(devices)]
     ).astype(jnp.int32)
 
-    made = bundles(where, queries, keys, values, groups, planes, range(groups))
-    got = {r: swap(made[r], "heads", r) if r else made[r] for r in range(groups)}
-
-    both_parts, share = 2 * tokens, tokens // planes
-    held = {r: [got[r]] for r in range(groups)}
-    for r in (0, 1, 2, 3):
-        for d in range(2, planes, 2):
-            asked = got[r][both_parts + d * share : both_parts + (d + 2) * share]
-            held[r].append(swap(jnp.concatenate([got[r][:both_parts], asked], axis=0), "plane", d))
-
-    keys_values, asked = [], {}
-    for distances in ((0, 1), (2,), (3,)):
-        passed = [h[:both_parts] for r in distances for h in held[r]]
-        passed += [h[both_parts + share : both_parts + 2 * share] for r in distances for h in held[r]]
-        mine = jnp.concatenate(passed, axis=0)
-        other = swap(mine, "plane", 1)
-        keys_values += [mine, other]
-        half = planes // 2
-        first = both_parts * half * len(distances)
-        for n, r in enumerate(distances):
-            start = first + n * half * share
-            asked[r] = jnp.concatenate(
-                [h[both_parts : both_parts + share] for h in held[r]]
-                + [other[start : start + half * share]],
-                axis=0,
-            )
-    asked = [asked[r] for r in range(groups)]
-
-    first, second = (1, 3), (2, 0)
-    near, far = (0, 1), (3, 2)
-    results = {}
-    for targets in (first, second):
-        for t, o in zip(targets, attend(asked, keys_values, targets, planes)):
-            results[t] = o if t == 0 else swap(o, "heads", t)
-    partial = project(where, [results[t] for t in near], near, w_out, 512)
-    sent = [results[t] for t in far]
+    cuts = [(r, low, high) for low, high in CHUNKS for r in (2, 1, 3, 0)]
+    made = dict(zip(cuts, bundles(queries, keys, values, groups, planes, cuts)))
+    made = {cut: swap(made[cut], "heads", cut[0]) if cut[0] else made[cut] for cut in cuts}
+
+    chunks = []
+    for low, high in CHUNKS:
+        got = [made[r, low, high] for r in range(groups)]
+        keys_values, asked = [], []
+        for batch in ((0, 1), (2,), (3,)):
+            kv, q = gather_plane(got, batch, both_parts, share)
+            keys_values += kv
+            asked += q
+        taken = []
+        for targets in ((3, 2), (1, 0)):
+            for t, o in zip(targets, attend(asked, keys_values, targets, planes)):
+                taken.append((t, low, o if t == 0 else swap(o, "heads", t)))
+        chunks.append(taken)
+
+    if len(chunks) == 1:
+        near, far = [chunks[0][n] for n in (3, 0)], [chunks[0][n] for n in (1, 2)]
+    else:
+        near, far = sum(chunks[:-1], []), chunks[-1]
+    partial = project(where, near, w_out, 512)
     even, odd = final_layer(
-        where, sent, far, partial, w_out, scale_mod, shift_mod, w_final, rows_dev, planes
+        where, far, partial, w_out, scale_mod, shift_mod, w_final, rows_dev, planes
     )
     both = ("heads", "plane")
     left = lax.ppermute(odd, both, [(i, i + 1) for i in range(devices - 1)])

time: 74.1 us -> 77.4 us (1.045); the launches traced: 73.9 us -> 76.4 us
  starting transfers between devices: 28.9 us -> 20.2 us
  local copies, waits for them, and re-layouts: 4.14 us -> 10.8 us
  other arithmetic: 0.33 us -> 2.63 us
  Pallas kernels: 14.4 us -> 16.2 us
    ppermute x13 -> x12, starting transfers between devices: 24.4 us -> 14.4 us  [swap(): return lax.ppermute(source, axis, [(i, i ^ distance) for i in range(count)])]
    slice x21 -> x20, local copies, waits for them, and re-layouts: 0.3 us -> 6.97 us  [the longest x4 3.2 us: gather_plane(): near = [[got[r][both_parts:both_parts + share] for r in batch]]]
    concatenate x9 -> x8, other arithmetic: 0.25 us -> 2.55 us  [the longest x3 2.35 us: gather_plane(): jnp.concatenate([pieces[n] for pieces in near] + [other[first:first + sha...]
    pallas_call x1, Pallas kernels: 0.83 us -> 2.45 us  [bundles(): pl.pallas_call(functools.partial(bundle_kernel, groups=groups, planes=pla...]
    ppermute x1, starting transfers between devices: 2.54 us -> 3.86 us  [shards(): left = lax.ppermute(odd, both, [(i, i + 1) for i in range(devices - 1)])]
    ppermute x13 -> x12, waiting for transfers between devices: 22.5 us -> 23 us  [swap(): return lax.ppermute(source, axis, [(i, i ^ distance) for i in range(count)])]
  transfers between devices with their start and end apart: 15 -> 14, of which waited for: 6 -> 6; matrix products, arithmetic and copies ran while one was open for 1% -> 12% of each run, Pallas kernels for 7% -> 7%
where the time goes in v6:
time: 77.4 us; the launch traced here: 76.4 us
  waiting for transfers between devices  26.3 us (34%)
  starting transfers between devices  20.2 us (26%)
  Pallas kernels  16.2 us (21%)
  local copies, waits for them, and re-layouts  10.8 us (14%)
  other arithmetic  2.63 us (3%)
    ppermute x12, waiting for transfers between devices, swap(): return lax.ppermute(source, axis, [(i, i ^ distance) for i in range(count)])  23 us
    ppermute x12, starting transfers between devices, swap(): return lax.ppermute(source, axis, [(i, i ^ distance) for i in range(count)])  14.4 us
    pallas_call x2, Pallas kernels, attend(): pl.pallas_call(functools.partial(attend_kernel, sources=sources, planes=p...  4.54 us
    pallas_call x1, Pallas kernels, final_layer(): pl.pallas_call(functools.partial(final_kernel, count=len(taken), planes=p...  4.09 us
    ppermute x1, starting transfers between devices, shards(): left = lax.ppermute(odd, both, [(i, i + 1) for i in range(devices - 1)])  3.86 us
    unnamed x20, local copies, waits for them, and re-layouts  3.79 us
    ppermute x1, waiting for transfers between devices, shards(): right = lax.ppermute(even, both, [(i + 1, i) for i in range(devices - 1)])  3.29 us
    slice x4, local copies, waits for them, and re-layouts, gather_plane(): near = [[got[r][both_parts:both_parts + share] for r in batch]]  3.2 us
  transfers between devices with their start and end apart: 14, of which 6 were waited for; matrix products, arithmetic and copies ran while one was open for 12% of the time, Pallas kernels for 7%

profile of v6, /device:TPU:1, one launch (start us, length us, event | category | flops | bytes accessed | tf_op | source)
XLA Modules:
  0.0 76.4 jit_solution(14479502828525987412)
XLA Ops:
  0.0 2.4 %shard_map.91 = (bf16[384,384]{1,0:T(8,128)(2,1)}, bf16[384,384]{1,0:T(8,128)(2,1)}, bf16[384,384]{1,0:T(8,128)(2,1)}, bf16[384,384]{1,0:T(8,128)(2,1)}) custom-call(bf16[128,1536]{1,0:T(8,128)(2,1)} %q_ref.1, bf16[128,1536]{1,0:T(8,128)(2,1)} %k_ref.1, bf16[128,1536]{1,0:T(8,128)(2,1)} %v_ref.1), custom_call_target="tpu_custom_call" | custom-call | tf_op jit(solution)/shard_map/pallas_call | solution.py:51
  2.4 2.1 %collective-permute-start = (bf16[384,384]{1,0:T(8,128)(2,1)}, bf16[384,384]{1,0:T(8,128)(2,1)S(1)}, u32[]{:S(2)}, u32[]{:S(2)}) collective-permute-start(bf16[384,384]{1,0:T(8,128)(2,1)} %get-tuple-element.16), channel_id=1, source_target_pairs={{0,4},{4,0},{8,12},{12,8},{1,5},{5,1},{9,13},{13,9},{2,6},{6,2},{1... | collective-permute-start | bytes 884744 | tf_op jit(solution)/shard_map/ppermute | solution.py:25
  4.6 2.2 %collective-permute-start.6 = (bf16[384,384]{1,0:T(8,128)(2,1)}, bf16[384,384]{1,0:T(8,128)(2,1)S(1)}, u32[]{:S(2)}, u32[]{:S(2)}) collective-permute-start(bf16[384,384]{1,0:T(8,128)(2,1)} %get-tuple-element.18), channel_id=1, source_target_pairs={{0,12},{4,8},{8,4},{12,0},{1,13},{5,9},{9,5},{13,1},{2,14},{6,10},... | collective-permute-start | bytes 884744 | tf_op jit(solution)/shard_map/ppermute | solution.py:25
  6.8 0.1 collective-permute-start.3
  6.9 0.8 %slice.110 = bf16[64,384]{1,0:T(8,128)(2,1)S(1)} slice(bf16[384,384]{1,0:T(8,128)(2,1)} %get-tuple-element.15), slice={[320:384], [0:384]} | slice | bytes 98304 | tf_op jit(solution)/shard_map/slice | solution.py:353
  7.7 1.0 %fusion.6 = (bf16[256,384]{1,0:T(8,128)(2,1)S(1)}, bf16[1152,384]{1,0:T(8,128)(2,1)S(1)}) fusion(bf16[384,384]{1,0:T(8,128)(2,1)} %get-tuple-element.15), kind=kLoop, calls=%fused_computation.23 | loop fusion | bytes 589824 | tf_op jit(solution)/shard_map/slice | solution.py:352
  8.7 2.9 %collective-permute-done = bf16[384,384]{1,0:T(8,128)(2,1)S(1)} collective-permute-done((bf16[384,384]{1,0:T(8,128)(2,1)}, bf16[384,384]{1,0:T(8,128)(2,1)S(1)}, u32[]{:S(2)}, u32[]{:S(2)}) %collective-permute-start) | collective-permute-done | bytes 294944 | tf_op jit(solution)/shard_map/ppermute | solution.py:25
  11.5 0.1 fusion.7
  11.6 0.1 pad_maximum_fusion
  11.6 1.1 %collective-permute-start.1 = (bf16[640,384]{1,0:T(8,128)(2,1)S(1)}, bf16[640,384]{1,0:T(8,128)(2,1)S(1)}, u32[]{:S(2)}, u32[]{:S(2)}) collective-permute-start(bf16[640,384]{1,0:T(8,128)(2,1)S(1)} %pad_maximum_fusion), channel_id=1, source_target_pairs={{0,2},{1,3},{2,0},{3,1},{4,6},{5,7},{6,4},{7,5},{8,10},{9,11},{10,... | collective-permute-start | bytes 1474568 | tf_op jit(solution)/shard_map/ppermute | solution.py:25
  12.8 7.0 %collective-permute-done.6 = bf16[384,384]{1,0:T(8,128)(2,1)S(1)} collective-permute-done((bf16[384,384]{1,0:T(8,128)(2,1)}, bf16[384,384]{1,0:T(8,128)(2,1)S(1)}, u32[]{:S(2)}, u32[]{:S(2)}) %collective-permute-start.6) | collective-permute-done | bytes 294944 | tf_op jit(solution)/shard_map/ppermute | solution.py:25
  19.8 1.3 %collective-permute-start.7 = (bf16[320,384]{1,0:T(8,128)(2,1)S(1)}, bf16[320,384]{1,0:T(8,128)(2,1)S(1)}, u32[]{:S(2)}, u32[]{:S(2)}) collective-permute-start(bf16[320,384]{1,0:T(8,128)(2,1)S(1)} %pad_maximum_fusion.4), channel_id=1, source_target_pairs={{0,2},{1,3},{2,0},{3,1},{4,6},{5,7},{6,4},{7,5},{8,10},{9,11},{10,... | collective-permute-start | bytes 737288 | tf_op jit(solution)/shard_map/ppermute | solution.py:25
  21.1 11.4 %collective-permute-done.3 = bf16[384,384]{1,0:T(8,128)(2,1)S(1)} collective-permute-done((bf16[384,384]{1,0:T(8,128)(2,1)}, bf16[384,384]{1,0:T(8,128)(2,1)S(1)}, u32[]{:S(2)}, u32[]{:S(2)}) %collective-permute-start.3) | collective-permute-done | bytes 294944 | tf_op jit(solution)/shard_map/ppermute | solution.py:25
  32.5 1.3 %collective-permute-start.4 = (bf16[320,384]{1,0:T(8,128)(2,1)S(1)}, bf16[320,384]{1,0:T(8,128)(2,1)S(1)}, u32[]{:S(2)}, u32[]{:S(2)}) collective-permute-start(bf16[320,384]{1,0:T(8,128)(2,1)S(1)} %pad_maximum_fusion.3), channel_id=1, source_target_pairs={{0,2},{1,3},{2,0},{3,1},{4,6},{5,7},{6,4},{7,5},{8,10},{9,11},{10,... | collective-permute-start | bytes 737288 | tf_op jit(solution)/shard_map/ppermute | solution.py:25
  33.8 0.6 fusion.2
  34.4 0.6 fusion.3
  35.0 0.0 collective-permute-done.7
  35.1 0.6 fusion.8
  35.7 1.9 %collective-permute-start.8 = (bf16[576,384]{1,0:T(8,128)(2,1)S(1)}, bf16[576,384]{1,0:T(8,128)(2,1)S(1)}, u32[]{:S(2)}, u32[]{:S(2)}) collective-permute-start(bf16[576,384]{1,0:T(8,128)(2,1)S(1)} %pad_maximum_fusion.2.refs_8_), channel_id=1, source_target_pairs={{0,1},{1,0},{2,3},{3,2},{4,5},{5,4},{6,7},{7,6},{8,9},{9,8},{10,11... | collective-permute-start | bytes 1327112 | tf_op jit(solution)/shard_map/ppermute | solution.py:25
  37.6 0.0 collective-permute-done.1
  37.6 0.1 slice_dynamic-update-slice_fusion
  37.7 1.4 %fusion.5 = (bf16[32,384]{1,0:T(8,128)(2,1)}, bf16[1152,384]{1,0:T(8,128)(2,1)S(1)}) fusion(bf16[384,384]{1,0:T(8,128)(2,1)} %get-tuple-element.15, bf16[1152,384]{1,0:T(8,128)(2,1)S(1)} %slice_dynamic-update-slice_fusion), kind=kLoop, calls=%fused_computation.22 | loop fusion | bytes 98304 | tf_op jit(solution)/shard_map/slice | solution.py:355
  39.1 0.6 fusion.4
  39.7 0.6 fusion.1
  40.3 0.0 collective-permute-start.2
  40.3 0.0 collective-permute-done.4
  40.3 0.6 fusion.9
  41.0 0.7 collective-permute-start.5
  41.7 0.0 collective-permute-done.8.refs_9_
  41.7 1.6 %collective-permute-done.5.refs_7_ = bf16[576,384]{1,0:T(8,128)(2,1)S(1)} collective-permute-done((bf16[576,384]{1,0:T(8,128)(2,1)S(1)}, bf16[576,384]{1,0:T(8,128)(2,1)S(1)}, u32[]{:S(2)}, u32[]{:S(2)}) %collective-permute-start.5) | collective-permute-done | bytes 442400 | tf_op jit(solution)/shard_map/ppermute | solution.py:25
  43.4 0.8 %pad_maximum_fusion.8.refs_3_ = bf16[128,384]{1,0:T(8,128)(2,1)S(1)} fusion(bf16[64,384]{1,0:T(8,128)(2,1)S(1)} %slice.168, bf16[32,384]{1,0:T(8,128)(2,1)} %get-tuple-element.44, bf16[32,384]{1,0:T(8,128)(2,1)} %get-tuple-element.32), kind=kLoop, calls=%fused_computation.9 | loop fusion | flops 294912 | bytes 196608 | tf_op jit(solution)/shard_map/concatenate | solution.py:368
  44.1 0.8 %pad_maximum_fusion.7.refs_2_ = bf16[128,384]{1,0:T(8,128)(2,1)S(1)} fusion(bf16[64,384]{1,0:T(8,128)(2,1)S(1)} %slice.160, bf16[32,384]{1,0:T(8,128)(2,1)} %get-tuple-element.46, bf16[32,384]{1,0:T(8,128)(2,1)} %get-tuple-element.34), kind=kLoop, calls=%fused_computation.8 | loop fusion | flops 294912 | bytes 196608 | tf_op jit(solution)/shard_map/concatenate | solution.py:368
  44.9 0.0 collective-permute-done.2.refs_5_
  44.9 0.8 %pad_maximum_fusion.5 = (bf16[128,384]{1,0:T(8,128)(2,1)S(1)}, bf16[128,384]{1,0:T(8,128)(2,1)S(1)}) fusion(bf16[32,384]{1,0:T(8,128)(2,1)S(1)} %get-tuple-element.27, bf16[32,384]{1,0:T(8,128)(2,1)S(1)} %get-tuple-element.28, bf16[32,384]{1,0:T(8,128)(2,1)} %get-tuple-element.31, bf16[32,384]{1,0:T(8,128)(2,1)} %get-tuple-element.38, ...), kind=kLoop, calls=%fused_computation.6 | loop fusion | flops 786432 | bytes 393216 | tf_op jit(solution)/shard_map/concatenate | solution.py:368
  45.8 0.0 slice-start
  45.8 2.3 %shard_map.92 = (bf16[4,32,384]{2,1,0:T(8,128)(2,1)S(1)}, bf16[4,32,384]{2,1,0:T(8,128)(2,1)S(1)}) custom-call(bf16[128,384]{1,0:T(8,128)(2,1)S(1)} %get-tuple-element.48.refs_0_, bf16[128,384]{1,0:T(8,128)(2,1)S(1)} %get-tuple-element.49.refs_1_, bf16[128,384]{1,0:T(8,128)(2,1)S(1)} %pad_maximum_fusion.7.refs_2_, ...), custom_call_target="tpu_custom_call" | custom-call | tf_op jit(solution)/shard_map/pallas_call | solution.py:138
  48.0 2.4 %collective-permute-start.11 = (bf16[4,32,384]{2,1,0:T(8,128)(2,1)S(1)}, bf16[4,32,384]{2,1,0:T(8,128)(2,1)S(1)}, u32[]{:S(2)}, u32[]{:S(2)}) collective-permute-start(bf16[4,32,384]{2,1,0:T(8,128)(2,1)S(1)} %get-tuple-element.22), channel_id=1, source_target_pairs={{0,12},{4,8},{8,4},{12,0},{1,13},{5,9},{9,5},{13,1},{2,14},{6,10},... | collective-permute-start | bytes 294920 | tf_op jit(solution)/shard_map/ppermute | solution.py:25
  50.5 2.3 %shard_map.93 = (bf16[4,32,384]{2,1,0:T(8,128)(2,1)S(1)}, bf16[4,32,384]{2,1,0:T(8,128)(2,1)S(1)}) custom-call(bf16[128,384]{1,0:T(8,128)(2,1)S(1)} %get-tuple-element.48.refs_0_, bf16[128,384]{1,0:T(8,128)(2,1)S(1)} %get-tuple-element.49.refs_1_, bf16[128,384]{1,0:T(8,128)(2,1)S(1)} %pad_maximum_fusion.7.refs_2_, ...), custom_call_target="tpu_custom_call" | custom-call | tf_op jit(solution)/shard_map/pallas_call | solution.py:138
  52.7 0.1 collective-permute-start.10
  52.8 1.2 %collective-permute-start.9 = (bf16[4,32,384]{2,1,0:T(8,128)(2,1)S(1)}, bf16[4,32,384]{2,1,0:T(8,128)(2,1)S(1)}, u32[]{:S(2)}, u32[]{:S(2)}) collective-permute-start(bf16[4,32,384]{2,1,0:T(8,128)(2,1)S(1)} %get-tuple-element.19), channel_id=1, source_target_pairs={{0,8},{4,12},{8,0},{12,4},{1,9},{5,13},{9,1},{13,5},{2,10},{6,14},... | collective-permute-start | bytes 294920 | tf_op jit(solution)/shard_map/ppermute | solution.py:25
  54.0 0.1 pad_add_fusion.where_ref
  54.1 0.1 collective-permute-done.11.refs_1_
  54.2 0.0 copy-start
  54.2 3.7 %copy-done = bf16[1536,3072]{1,0:T(8,128)(2,1)S(1)} copy-done((bf16[1536,3072]{1,0:T(8,128)(2,1)S(1)}, bf16[1536,3072]{1,0:T(8,128)(2,1)}, u32[]{:S(2)}) %copy-start) | copy-done | bytes 9437208
  57.9 0.0 copy-start.4
  57.9 3.0 %shard_map.94.refs_8_ = f32[6,128,512]{2,1,0:T(8,128)S(1)} custom-call(s32[4]{0:T(128)S(1)} %pad_add_fusion.where_ref, bf16[4,32,384]{2,1,0:T(8,128)(2,1)S(1)} %get-tuple-element.21.refs_0_, bf16[4,32,384]{2,1,0:T(8,128)(2,1)S(1)} %collective-permute-done.11.refs_1_, bf16[1536,3072]{1,0:T(8,128)(2,1)S(1)} %copy-done, bf16[1536,3072]{1,0:T(8,128)(2,1)S(1)} %copy-done, ...), custom_call_target="tpu_custom_call" | custom-call | tf_op jit(solution)/shard_map/pallas_call | solution.py:189
  60.9 0.0 collective-permute-done.10.refs_1_
  60.9 0.0 collective-permute-done.9.refs_0_
  60.9 0.0 slice-done
  61.0 0.0 slice-done.1
  61.0 0.0 slice-done.2
  61.0 0.0 copy-done.2
  61.0 0.0 copy-done.3
  61.0 0.0 copy-done.4
  61.0 0.0 copy-start.1
  61.0 0.0 copy-start.5
  61.0 4.1 %shard_map.95 = (bf16[128,32]{1,0:T(8,128)(2,1)S(1)}, bf16[128,32]{1,0:T(8,128)(2,1)S(1)}) custom-call(s32[4]{0:T(128)S(1)} %pad_add_fusion.where_ref, bf16[4,32,384]{2,1,0:T(8,128)(2,1)S(1)} %collective-permute-done.9.refs_0_, bf16[4,32,384]{2,1,0:T(8,128)(2,1)S(1)} %collective-permute-done.10.refs_1_, bf16[1536,3072]{1,0:T(8,128)(2,1)S(1)} %bitcast.8, ...), custom_call_target="tpu_custom_call" | custom-call | tf_op jit(solution)/shard_map/pallas_call | solution.py:263
  65.1 3.9 %collective-permute-start.12 = (bf16[128,32]{1,0:T(8,128)(2,1)S(1)}, bf16[128,32]{1,0:T(8,128)(2,1)S(1)}, u32[]{:S(2)}, u32[]{:S(2)}) collective-permute-start(bf16[128,32]{1,0:T(8,128)(2,1)S(1)} %get-tuple-element.24.odd_ref), channel_id=1, source_target_pairs={{0,1},{1,2},{2,3},{3,4},{4,5},{5,6},{6,7},{7,8},{8,9},{9,10},{10,1... | collective-permute-start | bytes 24584 | tf_op jit(solution)/shard_map/ppermute | solution.py:416
  69.0 1.9 %collective-permute-start.13 = (bf16[128,32]{1,0:T(8,128)(2,1)S(1)}, bf16[128,32]{1,0:T(8,128)(2,1)S(1)}, u32[]{:S(2)}, u32[]{:S(2)}) collective-permute-start(bf16[128,32]{1,0:T(8,128)(2,1)S(1)} %get-tuple-element.23.even_ref), channel_id=1, source_target_pairs={{1,0},{2,1},{3,2},{4,3},{5,4},{6,5},{7,6},{8,7},{9,8},{10,9},{11,1... | collective-permute-start | bytes 24584 | tf_op jit(solution)/shard_map/ppermute | solution.py:417
  70.9 0.0 collective-permute-done.12.left_ref
  70.9 3.3 %collective-permute-done.13.right_ref = bf16[128,32]{1,0:T(8,128)(2,1)S(1)} collective-permute-done((bf16[128,32]{1,0:T(8,128)(2,1)S(1)}, bf16[128,32]{1,0:T(8,128)(2,1)S(1)}, u32[]{:S(2)}, u32[]{:S(2)}) %collective-permute-start.13) | collective-permute-done | bytes 8224 | tf_op jit(solution)/shard_map/ppermute | solution.py:417
  74.2 0.0 copy-done.1
  74.2 0.0 copy-done.5
  74.2 2.2 %shard_map.96 = bf16[4,2,64,512]{3,2,1,0:T(8,128)(2,1)} custom-call(s32[4]{0:T(128)S(1)} %pad_add_fusion.where_ref, bf16[128,32]{1,0:T(8,128)(2,1)S(1)} %get-tuple-element.23.even_ref, bf16[128,32]{1,0:T(8,128)(2,1)S(1)} %get-tuple-element.24.odd_ref, bf16[128,32]{1,0:T(8,128)(2,1)S(1)} %collective-permute-done.12.left_ref, ...), custom_call_target="tpu_custom_call" | custom-call | tf_op jit(solution)/shard_map/pallas_call | solution.py:332
  (20 shorter events, 0.3 us)
Async XLA Ops:
  2.4 9.1 %collective-permute-start = (bf16[384,384]{1,0:T(8,128)(2,1)}, bf16[384,384]{1,0:T(8,128)(2,1)S(1)}, u32[]{:S(2)}, u32[]{:S(2)}) collective-permute-start(bf16[384,384]{1,0:T(8,128)(2,1)} %get-tuple-element.16), channel_id=1, source_target_pairs={{0,4},{4,0},{8,12},{12,8},{1,5},{5,1},{9,13},{13,9},{2,6},{6,2},{1... | collective-permute-start | bytes 884744 | tf_op jit(solution)/shard_map/ppermute | solution.py:25
  4.6 15.2 %collective-permute-start.6 = (bf16[384,384]{1,0:T(8,128)(2,1)}, bf16[384,384]{1,0:T(8,128)(2,1)S(1)}, u32[]{:S(2)}, u32[]{:S(2)}) collective-permute-start(bf16[384,384]{1,0:T(8,128)(2,1)} %get-tuple-element.18), channel_id=1, source_target_pairs={{0,12},{4,8},{8,4},{12,0},{1,13},{5,9},{9,5},{13,1},{2,14},{6,10},... | collective-permute-start | bytes 884744 | tf_op jit(solution)/shard_map/ppermute | solution.py:25
  6.8 25.7 %collective-permute-start.3 = (bf16[384,384]{1,0:T(8,128)(2,1)}, bf16[384,384]{1,0:T(8,128)(2,1)S(1)}, u32[]{:S(2)}, u32[]{:S(2)}) collective-permute-start(bf16[384,384]{1,0:T(8,128)(2,1)} %get-tuple-element.17), channel_id=1, source_target_pairs={{0,8},{4,12},{8,0},{12,4},{1,9},{5,13},{9,1},{13,5},{2,10},{6,14},... | collective-permute-start | bytes 884744 | tf_op jit(solution)/shard_map/ppermute | solution.py:25
  11.6 26.0 %collective-permute-start.1 = (bf16[640,384]{1,0:T(8,128)(2,1)S(1)}, bf16[640,384]{1,0:T(8,128)(2,1)S(1)}, u32[]{:S(2)}, u32[]{:S(2)}) collective-permute-start(bf16[640,384]{1,0:T(8,128)(2,1)S(1)} %pad_maximum_fusion), channel_id=1, source_target_pairs={{0,2},{1,3},{2,0},{3,1},{4,6},{5,7},{6,4},{7,5},{8,10},{9,11},{10,... | collective-permute-start | bytes 1474568 | tf_op jit(solution)/shard_map/ppermute | solution.py:25
  19.8 15.2 %collective-permute-start.7 = (bf16[320,384]{1,0:T(8,128)(2,1)S(1)}, bf16[320,384]{1,0:T(8,128)(2,1)S(1)}, u32[]{:S(2)}, u32[]{:S(2)}) collective-permute-start(bf16[320,384]{1,0:T(8,128)(2,1)S(1)} %pad_maximum_fusion.4), channel_id=1, source_target_pairs={{0,2},{1,3},{2,0},{3,1},{4,6},{5,7},{6,4},{7,5},{8,10},{9,11},{10,... | collective-permute-start | bytes 737288 | tf_op jit(solution)/shard_map/ppermute | solution.py:25
  32.5 7.8 %collective-permute-start.4 = (bf16[320,384]{1,0:T(8,128)(2,1)S(1)}, bf16[320,384]{1,0:T(8,128)(2,1)S(1)}, u32[]{:S(2)}, u32[]{:S(2)}) collective-permute-start(bf16[320,384]{1,0:T(8,128)(2,1)S(1)} %pad_maximum_fusion.3), channel_id=1, source_target_pairs={{0,2},{1,3},{2,0},{3,1},{4,6},{5,7},{6,4},{7,5},{8,10},{9,11},{10,... | collective-permute-start | bytes 737288 | tf_op jit(solution)/shard_map/ppermute | solution.py:25
  35.7 6.0 %collective-permute-start.8 = (bf16[576,384]{1,0:T(8,128)(2,1)S(1)}, bf16[576,384]{1,0:T(8,128)(2,1)S(1)}, u32[]{:S(2)}, u32[]{:S(2)}) collective-permute-start(bf16[576,384]{1,0:T(8,128)(2,1)S(1)} %pad_maximum_fusion.2.refs_8_), channel_id=1, source_target_pairs={{0,1},{1,0},{2,3},{3,2},{4,5},{5,4},{6,7},{7,6},{8,9},{9,8},{10,11... | collective-permute-start | bytes 1327112 | tf_op jit(solution)/shard_map/ppermute | solution.py:25
  40.3 4.6 %collective-permute-start.2 = (bf16[1152,384]{1,0:T(8,128)(2,1)S(1)}, bf16[1152,384]{1,0:T(8,128)(2,1)S(1)}, u32[]{:S(2)}, u32[]{:S(2)}) collective-permute-start(bf16[1152,384]{1,0:T(8,128)(2,1)S(1)} %get-tuple-element.30.refs_4_), channel_id=1, source_target_pairs={{0,1},{1,0},{2,3},{3,2},{4,5},{5,4},{6,7},{7,6},{8,9},{9,8},{10,11... | collective-permute-start | bytes 2654216 | tf_op jit(solution)/shard_map/ppermute | solution.py:25
  41.0 2.3 %collective-permute-start.5 = (bf16[576,384]{1,0:T(8,128)(2,1)S(1)}, bf16[576,384]{1,0:T(8,128)(2,1)S(1)}, u32[]{:S(2)}, u32[]{:S(2)}) collective-permute-start(bf16[576,384]{1,0:T(8,128)(2,1)S(1)} %pad_maximum_fusion.1.refs_6_), channel_id=1, source_target_pairs={{0,1},{1,0},{2,3},{3,2},{4,5},{5,4},{6,7},{7,6},{8,9},{9,8},{10,11... | collective-permute-start | bytes 1327112 | tf_op jit(solution)/shard_map/ppermute | solution.py:25
  45.8 15.2 %slice-start = ((s8[9437184]{0:T(1024)(128)(4,1)}), s8[4194304]{0:T(1024)(128)(4,1)S(1)}, s32[]{:S(2)}) async-start(s8[9437184]{0:T(1024)(128)(4,1)} %bitcast.7), calls=%async_computation | async-start | bytes 8388608
  48.0 6.2 %collective-permute-start.11 = (bf16[4,32,384]{2,1,0:T(8,128)(2,1)S(1)}, bf16[4,32,384]{2,1,0:T(8,128)(2,1)S(1)}, u32[]{:S(2)}, u32[]{:S(2)}) collective-permute-start(bf16[4,32,384]{2,1,0:T(8,128)(2,1)S(1)} %get-tuple-element.22), channel_id=1, source_target_pairs={{0,12},{4,8},{8,4},{12,0},{1,13},{5,9},{9,5},{13,1},{2,14},{6,10},... | collective-permute-start | bytes 294920 | tf_op jit(solution)/shard_map/ppermute | solution.py:25
  52.7 8.2 %collective-permute-start.10 = (bf16[4,32,384]{2,1,0:T(8,128)(2,1)S(1)}, bf16[4,32,384]{2,1,0:T(8,128)(2,1)S(1)}, u32[]{:S(2)}, u32[]{:S(2)}) collective-permute-start(bf16[4,32,384]{2,1,0:T(8,128)(2,1)S(1)} %get-tuple-element.20), channel_id=1, source_target_pairs={{0,4},{4,0},{8,12},{12,8},{1,5},{5,1},{9,13},{13,9},{2,6},{6,2},{1... | collective-permute-start | bytes 294920 | tf_op jit(solution)/shard_map/ppermute | solution.py:25
  52.8 8.1 %collective-permute-start.9 = (bf16[4,32,384]{2,1,0:T(8,128)(2,1)S(1)}, bf16[4,32,384]{2,1,0:T(8,128)(2,1)S(1)}, u32[]{:S(2)}, u32[]{:S(2)}) collective-permute-start(bf16[4,32,384]{2,1,0:T(8,128)(2,1)S(1)} %get-tuple-element.19), channel_id=1, source_target_pairs={{0,8},{4,12},{8,0},{12,4},{1,9},{5,13},{9,1},{13,5},{2,10},{6,14},... | collective-permute-start | bytes 294920 | tf_op jit(solution)/shard_map/ppermute | solution.py:25
  54.2 3.7 %copy-start = (bf16[1536,3072]{1,0:T(8,128)(2,1)S(1)}, bf16[1536,3072]{1,0:T(8,128)(2,1)}, u32[]{:S(2)}) copy-start(bf16[1536,3072]{1,0:T(8,128)(2,1)} %refs_7_.3) | copy-start | bytes 28311556
  57.9 3.1 %slice-start.1 = ((s8[9437184]{0:T(1024)(128)(4,1)}), s8[4194304]{0:T(1024)(128)(4,1)S(1)}, s32[]{:S(2)}) async-start(s8[9437184]{0:T(1024)(128)(4,1)} %bitcast.7), calls=%async_computation.1 | async-start | bytes 8388608
  57.9 3.1 %slice-start.2 = ((s8[9437184]{0:T(1024)(128)(4,1)}), s8[1048576]{0:T(1024)(128)(4,1)S(1)}, s32[]{:S(2)}) async-start(s8[9437184]{0:T(1024)(128)(4,1)} %bitcast.7), calls=%async_computation.2 | async-start | bytes 2097152
  57.9 3.1 %copy-start.2 = (bf16[3072,64]{0,1:T(8,128)(2,1)S(1)}, bf16[3072,64]{0,1:T(8,128)(2,1)}, u32[]{:S(2)}) copy-start(bf16[3072,64]{0,1:T(8,128)(2,1)} %param.15) | copy-start | bytes 1179652
  57.9 3.1 %copy-start.3 = (f32[3072]{0:T(1024)S(1)}, f32[3072]{0:T(1024)}, u32[]{:S(2)}) copy-start(f32[3072]{0:T(1024)} %param.14) | copy-start | bytes 36868
  57.9 3.1 %copy-start.4 = (f32[3072]{0:T(1024)S(1)}, f32[3072]{0:T(1024)}, u32[]{:S(2)}) copy-start(f32[3072]{0:T(1024)} %param.13) | copy-start | bytes 36868
  61.0 13.2 %copy-start.1 = (bf16[432,512]{1,0:T(8,128)(2,1)S(1)}, bf16[432,512]{1,0:T(8,128)(2,1)}, u32[]{:S(2)}) copy-start(bf16[432,512]{1,0:T(8,128)(2,1)} %w_ref.1) | copy-start | bytes 1327108
  61.0 13.2 %copy-start.5 = (f32[512]{0:T(512)S(1)}, f32[512]{0:T(512)}, u32[]{:S(2)}) copy-start(f32[512]{0:T(512)} %param.17) | copy-start | bytes 6148
  65.1 5.8 %collective-permute-start.12 = (bf16[128,32]{1,0:T(8,128)(2,1)S(1)}, bf16[128,32]{1,0:T(8,128)(2,1)S(1)}, u32[]{:S(2)}, u32[]{:S(2)}) collective-permute-start(bf16[128,32]{1,0:T(8,128)(2,1)S(1)} %get-tuple-element.24.odd_ref), channel_id=1, source_target_pairs={{0,1},{1,2},{2,3},{3,4},{4,5},{5,6},{6,7},{7,8},{8,9},{9,10},{10,1... | collective-permute-start | bytes 24584 | tf_op jit(solution)/shard_map/ppermute | solution.py:416
  69.0 5.2 %collective-permute-start.13 = (bf16[128,32]{1,0:T(8,128)(2,1)S(1)}, bf16[128,32]{1,0:T(8,128)(2,1)S(1)}, u32[]{:S(2)}, u32[]{:S(2)}) collective-permute-start(bf16[128,32]{1,0:T(8,128)(2,1)S(1)} %get-tuple-element.23.even_ref), channel_id=1, source_target_pairs={{1,0},{2,1},{3,2},{4,3},{5,4},{6,5},{7,6},{8,7},{9,8},{10,9},{11,1... | collective-permute-start | bytes 24584 | tf_op jit(solution)/shard_map/ppermute | solution.py:417

commit v7 on v6

--- a/solution.py
+++ b/solution.py
@@ -14,50 +14,13 @@
 LATENT_CH = 16
 FRAMES = 4
 VMEM_LIMIT = 16 * 1024 * 1024
-VMEM_WHOLE = 63 * 1024 * 1024
 CHUNKS = ((0, 3),)
-VMEM_WHOLE = 63 * 1024 * 1024
 EXP2_SCALE = math.log2(math.e) / math.sqrt(HEAD_DIM)
 
 
 def swap(source, axis, distance):
     count = lax.axis_size(axis)
     return lax.ppermute(source, axis, [(i, i ^ distance) for i in range(count)])
-
-
-def bundle_kernel(q_ref, k_ref, v_ref, *out_refs, groups, planes, cuts):
-    tokens, width = q_ref.shape
-    group_width = width // groups
-    rows_dev = tokens // (groups * planes)
-    heads_at, plane_at = lax.axis_index("heads"), lax.axis_index("plane")
-    to = lax.broadcasted_iota(jnp.int32, (tokens, tokens), 0)
-    at = lax.broadcasted_iota(jnp.int32, (tokens, tokens), 1)
-    j, t, row = to // (groups * rows_dev), (to // rows_dev) % groups, to % rows_dev
-    for (r, low, high), out_ref in zip(cuts, out_refs):
-        group = heads_at ^ r
-        first = pl.multiple_of(group * group_width + low * HEAD_DIM, HEAD_DIM)
-        lanes = pl.ds(first, (high - low) * HEAD_DIM)
-        place = row * (groups * planes) + (t ^ group) * planes + (j ^ plane_at)
-        order = (at == place).astype(jnp.bfloat16)
-        out_ref[:tokens] = k_ref[:, lanes]
-        out_ref[tokens : 2 * tokens] = v_ref[:, lanes]
-        mixed = jnp.dot(order, q_ref[:, lanes], preferred_element_type=jnp.float32)
-        out_ref[2 * tokens :] = mixed.astype(jnp.bfloat16)
-
-
-def bundles(queries, keys, values, groups, planes, cuts):
-    tokens = queries.shape[0]
-    vmem = pl.BlockSpec(memory_space=pltpu.VMEM)
-    return pl.pallas_call(
-        functools.partial(bundle_kernel, groups=groups, planes=planes, cuts=cuts),
-        in_specs=[vmem] * 3,
-        out_specs=[vmem] * len(cuts),
-        out_shape=[
-            jax.ShapeDtypeStruct((3 * tokens, (high - low) * HEAD_DIM), jnp.bfloat16)
-            for _, low, high in cuts
-        ],
-        compiler_params=pltpu.CompilerParams(vmem_limit_bytes=VMEM_WHOLE),
-    )(queries, keys, values)
 
 
 def attend_kernel(*refs, sources, planes, blocks, part, targets, rows_step):
@@ -343,7 +306,7 @@
     return lax.optimization_barrier((value,) + others)[0]
 
 
-def gather_plane(got, batch, both_parts, share):
+def gather_plane(got, batch, both_parts, share, waits):
     planes = lax.axis_size("plane")
     half, count = planes // 2, len(batch)
     kv_rows = both_parts * count
@@ -360,6 +323,8 @@
         far.append([x[first + share : first + 2 * share] for first in firsts])
     mine = [got[r][:both_parts] for r in batch] + [x[:kv_rows] for x in crossed]
     mine = jnp.concatenate(mine + [q for pieces in far for q in pieces], axis=0)
+    if waits and batch == (3,):
+        mine = after(mine, *waits)
     other = swap(mine, "plane", 1)
     asked = []
     for n in range(count):
@@ -382,26 +347,43 @@
     tokens = queries.shape[0]
     rows_dev = tokens // devices
     both_parts, share = 2 * tokens, tokens // planes
+    group_heads = queries.shape[1] // HEAD_DIM // groups
     where = jnp.stack(
         [heads_at, plane_at, heads_at * planes + plane_at, jnp.int32(devices)]
     ).astype(jnp.int32)
 
-    cuts = [(r, low, high) for low, high in CHUNKS for r in (2, 1, 3, 0)]
-    made = dict(zip(cuts, bundles(queries, keys, values, groups, planes, cuts)))
-    made = {cut: swap(made[cut], "heads", cut[0]) if cut[0] else made[cut] for cut in cuts}
-
-    chunks = []
+    to = lax.broadcasted_iota(jnp.int32, (tokens, tokens), 0)
+    at = lax.broadcasted_iota(jnp.int32, (tokens, tokens), 1)
+    j, t, row = to // (groups * rows_dev), (to // rows_dev) % groups, to % rows_dev
+
+    def bundle(r, low, high):
+        first = (heads_at ^ r) * (HEAD_DIM * group_heads) + low * HEAD_DIM
+        cut = [
+            lax.dynamic_slice_in_dim(source, first, (high - low) * HEAD_DIM, axis=1)
+            for source in (keys, values, queries)
+        ]
+        place = row * devices + (t ^ (r ^ heads_at)) * planes + (j ^ plane_at)
+        order = (at == place).astype(jnp.bfloat16)
+        cut[2] = jnp.dot(order, cut[2], preferred_element_type=jnp.float32).astype(jnp.bfloat16)
+        return jnp.concatenate(cut, axis=0)
+
+    chunks, begun, done = [], None, None
     for low, high in CHUNKS:
-        got = [made[r, low, high] for r in range(groups)]
+        got = [bundle(r, low, high) for r in range(groups)]
+        if begun is not None:
+            got = [after(b, begun) for b in got]
+        got = [swap(b, "heads", r) if r else b for r, b in enumerate(got)]
+        begun = got[1]
         keys_values, asked = [], []
         for batch in ((0, 1), (2,), (3,)):
-            kv, q = gather_plane(got, batch, both_parts, share)
+            kv, q = gather_plane(got, batch, both_parts, share, done)
             keys_values += kv
             asked += q
-        taken = []
+        taken, done = [], []
         for targets in ((3, 2), (1, 0)):
-            for t, o in zip(targets, attend(asked, keys_values, targets, planes)):
-                taken.append((t, low, o if t == 0 else swap(o, "heads", t)))
+            for target, o in zip(targets, attend(asked, keys_values, targets, planes)):
+                done.append(o)
+                taken.append((target, low, o if target == 0 else swap(o, "heads", target)))
         chunks.append(taken)
 
     if len(chunks) == 1:

time: 77.4 us -> 86.4 us (1.12)
  starting transfers between devices: 20.2 us -> 24.6 us
  waiting for transfers between devices: 26.3 us -> 29.5 us
  matrix products: 0 us -> 1.33 us
    ppermute x12, starting transfers between devices: 14.4 us -> 17.8 us  [swap(): return lax.ppermute(source, axis, [(i, i ^ distance) for i in range(count)])]
    ppermute x12, waiting for transfers between devices: 23 us -> 26.2 us  [swap(): return lax.ppermute(source, axis, [(i, i ^ distance) for i in range(count)])]
    pallas_call x1 -> x0, Pallas kernels: 2.45 us -> none  [bundles(): pl.pallas_call(functools.partial(bundle_kernel, groups=groups, planes=pla...]
    dynamic_slice x0 -> x2, local copies, waits for them, and re-layouts: none -> 2.24 us  [bundle(): lax.dynamic_slice_in_dim(source, first, (high - low) * HEAD_DIM, axis=1)]
    pallas_call x2, Pallas kernels: 4.54 us -> 6.74 us  [attend(): pl.pallas_call(functools.partial(attend_kernel, sources=sources, planes=p...]
    dot_general x0 -> x4, matrix products: none -> 1.33 us  [bundle(): jnp.dot(order, cut[2], preferred_element_type=jnp.float32)]
    slice x4 -> x2, local copies, waits for them, and re-layouts: 1.05 us -> 0.04 us  [gather_plane(): sent = [got[r][:both_parts] for r in batch]]
    ppermute x1, starting transfers between devices: 3.86 us -> 4.8 us  [shards(): left = lax.ppermute(odd, both, [(i, i + 1) for i in range(devices - 1)])]
  transfers between devices with their start and end apart: 14 -> 14, of which waited for: 6 -> 6; matrix products, arithmetic and copies ran while one was open for 12% -> 9% of each run, Pallas kernels for 7% -> 7%
where the time goes in v7:
time: 86.4 us; the launch traced here: 85.9 us
  waiting for transfers between devices  29.5 us (34%)
  starting transfers between devices  24.6 us (28%)
  Pallas kernels  16 us (19%)
  local copies, waits for them, and re-layouts  10.7 us (12%)
  other arithmetic  3.4 us (4%)
  matrix products  1.33 us (2%)
    ppermute x12, waiting for transfers between devices, swap(): return lax.ppermute(source, axis, [(i, i ^ distance) for i in range(count)])  26.2 us
    ppermute x12, starting transfers between devices, swap(): return lax.ppermute(source, axis, [(i, i ^ distance) for i in range(count)])  17.8 us
    pallas_call x2, Pallas kernels, attend(): pl.pallas_call(functools.partial(attend_kernel, sources=sources, planes=p...  6.74 us
    ppermute x1, starting transfers between devices, shards(): left = lax.ppermute(odd, both, [(i, i + 1) for i in range(devices - 1)])  4.8 us
    pallas_call x1, Pallas kernels, final_layer(): pl.pallas_call(functools.partial(final_kernel, count=len(taken), planes=p...  4.08 us
    unnamed x24, local copies, waits for them, and re-layouts  3.87 us
    ppermute x1, waiting for transfers between devices, shards(): right = lax.ppermute(even, both, [(i + 1, i) for i in range(devices - 1)])  3.29 us
    concatenate x4, other arithmetic, gather_plane(): jnp.concatenate([pieces[n] for pieces in near] + [other[first:first + sha...  3.04 us
  transfers between devices with their start and end apart: 14, of which 6 were waited for; matrix products, arithmetic and copies ran while one was open for 9% of the time, Pallas kernels for 7%

profile of v7, /device:TPU:1, one launch (start us, length us, event | category | flops | bytes accessed | tf_op | source)
XLA Modules:
  0.0 85.9 jit_solution(16779649958805429301)
XLA Ops:
  0.0 0.0 copy-start
  0.1 1.1 %constant_dynamic-slice_fusion.1 = (bf16[128,384]{1,0:T(8,128)(2,1)S(1)}, bf16[1152,384]{1,0:T(8,128)(2,1)S(1)}, bf16[128,384]{1,0:T(8,128)(2,1)S(1)}, bf16[640,384]{1,0:T(8,128)(2,1)S(1)}, bf16[128,384]{1,0:T(8,128)(2,1)S(1)}) fusion(bf16[128,1536]{1,0:T(8,128)(2,1)} %param.10, s32[]{:T(128)S(6)} %select_n.64, s32[]{:T(128)S(6)} %select_n.61, ...), kind=kLoop, calls=%fused_computation.86 | loop fusion | bytes 884752 | tf_op jit(solution)/shard_map/dynamic_slice | solution.py:362
  1.2 1.1 %constant_dynamic-slice_fusion = (bf16[128,384]{1,0:T(8,128)(2,1)S(1)}, bf16[1152,384]{1,0:T(8,128)(2,1)S(1)}, bf16[128,384]{1,0:T(8,128)(2,1)S(1)}, bf16[640,384]{1,0:T(8,128)(2,1)S(1)}, bf16[128,384]{1,0:T(8,128)(2,1)S(1)}) fusion(bf16[128,1536]{1,0:T(8,128)(2,1)} %param.11, s32[]{:T(128)S(6)} %select_n.64, bf16[1152,384]{1,0:T(8,128)(2,1)S(1)} %get-tuple-element.25, ...), kind=kLoop, calls=%fused_computation.85 | loop fusion | bytes 884752 | tf_op jit(solution)/shard_map/dynamic_slice | solution.py:362
  2.3 0.0 copy-done
  2.3 0.3 convolution_convert_fusion.2
  2.7 2.2 %collective-permute-start = (bf16[384,384]{1,0:T(8,128)(2,1)S(1)}, bf16[384,384]{1,0:T(8,128)(2,1)S(1)}, u32[]{:S(2)}, u32[]{:S(2)}) collective-permute-start(bf16[384,384]{1,0:T(8,128)(2,1)S(1)} %pad_maximum_fusion.2), channel_id=1, source_target_pairs={{0,4},{4,0},{8,12},{12,8},{1,5},{5,1},{9,13},{13,9},{2,6},{6,2},{1... | collective-permute-start | bytes 884744 | tf_op jit(solution)/shard_map/ppermute | solution.py:23
  4.9 0.3 convolution_convert_fusion.1
  5.3 2.4 %collective-permute-start.3 = (bf16[384,384]{1,0:T(8,128)(2,1)S(1)}, bf16[384,384]{1,0:T(8,128)(2,1)S(1)}, u32[]{:S(2)}, u32[]{:S(2)}) collective-permute-start(bf16[384,384]{1,0:T(8,128)(2,1)S(1)} %pad_maximum_fusion.3), channel_id=1, source_target_pairs={{0,8},{4,12},{8,0},{12,4},{1,9},{5,13},{9,1},{13,5},{2,10},{6,14},... | collective-permute-start | bytes 884744 | tf_op jit(solution)/shard_map/ppermute | solution.py:23
  7.6 0.3 convolution_convert_fusion
  8.0 0.1 collective-permute-start.6
  8.1 0.3 convolution_convert_fusion.3
  8.4 8.5 %collective-permute-done = bf16[384,384]{1,0:T(8,128)(2,1)S(1)} collective-permute-done((bf16[384,384]{1,0:T(8,128)(2,1)S(1)}, bf16[384,384]{1,0:T(8,128)(2,1)S(1)}, u32[]{:S(2)}, u32[]{:S(2)}) %collective-permute-start) | collective-permute-done | bytes 294944 | tf_op jit(solution)/shard_map/ppermute | solution.py:23
  17.0 0.1 slice_dynamic-update-slice_fusion.2
  17.1 1.1 %collective-permute-start.1 = (bf16[640,384]{1,0:T(8,128)(2,1)S(1)}, bf16[640,384]{1,0:T(8,128)(2,1)S(1)}, u32[]{:S(2)}, u32[]{:S(2)}) collective-permute-start(bf16[640,384]{1,0:T(8,128)(2,1)S(1)} %slice_dynamic-update-slice_fusion.3), channel_id=1, source_target_pairs={{0,2},{1,3},{2,0},{3,1},{4,6},{5,7},{6,4},{7,5},{8,10},{9,11},{10,... | collective-permute-start | bytes 1474568 | tf_op jit(solution)/shard_map/ppermute | solution.py:23
  18.2 0.0 collective-permute-done.3
  18.3 0.5 collective-permute-start.4
  18.7 7.5 %collective-permute-done.6 = bf16[384,384]{1,0:T(8,128)(2,1)S(1)} collective-permute-done((bf16[384,384]{1,0:T(8,128)(2,1)S(1)}, bf16[384,384]{1,0:T(8,128)(2,1)S(1)}, u32[]{:S(2)}, u32[]{:S(2)}) %collective-permute-start.6) | collective-permute-done | bytes 294944 | tf_op jit(solution)/shard_map/ppermute | solution.py:23
  26.3 1.3 %collective-permute-start.7 = (bf16[320,384]{1,0:T(8,128)(2,1)S(1)}, bf16[320,384]{1,0:T(8,128)(2,1)S(1)}, u32[]{:S(2)}, u32[]{:S(2)}) collective-permute-start(bf16[320,384]{1,0:T(8,128)(2,1)S(1)} %pad_maximum_fusion.6), channel_id=1, source_target_pairs={{0,2},{1,3},{2,0},{3,1},{4,6},{5,7},{6,4},{7,5},{8,10},{9,11},{10,... | collective-permute-start | bytes 737288 | tf_op jit(solution)/shard_map/ppermute | solution.py:23
  27.5 0.6 fusion.64
  28.1 0.6 fusion.63
  28.7 4.0 %collective-permute-done.4 = bf16[320,384]{1,0:T(8,128)(2,1)S(1)} collective-permute-done((bf16[320,384]{1,0:T(8,128)(2,1)S(1)}, bf16[320,384]{1,0:T(8,128)(2,1)S(1)}, u32[]{:S(2)}, u32[]{:S(2)}) %collective-permute-start.4) | collective-permute-done | bytes 245792 | tf_op jit(solution)/shard_map/ppermute | solution.py:23
  32.7 0.6 fusion.67
  33.4 6.0 %collective-permute-start.5 = (bf16[576,384]{1,0:T(8,128)(2,1)S(1)}, bf16[576,384]{1,0:T(8,128)(2,1)S(1)}, u32[]{:S(2)}, u32[]{:S(2)}) collective-permute-start(bf16[576,384]{1,0:T(8,128)(2,1)S(1)} %pad_maximum_fusion.refs_6_), channel_id=1, source_target_pairs={{0,1},{1,0},{2,3},{3,2},{4,5},{5,4},{6,7},{7,6},{8,9},{9,8},{10,11... | collective-permute-start | bytes 1327112 | tf_op jit(solution)/shard_map/ppermute | solution.py:23
  39.4 0.0 collective-permute-done.1
  39.4 0.1 slice_dynamic-update-slice_fusion
  39.5 0.6 fusion.68
  40.1 0.6 fusion.65
  40.7 0.1 collective-permute-start.2
  40.8 0.0 collective-permute-done.7
  40.8 0.6 fusion.66
  41.5 0.5 collective-permute-start.8
  42.1 0.0 collective-permute-done.5.refs_7_
  42.1 1.9 %collective-permute-done.8.refs_9_ = bf16[576,384]{1,0:T(8,128)(2,1)} collective-permute-done((bf16[576,384]{1,0:T(8,128)(2,1)S(1)}, bf16[576,384]{1,0:T(8,128)(2,1)}, u32[]{:S(2)}, u32[]{:S(2)}) %collective-permute-start.8) | collective-permute-done | bytes 442400 | tf_op jit(solution)/shard_map/ppermute | solution.py:23
  44.0 0.8 slice.169
  44.8 0.8 pad_maximum_fusion.9.refs_2_
  45.6 0.8 pad_maximum_fusion.10.refs_3_
  46.3 0.0 collective-permute-done.2.refs_5_
  46.4 0.8 pad_maximum_fusion.7.refs_0_
  47.1 0.8 pad_maximum_fusion.8.refs_1_
  47.9 0.0 slice-start
  47.9 3.5 %shard_map.91 = (bf16[4,32,384]{2,1,0:T(8,128)(2,1)S(1)}, bf16[4,32,384]{2,1,0:T(8,128)(2,1)S(1)}) custom-call(bf16[128,384]{1,0:T(8,128)(2,1)S(1)} %pad_maximum_fusion.7.refs_0_, bf16[128,384]{1,0:T(8,128)(2,1)S(1)} %pad_maximum_fusion.8.refs_1_, bf16[128,384]{1,0:T(8,128)(2,1)S(1)} %pad_maximum_fusion.9.refs_2_, ...), custom_call_target="tpu_custom_call" | custom-call | tf_op jit(solution)/shard_map/pallas_call | solution.py:101
  51.4 1.0 %collective-permute-start.9 = (bf16[4,32,384]{2,1,0:T(8,128)(2,1)S(1)}, bf16[4,32,384]{2,1,0:T(8,128)(2,1)S(1)}, u32[]{:S(2)}, u32[]{:S(2)}) collective-permute-start(bf16[4,32,384]{2,1,0:T(8,128)(2,1)S(1)} %get-tuple-element.11), channel_id=1, source_target_pairs={{0,8},{4,12},{8,0},{12,4},{1,9},{5,13},{9,1},{13,5},{2,10},{6,14},... | collective-permute-start | bytes 294920 | tf_op jit(solution)/shard_map/ppermute | solution.py:23
  52.4 3.3 %shard_map.92 = (bf16[4,32,384]{2,1,0:T(8,128)(2,1)S(1)}, bf16[4,32,384]{2,1,0:T(8,128)(2,1)S(1)}) custom-call(bf16[128,384]{1,0:T(8,128)(2,1)S(1)} %pad_maximum_fusion.7.refs_0_, bf16[128,384]{1,0:T(8,128)(2,1)S(1)} %pad_maximum_fusion.8.refs_1_, bf16[128,384]{1,0:T(8,128)(2,1)S(1)} %pad_maximum_fusion.9.refs_2_, ...), custom_call_target="tpu_custom_call" | custom-call | tf_op jit(solution)/shard_map/pallas_call | solution.py:101
  55.7 1.7 %collective-permute-start.10 = (bf16[4,32,384]{2,1,0:T(8,128)(2,1)S(1)}, bf16[4,32,384]{2,1,0:T(8,128)(2,1)S(1)}, u32[]{:S(2)}, u32[]{:S(2)}) collective-permute-start(bf16[4,32,384]{2,1,0:T(8,128)(2,1)S(1)} %get-tuple-element.12), channel_id=1, source_target_pairs={{0,4},{4,0},{8,12},{12,8},{1,5},{5,1},{9,13},{13,9},{2,6},{6,2},{1... | collective-permute-start | bytes 294920 | tf_op jit(solution)/shard_map/ppermute | solution.py:23
  57.4 0.9 %collective-permute-start.11 = (bf16[4,32,384]{2,1,0:T(8,128)(2,1)S(1)}, bf16[4,32,384]{2,1,0:T(8,128)(2,1)S(1)}, u32[]{:S(2)}, u32[]{:S(2)}) collective-permute-start(bf16[4,32,384]{2,1,0:T(8,128)(2,1)S(1)} %get-tuple-element.14), channel_id=1, source_target_pairs={{0,12},{4,8},{8,4},{12,0},{1,13},{5,9},{9,5},{13,1},{2,14},{6,10},... | collective-permute-start | bytes 294920 | tf_op jit(solution)/shard_map/ppermute | solution.py:23
  58.3 0.1 pad_add_fusion.where_ref
  58.4 4.4 %collective-permute-done.11.refs_1_ = bf16[4,32,384]{2,1,0:T(8,128)(2,1)S(1)} collective-permute-done((bf16[4,32,384]{2,1,0:T(8,128)(2,1)S(1)}, bf16[4,32,384]{2,1,0:T(8,128)(2,1)S(1)}, u32[]{:S(2)}, u32[]{:S(2)}) %collective-permute-start.11) | collective-permute-done | bytes 98336 | tf_op jit(solution)/shard_map/ppermute | solution.py:23
  62.8 3.7 %copy-done.1 = bf16[1536,3072]{1,0:T(8,128)(2,1)S(1)} copy-done((bf16[1536,3072]{1,0:T(8,128)(2,1)S(1)}, bf16[1536,3072]{1,0:T(8,128)(2,1)}, u32[]{:S(2)}) %copy-start.1) | copy-done | bytes 9437208
  66.4 0.0 copy-start.5
  66.5 3.0 %shard_map.93.refs_8_ = f32[6,128,512]{2,1,0:T(8,128)S(1)} custom-call(s32[4]{0:T(128)S(1)} %pad_add_fusion.where_ref, bf16[4,32,384]{2,1,0:T(8,128)(2,1)S(1)} %get-tuple-element.13.refs_0_, bf16[4,32,384]{2,1,0:T(8,128)(2,1)S(1)} %collective-permute-done.11.refs_1_, bf16[1536,3072]{1,0:T(8,128)(2,1)S(1)} %copy-done.1, bf16[1536,3072]{1,0:T(8,128)(2,1)S(1)} %copy-done.1, ...), custom_call_target="tpu_custom_call" | custom-call | tf_op jit(solution)/shard_map/pallas_call | solution.py:152
  69.4 0.0 collective-permute-done.9.refs_0_
  69.5 0.0 collective-permute-done.10.refs_1_
  69.5 0.0 slice-done
  69.5 0.0 slice-done.1
  69.5 0.0 slice-done.2
  69.5 0.0 copy-start.2
  69.6 0.0 copy-start.6
  69.6 4.1 %shard_map.94 = (bf16[128,32]{1,0:T(8,128)(2,1)S(1)}, bf16[128,32]{1,0:T(8,128)(2,1)S(1)}) custom-call(s32[4]{0:T(128)S(1)} %pad_add_fusion.where_ref, bf16[4,32,384]{2,1,0:T(8,128)(2,1)S(1)} %collective-permute-done.9.refs_0_, bf16[4,32,384]{2,1,0:T(8,128)(2,1)S(1)} %collective-permute-done.10.refs_1_, bf16[1536,3072]{1,0:T(8,128)(2,1)S(1)} %bitcast.8, ...), custom_call_target="tpu_custom_call" | custom-call | tf_op jit(solution)/shard_map/pallas_call | solution.py:226
  73.6 4.8 %collective-permute-start.12 = (bf16[128,32]{1,0:T(8,128)(2,1)S(1)}, bf16[128,32]{1,0:T(8,128)(2,1)S(1)}, u32[]{:S(2)}, u32[]{:S(2)}) collective-permute-start(bf16[128,32]{1,0:T(8,128)(2,1)S(1)} %get-tuple-element.16.odd_ref), channel_id=1, source_target_pairs={{0,1},{1,2},{2,3},{3,4},{4,5},{5,6},{6,7},{7,8},{8,9},{9,10},{10,1... | collective-permute-start | bytes 24584 | tf_op jit(solution)/shard_map/ppermute | solution.py:398
  78.5 1.9 %collective-permute-start.13 = (bf16[128,32]{1,0:T(8,128)(2,1)S(1)}, bf16[128,32]{1,0:T(8,128)(2,1)S(1)}, u32[]{:S(2)}, u32[]{:S(2)}) collective-permute-start(bf16[128,32]{1,0:T(8,128)(2,1)S(1)} %get-tuple-element.15.even_ref), channel_id=1, source_target_pairs={{1,0},{2,1},{3,2},{4,3},{5,4},{6,5},{7,6},{8,7},{9,8},{10,9},{11,1... | collective-permute-start | bytes 24584 | tf_op jit(solution)/shard_map/ppermute | solution.py:399
  80.4 0.0 collective-permute-done.12.left_ref
  80.4 3.3 %collective-permute-done.13.right_ref = bf16[128,32]{1,0:T(8,128)(2,1)S(1)} collective-permute-done((bf16[128,32]{1,0:T(8,128)(2,1)S(1)}, bf16[128,32]{1,0:T(8,128)(2,1)S(1)}, u32[]{:S(2)}, u32[]{:S(2)}) %collective-permute-start.13) | collective-permute-done | bytes 8224 | tf_op jit(solution)/shard_map/ppermute | solution.py:399
  83.7 0.0 copy-done.2
  83.7 2.2 %shard_map.95 = bf16[4,2,64,512]{3,2,1,0:T(8,128)(2,1)} custom-call(s32[4]{0:T(128)S(1)} %pad_add_fusion.where_ref, bf16[128,32]{1,0:T(8,128)(2,1)S(1)} %get-tuple-element.15.even_ref, bf16[128,32]{1,0:T(8,128)(2,1)S(1)} %get-tuple-element.16.odd_ref, bf16[128,32]{1,0:T(8,128)(2,1)S(1)} %collective-permute-done.12.left_ref, ...), custom_call_target="tpu_custom_call" | custom-call | tf_op jit(solution)/shard_map/pallas_call | solution.py:295
  (34 shorter events, 0.5 us)
Async XLA Ops:
  0.0 2.3 %copy-start = (bf16[128,1536]{1,0:T(8,128)(2,1)S(1)}, bf16[128,1536]{1,0:T(8,128)(2,1)}, u32[]{:S(2)}) copy-start(bf16[128,1536]{1,0:T(8,128)(2,1)} %param.9) | copy-start | bytes 1179652
  2.7 14.3 %collective-permute-start = (bf16[384,384]{1,0:T(8,128)(2,1)S(1)}, bf16[384,384]{1,0:T(8,128)(2,1)S(1)}, u32[]{:S(2)}, u32[]{:S(2)}) collective-permute-start(bf16[384,384]{1,0:T(8,128)(2,1)S(1)} %pad_maximum_fusion.2), channel_id=1, source_target_pairs={{0,4},{4,0},{8,12},{12,8},{1,5},{5,1},{9,13},{13,9},{2,6},{6,2},{1... | collective-permute-start | bytes 884744 | tf_op jit(solution)/shard_map/ppermute | solution.py:23
  5.3 12.9 %collective-permute-start.3 = (bf16[384,384]{1,0:T(8,128)(2,1)S(1)}, bf16[384,384]{1,0:T(8,128)(2,1)S(1)}, u32[]{:S(2)}, u32[]{:S(2)}) collective-permute-start(bf16[384,384]{1,0:T(8,128)(2,1)S(1)} %pad_maximum_fusion.3), channel_id=1, source_target_pairs={{0,8},{4,12},{8,0},{12,4},{1,9},{5,13},{9,1},{13,5},{2,10},{6,14},... | collective-permute-start | bytes 884744 | tf_op jit(solution)/shard_map/ppermute | solution.py:23
  8.0 18.2 %collective-permute-start.6 = (bf16[384,384]{1,0:T(8,128)(2,1)S(1)}, bf16[384,384]{1,0:T(8,128)(2,1)S(1)}, u32[]{:S(2)}, u32[]{:S(2)}) collective-permute-start(bf16[384,384]{1,0:T(8,128)(2,1)S(1)} %pad_maximum_fusion.4), channel_id=1, source_target_pairs={{0,12},{4,8},{8,4},{12,0},{1,13},{5,9},{9,5},{13,1},{2,14},{6,10},... | collective-permute-start | bytes 884744 | tf_op jit(solution)/shard_map/ppermute | solution.py:23
  17.1 22.4 %collective-permute-start.1 = (bf16[640,384]{1,0:T(8,128)(2,1)S(1)}, bf16[640,384]{1,0:T(8,128)(2,1)S(1)}, u32[]{:S(2)}, u32[]{:S(2)}) collective-permute-start(bf16[640,384]{1,0:T(8,128)(2,1)S(1)} %slice_dynamic-update-slice_fusion.3), channel_id=1, source_target_pairs={{0,2},{1,3},{2,0},{3,1},{4,6},{5,7},{6,4},{7,5},{8,10},{9,11},{10,... | collective-permute-start | bytes 1474568 | tf_op jit(solution)/shard_map/ppermute | solution.py:23
  18.3 14.4 %collective-permute-start.4 = (bf16[320,384]{1,0:T(8,128)(2,1)S(1)}, bf16[320,384]{1,0:T(8,128)(2,1)S(1)}, u32[]{:S(2)}, u32[]{:S(2)}) collective-permute-start(bf16[320,384]{1,0:T(8,128)(2,1)S(1)} %pad_maximum_fusion.5), channel_id=1, source_target_pairs={{0,2},{1,3},{2,0},{3,1},{4,6},{5,7},{6,4},{7,5},{8,10},{9,11},{10,... | collective-permute-start | bytes 737288 | tf_op jit(solution)/shard_map/ppermute | solution.py:23
  26.3 14.6 %collective-permute-start.7 = (bf16[320,384]{1,0:T(8,128)(2,1)S(1)}, bf16[320,384]{1,0:T(8,128)(2,1)S(1)}, u32[]{:S(2)}, u32[]{:S(2)}) collective-permute-start(bf16[320,384]{1,0:T(8,128)(2,1)S(1)} %pad_maximum_fusion.6), channel_id=1, source_target_pairs={{0,2},{1,3},{2,0},{3,1},{4,6},{5,7},{6,4},{7,5},{8,10},{9,11},{10,... | collective-permute-start | bytes 737288 | tf_op jit(solution)/shard_map/ppermute | solution.py:23
  33.4 8.7 %collective-permute-start.5 = (bf16[576,384]{1,0:T(8,128)(2,1)S(1)}, bf16[576,384]{1,0:T(8,128)(2,1)S(1)}, u32[]{:S(2)}, u32[]{:S(2)}) collective-permute-start(bf16[576,384]{1,0:T(8,128)(2,1)S(1)} %pad_maximum_fusion.refs_6_), channel_id=1, source_target_pairs={{0,1},{1,0},{2,3},{3,2},{4,5},{5,4},{6,7},{7,6},{8,9},{9,8},{10,11... | collective-permute-start | bytes 1327112 | tf_op jit(solution)/shard_map/ppermute | solution.py:23
  40.7 5.6 %collective-permute-start.2 = (bf16[1152,384]{1,0:T(8,128)(2,1)S(1)}, bf16[1152,384]{1,0:T(8,128)(2,1)S(1)}, u32[]{:S(2)}, u32[]{:S(2)}) collective-permute-start(bf16[1152,384]{1,0:T(8,128)(2,1)S(1)} %get-tuple-element.22.refs_4_), channel_id=1, source_target_pairs={{0,1},{1,0},{2,3},{3,2},{4,5},{5,4},{6,7},{7,6},{8,9},{9,8},{10,11... | collective-permute-start | bytes 2654216 | tf_op jit(solution)/shard_map/ppermute | solution.py:23
  41.5 2.5 %collective-permute-start.8 = (bf16[576,384]{1,0:T(8,128)(2,1)S(1)}, bf16[576,384]{1,0:T(8,128)(2,1)}, u32[]{:S(2)}, u32[]{:S(2)}) collective-permute-start(bf16[576,384]{1,0:T(8,128)(2,1)S(1)} %pad_maximum_fusion.1.refs_8_), channel_id=1, source_target_pairs={{0,1},{1,0},{2,3},{3,2},{4,5},{5,4},{6,7},{7,6},{8,9},{9,8},{10,11... | collective-permute-start | bytes 1327112 | tf_op jit(solution)/shard_map/ppermute | solution.py:23
  47.9 21.6 %slice-start = ((s8[9437184]{0:T(1024)(128)(4,1)}), s8[4194304]{0:T(1024)(128)(4,1)S(1)}, s32[]{:S(2)}) async-start(s8[9437184]{0:T(1024)(128)(4,1)} %bitcast.7), calls=%async_computation | async-start | bytes 8388608
  51.4 18.1 %collective-permute-start.9 = (bf16[4,32,384]{2,1,0:T(8,128)(2,1)S(1)}, bf16[4,32,384]{2,1,0:T(8,128)(2,1)S(1)}, u32[]{:S(2)}, u32[]{:S(2)}) collective-permute-start(bf16[4,32,384]{2,1,0:T(8,128)(2,1)S(1)} %get-tuple-element.11), channel_id=1, source_target_pairs={{0,8},{4,12},{8,0},{12,4},{1,9},{5,13},{9,1},{13,5},{2,10},{6,14},... | collective-permute-start | bytes 294920 | tf_op jit(solution)/shard_map/ppermute | solution.py:23
  55.7 13.8 %collective-permute-start.10 = (bf16[4,32,384]{2,1,0:T(8,128)(2,1)S(1)}, bf16[4,32,384]{2,1,0:T(8,128)(2,1)S(1)}, u32[]{:S(2)}, u32[]{:S(2)}) collective-permute-start(bf16[4,32,384]{2,1,0:T(8,128)(2,1)S(1)} %get-tuple-element.12), channel_id=1, source_target_pairs={{0,4},{4,0},{8,12},{12,8},{1,5},{5,1},{9,13},{13,9},{2,6},{6,2},{1... | collective-permute-start | bytes 294920 | tf_op jit(solution)/shard_map/ppermute | solution.py:23
  57.4 5.4 %collective-permute-start.11 = (bf16[4,32,384]{2,1,0:T(8,128)(2,1)S(1)}, bf16[4,32,384]{2,1,0:T(8,128)(2,1)S(1)}, u32[]{:S(2)}, u32[]{:S(2)}) collective-permute-start(bf16[4,32,384]{2,1,0:T(8,128)(2,1)S(1)} %get-tuple-element.14), channel_id=1, source_target_pairs={{0,12},{4,8},{8,4},{12,0},{1,13},{5,9},{9,5},{13,1},{2,14},{6,10},... | collective-permute-start | bytes 294920 | tf_op jit(solution)/shard_map/ppermute | solution.py:23
  62.8 3.7 %copy-start.1 = (bf16[1536,3072]{1,0:T(8,128)(2,1)S(1)}, bf16[1536,3072]{1,0:T(8,128)(2,1)}, u32[]{:S(2)}) copy-start(bf16[1536,3072]{1,0:T(8,128)(2,1)} %refs_7_.3) | copy-start | bytes 28311556
  66.4 3.0 %slice-start.1 = ((s8[9437184]{0:T(1024)(128)(4,1)}), s8[4194304]{0:T(1024)(128)(4,1)S(1)}, s32[]{:S(2)}) async-start(s8[9437184]{0:T(1024)(128)(4,1)} %bitcast.7), calls=%async_computation.1 | async-start | bytes 8388608
  66.4 3.1 %slice-start.2 = ((s8[9437184]{0:T(1024)(128)(4,1)}), s8[1048576]{0:T(1024)(128)(4,1)S(1)}, s32[]{:S(2)}) async-start(s8[9437184]{0:T(1024)(128)(4,1)} %bitcast.7), calls=%async_computation.2 | async-start | bytes 2097152
  66.4 3.1 %copy-start.3 = (bf16[3072,64]{0,1:T(8,128)(2,1)S(1)}, bf16[3072,64]{0,1:T(8,128)(2,1)}, u32[]{:S(2)}) copy-start(bf16[3072,64]{0,1:T(8,128)(2,1)} %param.15) | copy-start | bytes 1179652
  66.4 3.1 %copy-start.4 = (f32[3072]{0:T(1024)S(1)}, f32[3072]{0:T(1024)}, u32[]{:S(2)}) copy-start(f32[3072]{0:T(1024)} %param.14) | copy-start | bytes 36868
  66.4 3.1 %copy-start.5 = (f32[3072]{0:T(1024)S(1)}, f32[3072]{0:T(1024)}, u32[]{:S(2)}) copy-start(f32[3072]{0:T(1024)} %param.13) | copy-start | bytes 36868
  69.5 14.2 %copy-start.2 = (bf16[432,512]{1,0:T(8,128)(2,1)S(1)}, bf16[432,512]{1,0:T(8,128)(2,1)}, u32[]{:S(2)}) copy-start(bf16[432,512]{1,0:T(8,128)(2,1)} %w_ref.1) | copy-start | bytes 1327108
  69.6 14.1 %copy-start.6 = (f32[512]{0:T(512)S(1)}, f32[512]{0:T(512)}, u32[]{:S(2)}) copy-start(f32[512]{0:T(512)} %param.17) | copy-start | bytes 6148
  73.6 6.7 %collective-permute-start.12 = (bf16[128,32]{1,0:T(8,128)(2,1)S(1)}, bf16[128,32]{1,0:T(8,128)(2,1)S(1)}, u32[]{:S(2)}, u32[]{:S(2)}) collective-permute-start(bf16[128,32]{1,0:T(8,128)(2,1)S(1)} %get-tuple-element.16.odd_ref), channel_id=1, source_target_pairs={{0,1},{1,2},{2,3},{3,4},{4,5},{5,6},{6,7},{7,8},{8,9},{9,10},{10,1... | collective-permute-start | bytes 24584 | tf_op jit(solution)/shard_map/ppermute | solution.py:398
  78.5 5.2 %collective-permute-start.13 = (bf16[128,32]{1,0:T(8,128)(2,1)S(1)}, bf16[128,32]{1,0:T(8,128)(2,1)S(1)}, u32[]{:S(2)}, u32[]{:S(2)}) collective-permute-start(bf16[128,32]{1,0:T(8,128)(2,1)S(1)} %get-tuple-element.15.even_ref), channel_id=1, source_target_pairs={{1,0},{2,1},{3,2},{4,3},{5,4},{6,5},{7,6},{8,7},{9,8},{10,9},{11,1... | collective-permute-start | bytes 24584 | tf_op jit(solution)/shard_map/ppermute | solution.py:399

commit v8 on v7

--- a/solution.py
+++ b/solution.py
@@ -15,6 +15,7 @@
 FRAMES = 4
 VMEM_LIMIT = 16 * 1024 * 1024
 CHUNKS = ((0, 3),)
+
 EXP2_SCALE = math.log2(math.e) / math.sqrt(HEAD_DIM)
 
 
@@ -23,30 +24,43 @@
     return lax.ppermute(source, axis, [(i, i ^ distance) for i in range(count)])
 
 
-def attend_kernel(*refs, sources, planes, blocks, part, targets, rows_step):
-    q_refs = refs[:sources]
-    kv_refs = refs[sources : sources + len(blocks)]
-    o_refs = refs[sources + len(blocks) :]
-    tokens, width = q_refs[0].shape
+def attend_kernel(*refs, planes, tokens, sources, targets, rows_step):
+    held = [refs[4 * r : 4 * r + 4] for r in range(sources)]
+    o_refs = refs[4 * sources :]
+    width = o_refs[0].shape[2]
     rows = tokens // sources
     rows_dev = rows // planes
+    share = tokens // planes
+    stride = 2 * tokens + 2 * share
     to = lax.broadcasted_iota(jnp.int32, (tokens, tokens), 0)
     at = lax.broadcasted_iota(jnp.int32, (tokens, tokens), 1)
     t, j, row = to // rows, (to // rows_dev) % planes, to % rows_dev
     place = ((j % 2) * (planes // 2) + j // 2) * rows + t * rows_dev + row
     order = (at == place).astype(jnp.bfloat16)
-    asked = [
-        jnp.dot(order, q[...], preferred_element_type=jnp.float32).astype(jnp.bfloat16) for q in q_refs
-    ]
+    passed = [k * stride for k in range(planes // 2 - 1)]
+    asked = []
+    for own, crossed, other, other_crossed in held:
+        pieces = [own[:share]]
+        pieces += [crossed[at_row + 2 * tokens + share : at_row + stride] for at_row in passed]
+        pieces += [other[share : 2 * share]]
+        pieces += [other_crossed[at_row + 2 * tokens : at_row + 2 * tokens + share] for at_row in passed]
+        mixed = jnp.dot(order, jnp.concatenate(pieces, axis=0), preferred_element_type=jnp.float32)
+        asked.append(mixed.astype(jnp.bfloat16))
+    parts = []
+    for own, crossed, other, other_crossed in held:
+        for whole, several in ((own, crossed), (other, other_crossed)):
+            parts += [(whole, 2 * share)] + [(several, at_row) for at_row in passed]
+    parts = [parts[n : n + 4] for n in range(0, len(parts), 4)]
     works = [
         (h, range(first, min(first + rows_step, len(targets))))
         for h in range(width // HEAD_DIM)
         for first in range(0, len(targets), rows_step)
     ]
 
-    def taken(ref, count, h, which):
-        cut = ref[: count * 2 * part, h * HEAD_DIM : (h + 1) * HEAD_DIM]
-        return cut.reshape(count, 2, part, HEAD_DIM)[:, which].reshape(count * part, HEAD_DIM)
+    def taken(part, h, which):
+        lanes = slice(h * HEAD_DIM, (h + 1) * HEAD_DIM)
+        firsts = [(ref, first + which * tokens) for ref, first in part]
+        return jnp.concatenate([ref[first : first + tokens, lanes] for ref, first in firsts], axis=0)
 
     def scores_of(work):
         h, block = work
@@ -57,11 +71,11 @@
         return [
             lax.dot_general(
                 query,
-                taken(kv, count, h, 0),
+                taken(part, h, 0),
                 (((1,), (1,)), ((), ())),
                 preferred_element_type=jnp.float32,
             )
-            for kv, count in zip(kv_refs, blocks)
+            for part in parts
         ]
 
     def finish(work, scores):
@@ -69,9 +83,9 @@
         peak = functools.reduce(jnp.maximum, [jnp.max(s, axis=1, keepdims=True) for s in scores])
         peak = peak * EXP2_SCALE
         summed = None
-        for s, kv, count in zip(scores, kv_refs, blocks):
+        for s, part in zip(scores, parts):
             weights = jnp.exp2(s * EXP2_SCALE - peak).astype(jnp.bfloat16)
-            value = taken(kv, count, h, 1)
+            value = taken(part, h, 1)
             value = jnp.concatenate([value, jnp.ones_like(value)], axis=1)
             product = jnp.dot(weights, value, preferred_element_type=jnp.float32)
             summed = product if summed is None else summed + product
@@ -88,33 +102,30 @@
         scores = following
 
 
-def attend(queries, keys_values, targets, planes):
-    sources = len(queries)
-    tokens, width = queries[0].shape
+def attend(held, targets, tokens, planes):
+    width = held[0].shape[1]
+    sources = len(held) // 4
     rows = tokens // sources
-    blocks = [kv.shape[0] // (2 * tokens) for kv in keys_values]
-    key_count = sum(blocks) * tokens
+    key_count = sources * planes * tokens
     small = key_count <= 4096
     rows_step, step_width = (2, width) if small else (1, HEAD_DIM)
     score_bytes = rows_step * tokens * key_count * 4
-    limit = 8 * key_count * step_width + 3 * score_bytes + 6 * 1024 * 1024
+    limit = 2 * key_count * step_width * (2 if small else 8) + 3 * score_bytes + 4 * 1024 * 1024
     return pl.pallas_call(
         functools.partial(
             attend_kernel,
+            planes=planes,
+            tokens=tokens,
             sources=sources,
-            planes=planes,
-            blocks=blocks,
-            part=tokens,
             targets=targets,
             rows_step=rows_step,
         ),
         grid=(width // step_width,),
-        in_specs=[pl.BlockSpec((tokens, step_width), lambda h: (0, h))] * sources
-        + [pl.BlockSpec((kv.shape[0], step_width), lambda h: (0, h)) for kv in keys_values],
+        in_specs=[pl.BlockSpec((array.shape[0], step_width), lambda h: (0, h)) for array in held],
         out_specs=[pl.BlockSpec((sources, rows, step_width), lambda h: (0, 0, h))] * len(targets),
         out_shape=[jax.ShapeDtypeStruct((sources, rows, width), jnp.bfloat16)] * len(targets),
         compiler_params=pltpu.CompilerParams(vmem_limit_bytes=min(limit, 60 * 1024 * 1024)),
-    )(*queries, *keys_values)
+    )(*held)
 
 
 def projection_of(o_refs, w_refs, lined):
@@ -128,14 +139,28 @@
     return jnp.dot(lined[...], weights, preferred_element_type=jnp.float32)
 
 
+def row_blocks(taken, group_heads):
+    blocks = []
+    for target, low, o in taken:
+        heads = o.shape[2] // HEAD_DIM
+        step = heads if group_heads % heads == 0 and low % heads == 0 else 1
+        blocks += [
+            (target, (low + n) // step, step, group_heads // step) for n in range(0, heads, step)
+        ]
+    return blocks
+
+
 def projection_specs(taken, tile, group_heads):
     whole = [pl.BlockSpec(o.shape, lambda i, *_: (0, 0, 0)) for _, _, o in taken]
-    heads = [(t, low + n) for t, low, o in taken for n in range(o.shape[2] // HEAD_DIM)]
     return whole + [
         pl.BlockSpec(
-            (HEAD_DIM, tile), lambda i, where, t=t, h=h: ((where[0] ^ t) * group_heads + h, i)
+            (HEAD_DIM * step, tile),
+            lambda i, where, target=target, block=block, count=count: (
+                (where[0] ^ target) * count + block,
+                i,
+            ),
         )
-        for t, h in heads
+        for target, block, step, count in row_blocks(taken, group_heads)
     ]
 
 
@@ -160,7 +185,7 @@
         ),
         out_shape=jax.ShapeDtypeStruct((features // tile, tokens, tile), jnp.float32),
         compiler_params=pltpu.CompilerParams(vmem_limit_bytes=VMEM_LIMIT),
-    )(where, *[o for _, _, o in taken], *[w_out] * (depth // HEAD_DIM))
+    )(where, *[o for _, _, o in taken], *[w_out] * len(row_blocks(taken, inner // HEAD_DIM // HEAD_GROUPS)))
 
 
 def final_kernel(where_ref, *refs, count, planes, rows_dev):
@@ -246,7 +271,7 @@
     )(
         where,
         *[o for _, _, o in taken],
-        *[w_out] * (depth // HEAD_DIM),
+        *[w_out] * len(row_blocks(taken, inner // HEAD_DIM // HEAD_GROUPS)),
         partial,
         scale_mod[None],
         shift_mod[None],
@@ -306,36 +331,18 @@
     return lax.optimization_barrier((value,) + others)[0]
 
 
-def gather_plane(got, batch, both_parts, share, waits):
+def gather_plane(bundle, both_parts, share, waits):
     planes = lax.axis_size("plane")
-    half, count = planes // 2, len(batch)
-    kv_rows = both_parts * count
     crossed = []
     for d in range(2, planes, 2):
-        sent = [got[r][:both_parts] for r in batch]
-        sent += [got[r][both_parts + d * share : both_parts + (d + 2) * share] for r in batch]
-        crossed.append(swap(jnp.concatenate(sent, axis=0), "plane", d))
-    near = [[got[r][both_parts : both_parts + share] for r in batch]]
-    far = [[got[r][both_parts + share : both_parts + 2 * share] for r in batch]]
-    for x in crossed:
-        firsts = [kv_rows + 2 * n * share for n in range(count)]
-        near.append([x[first : first + share] for first in firsts])
-        far.append([x[first + share : first + 2 * share] for first in firsts])
-    mine = [got[r][:both_parts] for r in batch] + [x[:kv_rows] for x in crossed]
-    mine = jnp.concatenate(mine + [q for pieces in far for q in pieces], axis=0)
-    if waits and batch == (3,):
-        mine = after(mine, *waits)
-    other = swap(mine, "plane", 1)
-    asked = []
-    for n in range(count):
-        firsts = [kv_rows * half + (k * count + n) * share for k in range(half)]
-        asked.append(
-            jnp.concatenate(
-                [pieces[n] for pieces in near] + [other[first : first + share] for first in firsts],
-                axis=0,
-            )
-        )
-    return [mine, other], asked
+        if d == 2:
+            sent = bundle[2 * share : both_parts + 4 * share]
+        else:
+            asked = bundle[both_parts + d * share : both_parts + (d + 2) * share]
+            sent = jnp.concatenate([bundle[2 * share : both_parts + 2 * share], asked], axis=0)
+        crossed.append(swap(after(sent, *waits), "plane", d))
+    crossed = jnp.concatenate(crossed, axis=0) if len(crossed) > 1 else crossed[0]
+    return [bundle, crossed, swap(bundle, "plane", 1), swap(crossed, "plane", 1)]
 
 
 def shards(queries, keys, values, w_out, shift_mod, scale_mod, w_final, conv_weight, conv_bias):
@@ -355,6 +362,7 @@
     to = lax.broadcasted_iota(jnp.int32, (tokens, tokens), 0)
     at = lax.broadcasted_iota(jnp.int32, (tokens, tokens), 1)
     j, t, row = to // (groups * rows_dev), (to // rows_dev) % groups, to % rows_dev
+    j = jnp.where(j < 2, j, j ^ 1)
 
     def bundle(r, low, high):
         first = (heads_at ^ r) * (HEAD_DIM * group_heads) + low * HEAD_DIM
@@ -365,7 +373,7 @@
         place = row * devices + (t ^ (r ^ heads_at)) * planes + (j ^ plane_at)
         order = (at == place).astype(jnp.bfloat16)
         cut[2] = jnp.dot(order, cut[2], preferred_element_type=jnp.float32).astype(jnp.bfloat16)
-        return jnp.concatenate(cut, axis=0)
+        return jnp.concatenate([cut[2][: 2 * share], cut[0], cut[1], cut[2][2 * share :]], axis=0)
 
     chunks, begun, done = [], None, None
     for low, high in CHUNKS:
@@ -374,14 +382,12 @@
             got = [after(b, begun) for b in got]
         got = [swap(b, "heads", r) if r else b for r, b in enumerate(got)]
         begun = got[1]
-        keys_values, asked = [], []
-        for batch in ((0, 1), (2,), (3,)):
-            kv, q = gather_plane(got, batch, both_parts, share, done)
-            keys_values += kv
-            asked += q
+        held = []
+        for r, piece in enumerate(got):
+            held += gather_plane(piece, both_parts, share, got[1:2] if r == 0 else [])
         taken, done = [], []
         for targets in ((3, 2), (1, 0)):
-            for target, o in zip(targets, attend(asked, keys_values, targets, planes)):
+            for target, o in zip(targets, attend(held, targets, tokens, planes)):
                 done.append(o)
                 taken.append((target, low, o if target == 0 else swap(o, "heads", target)))
         chunks.append(taken)

time: 86.4 us -> 89.3 us (1.034)
  the two profiles are of different devices: /device:TPU:1 before, /device:TPU:24 now
where the time goes in v8:
time: 89.3 us; the launch traced here: 89 us
  waiting for transfers between devices  40.7 us (46%)
  starting transfers between devices  24.2 us (27%)
  Pallas kernels  16 us (18%)
  local copies, waits for them, and re-layouts  6.13 us (7%)
  matrix products  1.31 us (1%)
    ppermute x18, waiting for transfers between devices, swap(): return lax.ppermute(source, axis, [(i, i ^ distance) for i in range(count)])  36.6 us
    ppermute x18, starting transfers between devices, swap(): return lax.ppermute(source, axis, [(i, i ^ distance) for i in range(count)])  15.2 us
    pallas_call x2, Pallas kernels, attend(): pl.pallas_call(functools.partial(attend_kernel, planes=planes, tokens=tok...  7.41 us
    ppermute x1, starting transfers between devices, shards(): right = lax.ppermute(even, both, [(i + 1, i) for i in range(devices - 1)])  7.13 us
    unnamed x20, local copies, waits for them, and re-layouts  4.65 us
    ppermute x1, waiting for transfers between devices, shards(): left = lax.ppermute(odd, both, [(i, i + 1) for i in range(devices - 1)])  4.19 us
    pallas_call x1, Pallas kernels, final_layer(): pl.pallas_call(functools.partial(final_kernel, count=len(taken), planes=p...  3.78 us
    pallas_call x1, Pallas kernels, project(): pl.pallas_call(functools.partial(project_kernel, count=len(taken)), grid_...  2.67 us
  transfers between devices with their start and end apart: 20, of which 11 were waited for; matrix products, arithmetic and copies ran while one was open for 1% of the time, Pallas kernels for 7%

profile of v8, /device:TPU:24, one launch (start us, length us, event | category | flops | bytes accessed | tf_op | source)
XLA Modules:
  0.0 89.0 jit_solution(1204890761348008809)
XLA Ops:
  0.0 0.0 copy-start
  0.1 0.9 %copy-done = bf16[128,1536]{1,0:T(8,128)(2,1)S(1)} copy-done((bf16[128,1536]{1,0:T(8,128)(2,1)S(1)}, bf16[128,1536]{1,0:T(8,128)(2,1)}, u32[]{:S(2)}) %copy-start) | copy-done | bytes 393240
  1.0 0.3 convolution_convert_fusion.1
  1.4 1.3 %constant_dynamic-slice_fusion = (bf16[128,384]{1,0:T(8,128)(2,1)S(1)}, bf16[128,384]{1,0:T(8,128)(2,1)S(1)}, bf16[128,384]{1,0:T(8,128)(2,1)S(1)}, bf16[128,384...) fusion(bf16[128,1536]{1,0:T(8,128)(2,1)} %param.11, ...), kind=kLoop, calls=%fused_computation.74 | loop fusion | bytes 1572880 | tf_op jit(solution)/shard_map/dynamic_slice | solution.py:370
  2.7 0.4 collective-permute-start.7
  3.1 0.3 convolution_convert_fusion.2
  3.5 0.2 collective-permute-start
  3.7 0.3 convolution_convert_fusion
  4.1 4.0 %collective-permute-start.11 = (bf16[384,384]{1,0:T(8,128)(2,1)S(1)}, bf16[384,384]{1,0:T(8,128)(2,1)S(1)}, u32[]{:S(2)}, u32[]{:S(2)}) collective-permute-start(bf16[384,384]{1,0:T(8,128)(2,1)S(1)} %pad_maximum_fusion.3), channel_id=1, source_target_pairs={{0,12},{4,8},{8,4},{12,0},{1,13},{5,9},{9,5},{13,1},{2,14},{6,10},... | collective-permute-start | bytes 884744 | tf_op jit(solution)/shard_map/ppermute | solution.py:24
  8.1 0.3 convolution_convert_fusion.3
  8.5 0.1 collective-permute-start.2
  8.6 11.3 %collective-permute-done.7.refs_8_ = bf16[384,384]{1,0:T(8,128)(2,1)S(1)} collective-permute-done((bf16[384,384]{1,0:T(8,128)(2,1)S(1)}, bf16[384,384]{1,0:T(8,128)(2,1)S(1)}, u32[]{:S(2)}, u32[]{:S(2)}) %collective-permute-start.7) | collective-permute-done | bytes 294944 | tf_op jit(solution)/shard_map/ppermute | solution.py:24
  19.9 1.6 %collective-permute-start.8 = (bf16[320,384]{1,0:T(8,128)(2,1)S(1)}, bf16[320,384]{1,0:T(8,128)(2,1)S(1)}, u32[]{:S(2)}, u32[]{:S(2)}) collective-permute-start(bf16[320,384]{1,0:T(8,128)(2,1)S(1)} %slice.53), channel_id=1, source_target_pairs={{0,2},{1,3},{2,0},{3,1},{4,6},{5,7},{6,4},{7,5},{8,10},{9,11},{10,... | collective-permute-start | bytes 737288 | tf_op jit(solution)/shard_map/ppermute | solution.py:24
  21.5 0.0 collective-permute-done.refs_4_
  21.5 0.6 collective-permute-start.4
  22.1 0.0 collective-permute-start.9
  22.1 3.0 %collective-permute-done.11.refs_12_ = bf16[384,384]{1,0:T(8,128)(2,1)S(1)} collective-permute-done((bf16[384,384]{1,0:T(8,128)(2,1)S(1)}, bf16[384,384]{1,0:T(8,128)(2,1)S(1)}, u32[]{:S(2)}, u32[]{:S(2)}) %collective-permute-start.11) | collective-permute-done | bytes 294944 | tf_op jit(solution)/shard_map/ppermute | solution.py:24
  25.1 0.0 collective-permute-start.5
  25.2 0.0 collective-permute-done.2.refs_2_
  25.2 1.6 %collective-permute-start.1 = (bf16[320,384]{1,0:T(8,128)(2,1)S(1)}, bf16[320,384]{1,0:T(8,128)(2,1)S(1)}, u32[]{:S(2)}, u32[]{:S(2)}) collective-permute-start(bf16[320,384]{1,0:T(8,128)(2,1)S(1)} %pad_maximum_fusion.4), channel_id=1, source_target_pairs={{0,2},{1,3},{2,0},{3,1},{4,6},{5,7},{6,4},{7,5},{8,10},{9,11},{10,... | collective-permute-start | bytes 737288 | tf_op jit(solution)/shard_map/ppermute | solution.py:24
  26.8 2.1 %collective-permute-done.8.refs_9_ = bf16[320,384]{1,0:T(8,128)(2,1)S(1)} collective-permute-done((bf16[320,384]{1,0:T(8,128)(2,1)S(1)}, bf16[320,384]{1,0:T(8,128)(2,1)S(1)}, u32[]{:S(2)}, u32[]{:S(2)}) %collective-permute-start.8) | collective-permute-done | bytes 245792 | tf_op jit(solution)/shard_map/ppermute | solution.py:24
  28.9 1.5 %collective-permute-start.12 = (bf16[320,384]{1,0:T(8,128)(2,1)S(1)}, bf16[320,384]{1,0:T(8,128)(2,1)}, u32[]{:S(2)}, u32[]{:S(2)}) collective-permute-start(bf16[320,384]{1,0:T(8,128)(2,1)S(1)} %slice.56), channel_id=1, source_target_pairs={{0,2},{1,3},{2,0},{3,1},{4,6},{5,7},{6,4},{7,5},{8,10},{9,11},{10,... | collective-permute-start | bytes 737288 | tf_op jit(solution)/shard_map/ppermute | solution.py:24
  30.3 3.8 %collective-permute-done.4.refs_5_ = bf16[320,384]{1,0:T(8,128)(2,1)S(1)} collective-permute-done((bf16[320,384]{1,0:T(8,128)(2,1)S(1)}, bf16[320,384]{1,0:T(8,128)(2,1)S(1)}, u32[]{:S(2)}, u32[]{:S(2)}) %collective-permute-start.4) | collective-permute-done | bytes 245792 | tf_op jit(solution)/shard_map/ppermute | solution.py:24
  34.1 0.0 collective-permute-start.13
  34.1 5.3 %collective-permute-done.1.refs_1_ = bf16[320,384]{1,0:T(8,128)(2,1)S(1)} collective-permute-done((bf16[320,384]{1,0:T(8,128)(2,1)S(1)}, bf16[320,384]{1,0:T(8,128)(2,1)S(1)}, u32[]{:S(2)}, u32[]{:S(2)}) %collective-permute-start.1) | collective-permute-done | bytes 245792 | tf_op jit(solution)/shard_map/ppermute | solution.py:24
  39.4 0.0 collective-permute-start.10
  39.4 4.1 %collective-permute-done.12.refs_13_ = bf16[320,384]{1,0:T(8,128)(2,1)} collective-permute-done((bf16[320,384]{1,0:T(8,128)(2,1)S(1)}, bf16[320,384]{1,0:T(8,128)(2,1)}, u32[]{:S(2)}, u32[]{:S(2)}) %collective-permute-start.12) | collective-permute-done | bytes 245792 | tf_op jit(solution)/shard_map/ppermute | solution.py:24
  43.5 0.0 collective-permute-start.6
  43.5 0.0 collective-permute-done.9.refs_10_
  43.5 0.5 collective-permute-start.3
  44.1 0.0 collective-permute-done.5.refs_6_
  44.1 0.1 collective-permute-start.14
  44.1 0.0 collective-permute-done.13.refs_14_
  44.1 0.0 collective-permute-done.10.refs_11_
  44.1 1.0 %collective-permute-done.6.refs_7_ = bf16[320,384]{1,0:T(8,128)(2,1)} collective-permute-done((bf16[320,384]{1,0:T(8,128)(2,1)S(1)}, bf16[320,384]{1,0:T(8,128)(2,1)}, u32[]{:S(2)}, u32[]{:S(2)}) %collective-permute-start.6) | collective-permute-done | bytes 245792 | tf_op jit(solution)/shard_map/ppermute | solution.py:24
  45.2 0.4 collective-permute-done.3.refs_3_
  45.5 0.6 collective-permute-done.14.refs_15_
  46.1 3.8 %shard_map.92 = (bf16[4,32,384]{2,1,0:T(8,128)(2,1)S(1)}, bf16[4,32,384]{2,1,0:T(8,128)(2,1)S(1)}) custom-call(bf16[384,384]{1,0:T(8,128)(2,1)S(1)} %pad_maximum_fusion.refs_0_, bf16[320,384]{1,0:T(8,128)(2,1)S(1)} %collective-permute-done.1.refs_1_, bf16[384,384]{1,0:T(8,128)(2,1)S(1)} %collective-permute-done.2.refs_2_, ...), custom_call_target="tpu_custom_call" | custom-call | tf_op jit(solution)/shard_map/pallas_call | solution.py:114
  49.9 2.3 %collective-permute-start.16 = (bf16[4,32,384]{2,1,0:T(8,128)(2,1)S(1)}, bf16[4,32,384]{2,1,0:T(8,128)(2,1)S(1)}, u32[]{:S(2)}, u32[]{:S(2)}) collective-permute-start(bf16[4,32,384]{2,1,0:T(8,128)(2,1)S(1)} %get-tuple-element.14), channel_id=1, source_target_pairs={{0,4},{4,0},{8,12},{12,8},{1,5},{5,1},{9,13},{13,9},{2,6},{6,2},{1... | collective-permute-start | bytes 294920 | tf_op jit(solution)/shard_map/ppermute | solution.py:24
  52.1 3.7 %shard_map.91 = (bf16[4,32,384]{2,1,0:T(8,128)(2,1)S(1)}, bf16[4,32,384]{2,1,0:T(8,128)(2,1)S(1)}) custom-call(bf16[384,384]{1,0:T(8,128)(2,1)S(1)} %pad_maximum_fusion.refs_0_, bf16[320,384]{1,0:T(8,128)(2,1)S(1)} %collective-permute-done.1.refs_1_, bf16[384,384]{1,0:T(8,128)(2,1)S(1)} %collective-permute-done.2.refs_2_, ...), custom_call_target="tpu_custom_call" | custom-call | tf_op jit(solution)/shard_map/pallas_call | solution.py:114
  55.8 0.4 collective-permute-start.15
  56.2 2.1 %collective-permute-start.17 = (bf16[4,32,384]{2,1,0:T(8,128)(2,1)S(1)}, bf16[4,32,384]{2,1,0:T(8,128)(2,1)S(1)}, u32[]{:S(2)}, u32[]{:S(2)}) collective-permute-start(bf16[4,32,384]{2,1,0:T(8,128)(2,1)S(1)} %get-tuple-element.16), channel_id=1, source_target_pairs={{0,12},{4,8},{8,4},{12,0},{1,13},{5,9},{9,5},{13,1},{2,14},{6,10},... | collective-permute-start | bytes 294920 | tf_op jit(solution)/shard_map/ppermute | solution.py:24
  58.2 0.1 pad_add_fusion.where_ref
  58.3 5.0 %collective-permute-done.17.refs_1_ = bf16[4,32,384]{2,1,0:T(8,128)(2,1)S(1)} collective-permute-done((bf16[4,32,384]{2,1,0:T(8,128)(2,1)S(1)}, bf16[4,32,384]{2,1,0:T(8,128)(2,1)S(1)}, u32[]{:S(2)}, u32[]{:S(2)}) %collective-permute-start.17) | collective-permute-done | bytes 98336 | tf_op jit(solution)/shard_map/ppermute | solution.py:24
  63.3 3.7 %copy-done.1 = bf16[1536,3072]{1,0:T(8,128)(2,1)S(1)} copy-done((bf16[1536,3072]{1,0:T(8,128)(2,1)S(1)}, bf16[1536,3072]{1,0:T(8,128)(2,1)}, u32[]{:S(2)}) %copy-start.1) | copy-done | bytes 9437208
  67.0 0.0 copy-start.5
  67.0 2.7 %shard_map.93.refs_4_ = f32[6,128,512]{2,1,0:T(8,128)S(1)} custom-call(s32[4]{0:T(128)S(1)} %pad_add_fusion.where_ref, bf16[4,32,384]{2,1,0:T(8,128)(2,1)S(1)} %get-tuple-element.15.refs_0_, bf16[4,32,384]{2,1,0:T(8,128)(2,1)S(1)} %collective-permute-done.17.refs_1_, bf16[1536,3072]{1,0:T(8,128)(2,1)S(1)} %copy-done.1, bf16[1536,3072]{1,0:T(8,128)(2,1)S(1)} %copy-done.1), custom_call_target="tpu_custom_call" | custom-call | tf_op jit(solution)/shard_map/pallas_call | solution.py:177
  69.7 0.0 collective-permute-done.16.refs_1_
  69.7 0.0 collective-permute-done.15.refs_0_
  69.7 0.0 slice-done
  69.7 0.0 slice-done.1
  69.7 0.0 slice-done.2
  69.7 0.0 copy-done.3
  69.7 0.0 copy-done.4
  69.7 0.0 copy-done.5
  69.8 0.0 copy-start.2
  69.8 0.0 copy-start.6
  69.8 3.8 %shard_map.94 = (bf16[128,32]{1,0:T(8,128)(2,1)S(1)}, bf16[128,32]{1,0:T(8,128)(2,1)S(1)}) custom-call(s32[4]{0:T(128)S(1)} %pad_add_fusion.where_ref, bf16[4,32,384]{2,1,0:T(8,128)(2,1)S(1)} %collective-permute-done.15.refs_0_, bf16[4,32,384]{2,1,0:T(8,128)(2,1)S(1)} %collective-permute-done.16.refs_1_, bf16[1536,3072]{1,0:T(8,128)(2,1)S(1)} %bitcast.8, ...), custom_call_target="tpu_custom_call" | custom-call | tf_op jit(solution)/shard_map/pallas_call | solution.py:251
  73.6 7.1 %collective-permute-start.19 = (bf16[128,32]{1,0:T(8,128)(2,1)S(1)}, bf16[128,32]{1,0:T(8,128)(2,1)S(1)}, u32[]{:S(2)}, u32[]{:S(2)}) collective-permute-start(bf16[128,32]{1,0:T(8,128)(2,1)S(1)} %get-tuple-element.17.even_ref), channel_id=1, source_target_pairs={{1,0},{2,1},{3,2},{4,3},{5,4},{6,5},{7,6},{8,7},{9,8},{10,9},{11,1... | collective-permute-start | bytes 24584 | tf_op jit(solution)/shard_map/ppermute | solution.py:405
  80.7 1.9 %collective-permute-start.18 = (bf16[128,32]{1,0:T(8,128)(2,1)S(1)}, bf16[128,32]{1,0:T(8,128)(2,1)S(1)}, u32[]{:S(2)}, u32[]{:S(2)}) collective-permute-start(bf16[128,32]{1,0:T(8,128)(2,1)S(1)} %get-tuple-element.18.odd_ref), channel_id=1, source_target_pairs={{0,1},{1,2},{2,3},{3,4},{4,5},{5,6},{6,7},{7,8},{8,9},{9,10},{10,1... | collective-permute-start | bytes 24584 | tf_op jit(solution)/shard_map/ppermute | solution.py:404
  82.6 0.0 collective-permute-done.19.right_ref
  82.6 4.2 %collective-permute-done.18.left_ref = bf16[128,32]{1,0:T(8,128)(2,1)S(1)} collective-permute-done((bf16[128,32]{1,0:T(8,128)(2,1)S(1)}, bf16[128,32]{1,0:T(8,128)(2,1)S(1)}, u32[]{:S(2)}, u32[]{:S(2)}) %collective-permute-start.18) | collective-permute-done | bytes 8224 | tf_op jit(solution)/shard_map/ppermute | solution.py:404
  86.8 0.0 copy-done.2
  86.8 2.2 %shard_map.95 = bf16[4,2,64,512]{3,2,1,0:T(8,128)(2,1)} custom-call(s32[4]{0:T(128)S(1)} %pad_add_fusion.where_ref, bf16[128,32]{1,0:T(8,128)(2,1)S(1)} %get-tuple-element.17.even_ref, bf16[128,32]{1,0:T(8,128)(2,1)S(1)} %get-tuple-element.18.odd_ref, bf16[128,32]{1,0:T(8,128)(2,1)S(1)} %collective-permute-done.18.left_ref, ...), custom_call_target="tpu_custom_call" | custom-call | tf_op jit(solution)/shard_map/pallas_call | solution.py:320
  (25 shorter events, 0.3 us)
Async XLA Ops:
  0.0 1.0 %copy-start = (bf16[128,1536]{1,0:T(8,128)(2,1)S(1)}, bf16[128,1536]{1,0:T(8,128)(2,1)}, u32[]{:S(2)}) copy-start(bf16[128,1536]{1,0:T(8,128)(2,1)} %param.9) | copy-start | bytes 1179652
  2.7 17.2 %collective-permute-start.7 = (bf16[384,384]{1,0:T(8,128)(2,1)S(1)}, bf16[384,384]{1,0:T(8,128)(2,1)S(1)}, u32[]{:S(2)}, u32[]{:S(2)}) collective-permute-start(bf16[384,384]{1,0:T(8,128)(2,1)S(1)} %pad_maximum_fusion.2), channel_id=1, source_target_pairs={{0,8},{4,12},{8,0},{12,4},{1,9},{5,13},{9,1},{13,5},{2,10},{6,14},... | collective-permute-start | bytes 884744 | tf_op jit(solution)/shard_map/ppermute | solution.py:24
  3.5 18.0 %collective-permute-start = (bf16[384,384]{1,0:T(8,128)(2,1)S(1)}, bf16[384,384]{1,0:T(8,128)(2,1)S(1)}, u32[]{:S(2)}, u32[]{:S(2)}) collective-permute-start(bf16[384,384]{1,0:T(8,128)(2,1)S(1)} %pad_maximum_fusion.1), channel_id=1, source_target_pairs={{0,4},{4,0},{8,12},{12,8},{1,5},{5,1},{9,13},{13,9},{2,6},{6,2},{1... | collective-permute-start | bytes 884744 | tf_op jit(solution)/shard_map/ppermute | solution.py:24
  4.1 21.0 %collective-permute-start.11 = (bf16[384,384]{1,0:T(8,128)(2,1)S(1)}, bf16[384,384]{1,0:T(8,128)(2,1)S(1)}, u32[]{:S(2)}, u32[]{:S(2)}) collective-permute-start(bf16[384,384]{1,0:T(8,128)(2,1)S(1)} %pad_maximum_fusion.3), channel_id=1, source_target_pairs={{0,12},{4,8},{8,4},{12,0},{1,13},{5,9},{9,5},{13,1},{2,14},{6,10},... | collective-permute-start | bytes 884744 | tf_op jit(solution)/shard_map/ppermute | solution.py:24
  8.5 16.7 %collective-permute-start.2 = (bf16[384,384]{1,0:T(8,128)(2,1)S(1)}, bf16[384,384]{1,0:T(8,128)(2,1)S(1)}, u32[]{:S(2)}, u32[]{:S(2)}) collective-permute-start(bf16[384,384]{1,0:T(8,128)(2,1)S(1)} %pad_maximum_fusion.refs_0_), channel_id=1, source_target_pairs={{0,1},{1,0},{2,3},{3,2},{4,5},{5,4},{6,7},{7,6},{8,9},{9,8},{10,11... | collective-permute-start | bytes 884744 | tf_op jit(solution)/shard_map/ppermute | solution.py:24
  19.9 8.9 %collective-permute-start.8 = (bf16[320,384]{1,0:T(8,128)(2,1)S(1)}, bf16[320,384]{1,0:T(8,128)(2,1)S(1)}, u32[]{:S(2)}, u32[]{:S(2)}) collective-permute-start(bf16[320,384]{1,0:T(8,128)(2,1)S(1)} %slice.53), channel_id=1, source_target_pairs={{0,2},{1,3},{2,0},{3,1},{4,6},{5,7},{6,4},{7,5},{8,10},{9,11},{10,... | collective-permute-start | bytes 737288 | tf_op jit(solution)/shard_map/ppermute | solution.py:24
  21.5 12.6 %collective-permute-start.4 = (bf16[320,384]{1,0:T(8,128)(2,1)S(1)}, bf16[320,384]{1,0:T(8,128)(2,1)S(1)}, u32[]{:S(2)}, u32[]{:S(2)}) collective-permute-start(bf16[320,384]{1,0:T(8,128)(2,1)S(1)} %slice.50), channel_id=1, source_target_pairs={{0,2},{1,3},{2,0},{3,1},{4,6},{5,7},{6,4},{7,5},{8,10},{9,11},{10,... | collective-permute-start | bytes 737288 | tf_op jit(solution)/shard_map/ppermute | solution.py:24
  22.1 21.4 %collective-permute-start.9 = (bf16[384,384]{1,0:T(8,128)(2,1)S(1)}, bf16[384,384]{1,0:T(8,128)(2,1)S(1)}, u32[]{:S(2)}, u32[]{:S(2)}) collective-permute-start(bf16[384,384]{1,0:T(8,128)(2,1)S(1)} %collective-permute-done.7.refs_8_), channel_id=1, source_target_pairs={{0,1},{1,0},{2,3},{3,2},{4,5},{5,4},{6,7},{7,6},{8,9},{9,8},{10,11... | collective-permute-start | bytes 884744 | tf_op jit(solution)/shard_map/ppermute | solution.py:24
  25.1 18.9 %collective-permute-start.5 = (bf16[384,384]{1,0:T(8,128)(2,1)S(1)}, bf16[384,384]{1,0:T(8,128)(2,1)S(1)}, u32[]{:S(2)}, u32[]{:S(2)}) collective-permute-start(bf16[384,384]{1,0:T(8,128)(2,1)S(1)} %collective-permute-done.refs_4_), channel_id=1, source_target_pairs={{0,1},{1,0},{2,3},{3,2},{4,5},{5,4},{6,7},{7,6},{8,9},{9,8},{10,11... | collective-permute-start | bytes 884744 | tf_op jit(solution)/shard_map/ppermute | solution.py:24
  25.2 14.2 %collective-permute-start.1 = (bf16[320,384]{1,0:T(8,128)(2,1)S(1)}, bf16[320,384]{1,0:T(8,128)(2,1)S(1)}, u32[]{:S(2)}, u32[]{:S(2)}) collective-permute-start(bf16[320,384]{1,0:T(8,128)(2,1)S(1)} %pad_maximum_fusion.4), channel_id=1, source_target_pairs={{0,2},{1,3},{2,0},{3,1},{4,6},{5,7},{6,4},{7,5},{8,10},{9,11},{10,... | collective-permute-start | bytes 737288 | tf_op jit(solution)/shard_map/ppermute | solution.py:24
  28.9 14.7 %collective-permute-start.12 = (bf16[320,384]{1,0:T(8,128)(2,1)S(1)}, bf16[320,384]{1,0:T(8,128)(2,1)}, u32[]{:S(2)}, u32[]{:S(2)}) collective-permute-start(bf16[320,384]{1,0:T(8,128)(2,1)S(1)} %slice.56), channel_id=1, source_target_pairs={{0,2},{1,3},{2,0},{3,1},{4,6},{5,7},{6,4},{7,5},{8,10},{9,11},{10,... | collective-permute-start | bytes 737288 | tf_op jit(solution)/shard_map/ppermute | solution.py:24
  34.1 10.0 %collective-permute-start.13 = (bf16[384,384]{1,0:T(8,128)(2,1)S(1)}, bf16[384,384]{1,0:T(8,128)(2,1)S(1)}, u32[]{:S(2)}, u32[]{:S(2)}) collective-permute-start(bf16[384,384]{1,0:T(8,128)(2,1)S(1)} %collective-permute-done.11.refs_12_), channel_id=1, source_target_pairs={{0,1},{1,0},{2,3},{3,2},{4,5},{5,4},{6,7},{7,6},{8,9},{9,8},{10,11... | collective-permute-start | bytes 884744 | tf_op jit(solution)/shard_map/ppermute | solution.py:24
  39.4 4.7 %collective-permute-start.10 = (bf16[320,384]{1,0:T(8,128)(2,1)S(1)}, bf16[320,384]{1,0:T(8,128)(2,1)}, u32[]{:S(2)}, u32[]{:S(2)}) collective-permute-start(bf16[320,384]{1,0:T(8,128)(2,1)S(1)} %collective-permute-done.8.refs_9_), channel_id=1, source_target_pairs={{0,1},{1,0},{2,3},{3,2},{4,5},{5,4},{6,7},{7,6},{8,9},{9,8},{10,11... | collective-permute-start | bytes 737288 | tf_op jit(solution)/shard_map/ppermute | solution.py:24
  43.5 1.6 %collective-permute-start.6 = (bf16[320,384]{1,0:T(8,128)(2,1)S(1)}, bf16[320,384]{1,0:T(8,128)(2,1)}, u32[]{:S(2)}, u32[]{:S(2)}) collective-permute-start(bf16[320,384]{1,0:T(8,128)(2,1)S(1)} %collective-permute-done.4.refs_5_), channel_id=1, source_target_pairs={{0,1},{1,0},{2,3},{3,2},{4,5},{5,4},{6,7},{7,6},{8,9},{9,8},{10,11... | collective-permute-start | bytes 737288 | tf_op jit(solution)/shard_map/ppermute | solution.py:24
  43.5 2.0 %collective-permute-start.3 = (bf16[320,384]{1,0:T(8,128)(2,1)S(1)}, bf16[320,384]{1,0:T(8,128)(2,1)}, u32[]{:S(2)}, u32[]{:S(2)}) collective-permute-start(bf16[320,384]{1,0:T(8,128)(2,1)S(1)} %collective-permute-done.1.refs_1_), channel_id=1, source_target_pairs={{0,1},{1,0},{2,3},{3,2},{4,5},{5,4},{6,7},{7,6},{8,9},{9,8},{10,11... | collective-permute-start | bytes 737288 | tf_op jit(solution)/shard_map/ppermute | solution.py:24
  44.1 2.0 %collective-permute-start.14 = (bf16[320,384]{1,0:T(8,128)(2,1)}, bf16[320,384]{1,0:T(8,128)(2,1)}, u32[]{:S(2)}, u32[]{:S(2)}) collective-permute-start(bf16[320,384]{1,0:T(8,128)(2,1)} %collective-permute-done.12.refs_13_), channel_id=1, source_target_pairs={{0,1},{1,0},{2,3},{3,2},{4,5},{5,4},{6,7},{7,6},{8,9},{9,8},{10,11... | collective-permute-start | bytes 737288 | tf_op jit(solution)/shard_map/ppermute | solution.py:24
  46.1 23.6 %slice-start = ((s8[9437184]{0:T(1024)(128)(4,1)}), s8[4194304]{0:T(1024)(128)(4,1)S(1)}, s32[]{:S(2)}) async-start(s8[9437184]{0:T(1024)(128)(4,1)} %bitcast.7), calls=%async_computation | async-start | bytes 8388608
  49.9 19.8 %collective-permute-start.16 = (bf16[4,32,384]{2,1,0:T(8,128)(2,1)S(1)}, bf16[4,32,384]{2,1,0:T(8,128)(2,1)S(1)}, u32[]{:S(2)}, u32[]{:S(2)}) collective-permute-start(bf16[4,32,384]{2,1,0:T(8,128)(2,1)S(1)} %get-tuple-element.14), channel_id=1, source_target_pairs={{0,4},{4,0},{8,12},{12,8},{1,5},{5,1},{9,13},{13,9},{2,6},{6,2},{1... | collective-permute-start | bytes 294920 | tf_op jit(solution)/shard_map/ppermute | solution.py:24
  55.8 13.9 %collective-permute-start.15 = (bf16[4,32,384]{2,1,0:T(8,128)(2,1)S(1)}, bf16[4,32,384]{2,1,0:T(8,128)(2,1)S(1)}, u32[]{:S(2)}, u32[]{:S(2)}) collective-permute-start(bf16[4,32,384]{2,1,0:T(8,128)(2,1)S(1)} %get-tuple-element.13), channel_id=1, source_target_pairs={{0,8},{4,12},{8,0},{12,4},{1,9},{5,13},{9,1},{13,5},{2,10},{6,14},... | collective-permute-start | bytes 294920 | tf_op jit(solution)/shard_map/ppermute | solution.py:24
  56.2 7.1 %collective-permute-start.17 = (bf16[4,32,384]{2,1,0:T(8,128)(2,1)S(1)}, bf16[4,32,384]{2,1,0:T(8,128)(2,1)S(1)}, u32[]{:S(2)}, u32[]{:S(2)}) collective-permute-start(bf16[4,32,384]{2,1,0:T(8,128)(2,1)S(1)} %get-tuple-element.16), channel_id=1, source_target_pairs={{0,12},{4,8},{8,4},{12,0},{1,13},{5,9},{9,5},{13,1},{2,14},{6,10},... | collective-permute-start | bytes 294920 | tf_op jit(solution)/shard_map/ppermute | solution.py:24
  63.3 3.7 %copy-start.1 = (bf16[1536,3072]{1,0:T(8,128)(2,1)S(1)}, bf16[1536,3072]{1,0:T(8,128)(2,1)}, u32[]{:S(2)}) copy-start(bf16[1536,3072]{1,0:T(8,128)(2,1)} %refs_3_.3) | copy-start | bytes 28311556
  67.0 2.7 %slice-start.1 = ((s8[9437184]{0:T(1024)(128)(4,1)}), s8[4194304]{0:T(1024)(128)(4,1)S(1)}, s32[]{:S(2)}) async-start(s8[9437184]{0:T(1024)(128)(4,1)} %bitcast.7), calls=%async_computation.1 | async-start | bytes 8388608
  67.0 2.7 %slice-start.2 = ((s8[9437184]{0:T(1024)(128)(4,1)}), s8[1048576]{0:T(1024)(128)(4,1)S(1)}, s32[]{:S(2)}) async-start(s8[9437184]{0:T(1024)(128)(4,1)} %bitcast.7), calls=%async_computation.2 | async-start | bytes 2097152
  67.0 2.8 %copy-start.3 = (bf16[3072,64]{0,1:T(8,128)(2,1)S(1)}, bf16[3072,64]{0,1:T(8,128)(2,1)}, u32[]{:S(2)}) copy-start(bf16[3072,64]{0,1:T(8,128)(2,1)} %param.15) | copy-start | bytes 1179652
  67.0 2.8 %copy-start.4 = (f32[3072]{0:T(1024)S(1)}, f32[3072]{0:T(1024)}, u32[]{:S(2)}) copy-start(f32[3072]{0:T(1024)} %param.14) | copy-start | bytes 36868
  67.0 2.8 %copy-start.5 = (f32[3072]{0:T(1024)S(1)}, f32[3072]{0:T(1024)}, u32[]{:S(2)}) copy-start(f32[3072]{0:T(1024)} %param.13) | copy-start | bytes 36868
  69.8 17.1 %copy-start.2 = (bf16[432,512]{1,0:T(8,128)(2,1)S(1)}, bf16[432,512]{1,0:T(8,128)(2,1)}, u32[]{:S(2)}) copy-start(bf16[432,512]{1,0:T(8,128)(2,1)} %w_ref.1) | copy-start | bytes 1327108
  69.8 17.1 %copy-start.6 = (f32[512]{0:T(512)S(1)}, f32[512]{0:T(512)}, u32[]{:S(2)}) copy-start(f32[512]{0:T(512)} %param.17) | copy-start | bytes 6148
  73.6 9.1 %collective-permute-start.19 = (bf16[128,32]{1,0:T(8,128)(2,1)S(1)}, bf16[128,32]{1,0:T(8,128)(2,1)S(1)}, u32[]{:S(2)}, u32[]{:S(2)}) collective-permute-start(bf16[128,32]{1,0:T(8,128)(2,1)S(1)} %get-tuple-element.17.even_ref), channel_id=1, source_target_pairs={{1,0},{2,1},{3,2},{4,3},{5,4},{6,5},{7,6},{8,7},{9,8},{10,9},{11,1... | collective-permute-start | bytes 24584 | tf_op jit(solution)/shard_map/ppermute | solution.py:405
  80.7 6.1 %collective-permute-start.18 = (bf16[128,32]{1,0:T(8,128)(2,1)S(1)}, bf16[128,32]{1,0:T(8,128)(2,1)S(1)}, u32[]{:S(2)}, u32[]{:S(2)}) collective-permute-start(bf16[128,32]{1,0:T(8,128)(2,1)S(1)} %get-tuple-element.18.odd_ref), channel_id=1, source_target_pairs={{0,1},{1,2},{2,3},{3,4},{4,5},{5,6},{6,7},{7,8},{8,9},{9,10},{10,1... | collective-permute-start | bytes 24584 | tf_op jit(solution)/shard_map/ppermute | solution.py:404

commit v9 on v4

--- a/solution.py
+++ b/solution.py
@@ -22,33 +22,38 @@
     return lax.ppermute(source, axis, [(i, i ^ distance) for i in range(count)])
 
 
-def bundle_kernel(where_ref, q_ref, k_ref, v_ref, *out_refs, groups, planes, distances):
+def bundle_kernel(where_ref, q_ref, k_ref, v_ref, *out_refs, groups, planes, parts):
     tokens, width = q_ref.shape
     group_width = width // groups
     rows_dev = tokens // (groups * planes)
     to = lax.broadcasted_iota(jnp.int32, (tokens, tokens), 0)
     at = lax.broadcasted_iota(jnp.int32, (tokens, tokens), 1)
     j, t, row = to // (groups * rows_dev), (to // rows_dev) % groups, to % rows_dev
-    for r, out_ref in zip(distances, out_refs):
+    for (r, with_kv, with_q), out_ref in zip(parts, out_refs):
         group = where_ref[0] ^ r
         lanes = pl.ds(pl.multiple_of(group * group_width, 128), group_width)
-        place = row * (groups * planes) + (t ^ group) * planes + (j ^ where_ref[1])
-        order = (at == place).astype(jnp.bfloat16)
-        out_ref[:tokens] = k_ref[:, lanes]
-        out_ref[tokens : 2 * tokens] = v_ref[:, lanes]
-        mixed = jnp.dot(order, q_ref[:, lanes], preferred_element_type=jnp.float32)
-        out_ref[2 * tokens :] = mixed.astype(jnp.bfloat16)
-
-
-def bundles(where, queries, keys, values, groups, planes, distances):
+        if with_kv:
+            out_ref[:tokens] = k_ref[:, lanes]
+            out_ref[tokens : 2 * tokens] = v_ref[:, lanes]
+        if with_q:
+            place = row * (groups * planes) + (t ^ group) * planes + (j ^ where_ref[1])
+            order = (at == place).astype(jnp.bfloat16)
+            mixed = jnp.dot(order, q_ref[:, lanes], preferred_element_type=jnp.float32)
+            first = 2 * tokens if with_kv else 0
+            out_ref[first : first + tokens] = mixed.astype(jnp.bfloat16)
+
+
+def bundles(where, queries, keys, values, groups, planes, parts):
     tokens, width = queries.shape
     vmem = pl.BlockSpec(memory_space=pltpu.VMEM)
-    result = jax.ShapeDtypeStruct((3 * tokens, width // groups), jnp.bfloat16)
     return pl.pallas_call(
-        functools.partial(bundle_kernel, groups=groups, planes=planes, distances=distances),
+        functools.partial(bundle_kernel, groups=groups, planes=planes, parts=parts),
         in_specs=[pl.BlockSpec(memory_space=pltpu.SMEM)] + [vmem] * 3,
-        out_specs=[vmem] * len(distances),
-        out_shape=[result] * len(distances),
+        out_specs=[vmem] * len(parts),
+        out_shape=[
+            jax.ShapeDtypeStruct(((2 * kv + q) * tokens, width // groups), jnp.bfloat16)
+            for _, kv, q in parts
+        ],
         compiler_params=pltpu.CompilerParams(vmem_limit_bytes=VMEM_LIMIT),
     )(where, queries, keys, values)
 
@@ -320,6 +325,10 @@
     )(where, even, odd, left, right, conv_weight, conv_bias[None])
 
 
+def after(value, *others):
+    return lax.optimization_barrier((value,) + others)[0]
+
+
 def shards(queries, keys, values, w_out, shift_mod, scale_mod, w_final, conv_weight, conv_bias):
     groups = lax.axis_size("heads")
     planes = lax.axis_size("plane")
@@ -332,20 +341,38 @@
         [heads_at, plane_at, heads_at * planes + plane_at, jnp.int32(devices)]
     ).astype(jnp.int32)
 
-    made = bundles(where, queries, keys, values, groups, planes, range(groups))
-    got = {r: swap(made[r], "heads", r) if r else made[r] for r in range(groups)}
-
+    parts = ((2, 1, 0), (3, 1, 0), (1, 1, 1), (0, 1, 1), (2, 0, 1), (3, 0, 1))
+    made = bundles(where, queries, keys, values, groups, planes, parts)
+    w_out = after(w_out, *made)
     both_parts, share = 2 * tokens, tokens // planes
-    held = {r: [got[r]] for r in range(groups)}
-    for r in (0, 1, 2, 3):
+
+    def across(bundle, *waits):
+        crossed = []
         for d in range(2, planes, 2):
-            asked = got[r][both_parts + d * share : both_parts + (d + 2) * share]
-            held[r].append(swap(jnp.concatenate([got[r][:both_parts], asked], axis=0), "plane", d))
+            sent = bundle
+            if bundle.shape[0] > both_parts:
+                queried = bundle[both_parts + d * share : both_parts + (d + 2) * share]
+                sent = jnp.concatenate([bundle[:both_parts], queried], axis=0)
+            crossed.append(swap(after(sent, *waits), "plane", d))
+        return crossed
+
+    got = {0: made[3], 2: swap(made[0], "heads", 2), 1: swap(made[2], "heads", 1)}
+    held = {0: across(got[0])}
+    got[3] = swap(after(made[1], held[0][-1]), "heads", 3)
+    for r in (1, 2, 3):
+        held[r] = across(got[r])
+    late_q = [swap(after(made[2 + r], held[1][-1], held[2][-1]), "heads", r) for r in (2, 3)]
+    held = {r: [got[r]] + held[r] for r in range(groups)}
 
     keys_values, asked = [], {}
     for distances in ((0, 1), (2,), (3,)):
         passed = [h[:both_parts] for r in distances for h in held[r]]
-        passed += [h[both_parts + share : both_parts + 2 * share] for r in distances for h in held[r]]
+        passed += [
+            h[both_parts + share : both_parts + 2 * share]
+            for r in distances
+            for h in held[r]
+            if h.shape[0] > both_parts
+        ]
         mine = jnp.concatenate(passed, axis=0)
         other = swap(mine, "plane", 1)
         keys_values += [mine, other]
@@ -353,15 +380,20 @@
         first = both_parts * half * len(distances)
         for n, r in enumerate(distances):
             start = first + n * half * share
-            asked[r] = jnp.concatenate(
-                [h[both_parts : both_parts + share] for h in held[r]]
-                + [other[start : start + half * share]],
-                axis=0,
-            )
-    asked = [asked[r] for r in range(groups)]
-
-    first, second = (1, 3), (2, 0)
-    near, far = (0, 1), (3, 2)
+            if start < mine.shape[0]:
+                asked[r] = [h[both_parts : both_parts + share] for h in held[r]]
+                asked[r].append(other[start : start + half * share])
+    arrival = list(range(0, planes, 2)) + list(range(1, planes, 2))
+    by_distance = []
+    for d in arrival:
+        pair = jnp.concatenate([q[d * share : (d + 1) * share] for q in late_q], axis=0)
+        by_distance.append(swap(pair, "plane", d) if d else pair)
+    for n, r in enumerate((2, 3)):
+        asked[r] = [pair[n * share : (n + 1) * share] for pair in by_distance]
+    asked = [jnp.concatenate(asked[r], axis=0) for r in range(groups)]
+
+    first, second = (3, 2), (1, 0)
+    near, far = (0, 3), (2, 1)
     results = {}
     for targets in (first, second):
         for t, o in zip(targets, attend(asked, keys_values, targets, planes)):

time: 74.1 us -> 76.5 us (1.032)
  starting transfers between devices: 28.9 us -> 37.5 us
  waiting for transfers between devices: 25.8 us -> 19.8 us
    ppermute x13 -> x18, starting transfers between devices: 24.4 us -> 29.4 us  [swap(): return lax.ppermute(source, axis, [(i, i ^ distance) for i in range(count)])]
    ppermute x13 -> x18, waiting for transfers between devices: 22.5 us -> 18.8 us  [swap(): return lax.ppermute(source, axis, [(i, i ^ distance) for i in range(count)])]
    ppermute x1, waiting for transfers between devices: 3.29 us -> 0.01 us  [shards(): right = lax.ppermute(even, both, [(i + 1, i) for i in range(devices - 1)])]
    ppermute x1, starting transfers between devices: 1.92 us -> 4.09 us  [shards(): right = lax.ppermute(even, both, [(i + 1, i) for i in range(devices - 1)])]
    ppermute x1, starting transfers between devices: 2.54 us -> 4.02 us  [shards(): left = lax.ppermute(odd, both, [(i, i + 1) for i in range(devices - 1)])]
    ppermute x1, waiting for transfers between devices: 0.01 us -> 0.99 us  [shards(): left = lax.ppermute(odd, both, [(i, i + 1) for i in range(devices - 1)])]
    unnamed x20 -> x22, local copies, waits for them, and re-layouts: 3.84 us -> 3.87 us
  transfers between devices with their start and end apart: 15 -> 20, of which waited for: 6 -> 8; matrix products, arithmetic and copies ran while one was open for 1% -> 1% of each run, Pallas kernels for 7% -> 7%
where the time goes in v9:
time: 76.5 us; the launch traced here: 76.4 us
  starting transfers between devices  37.5 us (49%)
  waiting for transfers between devices  19.8 us (26%)
  Pallas kernels  14.4 us (19%)
  local copies, waits for them, and re-layouts  4.14 us (5%)
    ppermute x18, starting transfers between devices, swap(): return lax.ppermute(source, axis, [(i, i ^ distance) for i in range(count)])  29.4 us
    ppermute x18, waiting for transfers between devices, swap(): return lax.ppermute(source, axis, [(i, i ^ distance) for i in range(count)])  18.8 us
    pallas_call x2, Pallas kernels, attend(): pl.pallas_call(functools.partial(attend_kernel, sources=sources, planes=p...  4.53 us
    ppermute x1, starting transfers between devices, shards(): right = lax.ppermute(even, both, [(i + 1, i) for i in range(devices - 1)])  4.09 us
    ppermute x1, starting transfers between devices, shards(): left = lax.ppermute(odd, both, [(i, i + 1) for i in range(devices - 1)])  4.02 us
    pallas_call x1, Pallas kernels, final_layer(): pl.pallas_call(functools.partial(final_kernel, targets=targets, planes=pl...  3.99 us
    unnamed x22, local copies, waits for them, and re-layouts  3.87 us
    pallas_call x1, Pallas kernels, project(): pl.pallas_call(functools.partial(project_kernel, targets=targets), grid_s...  2.89 us
  transfers between devices with their start and end apart: 20, of which 8 were waited for; matrix products, arithmetic and copies ran while one was open for 1% of the time, Pallas kernels for 7%

profile of v9, /device:TPU:1, one launch (start us, length us, event | category | flops | bytes accessed | tf_op | source)
XLA Modules:
  0.0 76.4 jit_solution(17758749557769510158)
XLA Ops:
  0.0 0.0 copy-start
  0.0 0.1 pad_add_fusion.where_ref
  0.1 0.0 copy-start.3
  0.1 1.1 %copy-done.3 = bf16[128,1536]{1,0:T(8,128)(2,1)S(1)} copy-done((bf16[128,1536]{1,0:T(8,128)(2,1)S(1)}, bf16[128,1536]{1,0:T(8,128)(2,1)}, u32[]{:S(2)}) %copy-start.3) | copy-done | bytes 393240
  1.2 0.0 copy-start.4
  1.2 1.2 %copy-done.4 = bf16[128,1536]{1,0:T(8,128)(2,1)S(1)} copy-done((bf16[128,1536]{1,0:T(8,128)(2,1)S(1)}, bf16[128,1536]{1,0:T(8,128)(2,1)}, u32[]{:S(2)}) %copy-start.4) | copy-done | bytes 393240
  2.5 0.0 copy-start.5
  2.5 1.4 %copy-done.5 = bf16[128,1536]{1,0:T(8,128)(2,1)S(1)} copy-done((bf16[128,1536]{1,0:T(8,128)(2,1)S(1)}, bf16[128,1536]{1,0:T(8,128)(2,1)}, u32[]{:S(2)}) %copy-start.5) | copy-done | bytes 393240
  3.8 0.9 %shard_map.91 = (bf16[256,384]{1,0:T(8,128)(2,1)S(1)}, bf16[256,384]{1,0:T(8,128)(2,1)S(1)}, bf16[384,384]{1,0:T(8,128)(2,1)S(1)}, bf16[384,384]{1,0:T(8,128)(2,...) custom-call(s32[4]{0:T(128)S(1)} %pad_add_fusion.where_ref, bf16[128,1536]{1,0:T(8,128)(2,1)S(1)} %copy-done.3, ...), custom_call_target="tpu_custom_call" | custom-call | tf_op jit(solution)/shard_map/pallas_call | solution.py:49
  4.8 2.1 %collective-permute-start = (bf16[320,384]{1,0:T(8,128)(2,1)S(1)}, bf16[320,384]{1,0:T(8,128)(2,1)S(1)}, u32[]{:S(2)}, u32[]{:S(2)}) collective-permute-start(bf16[320,384]{1,0:T(8,128)(2,1)S(1)} %pad_maximum_fusion), channel_id=1, source_target_pairs={{0,2},{1,3},{2,0},{3,1},{4,6},{5,7},{6,4},{7,5},{8,10},{9,11},{10,... | collective-permute-start | bytes 737288 | tf_op jit(solution)/shard_map/ppermute | solution.py:22
  6.9 2.3 %collective-permute-start.4 = (bf16[256,384]{1,0:T(8,128)(2,1)S(1)}, bf16[256,384]{1,0:T(8,128)(2,1)S(1)}, u32[]{:S(2)}, u32[]{:S(2)}) collective-permute-start(bf16[256,384]{1,0:T(8,128)(2,1)S(1)} %get-tuple-element.24), channel_id=1, source_target_pairs={{0,8},{4,12},{8,0},{12,4},{1,9},{5,13},{9,1},{13,5},{2,10},{6,14},... | collective-permute-start | bytes 589832 | tf_op jit(solution)/shard_map/ppermute | solution.py:22
  9.2 1.3 %collective-permute-start.1 = (bf16[384,384]{1,0:T(8,128)(2,1)S(1)}, bf16[384,384]{1,0:T(8,128)(2,1)S(1)}, u32[]{:S(2)}, u32[]{:S(2)}) collective-permute-start(bf16[384,384]{1,0:T(8,128)(2,1)S(1)} %get-tuple-element.22), channel_id=1, source_target_pairs={{0,4},{4,0},{8,12},{12,8},{1,5},{5,1},{9,13},{13,9},{2,6},{6,2},{1... | collective-permute-start | bytes 884744 | tf_op jit(solution)/shard_map/ppermute | solution.py:22
  10.5 7.3 %collective-permute-done.4 = bf16[256,384]{1,0:T(8,128)(2,1)S(1)} collective-permute-done((bf16[256,384]{1,0:T(8,128)(2,1)S(1)}, bf16[256,384]{1,0:T(8,128)(2,1)S(1)}, u32[]{:S(2)}, u32[]{:S(2)}) %collective-permute-start.4) | collective-permute-done | bytes 196640 | tf_op jit(solution)/shard_map/ppermute | solution.py:22
  17.8 0.2 collective-permute-start.5
  18.0 0.0 collective-permute-done
  18.0 4.3 %collective-permute-start.12 = (bf16[256,384]{1,0:T(8,128)(2,1)S(1)}, bf16[256,384]{1,0:T(8,128)(2,1)S(1)}, u32[]{:S(2)}, u32[]{:S(2)}) collective-permute-start(bf16[256,384]{1,0:T(8,128)(2,1)S(1)} %get-tuple-element.29), channel_id=1, source_target_pairs={{0,12},{4,8},{8,4},{12,0},{1,13},{5,9},{9,5},{13,1},{2,14},{6,10},... | collective-permute-start | bytes 589832 | tf_op jit(solution)/shard_map/ppermute | solution.py:22
  22.4 0.0 collective-permute-done.1
  22.4 0.1 fusion.3
  22.5 1.3 %collective-permute-start.2 = (bf16[320,384]{1,0:T(8,128)(2,1)S(1)}, bf16[320,384]{1,0:T(8,128)(2,1)S(1)}, u32[]{:S(2)}, u32[]{:S(2)}) collective-permute-start(bf16[320,384]{1,0:T(8,128)(2,1)S(1)} %pad_maximum_fusion.1), channel_id=1, source_target_pairs={{0,2},{1,3},{2,0},{3,1},{4,6},{5,7},{6,4},{7,5},{8,10},{9,11},{10,... | collective-permute-start | bytes 737288 | tf_op jit(solution)/shard_map/ppermute | solution.py:22
  23.8 0.0 collective-permute-done.5
  23.8 1.5 %collective-permute-start.11 = (bf16[512,384]{1,0:T(8,128)(2,1)S(1)}, bf16[512,384]{1,0:T(8,128)(2,1)S(1)}, u32[]{:S(2)}, u32[]{:S(2)}) collective-permute-start(bf16[512,384]{1,0:T(8,128)(2,1)S(1)} %constant_dynamic-update-slice_fusion.6.refs_6_), channel_id=1, source_target_pairs={{0,1},{1,0},{2,3},{3,2},{4,5},{5,4},{6,7},{7,6},{8,9},{9,8},{10,11... | collective-permute-start | bytes 1179656 | tf_op jit(solution)/shard_map/ppermute | solution.py:22
  25.3 1.3 %collective-permute-done.12 = bf16[256,384]{1,0:T(8,128)(2,1)S(1)} collective-permute-done((bf16[256,384]{1,0:T(8,128)(2,1)S(1)}, bf16[256,384]{1,0:T(8,128)(2,1)S(1)}, u32[]{:S(2)}, u32[]{:S(2)}) %collective-permute-start.12) | collective-permute-done | bytes 196640 | tf_op jit(solution)/shard_map/ppermute | solution.py:22
  26.6 1.1 %collective-permute-start.13 = (bf16[256,384]{1,0:T(8,128)(2,1)S(1)}, bf16[256,384]{1,0:T(8,128)(2,1)S(1)}, u32[]{:S(2)}, u32[]{:S(2)}) collective-permute-start(bf16[256,384]{1,0:T(8,128)(2,1)S(1)} %collective-permute-done.12), channel_id=1, source_target_pairs={{0,2},{1,3},{2,0},{3,1},{4,6},{5,7},{6,4},{7,5},{8,10},{9,11},{10,... | collective-permute-start | bytes 589832 | tf_op jit(solution)/shard_map/ppermute | solution.py:22
  27.7 1.2 %collective-permute-done.2 = bf16[320,384]{1,0:T(8,128)(2,1)S(1)} collective-permute-done((bf16[320,384]{1,0:T(8,128)(2,1)S(1)}, bf16[320,384]{1,0:T(8,128)(2,1)S(1)}, u32[]{:S(2)}, u32[]{:S(2)}) %collective-permute-start.2) | collective-permute-done | bytes 245792 | tf_op jit(solution)/shard_map/ppermute | solution.py:22
  28.9 4.4 %collective-permute-start.7 = (bf16[128,384]{1,0:T(8,128)(2,1)S(1)}, bf16[128,384]{1,0:T(8,128)(2,1)S(1)}, u32[]{:S(2)}, u32[]{:S(2)}) collective-permute-start(bf16[128,384]{1,0:T(8,128)(2,1)S(1)} %get-tuple-element.27), channel_id=1, source_target_pairs={{0,12},{4,8},{8,4},{12,0},{1,13},{5,9},{9,5},{13,1},{2,14},{6,10},... | collective-permute-start | bytes 294920 | tf_op jit(solution)/shard_map/ppermute | solution.py:22
  33.4 0.0 collective-permute-start.6
  33.4 2.8 %collective-permute-start.3 = (bf16[1152,384]{1,0:T(8,128)(2,1)S(1)}, bf16[1152,384]{1,0:T(8,128)(2,1)S(1)}, u32[]{:S(2)}, u32[]{:S(2)}) collective-permute-start(bf16[1152,384]{1,0:T(8,128)(2,1)S(1)} %get-tuple-element.48.refs_4_), channel_id=1, source_target_pairs={{0,1},{1,0},{2,3},{3,2},{4,5},{5,4},{6,7},{7,6},{8,9},{9,8},{10,11... | collective-permute-start | bytes 2654216 | tf_op jit(solution)/shard_map/ppermute | solution.py:22
  36.2 0.0 collective-permute-done.13
  36.2 0.1 collective-permute-start.14
  36.3 0.0 collective-permute-done.7
  36.3 4.9 %collective-permute-done.6 = bf16[128,384]{1,0:T(8,128)(2,1)S(1)} collective-permute-done((bf16[128,384]{1,0:T(8,128)(2,1)S(1)}, bf16[128,384]{1,0:T(8,128)(2,1)S(1)}, u32[]{:S(2)}, u32[]{:S(2)}) %collective-permute-start.6) | collective-permute-done | bytes 98336 | tf_op jit(solution)/shard_map/ppermute | solution.py:22
  41.2 0.3 collective-permute-start.8
  41.6 1.5 %collective-permute-start.9 = (bf16[64,384]{1,0:T(8,128)(2,1)S(1)}, bf16[64,384]{1,0:T(8,128)(2,1)S(1)}, u32[]{:S(2)}, u32[]{:S(2)}) collective-permute-start(bf16[64,384]{1,0:T(8,128)(2,1)S(1)} %pad_maximum_fusion.7), channel_id=1, source_target_pairs={{0,1},{1,0},{2,3},{3,2},{4,5},{5,4},{6,7},{7,6},{8,9},{9,8},{10,11... | collective-permute-start | bytes 147464 | tf_op jit(solution)/shard_map/ppermute | solution.py:22
  43.0 1.2 %collective-permute-done.8 = bf16[64,384]{1,0:T(8,128)(2,1)S(1)} collective-permute-done((bf16[64,384]{1,0:T(8,128)(2,1)S(1)}, bf16[64,384]{1,0:T(8,128)(2,1)S(1)}, u32[]{:S(2)}, u32[]{:S(2)}) %collective-permute-start.8) | collective-permute-done | bytes 49184 | tf_op jit(solution)/shard_map/ppermute | solution.py:22
  44.2 2.5 %collective-permute-start.10 = (bf16[64,384]{1,0:T(8,128)(2,1)S(1)}, bf16[64,384]{1,0:T(8,128)(2,1)S(1)}, u32[]{:S(2)}, u32[]{:S(2)}) collective-permute-start(bf16[64,384]{1,0:T(8,128)(2,1)S(1)} %pad_maximum_fusion.8), channel_id=1, source_target_pairs={{0,3},{1,2},{2,1},{3,0},{4,7},{5,6},{6,5},{7,4},{8,11},{9,10},{10,... | collective-permute-start | bytes 147464 | tf_op jit(solution)/shard_map/ppermute | solution.py:22
  46.7 0.0 collective-permute-done.9
  46.7 1.7 %collective-permute-done.10 = bf16[64,384]{1,0:T(8,128)(2,1)S(1)} collective-permute-done((bf16[64,384]{1,0:T(8,128)(2,1)S(1)}, bf16[64,384]{1,0:T(8,128)(2,1)S(1)}, u32[]{:S(2)}, u32[]{:S(2)}) %collective-permute-start.10) | collective-permute-done | bytes 49184 | tf_op jit(solution)/shard_map/ppermute | solution.py:22
  48.5 0.0 collective-permute-done.3.refs_5_
  48.6 0.0 copy-start.2
  48.6 0.0 copy-start.6
  48.6 0.0 copy-start.7
  48.6 0.0 collective-permute-done.11.refs_7_
  48.6 0.0 collective-permute-done.14.refs_9_
  48.6 2.3 %shard_map.92 = (bf16[4,32,384]{2,1,0:T(8,128)(2,1)S(1)}, bf16[4,32,384]{2,1,0:T(8,128)(2,1)S(1)}) custom-call(bf16[128,384]{1,0:T(8,128)(2,1)S(1)} %get-tuple-element.65.refs_0_, bf16[128,384]{1,0:T(8,128)(2,1)S(1)} %get-tuple-element.66.refs_1_, bf16[128,384]{1,0:T(8,128)(2,1)S(1)} %get-tuple-element.67.refs_2_, ...), custom_call_target="tpu_custom_call" | custom-call | tf_op jit(solution)/shard_map/pallas_call | solution.py:136
  50.9 1.9 %collective-permute-start.17 = (bf16[4,32,384]{2,1,0:T(8,128)(2,1)S(1)}, bf16[4,32,384]{2,1,0:T(8,128)(2,1)S(1)}, u32[]{:S(2)}, u32[]{:S(2)}) collective-permute-start(bf16[4,32,384]{2,1,0:T(8,128)(2,1)S(1)} %get-tuple-element.33), channel_id=1, source_target_pairs={{0,12},{4,8},{8,4},{12,0},{1,13},{5,9},{9,5},{13,1},{2,14},{6,10},... | collective-permute-start | bytes 294920 | tf_op jit(solution)/shard_map/ppermute | solution.py:22
  52.9 2.3 %shard_map.93 = (bf16[4,32,384]{2,1,0:T(8,128)(2,1)S(1)}, bf16[4,32,384]{2,1,0:T(8,128)(2,1)S(1)}) custom-call(bf16[128,384]{1,0:T(8,128)(2,1)S(1)} %get-tuple-element.65.refs_0_, bf16[128,384]{1,0:T(8,128)(2,1)S(1)} %get-tuple-element.66.refs_1_, bf16[128,384]{1,0:T(8,128)(2,1)S(1)} %get-tuple-element.67.refs_2_, ...), custom_call_target="tpu_custom_call" | custom-call | tf_op jit(solution)/shard_map/pallas_call | solution.py:136
  55.1 0.1 collective-permute-start.16
  55.2 1.7 %collective-permute-start.15 = (bf16[4,32,384]{2,1,0:T(8,128)(2,1)S(1)}, bf16[4,32,384]{2,1,0:T(8,128)(2,1)S(1)}, u32[]{:S(2)}, u32[]{:S(2)}) collective-permute-start(bf16[4,32,384]{2,1,0:T(8,128)(2,1)S(1)} %get-tuple-element.30), channel_id=1, source_target_pairs={{0,8},{4,12},{8,0},{12,4},{1,9},{5,13},{9,1},{13,5},{2,10},{6,14},... | collective-permute-start | bytes 294920 | tf_op jit(solution)/shard_map/ppermute | solution.py:22
  56.9 0.0 collective-permute-done.17.refs_1_
  56.9 0.0 copy-done
  56.9 2.9 %shard_map.94.refs_2_ = f32[6,128,512]{2,1,0:T(8,128)S(1)} custom-call(s32[4]{0:T(128)S(1)} %pad_add_fusion.where_ref, bf16[4,32,384]{2,1,0:T(8,128)(2,1)S(1)} %get-tuple-element.32.refs_0_, bf16[4,32,384]{2,1,0:T(8,128)(2,1)S(1)} %collective-permute-done.17.refs_1_, bf16[1536,3072]{1,0:T(8,128)(2,1)S(1)} %copy-done), custom_call_target="tpu_custom_call" | custom-call | tf_op jit(solution)/shard_map/pallas_call | solution.py:171
  59.8 1.3 %collective-permute-done.16.refs_1_ = bf16[4,32,384]{2,1,0:T(8,128)(2,1)S(1)} collective-permute-done((bf16[4,32,384]{2,1,0:T(8,128)(2,1)S(1)}, bf16[4,32,384]{2,1,0:T(8,128)(2,1)S(1)}, u32[]{:S(2)}, u32[]{:S(2)}) %collective-permute-start.16) | collective-permute-done | bytes 98336 | tf_op jit(solution)/shard_map/ppermute | solution.py:22
  61.1 0.0 collective-permute-done.15.refs_0_
  61.1 0.0 copy-done.2
  61.1 0.0 copy-done.6
  61.1 0.0 copy-done.7
  61.1 4.0 %shard_map.95 = (bf16[128,32]{1,0:T(8,128)(2,1)S(1)}, bf16[128,32]{1,0:T(8,128)(2,1)S(1)}) custom-call(s32[4]{0:T(128)S(1)} %pad_add_fusion.where_ref, bf16[4,32,384]{2,1,0:T(8,128)(2,1)S(1)} %collective-permute-done.15.refs_0_, bf16[4,32,384]{2,1,0:T(8,128)(2,1)S(1)} %collective-permute-done.16.refs_1_, f32[6,128,512]{2,1,0:T(8,128)S(1)} %shard_map.94.refs_2_, ...), custom_call_target="tpu_custom_call" | custom-call | tf_op jit(solution)/shard_map/pallas_call | solution.py:256
  65.1 4.1 %collective-permute-start.19 = (bf16[128,32]{1,0:T(8,128)(2,1)S(1)}, bf16[128,32]{1,0:T(8,128)(2,1)S(1)}, u32[]{:S(2)}, u32[]{:S(2)}) collective-permute-start(bf16[128,32]{1,0:T(8,128)(2,1)S(1)} %get-tuple-element.35.even_ref), channel_id=1, source_target_pairs={{1,0},{2,1},{3,2},{4,3},{5,4},{6,5},{7,6},{8,7},{9,8},{10,9},{11,1... | collective-permute-start | bytes 24584 | tf_op jit(solution)/shard_map/ppermute | solution.py:408
  69.2 4.0 %collective-permute-start.18 = (bf16[128,32]{1,0:T(8,128)(2,1)S(1)}, bf16[128,32]{1,0:T(8,128)(2,1)S(1)}, u32[]{:S(2)}, u32[]{:S(2)}) collective-permute-start(bf16[128,32]{1,0:T(8,128)(2,1)S(1)} %get-tuple-element.36.odd_ref), channel_id=1, source_target_pairs={{0,1},{1,2},{2,3},{3,4},{4,5},{5,6},{6,7},{7,8},{8,9},{9,10},{10,1... | collective-permute-start | bytes 24584 | tf_op jit(solution)/shard_map/ppermute | solution.py:407
  73.2 0.0 collective-permute-done.19.right_ref
  73.2 1.0 %collective-permute-done.18.left_ref = bf16[128,32]{1,0:T(8,128)(2,1)S(1)} collective-permute-done((bf16[128,32]{1,0:T(8,128)(2,1)S(1)}, bf16[128,32]{1,0:T(8,128)(2,1)S(1)}, u32[]{:S(2)}, u32[]{:S(2)}) %collective-permute-start.18) | collective-permute-done | bytes 8224 | tf_op jit(solution)/shard_map/ppermute | solution.py:407
  74.2 0.0 copy-done.1
  74.2 0.0 copy-done.8
  74.2 2.2 %shard_map.96 = bf16[4,2,64,512]{3,2,1,0:T(8,128)(2,1)} custom-call(s32[4]{0:T(128)S(1)} %pad_add_fusion.where_ref, bf16[128,32]{1,0:T(8,128)(2,1)S(1)} %get-tuple-element.35.even_ref, bf16[128,32]{1,0:T(8,128)(2,1)S(1)} %get-tuple-element.36.odd_ref, bf16[128,32]{1,0:T(8,128)(2,1)S(1)} %collective-permute-done.18.left_ref, ...), custom_call_target="tpu_custom_call" | custom-call | tf_op jit(solution)/shard_map/pallas_call | solution.py:318
  (28 shorter events, 0.4 us)
Async XLA Ops:
  0.0 56.9 %copy-start = (bf16[1536,3072]{1,0:T(8,128)(2,1)S(1)}, bf16[1536,3072]{1,0:T(8,128)(2,1)}, u32[]{:S(2)}) copy-start(bf16[1536,3072]{1,0:T(8,128)(2,1)} %refs_3_) | copy-start | bytes 28311556
  0.1 1.1 %copy-start.3 = (bf16[128,1536]{1,0:T(8,128)(2,1)S(1)}, bf16[128,1536]{1,0:T(8,128)(2,1)}, u32[]{:S(2)}) copy-start(bf16[128,1536]{1,0:T(8,128)(2,1)} %q_ref.1) | copy-start | bytes 1179652
  1.2 1.2 %copy-start.4 = (bf16[128,1536]{1,0:T(8,128)(2,1)S(1)}, bf16[128,1536]{1,0:T(8,128)(2,1)}, u32[]{:S(2)}) copy-start(bf16[128,1536]{1,0:T(8,128)(2,1)} %k_ref.1) | copy-start | bytes 1179652
  2.5 1.4 %copy-start.5 = (bf16[128,1536]{1,0:T(8,128)(2,1)S(1)}, bf16[128,1536]{1,0:T(8,128)(2,1)}, u32[]{:S(2)}) copy-start(bf16[128,1536]{1,0:T(8,128)(2,1)} %v_ref.1) | copy-start | bytes 1179652
  4.8 13.2 %collective-permute-start = (bf16[320,384]{1,0:T(8,128)(2,1)S(1)}, bf16[320,384]{1,0:T(8,128)(2,1)S(1)}, u32[]{:S(2)}, u32[]{:S(2)}) collective-permute-start(bf16[320,384]{1,0:T(8,128)(2,1)S(1)} %pad_maximum_fusion), channel_id=1, source_target_pairs={{0,2},{1,3},{2,0},{3,1},{4,6},{5,7},{6,4},{7,5},{8,10},{9,11},{10,... | collective-permute-start | bytes 737288 | tf_op jit(solution)/shard_map/ppermute | solution.py:22
  6.9 10.9 %collective-permute-start.4 = (bf16[256,384]{1,0:T(8,128)(2,1)S(1)}, bf16[256,384]{1,0:T(8,128)(2,1)S(1)}, u32[]{:S(2)}, u32[]{:S(2)}) collective-permute-start(bf16[256,384]{1,0:T(8,128)(2,1)S(1)} %get-tuple-element.24), channel_id=1, source_target_pairs={{0,8},{4,12},{8,0},{12,4},{1,9},{5,13},{9,1},{13,5},{2,10},{6,14},... | collective-permute-start | bytes 589832 | tf_op jit(solution)/shard_map/ppermute | solution.py:22
  9.2 13.2 %collective-permute-start.1 = (bf16[384,384]{1,0:T(8,128)(2,1)S(1)}, bf16[384,384]{1,0:T(8,128)(2,1)S(1)}, u32[]{:S(2)}, u32[]{:S(2)}) collective-permute-start(bf16[384,384]{1,0:T(8,128)(2,1)S(1)} %get-tuple-element.22), channel_id=1, source_target_pairs={{0,4},{4,0},{8,12},{12,8},{1,5},{5,1},{9,13},{13,9},{2,6},{6,2},{1... | collective-permute-start | bytes 884744 | tf_op jit(solution)/shard_map/ppermute | solution.py:22
  17.8 6.0 %collective-permute-start.5 = (bf16[256,384]{1,0:T(8,128)(2,1)S(1)}, bf16[256,384]{1,0:T(8,128)(2,1)S(1)}, u32[]{:S(2)}, u32[]{:S(2)}) collective-permute-start(bf16[256,384]{1,0:T(8,128)(2,1)S(1)} %collective-permute-done.4), channel_id=1, source_target_pairs={{0,2},{1,3},{2,0},{3,1},{4,6},{5,7},{6,4},{7,5},{8,10},{9,11},{10,... | collective-permute-start | bytes 589832 | tf_op jit(solution)/shard_map/ppermute | solution.py:22
  18.0 8.6 %collective-permute-start.12 = (bf16[256,384]{1,0:T(8,128)(2,1)S(1)}, bf16[256,384]{1,0:T(8,128)(2,1)S(1)}, u32[]{:S(2)}, u32[]{:S(2)}) collective-permute-start(bf16[256,384]{1,0:T(8,128)(2,1)S(1)} %get-tuple-element.29), channel_id=1, source_target_pairs={{0,12},{4,8},{8,4},{12,0},{1,13},{5,9},{9,5},{13,1},{2,14},{6,10},... | collective-permute-start | bytes 589832 | tf_op jit(solution)/shard_map/ppermute | solution.py:22
  22.5 6.4 %collective-permute-start.2 = (bf16[320,384]{1,0:T(8,128)(2,1)S(1)}, bf16[320,384]{1,0:T(8,128)(2,1)S(1)}, u32[]{:S(2)}, u32[]{:S(2)}) collective-permute-start(bf16[320,384]{1,0:T(8,128)(2,1)S(1)} %pad_maximum_fusion.1), channel_id=1, source_target_pairs={{0,2},{1,3},{2,0},{3,1},{4,6},{5,7},{6,4},{7,5},{8,10},{9,11},{10,... | collective-permute-start | bytes 737288 | tf_op jit(solution)/shard_map/ppermute | solution.py:22
  23.8 24.8 %collective-permute-start.11 = (bf16[512,384]{1,0:T(8,128)(2,1)S(1)}, bf16[512,384]{1,0:T(8,128)(2,1)S(1)}, u32[]{:S(2)}, u32[]{:S(2)}) collective-permute-start(bf16[512,384]{1,0:T(8,128)(2,1)S(1)} %constant_dynamic-update-slice_fusion.6.refs_6_), channel_id=1, source_target_pairs={{0,1},{1,0},{2,3},{3,2},{4,5},{5,4},{6,7},{7,6},{8,9},{9,8},{10,11... | collective-permute-start | bytes 1179656 | tf_op jit(solution)/shard_map/ppermute | solution.py:22
  26.6 9.6 %collective-permute-start.13 = (bf16[256,384]{1,0:T(8,128)(2,1)S(1)}, bf16[256,384]{1,0:T(8,128)(2,1)S(1)}, u32[]{:S(2)}, u32[]{:S(2)}) collective-permute-start(bf16[256,384]{1,0:T(8,128)(2,1)S(1)} %collective-permute-done.12), channel_id=1, source_target_pairs={{0,2},{1,3},{2,0},{3,1},{4,6},{5,7},{6,4},{7,5},{8,10},{9,11},{10,... | collective-permute-start | bytes 589832 | tf_op jit(solution)/shard_map/ppermute | solution.py:22
  28.9 7.4 %collective-permute-start.7 = (bf16[128,384]{1,0:T(8,128)(2,1)S(1)}, bf16[128,384]{1,0:T(8,128)(2,1)S(1)}, u32[]{:S(2)}, u32[]{:S(2)}) collective-permute-start(bf16[128,384]{1,0:T(8,128)(2,1)S(1)} %get-tuple-element.27), channel_id=1, source_target_pairs={{0,12},{4,8},{8,4},{12,0},{1,13},{5,9},{9,5},{13,1},{2,14},{6,10},... | collective-permute-start | bytes 294920 | tf_op jit(solution)/shard_map/ppermute | solution.py:22
  33.4 7.8 %collective-permute-start.6 = (bf16[128,384]{1,0:T(8,128)(2,1)S(1)}, bf16[128,384]{1,0:T(8,128)(2,1)S(1)}, u32[]{:S(2)}, u32[]{:S(2)}) collective-permute-start(bf16[128,384]{1,0:T(8,128)(2,1)S(1)} %get-tuple-element.25), channel_id=1, source_target_pairs={{0,8},{4,12},{8,0},{12,4},{1,9},{5,13},{9,1},{13,5},{2,10},{6,14},... | collective-permute-start | bytes 294920 | tf_op jit(solution)/shard_map/ppermute | solution.py:22
  33.4 15.1 %collective-permute-start.3 = (bf16[1152,384]{1,0:T(8,128)(2,1)S(1)}, bf16[1152,384]{1,0:T(8,128)(2,1)S(1)}, u32[]{:S(2)}, u32[]{:S(2)}) collective-permute-start(bf16[1152,384]{1,0:T(8,128)(2,1)S(1)} %get-tuple-element.48.refs_4_), channel_id=1, source_target_pairs={{0,1},{1,0},{2,3},{3,2},{4,5},{5,4},{6,7},{7,6},{8,9},{9,8},{10,11... | collective-permute-start | bytes 2654216 | tf_op jit(solution)/shard_map/ppermute | solution.py:22
  36.2 12.4 %collective-permute-start.14 = (bf16[512,384]{1,0:T(8,128)(2,1)S(1)}, bf16[512,384]{1,0:T(8,128)(2,1)S(1)}, u32[]{:S(2)}, u32[]{:S(2)}) collective-permute-start(bf16[512,384]{1,0:T(8,128)(2,1)S(1)} %constant_dynamic-update-slice_fusion.8.refs_8_), channel_id=1, source_target_pairs={{0,1},{1,0},{2,3},{3,2},{4,5},{5,4},{6,7},{7,6},{8,9},{9,8},{10,11... | collective-permute-start | bytes 1179656 | tf_op jit(solution)/shard_map/ppermute | solution.py:22
  41.2 3.0 %collective-permute-start.8 = (bf16[64,384]{1,0:T(8,128)(2,1)S(1)}, bf16[64,384]{1,0:T(8,128)(2,1)S(1)}, u32[]{:S(2)}, u32[]{:S(2)}) collective-permute-start(bf16[64,384]{1,0:T(8,128)(2,1)S(1)} %pad_maximum_fusion.6), channel_id=1, source_target_pairs={{0,2},{1,3},{2,0},{3,1},{4,6},{5,7},{6,4},{7,5},{8,10},{9,11},{10,... | collective-permute-start | bytes 147464 | tf_op jit(solution)/shard_map/ppermute | solution.py:22
  41.6 5.2 %collective-permute-start.9 = (bf16[64,384]{1,0:T(8,128)(2,1)S(1)}, bf16[64,384]{1,0:T(8,128)(2,1)S(1)}, u32[]{:S(2)}, u32[]{:S(2)}) collective-permute-start(bf16[64,384]{1,0:T(8,128)(2,1)S(1)} %pad_maximum_fusion.7), channel_id=1, source_target_pairs={{0,1},{1,0},{2,3},{3,2},{4,5},{5,4},{6,7},{7,6},{8,9},{9,8},{10,11... | collective-permute-start | bytes 147464 | tf_op jit(solution)/shard_map/ppermute | solution.py:22
  44.2 4.3 %collective-permute-start.10 = (bf16[64,384]{1,0:T(8,128)(2,1)S(1)}, bf16[64,384]{1,0:T(8,128)(2,1)S(1)}, u32[]{:S(2)}, u32[]{:S(2)}) collective-permute-start(bf16[64,384]{1,0:T(8,128)(2,1)S(1)} %pad_maximum_fusion.8), channel_id=1, source_target_pairs={{0,3},{1,2},{2,1},{3,0},{4,7},{5,6},{6,5},{7,4},{8,11},{9,10},{10,... | collective-permute-start | bytes 147464 | tf_op jit(solution)/shard_map/ppermute | solution.py:22
  48.6 12.5 %copy-start.2 = (bf16[3072,64]{0,1:T(8,128)(2,1)S(1)}, bf16[3072,64]{0,1:T(8,128)(2,1)}, u32[]{:S(2)}) copy-start(bf16[3072,64]{0,1:T(8,128)(2,1)} %param.15) | copy-start | bytes 1179652
  48.6 12.5 %copy-start.6 = (f32[3072]{0:T(1024)S(1)}, f32[3072]{0:T(1024)}, u32[]{:S(2)}) copy-start(f32[3072]{0:T(1024)} %param.14) | copy-start | bytes 36868
  48.6 12.5 %copy-start.7 = (f32[3072]{0:T(1024)S(1)}, f32[3072]{0:T(1024)}, u32[]{:S(2)}) copy-start(f32[3072]{0:T(1024)} %param.13) | copy-start | bytes 36868
  50.9 5.9 %collective-permute-start.17 = (bf16[4,32,384]{2,1,0:T(8,128)(2,1)S(1)}, bf16[4,32,384]{2,1,0:T(8,128)(2,1)S(1)}, u32[]{:S(2)}, u32[]{:S(2)}) collective-permute-start(bf16[4,32,384]{2,1,0:T(8,128)(2,1)S(1)} %get-tuple-element.33), channel_id=1, source_target_pairs={{0,12},{4,8},{8,4},{12,0},{1,13},{5,9},{9,5},{13,1},{2,14},{6,10},... | collective-permute-start | bytes 294920 | tf_op jit(solution)/shard_map/ppermute | solution.py:22
  55.1 6.0 %collective-permute-start.16 = (bf16[4,32,384]{2,1,0:T(8,128)(2,1)S(1)}, bf16[4,32,384]{2,1,0:T(8,128)(2,1)S(1)}, u32[]{:S(2)}, u32[]{:S(2)}) collective-permute-start(bf16[4,32,384]{2,1,0:T(8,128)(2,1)S(1)} %get-tuple-element.31), channel_id=1, source_target_pairs={{0,4},{4,0},{8,12},{12,8},{1,5},{5,1},{9,13},{13,9},{2,6},{6,2},{1... | collective-permute-start | bytes 294920 | tf_op jit(solution)/shard_map/ppermute | solution.py:22
  55.2 5.9 %collective-permute-start.15 = (bf16[4,32,384]{2,1,0:T(8,128)(2,1)S(1)}, bf16[4,32,384]{2,1,0:T(8,128)(2,1)S(1)}, u32[]{:S(2)}, u32[]{:S(2)}) collective-permute-start(bf16[4,32,384]{2,1,0:T(8,128)(2,1)S(1)} %get-tuple-element.30), channel_id=1, source_target_pairs={{0,8},{4,12},{8,0},{12,4},{1,9},{5,13},{9,1},{13,5},{2,10},{6,14},... | collective-permute-start | bytes 294920 | tf_op jit(solution)/shard_map/ppermute | solution.py:22
  56.9 17.3 %copy-start.1 = (bf16[432,512]{1,0:T(8,128)(2,1)S(1)}, bf16[432,512]{1,0:T(8,128)(2,1)}, u32[]{:S(2)}) copy-start(bf16[432,512]{1,0:T(8,128)(2,1)} %w_ref.1) | copy-start | bytes 1327108
  56.9 17.3 %copy-start.8 = (f32[512]{0:T(512)S(1)}, f32[512]{0:T(512)}, u32[]{:S(2)}) copy-start(f32[512]{0:T(512)} %param.17) | copy-start | bytes 6148
  65.1 8.1 %collective-permute-start.19 = (bf16[128,32]{1,0:T(8,128)(2,1)S(1)}, bf16[128,32]{1,0:T(8,128)(2,1)S(1)}, u32[]{:S(2)}, u32[]{:S(2)}) collective-permute-start(bf16[128,32]{1,0:T(8,128)(2,1)S(1)} %get-tuple-element.35.even_ref), channel_id=1, source_target_pairs={{1,0},{2,1},{3,2},{4,3},{5,4},{6,5},{7,6},{8,7},{9,8},{10,9},{11,1... | collective-permute-start | bytes 24584 | tf_op jit(solution)/shard_map/ppermute | solution.py:408
  69.2 5.0 %collective-permute-start.18 = (bf16[128,32]{1,0:T(8,128)(2,1)S(1)}, bf16[128,32]{1,0:T(8,128)(2,1)S(1)}, u32[]{:S(2)}, u32[]{:S(2)}) collective-permute-start(bf16[128,32]{1,0:T(8,128)(2,1)S(1)} %get-tuple-element.36.odd_ref), channel_id=1, source_target_pairs={{0,1},{1,2},{2,3},{3,4},{4,5},{5,6},{6,7},{7,8},{8,9},{9,10},{10,1... | collective-permute-start | bytes 24584 | tf_op jit(solution)/shard_map/ppermute | solution.py:407

commit v10 on v4

--- a/solution.py
+++ b/solution.py
@@ -22,35 +22,39 @@
     return lax.ppermute(source, axis, [(i, i ^ distance) for i in range(count)])
 
 
-def bundle_kernel(where_ref, q_ref, k_ref, v_ref, *out_refs, groups, planes, distances):
-    tokens, width = q_ref.shape
-    group_width = width // groups
+def bundle_kernel(where_ref, *refs, groups, planes, distances):
+    tokens = refs[0].shape[0]
     rows_dev = tokens // (groups * planes)
     to = lax.broadcasted_iota(jnp.int32, (tokens, tokens), 0)
     at = lax.broadcasted_iota(jnp.int32, (tokens, tokens), 1)
     j, t, row = to // (groups * rows_dev), (to // rows_dev) % groups, to % rows_dev
-    for r, out_ref in zip(distances, out_refs):
+    count = len(distances)
+    cut = [refs[n * count : (n + 1) * count] for n in range(4)]
+    for r, q_ref, k_ref, v_ref, out_ref in zip(distances, *cut):
         group = where_ref[0] ^ r
-        lanes = pl.ds(pl.multiple_of(group * group_width, 128), group_width)
         place = row * (groups * planes) + (t ^ group) * planes + (j ^ where_ref[1])
         order = (at == place).astype(jnp.bfloat16)
-        out_ref[:tokens] = k_ref[:, lanes]
-        out_ref[tokens : 2 * tokens] = v_ref[:, lanes]
-        mixed = jnp.dot(order, q_ref[:, lanes], preferred_element_type=jnp.float32)
+        out_ref[:tokens] = k_ref[...]
+        out_ref[tokens : 2 * tokens] = v_ref[...]
+        mixed = jnp.dot(order, q_ref[...], preferred_element_type=jnp.float32)
         out_ref[2 * tokens :] = mixed.astype(jnp.bfloat16)
 
 
 def bundles(where, queries, keys, values, groups, planes, distances):
+    def cut(source, r):
+        width = source.shape[1] // groups
+        return lax.dynamic_slice_in_dim(source, (lax.axis_index("heads") ^ r) * width, width, axis=1)
+
     tokens, width = queries.shape
     vmem = pl.BlockSpec(memory_space=pltpu.VMEM)
     result = jax.ShapeDtypeStruct((3 * tokens, width // groups), jnp.bfloat16)
     return pl.pallas_call(
         functools.partial(bundle_kernel, groups=groups, planes=planes, distances=distances),
-        in_specs=[pl.BlockSpec(memory_space=pltpu.SMEM)] + [vmem] * 3,
+        in_specs=[pl.BlockSpec(memory_space=pltpu.SMEM)] + [vmem] * (3 * len(distances)),
         out_specs=[vmem] * len(distances),
         out_shape=[result] * len(distances),
         compiler_params=pltpu.CompilerParams(vmem_limit_bytes=VMEM_LIMIT),
-    )(where, queries, keys, values)
+    )(where, *[cut(source, r) for source in (queries, keys, values) for r in distances])
 
 
 def attend_kernel(*refs, sources, planes, blocks, part, targets, rows_step):
@@ -147,54 +151,54 @@
     )(*queries, *keys_values)
 
 
+def projection_of(o_refs, w_refs, lined):
+    tokens, width = lined.shape[0], o_refs[0].shape[2]
+    for n, o_ref in enumerate(o_refs):
+        lined[:, n * width : (n + 1) * width] = o_ref[...].reshape(tokens, width)
+    weights = jnp.concatenate([w[...] for w in w_refs], axis=0)
+    return jnp.dot(lined[...], weights, preferred_element_type=jnp.float32)
+
+
+def projection_specs(attended, targets, tile):
+    o_spec = pl.BlockSpec(attended[0].shape, lambda i, *_: (0, 0, 0))
+    width = attended[0].shape[2]
+    return [o_spec] * len(targets) + [
+        pl.BlockSpec((width, tile), lambda i, where, t=t: (where[0] ^ t, i)) for t in targets
+    ]
+
+
 def project_kernel(where_ref, *refs, targets):
-    o_refs = refs[: len(targets)]
-    w_ref, out_ref, lined = refs[len(targets) :]
-    width = o_refs[0].shape[2]
-    tokens = lined.shape[0]
-    for n in range(len(targets)):
-        lined[:, n * width : (n + 1) * width] = o_refs[n][...].reshape(tokens, width)
-    rows = [pl.ds(pl.multiple_of((where_ref[0] ^ t) * width, 128), width) for t in targets]
-    weights = jnp.concatenate([w_ref[r, :] for r in rows], axis=0)
-    out_ref[...] = jnp.dot(lined[...], weights, preferred_element_type=jnp.float32)
+    count = len(targets)
+    out_ref, lined = refs[2 * count :]
+    out_ref[...] = projection_of(refs[:count], refs[count : 2 * count], lined)
 
 
 def project(where, attended, targets, w_out, tile):
     sources, rows, width = attended[0].shape
     tokens = sources * rows
-    inner, features = w_out.shape
+    features = w_out.shape[1]
     return pl.pallas_call(
         functools.partial(project_kernel, targets=targets),
         grid_spec=pltpu.PrefetchScalarGridSpec(
             num_scalar_prefetch=1,
             grid=(features // tile,),
-            in_specs=[pl.BlockSpec((sources, rows, width), lambda i, *_: (0, 0, 0))] * len(targets)
-            + [pl.BlockSpec((inner, tile), lambda i, *_: (0, i))],
+            in_specs=projection_specs(attended, targets, tile),
             out_specs=pl.BlockSpec((None, tokens, tile), lambda i, *_: (i, 0, 0)),
             scratch_shapes=[pltpu.VMEM((tokens, len(targets) * width), jnp.bfloat16)],
         ),
         out_shape=jax.ShapeDtypeStruct((features // tile, tokens, tile), jnp.float32),
         compiler_params=pltpu.CompilerParams(vmem_limit_bytes=VMEM_LIMIT),
-    )(where, *attended, w_out)
+    )(where, *attended, *[w_out] * len(targets))
 
 
 def final_kernel(where_ref, *refs, targets, planes, rows_dev):
-    o_refs = refs[: len(targets)]
-    partial_ref, w_ref, scale_ref, shift_ref, w_final_ref, even_ref, odd_ref, lined, projected = refs[
-        len(targets) :
-    ]
+    count = len(targets)
+    partial_ref, scale_ref, shift_ref, w_final_ref, even_ref, odd_ref, lined, projected = refs[2 * count :]
     step = pl.program_id(0)
     heads_at, plane_at = where_ref[0], where_ref[1]
     tokens = lined.shape[0]
-    width = o_refs[0].shape[2]
-    tile = w_ref.shape[1]
-    for n in range(len(targets)):
-        lined[:, n * width : (n + 1) * width] = o_refs[n][...].reshape(tokens, width)
-    rows = [pl.ds(pl.multiple_of((heads_at ^ t) * width, 128), width) for t in targets]
-    weights = jnp.concatenate([w_ref[r, :] for r in rows], axis=0)
-    projected[step] = partial_ref[...] + jnp.dot(
-        lined[...], weights, preferred_element_type=jnp.float32
-    )
+    tile = partial_ref.shape[1]
+    projected[step] = partial_ref[...] + projection_of(refs[:count], refs[count : 2 * count], lined)
 
     @pl.when(step == pl.num_programs(0) - 1)
     def _():
@@ -243,7 +247,7 @@
 
 def final_layer(where, attended, targets, partial, w_out, scale_mod, shift_mod, w_final, rows_dev, planes):
     sources, rows, width = attended[0].shape
-    inner, features = w_out.shape
+    features = w_out.shape[1]
     steps, tokens, tile = partial.shape
     channels = w_final.shape[1]
     whole = lambda shape: pl.BlockSpec(shape, lambda i, *_: (0,) * len(shape))
@@ -253,10 +257,9 @@
         grid_spec=pltpu.PrefetchScalarGridSpec(
             num_scalar_prefetch=1,
             grid=(steps,),
-            in_specs=[whole((sources, rows, width))] * len(targets)
+            in_specs=projection_specs(attended, targets, tile)
             + [
                 pl.BlockSpec((None, tokens, tile), lambda i, *_: (i, 0, 0)),
-                pl.BlockSpec((inner, tile), lambda i, *_: (0, i)),
                 whole((1, features)),
                 whole((1, features)),
                 whole((channels, features)),
@@ -269,7 +272,7 @@
         ),
         out_shape=[result] * 2,
         compiler_params=pltpu.CompilerParams(vmem_limit_bytes=VMEM_LIMIT),
-    )(where, *attended, partial, w_out, scale_mod[None], shift_mod[None], w_final.T)
+    )(where, *attended, *[w_out] * len(targets), partial, scale_mod[None], shift_mod[None], w_final.T)
 
 
 def convolve_kernel(where_ref, even_ref, odd_ref, left_ref, right_ref, w_ref, bias_ref, out_ref, latent):
@@ -360,8 +363,8 @@
             )
     asked = [asked[r] for r in range(groups)]
 
-    first, second = (1, 3), (2, 0)
-    near, far = (0, 1), (3, 2)
+    first, second = (3, 2), (1, 0)
+    near, far = (0, 3), (2, 1)
     results = {}
     for targets in (first, second):
         for t, o in zip(targets, attend(asked, keys_values, targets, planes)):

time: 74.1 us -> 72.1 us (0.973)
  local copies, waits for them, and re-layouts: 4.14 us -> 2.79 us
  starting transfers between devices: 28.9 us -> 28.1 us
    unnamed x20 -> x14, local copies, waits for them, and re-layouts: 3.84 us -> 0.1 us
    dynamic_slice x0 -> x2, local copies, waits for them, and re-layouts: none -> 2.39 us  [cut(): lax.dynamic_slice_in_dim(source, (lax.axis_index('heads') ^ r) * width, w...]
    ppermute x13, starting transfers between devices: 24.4 us -> 23.5 us  [swap(): return lax.ppermute(source, axis, [(i, i ^ distance) for i in range(count)])]
where the time goes in v10:
time: 72.1 us; the launch traced here: 71.3 us
  starting transfers between devices  28.1 us (39%)
  waiting for transfers between devices  25.8 us (36%)
  Pallas kernels  14 us (19%)
  local copies, waits for them, and re-layouts  2.79 us (4%)
    ppermute x13, starting transfers between devices, swap(): return lax.ppermute(source, axis, [(i, i ^ distance) for i in range(count)])  23.5 us
    ppermute x13, waiting for transfers between devices, swap(): return lax.ppermute(source, axis, [(i, i ^ distance) for i in range(count)])  22.5 us
    pallas_call x2, Pallas kernels, attend(): pl.pallas_call(functools.partial(attend_kernel, sources=sources, planes=p...  4.53 us
    pallas_call x1, Pallas kernels, final_layer(): pl.pallas_call(functools.partial(final_kernel, targets=targets, planes=pl...  3.78 us
    ppermute x1, waiting for transfers between devices, shards(): right = lax.ppermute(even, both, [(i + 1, i) for i in range(devices - 1)])  3.29 us
    pallas_call x1, Pallas kernels, project(): pl.pallas_call(functools.partial(project_kernel, targets=targets), grid_s...  2.66 us
    ppermute x1, starting transfers between devices, shards(): left = lax.ppermute(odd, both, [(i, i + 1) for i in range(devices - 1)])  2.61 us
    dynamic_slice x2, local copies, waits for them, and re-layouts, cut(): lax.dynamic_slice_in_dim(source, (lax.axis_index('heads') ^ r) * width, w...  2.39 us
  transfers between devices with their start and end apart: 15, of which 6 were waited for; matrix products, arithmetic and copies ran while one was open for 1% of the time, Pallas kernels for 7%

profile of v10, /device:TPU:1, one launch (start us, length us, event | category | flops | bytes accessed | tf_op | source)
XLA Modules:
  0.0 71.3 jit_solution(5897305442136933986)
XLA Ops:
  0.0 1.1 %constant_dynamic-slice_fusion.8 = (bf16[128,384]{1,0:T(8,128)(2,1)S(1)}, bf16[128,384]{1,0:T(8,128)(2,1)S(1)}, bf16[128,384]{1,0:T(8,128)(2,1)S(1)}, bf16[128,384]{1,0:T(8,128)(2,1)S(1)}) fusion(bf16[128,1536]{1,0:T(8,128)(2,1)} %param.9, s32[]{:T(128)S(6)} %select_n.11, s32[]{:T(128)S(6)} %select_n.9, s32[]{:T(128)S(6)} %select_n.8, s32[]{:T(128)S(6)} %select_n.10), kind=kLoop, calls=%fused_computation.26 | loop fusion | bytes 786448 | tf_op jit(solution)/shard_map/dynamic_slice | solution.py:46
  1.1 1.3 %constant_dynamic-slice_fusion = (bf16[128,384]{1,0:T(8,128)(2,1)S(1)}, bf16[128,384]{1,0:T(8,128)(2,1)S(1)}, bf16[128,384]{1,0:T(8,128)(2,1)S(1)}, bf16[128,384...) fusion(bf16[128,1536]{1,0:T(8,128)(2,1)} %param.11, ...), kind=kLoop, calls=%fused_computation.18 | loop fusion | bytes 1572880 | tf_op jit(solution)/shard_map/dynamic_slice | solution.py:46
  2.4 0.0 copy-start
  2.4 0.1 pad_add_fusion.where_ref
  2.5 0.8 %shard_map.91 = (bf16[384,384]{1,0:T(8,128)(2,1)S(1)}, bf16[384,384]{1,0:T(8,128)(2,1)S(1)}, bf16[384,384]{1,0:T(8,128)(2,1)S(1)}, bf16[384,384]{1,0:T(8,128)(2,1)S(1)}) custom-call(s32[4]{0:T(128)S(1)} %pad_add_fusion.where_ref, bf16[128,384]{1,0:T(8,128)(2,1)S(1)} %get-tuple-element.37.refs_0_, bf16[128,384]{1,0:T(8,128)(2,1)S(1)} %get-tuple-element.36.refs_1_, ...), custom_call_target="tpu_custom_call" | custom-call | tf_op jit(solution)/shard_map/pallas_call | solution.py:51
  3.4 2.1 %collective-permute-start = (bf16[320,384]{1,0:T(8,128)(2,1)S(1)}, bf16[320,384]{1,0:T(8,128)(2,1)S(1)}, u32[]{:S(2)}, u32[]{:S(2)}) collective-permute-start(bf16[320,384]{1,0:T(8,128)(2,1)S(1)} %pad_maximum_fusion.2), channel_id=1, source_target_pairs={{0,2},{1,3},{2,0},{3,1},{4,6},{5,7},{6,4},{7,5},{8,10},{9,11},{10,... | collective-permute-start | bytes 737288 | tf_op jit(solution)/shard_map/ppermute | solution.py:22
  5.5 1.3 %collective-permute-start.1 = (bf16[384,384]{1,0:T(8,128)(2,1)S(1)}, bf16[384,384]{1,0:T(8,128)(2,1)S(1)}, u32[]{:S(2)}, u32[]{:S(2)}) collective-permute-start(bf16[384,384]{1,0:T(8,128)(2,1)S(1)} %get-tuple-element.16), channel_id=1, source_target_pairs={{0,4},{4,0},{8,12},{12,8},{1,5},{5,1},{9,13},{13,9},{2,6},{6,2},{1... | collective-permute-start | bytes 884744 | tf_op jit(solution)/shard_map/ppermute | solution.py:22
  6.8 2.3 %collective-permute-start.4 = (bf16[384,384]{1,0:T(8,128)(2,1)S(1)}, bf16[384,384]{1,0:T(8,128)(2,1)S(1)}, u32[]{:S(2)}, u32[]{:S(2)}) collective-permute-start(bf16[384,384]{1,0:T(8,128)(2,1)S(1)} %get-tuple-element.17), channel_id=1, source_target_pairs={{0,8},{4,12},{8,0},{12,4},{1,9},{5,13},{9,1},{13,5},{2,10},{6,14},... | collective-permute-start | bytes 884744 | tf_op jit(solution)/shard_map/ppermute | solution.py:22
  9.1 0.0 collective-permute-start.7
  9.1 2.1 %collective-permute-done = bf16[320,384]{1,0:T(8,128)(2,1)S(1)} collective-permute-done((bf16[320,384]{1,0:T(8,128)(2,1)S(1)}, bf16[320,384]{1,0:T(8,128)(2,1)S(1)}, u32[]{:S(2)}, u32[]{:S(2)}) %collective-permute-start) | collective-permute-done | bytes 245792 | tf_op jit(solution)/shard_map/ppermute | solution.py:22
  11.3 7.2 %collective-permute-done.1 = bf16[384,384]{1,0:T(8,128)(2,1)S(1)} collective-permute-done((bf16[384,384]{1,0:T(8,128)(2,1)S(1)}, bf16[384,384]{1,0:T(8,128)(2,1)S(1)}, u32[]{:S(2)}, u32[]{:S(2)}) %collective-permute-start.1) | collective-permute-done | bytes 294944 | tf_op jit(solution)/shard_map/ppermute | solution.py:22
  18.5 0.1 fusion.5
  18.6 0.5 collective-permute-start.2
  19.1 0.0 collective-permute-done.4
  19.1 1.1 %collective-permute-start.5 = (bf16[320,384]{1,0:T(8,128)(2,1)S(1)}, bf16[320,384]{1,0:T(8,128)(2,1)S(1)}, u32[]{:S(2)}, u32[]{:S(2)}) collective-permute-start(bf16[320,384]{1,0:T(8,128)(2,1)S(1)} %pad_maximum_fusion.4), channel_id=1, source_target_pairs={{0,2},{1,3},{2,0},{3,1},{4,6},{5,7},{6,4},{7,5},{8,10},{9,11},{10,... | collective-permute-start | bytes 737288 | tf_op jit(solution)/shard_map/ppermute | solution.py:22
  20.3 7.5 %collective-permute-done.7 = bf16[384,384]{1,0:T(8,128)(2,1)S(1)} collective-permute-done((bf16[384,384]{1,0:T(8,128)(2,1)S(1)}, bf16[384,384]{1,0:T(8,128)(2,1)S(1)}, u32[]{:S(2)}, u32[]{:S(2)}) %collective-permute-start.7) | collective-permute-done | bytes 294944 | tf_op jit(solution)/shard_map/ppermute | solution.py:22
  27.9 0.3 collective-permute-start.8
  28.2 0.0 collective-permute-done.2
  28.3 5.7 %collective-permute-start.3 = (bf16[1152,384]{1,0:T(8,128)(2,1)S(1)}, bf16[1152,384]{1,0:T(8,128)(2,1)S(1)}, u32[]{:S(2)}, u32[]{:S(2)}) collective-permute-start(bf16[1152,384]{1,0:T(8,128)(2,1)S(1)} %get-tuple-element.56.refs_4_), channel_id=1, source_target_pairs={{0,1},{1,0},{2,3},{3,2},{4,5},{5,4},{6,7},{7,6},{8,9},{9,8},{10,11... | collective-permute-start | bytes 2654216 | tf_op jit(solution)/shard_map/ppermute | solution.py:22
  34.1 0.0 collective-permute-done.5
  34.2 3.9 %collective-permute-start.6 = (bf16[576,384]{1,0:T(8,128)(2,1)S(1)}, bf16[576,384]{1,0:T(8,128)(2,1)S(1)}, u32[]{:S(2)}, u32[]{:S(2)}) collective-permute-start(bf16[576,384]{1,0:T(8,128)(2,1)S(1)} %pad_maximum_fusion.refs_6_), channel_id=1, source_target_pairs={{0,1},{1,0},{2,3},{3,2},{4,5},{5,4},{6,7},{7,6},{8,9},{9,8},{10,11... | collective-permute-start | bytes 1327112 | tf_op jit(solution)/shard_map/ppermute | solution.py:22
  38.0 0.0 collective-permute-done.8
  38.1 2.5 %collective-permute-start.9 = (bf16[576,384]{1,0:T(8,128)(2,1)S(1)}, bf16[576,384]{1,0:T(8,128)(2,1)S(1)}, u32[]{:S(2)}, u32[]{:S(2)}) collective-permute-start(bf16[576,384]{1,0:T(8,128)(2,1)S(1)} %pad_maximum_fusion.1.refs_8_), channel_id=1, source_target_pairs={{0,1},{1,0},{2,3},{3,2},{4,5},{5,4},{6,7},{7,6},{8,9},{9,8},{10,11... | collective-permute-start | bytes 1327112 | tf_op jit(solution)/shard_map/ppermute | solution.py:22
  40.7 0.0 collective-permute-done.6.refs_7_
  40.7 1.4 %collective-permute-done.9.refs_9_ = bf16[576,384]{1,0:T(8,128)(2,1)S(1)} collective-permute-done((bf16[576,384]{1,0:T(8,128)(2,1)S(1)}, bf16[576,384]{1,0:T(8,128)(2,1)S(1)}, u32[]{:S(2)}, u32[]{:S(2)}) %collective-permute-start.9) | collective-permute-done | bytes 442400 | tf_op jit(solution)/shard_map/ppermute | solution.py:22
  42.1 0.0 collective-permute-done.3.refs_5_
  42.2 2.3 %shard_map.92 = (bf16[4,32,384]{2,1,0:T(8,128)(2,1)S(1)}, bf16[4,32,384]{2,1,0:T(8,128)(2,1)S(1)}) custom-call(bf16[128,384]{1,0:T(8,128)(2,1)S(1)} %pad_maximum_fusion.6.refs_0_, bf16[128,384]{1,0:T(8,128)(2,1)S(1)} %pad_maximum_fusion.7.refs_1_, bf16[128,384]{1,0:T(8,128)(2,1)S(1)} %pad_maximum_fusion.8.refs_2_, ...), custom_call_target="tpu_custom_call" | custom-call | tf_op jit(solution)/shard_map/pallas_call | solution.py:135
  44.5 2.3 %collective-permute-start.12 = (bf16[4,32,384]{2,1,0:T(8,128)(2,1)S(1)}, bf16[4,32,384]{2,1,0:T(8,128)(2,1)S(1)}, u32[]{:S(2)}, u32[]{:S(2)}) collective-permute-start(bf16[4,32,384]{2,1,0:T(8,128)(2,1)S(1)} %get-tuple-element.22), channel_id=1, source_target_pairs={{0,12},{4,8},{8,4},{12,0},{1,13},{5,9},{9,5},{13,1},{2,14},{6,10},... | collective-permute-start | bytes 294920 | tf_op jit(solution)/shard_map/ppermute | solution.py:22
  46.7 1.3 %collective-permute-start.10 = (bf16[4,32,384]{2,1,0:T(8,128)(2,1)S(1)}, bf16[4,32,384]{2,1,0:T(8,128)(2,1)S(1)}, u32[]{:S(2)}, u32[]{:S(2)}) collective-permute-start(bf16[4,32,384]{2,1,0:T(8,128)(2,1)S(1)} %get-tuple-element.19), channel_id=1, source_target_pairs={{0,8},{4,12},{8,0},{12,4},{1,9},{5,13},{9,1},{13,5},{2,10},{6,14},... | collective-permute-start | bytes 294920 | tf_op jit(solution)/shard_map/ppermute | solution.py:22
  48.0 2.3 %shard_map.93 = (bf16[4,32,384]{2,1,0:T(8,128)(2,1)S(1)}, bf16[4,32,384]{2,1,0:T(8,128)(2,1)S(1)}) custom-call(bf16[128,384]{1,0:T(8,128)(2,1)S(1)} %pad_maximum_fusion.6.refs_0_, bf16[128,384]{1,0:T(8,128)(2,1)S(1)} %pad_maximum_fusion.7.refs_1_, bf16[128,384]{1,0:T(8,128)(2,1)S(1)} %pad_maximum_fusion.8.refs_2_, ...), custom_call_target="tpu_custom_call" | custom-call | tf_op jit(solution)/shard_map/pallas_call | solution.py:135
  50.3 0.2 collective-permute-start.11
  50.5 0.0 collective-permute-done.12.refs_1_
  50.5 0.0 copy-done
  50.5 0.0 copy-start.2
  50.5 0.0 copy-start.3
  50.5 0.0 copy-start.4
  50.5 2.7 %shard_map.94.refs_4_ = f32[6,128,512]{2,1,0:T(8,128)S(1)} custom-call(s32[4]{0:T(128)S(1)} %pad_add_fusion.where_ref, bf16[4,32,384]{2,1,0:T(8,128)(2,1)S(1)} %get-tuple-element.21.refs_0_, bf16[4,32,384]{2,1,0:T(8,128)(2,1)S(1)} %collective-permute-done.12.refs_1_, bf16[1536,3072]{1,0:T(8,128)(2,1)S(1)} %copy-done, bf16[1536,3072]{1,0:T(8,128)(2,1)S(1)} %copy-done), custom_call_target="tpu_custom_call" | custom-call | tf_op jit(solution)/shard_map/pallas_call | solution.py:180
  53.2 4.3 %collective-permute-done.10.refs_0_ = bf16[4,32,384]{2,1,0:T(8,128)(2,1)S(1)} collective-permute-done((bf16[4,32,384]{2,1,0:T(8,128)(2,1)S(1)}, bf16[4,32,384]{2,1,0:T(8,128)(2,1)S(1)}, u32[]{:S(2)}, u32[]{:S(2)}) %collective-permute-start.10) | collective-permute-done | bytes 98336 | tf_op jit(solution)/shard_map/ppermute | solution.py:22
  57.4 0.0 collective-permute-done.11.refs_1_
  57.4 0.0 copy-done.2
  57.4 0.0 copy-done.3
  57.5 0.0 copy-done.4
  57.5 0.0 copy-start.1
  57.5 0.0 copy-start.5
  57.5 3.8 %shard_map.95 = (bf16[128,32]{1,0:T(8,128)(2,1)S(1)}, bf16[128,32]{1,0:T(8,128)(2,1)S(1)}) custom-call(s32[4]{0:T(128)S(1)} %pad_add_fusion.where_ref, bf16[4,32,384]{2,1,0:T(8,128)(2,1)S(1)} %collective-permute-done.10.refs_0_, bf16[4,32,384]{2,1,0:T(8,128)(2,1)S(1)} %collective-permute-done.11.refs_1_, bf16[1536,3072]{1,0:T(8,128)(2,1)S(1)} %copy-done, ...), custom_call_target="tpu_custom_call" | custom-call | tf_op jit(solution)/shard_map/pallas_call | solution.py:255
  61.3 2.6 %collective-permute-start.13 = (bf16[128,32]{1,0:T(8,128)(2,1)S(1)}, bf16[128,32]{1,0:T(8,128)(2,1)S(1)}, u32[]{:S(2)}, u32[]{:S(2)}) collective-permute-start(bf16[128,32]{1,0:T(8,128)(2,1)S(1)} %get-tuple-element.24.odd_ref), channel_id=1, source_target_pairs={{0,1},{1,2},{2,3},{3,4},{4,5},{5,6},{6,7},{7,8},{8,9},{9,10},{10,1... | collective-permute-start | bytes 24584 | tf_op jit(solution)/shard_map/ppermute | solution.py:378
  63.9 1.9 %collective-permute-start.14 = (bf16[128,32]{1,0:T(8,128)(2,1)S(1)}, bf16[128,32]{1,0:T(8,128)(2,1)S(1)}, u32[]{:S(2)}, u32[]{:S(2)}) collective-permute-start(bf16[128,32]{1,0:T(8,128)(2,1)S(1)} %get-tuple-element.23.even_ref), channel_id=1, source_target_pairs={{1,0},{2,1},{3,2},{4,3},{5,4},{6,5},{7,6},{8,7},{9,8},{10,9},{11,1... | collective-permute-start | bytes 24584 | tf_op jit(solution)/shard_map/ppermute | solution.py:379
  65.8 0.0 collective-permute-done.13.left_ref
  65.8 3.3 %collective-permute-done.14.right_ref = bf16[128,32]{1,0:T(8,128)(2,1)S(1)} collective-permute-done((bf16[128,32]{1,0:T(8,128)(2,1)S(1)}, bf16[128,32]{1,0:T(8,128)(2,1)S(1)}, u32[]{:S(2)}, u32[]{:S(2)}) %collective-permute-start.14) | collective-permute-done | bytes 8224 | tf_op jit(solution)/shard_map/ppermute | solution.py:379
  69.1 0.0 copy-done.1
  69.1 0.0 copy-done.5
  69.1 2.2 %shard_map.96 = bf16[4,2,64,512]{3,2,1,0:T(8,128)(2,1)} custom-call(s32[4]{0:T(128)S(1)} %pad_add_fusion.where_ref, bf16[128,32]{1,0:T(8,128)(2,1)S(1)} %get-tuple-element.23.even_ref, bf16[128,32]{1,0:T(8,128)(2,1)S(1)} %get-tuple-element.24.odd_ref, bf16[128,32]{1,0:T(8,128)(2,1)S(1)} %collective-permute-done.13.left_ref, ...), custom_call_target="tpu_custom_call" | custom-call | tf_op jit(solution)/shard_map/pallas_call | solution.py:316
  (32 shorter events, 0.6 us)
Async XLA Ops:
  2.4 48.1 %copy-start = (bf16[1536,3072]{1,0:T(8,128)(2,1)S(1)}, bf16[1536,3072]{1,0:T(8,128)(2,1)}, u32[]{:S(2)}) copy-start(bf16[1536,3072]{1,0:T(8,128)(2,1)} %refs_3_.3) | copy-start | bytes 28311556
  3.4 7.8 %collective-permute-start = (bf16[320,384]{1,0:T(8,128)(2,1)S(1)}, bf16[320,384]{1,0:T(8,128)(2,1)S(1)}, u32[]{:S(2)}, u32[]{:S(2)}) collective-permute-start(bf16[320,384]{1,0:T(8,128)(2,1)S(1)} %pad_maximum_fusion.2), channel_id=1, source_target_pairs={{0,2},{1,3},{2,0},{3,1},{4,6},{5,7},{6,4},{7,5},{8,10},{9,11},{10,... | collective-permute-start | bytes 737288 | tf_op jit(solution)/shard_map/ppermute | solution.py:22
  5.5 13.0 %collective-permute-start.1 = (bf16[384,384]{1,0:T(8,128)(2,1)S(1)}, bf16[384,384]{1,0:T(8,128)(2,1)S(1)}, u32[]{:S(2)}, u32[]{:S(2)}) collective-permute-start(bf16[384,384]{1,0:T(8,128)(2,1)S(1)} %get-tuple-element.16), channel_id=1, source_target_pairs={{0,4},{4,0},{8,12},{12,8},{1,5},{5,1},{9,13},{13,9},{2,6},{6,2},{1... | collective-permute-start | bytes 884744 | tf_op jit(solution)/shard_map/ppermute | solution.py:22
  6.8 12.2 %collective-permute-start.4 = (bf16[384,384]{1,0:T(8,128)(2,1)S(1)}, bf16[384,384]{1,0:T(8,128)(2,1)S(1)}, u32[]{:S(2)}, u32[]{:S(2)}) collective-permute-start(bf16[384,384]{1,0:T(8,128)(2,1)S(1)} %get-tuple-element.17), channel_id=1, source_target_pairs={{0,8},{4,12},{8,0},{12,4},{1,9},{5,13},{9,1},{13,5},{2,10},{6,14},... | collective-permute-start | bytes 884744 | tf_op jit(solution)/shard_map/ppermute | solution.py:22
  9.1 18.7 %collective-permute-start.7 = (bf16[384,384]{1,0:T(8,128)(2,1)S(1)}, bf16[384,384]{1,0:T(8,128)(2,1)S(1)}, u32[]{:S(2)}, u32[]{:S(2)}) collective-permute-start(bf16[384,384]{1,0:T(8,128)(2,1)S(1)} %get-tuple-element.18), channel_id=1, source_target_pairs={{0,12},{4,8},{8,4},{12,0},{1,13},{5,9},{9,5},{13,1},{2,14},{6,10},... | collective-permute-start | bytes 884744 | tf_op jit(solution)/shard_map/ppermute | solution.py:22
  18.6 9.6 %collective-permute-start.2 = (bf16[320,384]{1,0:T(8,128)(2,1)S(1)}, bf16[320,384]{1,0:T(8,128)(2,1)S(1)}, u32[]{:S(2)}, u32[]{:S(2)}) collective-permute-start(bf16[320,384]{1,0:T(8,128)(2,1)S(1)} %pad_maximum_fusion.3), channel_id=1, source_target_pairs={{0,2},{1,3},{2,0},{3,1},{4,6},{5,7},{6,4},{7,5},{8,10},{9,11},{10,... | collective-permute-start | bytes 737288 | tf_op jit(solution)/shard_map/ppermute | solution.py:22
  19.1 14.9 %collective-permute-start.5 = (bf16[320,384]{1,0:T(8,128)(2,1)S(1)}, bf16[320,384]{1,0:T(8,128)(2,1)S(1)}, u32[]{:S(2)}, u32[]{:S(2)}) collective-permute-start(bf16[320,384]{1,0:T(8,128)(2,1)S(1)} %pad_maximum_fusion.4), channel_id=1, source_target_pairs={{0,2},{1,3},{2,0},{3,1},{4,6},{5,7},{6,4},{7,5},{8,10},{9,11},{10,... | collective-permute-start | bytes 737288 | tf_op jit(solution)/shard_map/ppermute | solution.py:22
  27.9 10.2 %collective-permute-start.8 = (bf16[320,384]{1,0:T(8,128)(2,1)S(1)}, bf16[320,384]{1,0:T(8,128)(2,1)S(1)}, u32[]{:S(2)}, u32[]{:S(2)}) collective-permute-start(bf16[320,384]{1,0:T(8,128)(2,1)S(1)} %pad_maximum_fusion.5), channel_id=1, source_target_pairs={{0,2},{1,3},{2,0},{3,1},{4,6},{5,7},{6,4},{7,5},{8,10},{9,11},{10,... | collective-permute-start | bytes 737288 | tf_op jit(solution)/shard_map/ppermute | solution.py:22
  28.3 13.8 %collective-permute-start.3 = (bf16[1152,384]{1,0:T(8,128)(2,1)S(1)}, bf16[1152,384]{1,0:T(8,128)(2,1)S(1)}, u32[]{:S(2)}, u32[]{:S(2)}) collective-permute-start(bf16[1152,384]{1,0:T(8,128)(2,1)S(1)} %get-tuple-element.56.refs_4_), channel_id=1, source_target_pairs={{0,1},{1,0},{2,3},{3,2},{4,5},{5,4},{6,7},{7,6},{8,9},{9,8},{10,11... | collective-permute-start | bytes 2654216 | tf_op jit(solution)/shard_map/ppermute | solution.py:22
  34.2 6.5 %collective-permute-start.6 = (bf16[576,384]{1,0:T(8,128)(2,1)S(1)}, bf16[576,384]{1,0:T(8,128)(2,1)S(1)}, u32[]{:S(2)}, u32[]{:S(2)}) collective-permute-start(bf16[576,384]{1,0:T(8,128)(2,1)S(1)} %pad_maximum_fusion.refs_6_), channel_id=1, source_target_pairs={{0,1},{1,0},{2,3},{3,2},{4,5},{5,4},{6,7},{7,6},{8,9},{9,8},{10,11... | collective-permute-start | bytes 1327112 | tf_op jit(solution)/shard_map/ppermute | solution.py:22
  38.1 3.9 %collective-permute-start.9 = (bf16[576,384]{1,0:T(8,128)(2,1)S(1)}, bf16[576,384]{1,0:T(8,128)(2,1)S(1)}, u32[]{:S(2)}, u32[]{:S(2)}) collective-permute-start(bf16[576,384]{1,0:T(8,128)(2,1)S(1)} %pad_maximum_fusion.1.refs_8_), channel_id=1, source_target_pairs={{0,1},{1,0},{2,3},{3,2},{4,5},{5,4},{6,7},{7,6},{8,9},{9,8},{10,11... | collective-permute-start | bytes 1327112 | tf_op jit(solution)/shard_map/ppermute | solution.py:22
  44.5 6.0 %collective-permute-start.12 = (bf16[4,32,384]{2,1,0:T(8,128)(2,1)S(1)}, bf16[4,32,384]{2,1,0:T(8,128)(2,1)S(1)}, u32[]{:S(2)}, u32[]{:S(2)}) collective-permute-start(bf16[4,32,384]{2,1,0:T(8,128)(2,1)S(1)} %get-tuple-element.22), channel_id=1, source_target_pairs={{0,12},{4,8},{8,4},{12,0},{1,13},{5,9},{9,5},{13,1},{2,14},{6,10},... | collective-permute-start | bytes 294920 | tf_op jit(solution)/shard_map/ppermute | solution.py:22
  46.7 10.7 %collective-permute-start.10 = (bf16[4,32,384]{2,1,0:T(8,128)(2,1)S(1)}, bf16[4,32,384]{2,1,0:T(8,128)(2,1)S(1)}, u32[]{:S(2)}, u32[]{:S(2)}) collective-permute-start(bf16[4,32,384]{2,1,0:T(8,128)(2,1)S(1)} %get-tuple-element.19), channel_id=1, source_target_pairs={{0,8},{4,12},{8,0},{12,4},{1,9},{5,13},{9,1},{13,5},{2,10},{6,14},... | collective-permute-start | bytes 294920 | tf_op jit(solution)/shard_map/ppermute | solution.py:22
  50.3 7.1 %collective-permute-start.11 = (bf16[4,32,384]{2,1,0:T(8,128)(2,1)S(1)}, bf16[4,32,384]{2,1,0:T(8,128)(2,1)S(1)}, u32[]{:S(2)}, u32[]{:S(2)}) collective-permute-start(bf16[4,32,384]{2,1,0:T(8,128)(2,1)S(1)} %get-tuple-element.20), channel_id=1, source_target_pairs={{0,4},{4,0},{8,12},{12,8},{1,5},{5,1},{9,13},{13,9},{2,6},{6,2},{1... | collective-permute-start | bytes 294920 | tf_op jit(solution)/shard_map/ppermute | solution.py:22
  50.5 6.9 %copy-start.2 = (bf16[3072,64]{0,1:T(8,128)(2,1)S(1)}, bf16[3072,64]{0,1:T(8,128)(2,1)}, u32[]{:S(2)}) copy-start(bf16[3072,64]{0,1:T(8,128)(2,1)} %param.15) | copy-start | bytes 1179652
  50.5 6.9 %copy-start.3 = (f32[3072]{0:T(1024)S(1)}, f32[3072]{0:T(1024)}, u32[]{:S(2)}) copy-start(f32[3072]{0:T(1024)} %param.14) | copy-start | bytes 36868
  50.5 6.9 %copy-start.4 = (f32[3072]{0:T(1024)S(1)}, f32[3072]{0:T(1024)}, u32[]{:S(2)}) copy-start(f32[3072]{0:T(1024)} %param.13) | copy-start | bytes 36868
  57.5 11.7 %copy-start.1 = (bf16[432,512]{1,0:T(8,128)(2,1)S(1)}, bf16[432,512]{1,0:T(8,128)(2,1)}, u32[]{:S(2)}) copy-start(bf16[432,512]{1,0:T(8,128)(2,1)} %w_ref.1) | copy-start | bytes 1327108
  57.5 11.7 %copy-start.5 = (f32[512]{0:T(512)S(1)}, f32[512]{0:T(512)}, u32[]{:S(2)}) copy-start(f32[512]{0:T(512)} %param.17) | copy-start | bytes 6148
  61.3 4.5 %collective-permute-start.13 = (bf16[128,32]{1,0:T(8,128)(2,1)S(1)}, bf16[128,32]{1,0:T(8,128)(2,1)S(1)}, u32[]{:S(2)}, u32[]{:S(2)}) collective-permute-start(bf16[128,32]{1,0:T(8,128)(2,1)S(1)} %get-tuple-element.24.odd_ref), channel_id=1, source_target_pairs={{0,1},{1,2},{2,3},{3,4},{4,5},{5,6},{6,7},{7,8},{8,9},{9,10},{10,1... | collective-permute-start | bytes 24584 | tf_op jit(solution)/shard_map/ppermute | solution.py:378
  63.9 5.2 %collective-permute-start.14 = (bf16[128,32]{1,0:T(8,128)(2,1)S(1)}, bf16[128,32]{1,0:T(8,128)(2,1)S(1)}, u32[]{:S(2)}, u32[]{:S(2)}) collective-permute-start(bf16[128,32]{1,0:T(8,128)(2,1)S(1)} %get-tuple-element.23.even_ref), channel_id=1, source_target_pairs={{1,0},{2,1},{3,2},{4,3},{5,4},{6,5},{7,6},{8,7},{9,8},{10,9},{11,1... | collective-permute-start | bytes 24584 | tf_op jit(solution)/shard_map/ppermute | solution.py:379

commit v11 on v10

--- a/solution.py
+++ b/solution.py
@@ -155,8 +155,14 @@
     tokens, width = lined.shape[0], o_refs[0].shape[2]
     for n, o_ref in enumerate(o_refs):
         lined[:, n * width : (n + 1) * width] = o_ref[...].reshape(tokens, width)
-    weights = jnp.concatenate([w[...] for w in w_refs], axis=0)
-    return jnp.dot(lined[...], weights, preferred_element_type=jnp.float32)
+    pieces = [(w, first) for w in w_refs for first in range(0, width, 128)]
+    total = None
+    for n in range(0, len(pieces), 2):
+        rows = [w[first : first + 128, :] for w, first in pieces[n : n + 2]]
+        lanes = lined[:, n * 128 : (n + len(rows)) * 128]
+        part = jnp.dot(lanes, jnp.concatenate(rows, axis=0), preferred_element_type=jnp.float32)
+        total = part if total is None else total + part
+    return total
 
 
 def projection_specs(attended, targets, tile):
@@ -193,26 +199,34 @@
 
 def final_kernel(where_ref, *refs, targets, planes, rows_dev):
     count = len(targets)
-    partial_ref, scale_ref, shift_ref, w_final_ref, even_ref, odd_ref, lined, projected = refs[2 * count :]
+    partial_ref, scale_ref, shift_ref, w_final_ref, even_ref, odd_ref, lined, projected, pivot, sums = refs[
+        2 * count :
+    ]
     step = pl.program_id(0)
     heads_at, plane_at = where_ref[0], where_ref[1]
     tokens = lined.shape[0]
     tile = partial_ref.shape[1]
-    projected[step] = partial_ref[...] + projection_of(refs[:count], refs[count : 2 * count], lined)
+    row = partial_ref[...] + projection_of(refs[:count], refs[count : 2 * count], lined)
+    projected[step] = row
+
+    @pl.when(step == 0)
+    def _():
+        pivot[...] = jnp.broadcast_to(jnp.mean(row, axis=1, keepdims=True), pivot.shape)
+        sums[...] = jnp.zeros_like(sums)
+
+    for first in range(0, tile, 128):
+        off = row[:, first : first + 128] - pivot[...]
+        sums[0] += off
+        sums[1] += off * off
 
     @pl.when(step == pl.num_programs(0) - 1)
     def _():
         steps = projected.shape[0]
         features = steps * tile
-        total = projected[0]
-        for i in range(1, steps):
-            total = total + projected[i]
-        mean = jnp.sum(total, axis=1, keepdims=True) * (1.0 / features)
-        squares = None
-        for i in range(steps):
-            centered = projected[i] - mean
-            squares = centered * centered if squares is None else squares + centered * centered
-        variance = jnp.sum(squares, axis=1, keepdims=True) * (1.0 / features)
+        off_mean = jnp.sum(sums[0], axis=1, keepdims=True) * (1.0 / features)
+        mean = pivot[:, :1] + off_mean
+        variance = jnp.sum(sums[1], axis=1, keepdims=True) * (1.0 / features) - off_mean * off_mean
+        variance = jnp.maximum(variance, 0.0)
         inverse = lax.rsqrt(variance + 1e-06)
         patches = None
         for i in range(steps):
@@ -268,6 +282,8 @@
             scratch_shapes=[
                 pltpu.VMEM((tokens, len(targets) * width), jnp.bfloat16),
                 pltpu.VMEM((steps, tokens, tile), jnp.float32),
+                pltpu.VMEM((tokens, 128), jnp.float32),
+                pltpu.VMEM((2, tokens, 128), jnp.float32),
             ],
         ),
         out_shape=[result] * 2,
@@ -363,10 +379,9 @@
             )
     asked = [asked[r] for r in range(groups)]
 
-    first, second = (3, 2), (1, 0)
     near, far = (0, 3), (2, 1)
     results = {}
-    for targets in (first, second):
+    for targets in ((3,), (2,), (1, 0)):
         for t, o in zip(targets, attend(asked, keys_values, targets, planes)):
             results[t] = o if t == 0 else swap(o, "heads", t)
     partial = project(where, [results[t] for t in near], near, w_out, 512)

time: 72.1 us -> 72.1 us (level)
  waiting for transfers between devices: 25.8 us -> 24.7 us
  Pallas kernels: 14 us -> 14.8 us
  starting transfers between devices: 28.1 us -> 28.9 us
    ppermute x13, waiting for transfers between devices: 22.5 us -> 21.4 us  [swap(): return lax.ppermute(source, axis, [(i, i ^ distance) for i in range(count)])]
    ppermute x1, starting transfers between devices: 2.61 us -> 3.38 us  [shards(): left = lax.ppermute(odd, both, [(i, i + 1) for i in range(devices - 1)])]
    pallas_call x2 -> x3, Pallas kernels: 4.53 us -> 5.12 us  [attend(): pl.pallas_call(functools.partial(attend_kernel, sources=sources, planes=p...]
  transfers between devices with their start and end apart: 15 -> 15, of which waited for: 6 -> 7; matrix products, arithmetic and copies ran while one was open for 1% -> 1% of each run, Pallas kernels for 7% -> 9%
where the time goes in v11:
time: 72.1 us; the launch traced here: 71.9 us
  starting transfers between devices  28.9 us (40%)
  waiting for transfers between devices  24.7 us (34%)
  Pallas kernels  14.8 us (21%)
  local copies, waits for them, and re-layouts  2.81 us (4%)
    ppermute x13, starting transfers between devices, swap(): return lax.ppermute(source, axis, [(i, i ^ distance) for i in range(count)])  23.6 us
    ppermute x13, waiting for transfers between devices, swap(): return lax.ppermute(source, axis, [(i, i ^ distance) for i in range(count)])  21.4 us
    pallas_call x3, Pallas kernels, attend(): pl.pallas_call(functools.partial(attend_kernel, sources=sources, planes=p...  5.12 us
    pallas_call x1, Pallas kernels, final_layer(): pl.pallas_call(functools.partial(final_kernel, targets=targets, planes=pl...  4.03 us
    ppermute x1, starting transfers between devices, shards(): left = lax.ppermute(odd, both, [(i, i + 1) for i in range(devices - 1)])  3.38 us
    ppermute x1, waiting for transfers between devices, shards(): right = lax.ppermute(even, both, [(i + 1, i) for i in range(devices - 1)])  3.29 us
    pallas_call x1, Pallas kernels, project(): pl.pallas_call(functools.partial(project_kernel, targets=targets), grid_s...  2.66 us
    dynamic_slice x2, local copies, waits for them, and re-layouts, cut(): lax.dynamic_slice_in_dim(source, (lax.axis_index('heads') ^ r) * width, w...  2.39 us
  transfers between devices with their start and end apart: 15, of which 7 were waited for; matrix products, arithmetic and copies ran while one was open for 1% of the time, Pallas kernels for 9%

profile of v11, /device:TPU:1, one launch (start us, length us, event | category | flops | bytes accessed | tf_op | source)
XLA Modules:
  0.0 71.9 jit_solution(6326482795654434333)
XLA Ops:
  0.0 1.1 %constant_dynamic-slice_fusion.8 = (bf16[128,384]{1,0:T(8,128)(2,1)S(1)}, bf16[128,384]{1,0:T(8,128)(2,1)S(1)}, bf16[128,384]{1,0:T(8,128)(2,1)S(1)}, bf16[128,384]{1,0:T(8,128)(2,1)S(1)}) fusion(bf16[128,1536]{1,0:T(8,128)(2,1)} %param.9, s32[]{:T(128)S(6)} %select_n.11, s32[]{:T(128)S(6)} %select_n.9, s32[]{:T(128)S(6)} %select_n.8, s32[]{:T(128)S(6)} %select_n.10), kind=kLoop, calls=%fused_computation.26 | loop fusion | bytes 786448 | tf_op jit(solution)/shard_map/dynamic_slice | solution.py:46
  1.1 1.3 %constant_dynamic-slice_fusion = (bf16[128,384]{1,0:T(8,128)(2,1)S(1)}, bf16[128,384]{1,0:T(8,128)(2,1)S(1)}, bf16[128,384]{1,0:T(8,128)(2,1)S(1)}, bf16[128,384...) fusion(bf16[128,1536]{1,0:T(8,128)(2,1)} %param.11, ...), kind=kLoop, calls=%fused_computation.18 | loop fusion | bytes 1572880 | tf_op jit(solution)/shard_map/dynamic_slice | solution.py:46
  2.4 0.1 pad_add_fusion.where_ref
  2.5 0.0 slice-start
  2.5 0.8 %shard_map.91 = (bf16[384,384]{1,0:T(8,128)(2,1)S(1)}, bf16[384,384]{1,0:T(8,128)(2,1)S(1)}, bf16[384,384]{1,0:T(8,128)(2,1)S(1)}, bf16[384,384]{1,0:T(8,128)(2,1)S(1)}) custom-call(s32[4]{0:T(128)S(1)} %pad_add_fusion.where_ref, bf16[128,384]{1,0:T(8,128)(2,1)S(1)} %get-tuple-element.33.refs_0_, bf16[128,384]{1,0:T(8,128)(2,1)S(1)} %get-tuple-element.32.refs_1_, ...), custom_call_target="tpu_custom_call" | custom-call | tf_op jit(solution)/shard_map/pallas_call | solution.py:51
  3.4 2.1 %collective-permute-start = (bf16[320,384]{1,0:T(8,128)(2,1)S(1)}, bf16[320,384]{1,0:T(8,128)(2,1)S(1)}, u32[]{:S(2)}, u32[]{:S(2)}) collective-permute-start(bf16[320,384]{1,0:T(8,128)(2,1)S(1)} %pad_maximum_fusion.2), channel_id=1, source_target_pairs={{0,2},{1,3},{2,0},{3,1},{4,6},{5,7},{6,4},{7,5},{8,10},{9,11},{10,... | collective-permute-start | bytes 737288 | tf_op jit(solution)/shard_map/ppermute | solution.py:22
  5.5 1.3 %collective-permute-start.1 = (bf16[384,384]{1,0:T(8,128)(2,1)S(1)}, bf16[384,384]{1,0:T(8,128)(2,1)S(1)}, u32[]{:S(2)}, u32[]{:S(2)}) collective-permute-start(bf16[384,384]{1,0:T(8,128)(2,1)S(1)} %get-tuple-element.14), channel_id=1, source_target_pairs={{0,4},{4,0},{8,12},{12,8},{1,5},{5,1},{9,13},{13,9},{2,6},{6,2},{1... | collective-permute-start | bytes 884744 | tf_op jit(solution)/shard_map/ppermute | solution.py:22
  6.8 2.3 %collective-permute-start.4 = (bf16[384,384]{1,0:T(8,128)(2,1)S(1)}, bf16[384,384]{1,0:T(8,128)(2,1)S(1)}, u32[]{:S(2)}, u32[]{:S(2)}) collective-permute-start(bf16[384,384]{1,0:T(8,128)(2,1)S(1)} %get-tuple-element.15), channel_id=1, source_target_pairs={{0,8},{4,12},{8,0},{12,4},{1,9},{5,13},{9,1},{13,5},{2,10},{6,14},... | collective-permute-start | bytes 884744 | tf_op jit(solution)/shard_map/ppermute | solution.py:22
  9.1 0.0 collective-permute-start.7
  9.1 2.1 %collective-permute-done = bf16[320,384]{1,0:T(8,128)(2,1)S(1)} collective-permute-done((bf16[320,384]{1,0:T(8,128)(2,1)S(1)}, bf16[320,384]{1,0:T(8,128)(2,1)S(1)}, u32[]{:S(2)}, u32[]{:S(2)}) %collective-permute-start) | collective-permute-done | bytes 245792 | tf_op jit(solution)/shard_map/ppermute | solution.py:22
  11.2 7.2 %collective-permute-done.1 = bf16[384,384]{1,0:T(8,128)(2,1)S(1)} collective-permute-done((bf16[384,384]{1,0:T(8,128)(2,1)S(1)}, bf16[384,384]{1,0:T(8,128)(2,1)S(1)}, u32[]{:S(2)}, u32[]{:S(2)}) %collective-permute-start.1) | collective-permute-done | bytes 294944 | tf_op jit(solution)/shard_map/ppermute | solution.py:22
  18.5 0.1 fusion.5
  18.6 0.5 collective-permute-start.2
  19.1 0.0 collective-permute-done.4
  19.1 1.1 %collective-permute-start.5 = (bf16[320,384]{1,0:T(8,128)(2,1)S(1)}, bf16[320,384]{1,0:T(8,128)(2,1)S(1)}, u32[]{:S(2)}, u32[]{:S(2)}) collective-permute-start(bf16[320,384]{1,0:T(8,128)(2,1)S(1)} %pad_maximum_fusion.4), channel_id=1, source_target_pairs={{0,2},{1,3},{2,0},{3,1},{4,6},{5,7},{6,4},{7,5},{8,10},{9,11},{10,... | collective-permute-start | bytes 737288 | tf_op jit(solution)/shard_map/ppermute | solution.py:22
  20.3 7.5 %collective-permute-done.7 = bf16[384,384]{1,0:T(8,128)(2,1)S(1)} collective-permute-done((bf16[384,384]{1,0:T(8,128)(2,1)S(1)}, bf16[384,384]{1,0:T(8,128)(2,1)S(1)}, u32[]{:S(2)}, u32[]{:S(2)}) %collective-permute-start.7) | collective-permute-done | bytes 294944 | tf_op jit(solution)/shard_map/ppermute | solution.py:22
  27.9 0.3 collective-permute-start.8
  28.2 0.0 collective-permute-done.2
  28.3 5.7 %collective-permute-start.3 = (bf16[1152,384]{1,0:T(8,128)(2,1)S(1)}, bf16[1152,384]{1,0:T(8,128)(2,1)S(1)}, u32[]{:S(2)}, u32[]{:S(2)}) collective-permute-start(bf16[1152,384]{1,0:T(8,128)(2,1)S(1)} %get-tuple-element.52.refs_4_), channel_id=1, source_target_pairs={{0,1},{1,0},{2,3},{3,2},{4,5},{5,4},{6,7},{7,6},{8,9},{9,8},{10,11... | collective-permute-start | bytes 2654216 | tf_op jit(solution)/shard_map/ppermute | solution.py:22
  34.1 0.0 collective-permute-done.5
  34.1 0.0 slice-start.1
  34.2 3.9 %collective-permute-start.6 = (bf16[576,384]{1,0:T(8,128)(2,1)S(1)}, bf16[576,384]{1,0:T(8,128)(2,1)S(1)}, u32[]{:S(2)}, u32[]{:S(2)}) collective-permute-start(bf16[576,384]{1,0:T(8,128)(2,1)S(1)} %pad_maximum_fusion.refs_6_), channel_id=1, source_target_pairs={{0,1},{1,0},{2,3},{3,2},{4,5},{5,4},{6,7},{7,6},{8,9},{9,8},{10,11... | collective-permute-start | bytes 1327112 | tf_op jit(solution)/shard_map/ppermute | solution.py:22
  38.0 0.0 collective-permute-done.8
  38.1 2.5 %collective-permute-start.9 = (bf16[576,384]{1,0:T(8,128)(2,1)S(1)}, bf16[576,384]{1,0:T(8,128)(2,1)S(1)}, u32[]{:S(2)}, u32[]{:S(2)}) collective-permute-start(bf16[576,384]{1,0:T(8,128)(2,1)S(1)} %pad_maximum_fusion.1.refs_8_), channel_id=1, source_target_pairs={{0,1},{1,0},{2,3},{3,2},{4,5},{5,4},{6,7},{7,6},{8,9},{9,8},{10,11... | collective-permute-start | bytes 1327112 | tf_op jit(solution)/shard_map/ppermute | solution.py:22
  40.7 0.0 collective-permute-done.6.refs_7_
  40.7 1.4 %collective-permute-done.9.refs_9_ = bf16[576,384]{1,0:T(8,128)(2,1)S(1)} collective-permute-done((bf16[576,384]{1,0:T(8,128)(2,1)S(1)}, bf16[576,384]{1,0:T(8,128)(2,1)S(1)}, u32[]{:S(2)}, u32[]{:S(2)}) %collective-permute-start.9) | collective-permute-done | bytes 442400 | tf_op jit(solution)/shard_map/ppermute | solution.py:22
  42.1 0.0 collective-permute-done.3.refs_5_
  42.2 1.4 %shard_map.94 = bf16[4,32,384]{2,1,0:T(8,128)(2,1)S(1)} custom-call(bf16[128,384]{1,0:T(8,128)(2,1)S(1)} %pad_maximum_fusion.6.refs_0_, bf16[128,384]{1,0:T(8,128)(2,1)S(1)} %pad_maximum_fusion.7.refs_1_, bf16[128,384]{1,0:T(8,128)(2,1)S(1)} %pad_maximum_fusion.8.refs_2_, bf16[128,384]{1,0:T(8,128)(2,1)S(1)} %pad_maximum_fusion.9.refs_3_, ...), custom_call_target="tpu_custom_call" | custom-call | tf_op jit(solution)/shard_map/pallas_call | solution.py:135
  43.6 0.0 slice-start.2
  43.7 2.3 %collective-permute-start.12 = (bf16[4,32,384]{2,1,0:T(8,128)(2,1)S(1)}, bf16[4,32,384]{2,1,0:T(8,128)(2,1)S(1)}, u32[]{:S(2)}, u32[]{:S(2)}) collective-permute-start(bf16[4,32,384]{2,1,0:T(8,128)(2,1)S(1)} %shard_map.94), channel_id=1, source_target_pairs={{0,12},{4,8},{8,4},{12,0},{1,13},{5,9},{9,5},{13,1},{2,14},{6,10},... | collective-permute-start | bytes 294920 | tf_op jit(solution)/shard_map/ppermute | solution.py:22
  45.9 1.4 %shard_map.92 = bf16[4,32,384]{2,1,0:T(8,128)(2,1)S(1)} custom-call(bf16[128,384]{1,0:T(8,128)(2,1)S(1)} %pad_maximum_fusion.6.refs_0_, bf16[128,384]{1,0:T(8,128)(2,1)S(1)} %pad_maximum_fusion.7.refs_1_, bf16[128,384]{1,0:T(8,128)(2,1)S(1)} %pad_maximum_fusion.8.refs_2_, bf16[128,384]{1,0:T(8,128)(2,1)S(1)} %pad_maximum_fusion.9.refs_3_, ...), custom_call_target="tpu_custom_call" | custom-call | tf_op jit(solution)/shard_map/pallas_call | solution.py:135
  47.3 1.4 %collective-permute-start.10 = (bf16[4,32,384]{2,1,0:T(8,128)(2,1)S(1)}, bf16[4,32,384]{2,1,0:T(8,128)(2,1)S(1)}, u32[]{:S(2)}, u32[]{:S(2)}) collective-permute-start(bf16[4,32,384]{2,1,0:T(8,128)(2,1)S(1)} %shard_map.92), channel_id=1, source_target_pairs={{0,8},{4,12},{8,0},{12,4},{1,9},{5,13},{9,1},{13,5},{2,10},{6,14},... | collective-permute-start | bytes 294920 | tf_op jit(solution)/shard_map/ppermute | solution.py:22
  48.7 2.3 %shard_map.93 = (bf16[4,32,384]{2,1,0:T(8,128)(2,1)S(1)}, bf16[4,32,384]{2,1,0:T(8,128)(2,1)S(1)}) custom-call(bf16[128,384]{1,0:T(8,128)(2,1)S(1)} %pad_maximum_fusion.6.refs_0_, bf16[128,384]{1,0:T(8,128)(2,1)S(1)} %pad_maximum_fusion.7.refs_1_, bf16[128,384]{1,0:T(8,128)(2,1)S(1)} %pad_maximum_fusion.8.refs_2_, ...), custom_call_target="tpu_custom_call" | custom-call | tf_op jit(solution)/shard_map/pallas_call | solution.py:135
  51.0 0.2 collective-permute-start.11
  51.1 0.0 collective-permute-done.12.refs_1_
  51.2 0.0 slice-done
  51.2 0.0 slice-done.1
  51.2 0.0 slice-done.2
  51.2 0.0 copy-start.1
  51.2 0.0 copy-start.2
  51.2 0.0 copy-start.3
  51.2 2.7 %shard_map.95.refs_4_ = f32[6,128,512]{2,1,0:T(8,128)S(1)} custom-call(s32[4]{0:T(128)S(1)} %pad_add_fusion.where_ref, bf16[4,32,384]{2,1,0:T(8,128)(2,1)S(1)} %get-tuple-element.18.refs_0_, bf16[4,32,384]{2,1,0:T(8,128)(2,1)S(1)} %collective-permute-done.12.refs_1_, bf16[1536,3072]{1,0:T(8,128)(2,1)S(1)} %bitcast.8, bf16[1536,3072]{1,0:T(8,128)(2,1)S(1)} %bitcast.8), custom_call_target="tpu_custom_call" | custom-call | tf_op jit(solution)/shard_map/pallas_call | solution.py:186
  53.9 2.7 %collective-permute-done.10.refs_0_ = bf16[4,32,384]{2,1,0:T(8,128)(2,1)S(1)} collective-permute-done((bf16[4,32,384]{2,1,0:T(8,128)(2,1)S(1)}, bf16[4,32,384]{2,1,0:T(8,128)(2,1)S(1)}, u32[]{:S(2)}, u32[]{:S(2)}) %collective-permute-start.10) | collective-permute-done | bytes 98336 | tf_op jit(solution)/shard_map/ppermute | solution.py:22
  56.6 0.4 collective-permute-done.11.refs_1_
  57.0 0.0 copy-done.1
  57.0 0.0 copy-done.2
  57.0 0.0 copy-done.3
  57.0 0.0 copy-start
  57.0 0.0 copy-start.4
  57.0 4.0 %shard_map.96 = (bf16[128,32]{1,0:T(8,128)(2,1)S(1)}, bf16[128,32]{1,0:T(8,128)(2,1)S(1)}) custom-call(s32[4]{0:T(128)S(1)} %pad_add_fusion.where_ref, bf16[4,32,384]{2,1,0:T(8,128)(2,1)S(1)} %collective-permute-done.10.refs_0_, bf16[4,32,384]{2,1,0:T(8,128)(2,1)S(1)} %collective-permute-done.11.refs_1_, bf16[1536,3072]{1,0:T(8,128)(2,1)S(1)} %bitcast.8, ...), custom_call_target="tpu_custom_call" | custom-call | tf_op jit(solution)/shard_map/pallas_call | solution.py:269
  61.1 3.4 %collective-permute-start.13 = (bf16[128,32]{1,0:T(8,128)(2,1)S(1)}, bf16[128,32]{1,0:T(8,128)(2,1)S(1)}, u32[]{:S(2)}, u32[]{:S(2)}) collective-permute-start(bf16[128,32]{1,0:T(8,128)(2,1)S(1)} %get-tuple-element.20.odd_ref), channel_id=1, source_target_pairs={{0,1},{1,2},{2,3},{3,4},{4,5},{5,6},{6,7},{7,8},{8,9},{9,10},{10,1... | collective-permute-start | bytes 24584 | tf_op jit(solution)/shard_map/ppermute | solution.py:393
  64.5 1.9 %collective-permute-start.14 = (bf16[128,32]{1,0:T(8,128)(2,1)S(1)}, bf16[128,32]{1,0:T(8,128)(2,1)S(1)}, u32[]{:S(2)}, u32[]{:S(2)}) collective-permute-start(bf16[128,32]{1,0:T(8,128)(2,1)S(1)} %get-tuple-element.19.even_ref), channel_id=1, source_target_pairs={{1,0},{2,1},{3,2},{4,3},{5,4},{6,5},{7,6},{8,7},{9,8},{10,9},{11,1... | collective-permute-start | bytes 24584 | tf_op jit(solution)/shard_map/ppermute | solution.py:394
  66.4 0.0 collective-permute-done.13.left_ref
  66.4 3.3 %collective-permute-done.14.right_ref = bf16[128,32]{1,0:T(8,128)(2,1)S(1)} collective-permute-done((bf16[128,32]{1,0:T(8,128)(2,1)S(1)}, bf16[128,32]{1,0:T(8,128)(2,1)S(1)}, u32[]{:S(2)}, u32[]{:S(2)}) %collective-permute-start.14) | collective-permute-done | bytes 8224 | tf_op jit(solution)/shard_map/ppermute | solution.py:394
  69.7 0.0 copy-done
  69.7 0.0 copy-done.4
  69.7 2.2 %shard_map.97 = bf16[4,2,64,512]{3,2,1,0:T(8,128)(2,1)} custom-call(s32[4]{0:T(128)S(1)} %pad_add_fusion.where_ref, bf16[128,32]{1,0:T(8,128)(2,1)S(1)} %get-tuple-element.19.even_ref, bf16[128,32]{1,0:T(8,128)(2,1)S(1)} %get-tuple-element.20.odd_ref, bf16[128,32]{1,0:T(8,128)(2,1)S(1)} %collective-permute-done.13.left_ref, ...), custom_call_target="tpu_custom_call" | custom-call | tf_op jit(solution)/shard_map/pallas_call | solution.py:332
  (33 shorter events, 0.6 us)
Async XLA Ops:
  2.5 48.7 %slice-start = ((s8[9437184]{0:T(1024)(128)(4,1)}), s8[4194304]{0:T(1024)(128)(4,1)S(1)}, s32[]{:S(2)}) async-start(s8[9437184]{0:T(1024)(128)(4,1)} %bitcast.7), calls=%async_computation | async-start | bytes 8388608
  3.4 7.8 %collective-permute-start = (bf16[320,384]{1,0:T(8,128)(2,1)S(1)}, bf16[320,384]{1,0:T(8,128)(2,1)S(1)}, u32[]{:S(2)}, u32[]{:S(2)}) collective-permute-start(bf16[320,384]{1,0:T(8,128)(2,1)S(1)} %pad_maximum_fusion.2), channel_id=1, source_target_pairs={{0,2},{1,3},{2,0},{3,1},{4,6},{5,7},{6,4},{7,5},{8,10},{9,11},{10,... | collective-permute-start | bytes 737288 | tf_op jit(solution)/shard_map/ppermute | solution.py:22
  5.5 13.0 %collective-permute-start.1 = (bf16[384,384]{1,0:T(8,128)(2,1)S(1)}, bf16[384,384]{1,0:T(8,128)(2,1)S(1)}, u32[]{:S(2)}, u32[]{:S(2)}) collective-permute-start(bf16[384,384]{1,0:T(8,128)(2,1)S(1)} %get-tuple-element.14), channel_id=1, source_target_pairs={{0,4},{4,0},{8,12},{12,8},{1,5},{5,1},{9,13},{13,9},{2,6},{6,2},{1... | collective-permute-start | bytes 884744 | tf_op jit(solution)/shard_map/ppermute | solution.py:22
  6.8 12.2 %collective-permute-start.4 = (bf16[384,384]{1,0:T(8,128)(2,1)S(1)}, bf16[384,384]{1,0:T(8,128)(2,1)S(1)}, u32[]{:S(2)}, u32[]{:S(2)}) collective-permute-start(bf16[384,384]{1,0:T(8,128)(2,1)S(1)} %get-tuple-element.15), channel_id=1, source_target_pairs={{0,8},{4,12},{8,0},{12,4},{1,9},{5,13},{9,1},{13,5},{2,10},{6,14},... | collective-permute-start | bytes 884744 | tf_op jit(solution)/shard_map/ppermute | solution.py:22
  9.1 18.7 %collective-permute-start.7 = (bf16[384,384]{1,0:T(8,128)(2,1)S(1)}, bf16[384,384]{1,0:T(8,128)(2,1)S(1)}, u32[]{:S(2)}, u32[]{:S(2)}) collective-permute-start(bf16[384,384]{1,0:T(8,128)(2,1)S(1)} %get-tuple-element.16), channel_id=1, source_target_pairs={{0,12},{4,8},{8,4},{12,0},{1,13},{5,9},{9,5},{13,1},{2,14},{6,10},... | collective-permute-start | bytes 884744 | tf_op jit(solution)/shard_map/ppermute | solution.py:22
  18.6 9.6 %collective-permute-start.2 = (bf16[320,384]{1,0:T(8,128)(2,1)S(1)}, bf16[320,384]{1,0:T(8,128)(2,1)S(1)}, u32[]{:S(2)}, u32[]{:S(2)}) collective-permute-start(bf16[320,384]{1,0:T(8,128)(2,1)S(1)} %pad_maximum_fusion.3), channel_id=1, source_target_pairs={{0,2},{1,3},{2,0},{3,1},{4,6},{5,7},{6,4},{7,5},{8,10},{9,11},{10,... | collective-permute-start | bytes 737288 | tf_op jit(solution)/shard_map/ppermute | solution.py:22
  19.1 14.9 %collective-permute-start.5 = (bf16[320,384]{1,0:T(8,128)(2,1)S(1)}, bf16[320,384]{1,0:T(8,128)(2,1)S(1)}, u32[]{:S(2)}, u32[]{:S(2)}) collective-permute-start(bf16[320,384]{1,0:T(8,128)(2,1)S(1)} %pad_maximum_fusion.4), channel_id=1, source_target_pairs={{0,2},{1,3},{2,0},{3,1},{4,6},{5,7},{6,4},{7,5},{8,10},{9,11},{10,... | collective-permute-start | bytes 737288 | tf_op jit(solution)/shard_map/ppermute | solution.py:22
  27.9 10.2 %collective-permute-start.8 = (bf16[320,384]{1,0:T(8,128)(2,1)S(1)}, bf16[320,384]{1,0:T(8,128)(2,1)S(1)}, u32[]{:S(2)}, u32[]{:S(2)}) collective-permute-start(bf16[320,384]{1,0:T(8,128)(2,1)S(1)} %pad_maximum_fusion.5), channel_id=1, source_target_pairs={{0,2},{1,3},{2,0},{3,1},{4,6},{5,7},{6,4},{7,5},{8,10},{9,11},{10,... | collective-permute-start | bytes 737288 | tf_op jit(solution)/shard_map/ppermute | solution.py:22
  28.3 13.8 %collective-permute-start.3 = (bf16[1152,384]{1,0:T(8,128)(2,1)S(1)}, bf16[1152,384]{1,0:T(8,128)(2,1)S(1)}, u32[]{:S(2)}, u32[]{:S(2)}) collective-permute-start(bf16[1152,384]{1,0:T(8,128)(2,1)S(1)} %get-tuple-element.52.refs_4_), channel_id=1, source_target_pairs={{0,1},{1,0},{2,3},{3,2},{4,5},{5,4},{6,7},{7,6},{8,9},{9,8},{10,11... | collective-permute-start | bytes 2654216 | tf_op jit(solution)/shard_map/ppermute | solution.py:22
  34.1 17.1 %slice-start.1 = ((s8[9437184]{0:T(1024)(128)(4,1)}), s8[4194304]{0:T(1024)(128)(4,1)S(1)}, s32[]{:S(2)}) async-start(s8[9437184]{0:T(1024)(128)(4,1)} %bitcast.7), calls=%async_computation.1 | async-start | bytes 8388608
  34.2 6.5 %collective-permute-start.6 = (bf16[576,384]{1,0:T(8,128)(2,1)S(1)}, bf16[576,384]{1,0:T(8,128)(2,1)S(1)}, u32[]{:S(2)}, u32[]{:S(2)}) collective-permute-start(bf16[576,384]{1,0:T(8,128)(2,1)S(1)} %pad_maximum_fusion.refs_6_), channel_id=1, source_target_pairs={{0,1},{1,0},{2,3},{3,2},{4,5},{5,4},{6,7},{7,6},{8,9},{9,8},{10,11... | collective-permute-start | bytes 1327112 | tf_op jit(solution)/shard_map/ppermute | solution.py:22
  38.1 3.9 %collective-permute-start.9 = (bf16[576,384]{1,0:T(8,128)(2,1)S(1)}, bf16[576,384]{1,0:T(8,128)(2,1)S(1)}, u32[]{:S(2)}, u32[]{:S(2)}) collective-permute-start(bf16[576,384]{1,0:T(8,128)(2,1)S(1)} %pad_maximum_fusion.1.refs_8_), channel_id=1, source_target_pairs={{0,1},{1,0},{2,3},{3,2},{4,5},{5,4},{6,7},{7,6},{8,9},{9,8},{10,11... | collective-permute-start | bytes 1327112 | tf_op jit(solution)/shard_map/ppermute | solution.py:22
  43.6 7.5 %slice-start.2 = ((s8[9437184]{0:T(1024)(128)(4,1)}), s8[1048576]{0:T(1024)(128)(4,1)S(1)}, s32[]{:S(2)}) async-start(s8[9437184]{0:T(1024)(128)(4,1)} %bitcast.7), calls=%async_computation.2 | async-start | bytes 2097152
  43.7 7.5 %collective-permute-start.12 = (bf16[4,32,384]{2,1,0:T(8,128)(2,1)S(1)}, bf16[4,32,384]{2,1,0:T(8,128)(2,1)S(1)}, u32[]{:S(2)}, u32[]{:S(2)}) collective-permute-start(bf16[4,32,384]{2,1,0:T(8,128)(2,1)S(1)} %shard_map.94), channel_id=1, source_target_pairs={{0,12},{4,8},{8,4},{12,0},{1,13},{5,9},{9,5},{13,1},{2,14},{6,10},... | collective-permute-start | bytes 294920 | tf_op jit(solution)/shard_map/ppermute | solution.py:22
  47.3 9.3 %collective-permute-start.10 = (bf16[4,32,384]{2,1,0:T(8,128)(2,1)S(1)}, bf16[4,32,384]{2,1,0:T(8,128)(2,1)S(1)}, u32[]{:S(2)}, u32[]{:S(2)}) collective-permute-start(bf16[4,32,384]{2,1,0:T(8,128)(2,1)S(1)} %shard_map.92), channel_id=1, source_target_pairs={{0,8},{4,12},{8,0},{12,4},{1,9},{5,13},{9,1},{13,5},{2,10},{6,14},... | collective-permute-start | bytes 294920 | tf_op jit(solution)/shard_map/ppermute | solution.py:22
  51.0 6.0 %collective-permute-start.11 = (bf16[4,32,384]{2,1,0:T(8,128)(2,1)S(1)}, bf16[4,32,384]{2,1,0:T(8,128)(2,1)S(1)}, u32[]{:S(2)}, u32[]{:S(2)}) collective-permute-start(bf16[4,32,384]{2,1,0:T(8,128)(2,1)S(1)} %get-tuple-element.17), channel_id=1, source_target_pairs={{0,4},{4,0},{8,12},{12,8},{1,5},{5,1},{9,13},{13,9},{2,6},{6,2},{1... | collective-permute-start | bytes 294920 | tf_op jit(solution)/shard_map/ppermute | solution.py:22
  51.2 5.8 %copy-start.1 = (bf16[3072,64]{0,1:T(8,128)(2,1)S(1)}, bf16[3072,64]{0,1:T(8,128)(2,1)}, u32[]{:S(2)}) copy-start(bf16[3072,64]{0,1:T(8,128)(2,1)} %param.15) | copy-start | bytes 1179652
  51.2 5.8 %copy-start.2 = (f32[3072]{0:T(1024)S(1)}, f32[3072]{0:T(1024)}, u32[]{:S(2)}) copy-start(f32[3072]{0:T(1024)} %param.14) | copy-start | bytes 36868
  51.2 5.8 %copy-start.3 = (f32[3072]{0:T(1024)S(1)}, f32[3072]{0:T(1024)}, u32[]{:S(2)}) copy-start(f32[3072]{0:T(1024)} %param.13) | copy-start | bytes 36868
  57.0 12.7 %copy-start = (bf16[432,512]{1,0:T(8,128)(2,1)S(1)}, bf16[432,512]{1,0:T(8,128)(2,1)}, u32[]{:S(2)}) copy-start(bf16[432,512]{1,0:T(8,128)(2,1)} %w_ref.1) | copy-start | bytes 1327108
  57.0 12.7 %copy-start.4 = (f32[512]{0:T(512)S(1)}, f32[512]{0:T(512)}, u32[]{:S(2)}) copy-start(f32[512]{0:T(512)} %param.17) | copy-start | bytes 6148
  61.1 5.3 %collective-permute-start.13 = (bf16[128,32]{1,0:T(8,128)(2,1)S(1)}, bf16[128,32]{1,0:T(8,128)(2,1)S(1)}, u32[]{:S(2)}, u32[]{:S(2)}) collective-permute-start(bf16[128,32]{1,0:T(8,128)(2,1)S(1)} %get-tuple-element.20.odd_ref), channel_id=1, source_target_pairs={{0,1},{1,2},{2,3},{3,4},{4,5},{5,6},{6,7},{7,8},{8,9},{9,10},{10,1... | collective-permute-start | bytes 24584 | tf_op jit(solution)/shard_map/ppermute | solution.py:393
  64.5 5.2 %collective-permute-start.14 = (bf16[128,32]{1,0:T(8,128)(2,1)S(1)}, bf16[128,32]{1,0:T(8,128)(2,1)S(1)}, u32[]{:S(2)}, u32[]{:S(2)}) collective-permute-start(bf16[128,32]{1,0:T(8,128)(2,1)S(1)} %get-tuple-element.19.even_ref), channel_id=1, source_target_pairs={{1,0},{2,1},{3,2},{4,3},{5,4},{6,5},{7,6},{8,7},{9,8},{10,9},{11,1... | collective-permute-start | bytes 24584 | tf_op jit(solution)/shard_map/ppermute | solution.py:394

commit v12 on v6

--- a/solution.py
+++ b/solution.py
@@ -11,12 +11,10 @@
 
 HEAD_DIM = 128
 HEAD_GROUPS = 4
+CHUNKS = ((0, 1), (1, 3))
 LATENT_CH = 16
 FRAMES = 4
 VMEM_LIMIT = 16 * 1024 * 1024
-VMEM_WHOLE = 63 * 1024 * 1024
-CHUNKS = ((0, 3),)
-VMEM_WHOLE = 63 * 1024 * 1024
 EXP2_SCALE = math.log2(math.e) / math.sqrt(HEAD_DIM)
 
 
@@ -25,39 +23,46 @@
     return lax.ppermute(source, axis, [(i, i ^ distance) for i in range(count)])
 
 
-def bundle_kernel(q_ref, k_ref, v_ref, *out_refs, groups, planes, cuts):
-    tokens, width = q_ref.shape
-    group_width = width // groups
+def bundle_kernel(where_ref, *refs, groups, planes, distances):
+    tokens = refs[0].shape[0]
     rows_dev = tokens // (groups * planes)
-    heads_at, plane_at = lax.axis_index("heads"), lax.axis_index("plane")
     to = lax.broadcasted_iota(jnp.int32, (tokens, tokens), 0)
     at = lax.broadcasted_iota(jnp.int32, (tokens, tokens), 1)
     j, t, row = to // (groups * rows_dev), (to // rows_dev) % groups, to % rows_dev
-    for (r, low, high), out_ref in zip(cuts, out_refs):
-        group = heads_at ^ r
-        first = pl.multiple_of(group * group_width + low * HEAD_DIM, HEAD_DIM)
-        lanes = pl.ds(first, (high - low) * HEAD_DIM)
-        place = row * (groups * planes) + (t ^ group) * planes + (j ^ plane_at)
+    count = len(distances)
+    cut = [refs[n * count : (n + 1) * count] for n in range(3)]
+    out_refs = refs[3 * count :]
+    for n, (r, q_ref, k_ref, v_ref) in enumerate(zip(distances, *cut)):
+        group = where_ref[0] ^ r
+        place = row * (groups * planes) + (t ^ group) * planes + (j ^ where_ref[1])
         order = (at == place).astype(jnp.bfloat16)
-        out_ref[:tokens] = k_ref[:, lanes]
-        out_ref[tokens : 2 * tokens] = v_ref[:, lanes]
-        mixed = jnp.dot(order, q_ref[:, lanes], preferred_element_type=jnp.float32)
-        out_ref[2 * tokens :] = mixed.astype(jnp.bfloat16)
-
-
-def bundles(queries, keys, values, groups, planes, cuts):
+        mixed = jnp.dot(order, q_ref[...], preferred_element_type=jnp.float32).astype(jnp.bfloat16)
+        for c, (low, high) in enumerate(CHUNKS):
+            lanes = slice(low * HEAD_DIM, high * HEAD_DIM)
+            out_ref = out_refs[c * count + n]
+            out_ref[:tokens] = k_ref[:, lanes]
+            out_ref[tokens : 2 * tokens] = v_ref[:, lanes]
+            out_ref[2 * tokens :] = mixed[:, lanes]
+
+
+def bundles(where, queries, keys, values, groups, planes, distances):
+    def cut(source, r):
+        width = source.shape[1] // groups
+        return lax.dynamic_slice_in_dim(source, (lax.axis_index("heads") ^ r) * width, width, axis=1)
+
     tokens = queries.shape[0]
     vmem = pl.BlockSpec(memory_space=pltpu.VMEM)
     return pl.pallas_call(
-        functools.partial(bundle_kernel, groups=groups, planes=planes, cuts=cuts),
-        in_specs=[vmem] * 3,
-        out_specs=[vmem] * len(cuts),
+        functools.partial(bundle_kernel, groups=groups, planes=planes, distances=distances),
+        in_specs=[pl.BlockSpec(memory_space=pltpu.SMEM)] + [vmem] * (3 * len(distances)),
+        out_specs=[vmem] * (len(distances) * len(CHUNKS)),
         out_shape=[
             jax.ShapeDtypeStruct((3 * tokens, (high - low) * HEAD_DIM), jnp.bfloat16)
-            for _, low, high in cuts
+            for low, high in CHUNKS
+            for _ in distances
         ],
-        compiler_params=pltpu.CompilerParams(vmem_limit_bytes=VMEM_WHOLE),
-    )(queries, keys, values)
+        compiler_params=pltpu.CompilerParams(vmem_limit_bytes=VMEM_LIMIT),
+    )(where, *[cut(source, r) for source in (queries, keys, values) for r in distances])
 
 
 def attend_kernel(*refs, sources, planes, blocks, part, targets, rows_step):
@@ -165,14 +170,28 @@
     return jnp.dot(lined[...], weights, preferred_element_type=jnp.float32)
 
 
+def row_blocks(taken, group_heads):
+    blocks = []
+    for target, low, o in taken:
+        heads = o.shape[2] // HEAD_DIM
+        step = heads if group_heads % heads == 0 and low % heads == 0 else 1
+        blocks += [
+            (target, (low + n) // step, step, group_heads // step) for n in range(0, heads, step)
+        ]
+    return blocks
+
+
 def projection_specs(taken, tile, group_heads):
     whole = [pl.BlockSpec(o.shape, lambda i, *_: (0, 0, 0)) for _, _, o in taken]
-    heads = [(t, low + n) for t, low, o in taken for n in range(o.shape[2] // HEAD_DIM)]
     return whole + [
         pl.BlockSpec(
-            (HEAD_DIM, tile), lambda i, where, t=t, h=h: ((where[0] ^ t) * group_heads + h, i)
+            (HEAD_DIM * step, tile),
+            lambda i, where, target=target, block=block, count=count: (
+                (where[0] ^ target) * count + block,
+                i,
+            ),
         )
-        for t, h in heads
+        for target, block, step, count in row_blocks(taken, group_heads)
     ]
 
 
@@ -197,7 +216,7 @@
         ),
         out_shape=jax.ShapeDtypeStruct((features // tile, tokens, tile), jnp.float32),
         compiler_params=pltpu.CompilerParams(vmem_limit_bytes=VMEM_LIMIT),
-    )(where, *[o for _, _, o in taken], *[w_out] * (depth // HEAD_DIM))
+    )(where, *[o for _, _, o in taken], *[w_out] * len(row_blocks(taken, inner // HEAD_DIM // HEAD_GROUPS)))
 
 
 def final_kernel(where_ref, *refs, count, planes, rows_dev):
@@ -283,7 +302,7 @@
     )(
         where,
         *[o for _, _, o in taken],
-        *[w_out] * (depth // HEAD_DIM),
+        *[w_out] * len(row_blocks(taken, inner // HEAD_DIM // HEAD_GROUPS)),
         partial,
         scale_mod[None],
         shift_mod[None],
@@ -340,37 +359,7 @@
 
 
 def after(value, *others):
-    return lax.optimization_barrier((value,) + others)[0]
-
-
-def gather_plane(got, batch, both_parts, share):
-    planes = lax.axis_size("plane")
-    half, count = planes // 2, len(batch)
-    kv_rows = both_parts * count
-    crossed = []
-    for d in range(2, planes, 2):
-        sent = [got[r][:both_parts] for r in batch]
-        sent += [got[r][both_parts + d * share : both_parts + (d + 2) * share] for r in batch]
-        crossed.append(swap(jnp.concatenate(sent, axis=0), "plane", d))
-    near = [[got[r][both_parts : both_parts + share] for r in batch]]
-    far = [[got[r][both_parts + share : both_parts + 2 * share] for r in batch]]
-    for x in crossed:
-        firsts = [kv_rows + 2 * n * share for n in range(count)]
-        near.append([x[first : first + share] for first in firsts])
-        far.append([x[first + share : first + 2 * share] for first in firsts])
-    mine = [got[r][:both_parts] for r in batch] + [x[:kv_rows] for x in crossed]
-    mine = jnp.concatenate(mine + [q for pieces in far for q in pieces], axis=0)
-    other = swap(mine, "plane", 1)
-    asked = []
-    for n in range(count):
-        firsts = [kv_rows * half + (k * count + n) * share for k in range(half)]
-        asked.append(
-            jnp.concatenate(
-                [pieces[n] for pieces in near] + [other[first : first + share] for first in firsts],
-                axis=0,
-            )
-        )
-    return [mine, other], asked
+    return lax.optimization_barrier((value,) + others)[0] if others else value
 
 
 def shards(queries, keys, values, w_out, shift_mod, scale_mod, w_final, conv_weight, conv_bias):
@@ -381,33 +370,55 @@
     devices = groups * planes
     tokens = queries.shape[0]
     rows_dev = tokens // devices
-    both_parts, share = 2 * tokens, tokens // planes
     where = jnp.stack(
         [heads_at, plane_at, heads_at * planes + plane_at, jnp.int32(devices)]
     ).astype(jnp.int32)
 
-    cuts = [(r, low, high) for low, high in CHUNKS for r in (2, 1, 3, 0)]
-    made = dict(zip(cuts, bundles(queries, keys, values, groups, planes, cuts)))
-    made = {cut: swap(made[cut], "heads", cut[0]) if cut[0] else made[cut] for cut in cuts}
-
-    chunks = []
-    for low, high in CHUNKS:
-        got = [made[r, low, high] for r in range(groups)]
-        keys_values, asked = [], []
-        for batch in ((0, 1), (2,), (3,)):
-            kv, q = gather_plane(got, batch, both_parts, share)
-            keys_values += kv
-            asked += q
-        taken = []
+    made = bundles(where, queries, keys, values, groups, planes, range(groups))
+    both_parts, share = 2 * tokens, tokens // planes
+    chunks, done, arrived = [], [], []
+    for chunk, (low, high) in enumerate(CHUNKS):
+        mine_made = made[chunk * groups : (chunk + 1) * groups]
+        got = {r: swap(mine_made[r], "heads", r) if r else mine_made[r] for r in range(groups)}
+
+        held = {r: [got[r]] for r in range(groups)}
+        for r in (0, 1, 2, 3):
+            for d in range(2, planes, 2):
+                asked = got[r][both_parts + d * share : both_parts + (d + 2) * share]
+                sent = jnp.concatenate([got[r][:both_parts], asked], axis=0)
+                held[r].append(swap(after(sent, *done) if r == 3 else sent, "plane", d))
+
+        keys_values, asked = [], {}
+        for distances in ((0, 1), (2,), (3,)):
+            passed = [h[:both_parts] for r in distances for h in held[r]]
+            passed += [h[both_parts + share : both_parts + 2 * share] for r in distances for h in held[r]]
+            mine = jnp.concatenate(passed, axis=0)
+            if distances == (3,):
+                mine = after(mine, *arrived)
+            other = swap(mine, "plane", 1)
+            keys_values += [mine, other]
+            half = planes // 2
+            first = both_parts * half * len(distances)
+            for n, r in enumerate(distances):
+                start = first + n * half * share
+                asked[r] = jnp.concatenate(
+                    [h[both_parts : both_parts + share] for h in held[r]]
+                    + [other[start : start + half * share]],
+                    axis=0,
+                )
+        asked = [asked[r] for r in range(groups)]
+
+        taken, done = {}, []
         for targets in ((3, 2), (1, 0)):
-            for t, o in zip(targets, attend(asked, keys_values, targets, planes)):
-                taken.append((t, low, o if t == 0 else swap(o, "heads", t)))
+            for target, o in zip(targets, attend(asked, keys_values, targets, planes)):
+                done.append(o)
+                taken[target] = (target, low, swap(o, "heads", target) if target else o)
         chunks.append(taken)
-
-    if len(chunks) == 1:
-        near, far = [chunks[0][n] for n in (3, 0)], [chunks[0][n] for n in (1, 2)]
-    else:
-        near, far = sum(chunks[:-1], []), chunks[-1]
+        arrived = [taken[target][2] for target in range(1, groups)]
+
+    near = [chunk[target] for chunk in chunks[:-1] for target in (0, 1, 2, 3)]
+    near += [chunks[-1][target] for target in (0, 3)]
+    far = [chunks[-1][target] for target in (2, 1)]
     partial = project(where, near, w_out, 512)
     even, odd = final_layer(
         where, far, partial, w_out, scale_mod, shift_mod, w_final, rows_dev, planes

time: 77.4 us -> 91.7 us (1.18)
  starting transfers between devices: 20.2 us -> 50.7 us
  local copies, waits for them, and re-layouts: 10.8 us -> 2.72 us
  waiting for transfers between devices: 26.3 us -> 19.5 us
  other arithmetic: 2.63 us -> 0.28 us
    ppermute x12 -> x26, starting transfers between devices: 14.4 us -> 44.9 us  [swap(): return lax.ppermute(source, axis, [(i, i ^ distance) for i in range(count)])]
    slice x20 -> x42, local copies, waits for them, and re-layouts: 6.97 us -> 0.25 us  [the longest x16 0.08 us: shards(): h[both_parts:both_parts + share]]
    ppermute x12 -> x26, waiting for transfers between devices: 23 us -> 18.5 us  [swap(): return lax.ppermute(source, axis, [(i, i ^ distance) for i in range(count)])]
    unnamed x20 -> x16, local copies, waits for them, and re-layouts: 3.79 us -> 0.08 us
    ppermute x1, waiting for transfers between devices: 3.29 us -> 0.01 us  [shards(): right = lax.ppermute(even, both, [(i + 1, i) for i in range(devices - 1)])]
    dynamic_slice x0 -> x2, local copies, waits for them, and re-layouts: none -> 2.39 us  [cut(): lax.dynamic_slice_in_dim(source, (lax.axis_index('heads') ^ r) * width, w...]
    concatenate x8 -> x20, other arithmetic: 2.55 us -> 0.2 us  [the longest x8 0.08 us: shards(): sent = jnp.concatenate([got[r][:both_parts], asked], axis=0)]
    pallas_call x2 -> x4, Pallas kernels: 4.54 us -> 6.28 us  [attend(): pl.pallas_call(functools.partial(attend_kernel, sources=sources, planes=p...]
  transfers between devices with their start and end apart: 14 -> 28, of which waited for: 6 -> 10; matrix products, arithmetic and copies ran while one was open for 12% -> 1% of each run, Pallas kernels for 7% -> 9%
where the time goes in v12:
time: 91.7 us; the launch traced here: 90.1 us
  starting transfers between devices  50.7 us (55%)
  waiting for transfers between devices  19.5 us (21%)
  Pallas kernels  16.3 us (18%)
  local copies, waits for them, and re-layouts  2.72 us (3%)
    ppermute x26, starting transfers between devices, swap(): return lax.ppermute(source, axis, [(i, i ^ distance) for i in range(count)])  44.9 us
    ppermute x26, waiting for transfers between devices, swap(): return lax.ppermute(source, axis, [(i, i ^ distance) for i in range(count)])  18.5 us
    pallas_call x4, Pallas kernels, attend(): pl.pallas_call(functools.partial(attend_kernel, sources=sources, planes=p...  6.28 us
    pallas_call x1, Pallas kernels, final_layer(): pl.pallas_call(functools.partial(final_kernel, count=len(taken), planes=p...  3.54 us
    pallas_call x1, Pallas kernels, project(): pl.pallas_call(functools.partial(project_kernel, count=len(taken)), grid_...  3.52 us
    ppermute x1, starting transfers between devices, shards(): left = lax.ppermute(odd, both, [(i, i + 1) for i in range(devices - 1)])  3.01 us
    ppermute x1, starting transfers between devices, shards(): right = lax.ppermute(even, both, [(i + 1, i) for i in range(devices - 1)])  2.79 us
    dynamic_slice x2, local copies, waits for them, and re-layouts, cut(): lax.dynamic_slice_in_dim(source, (lax.axis_index('heads') ^ r) * width, w...  2.39 us
  transfers between devices with their start and end apart: 28, of which 10 were waited for; matrix products, arithmetic and copies ran while one was open for 1% of the time, Pallas kernels for 9%

profile of v12, /device:TPU:1, one launch (start us, length us, event | category | flops | bytes accessed | tf_op | source)
XLA Modules:
  0.0 90.1 jit_solution(4328350923745900690)
XLA Ops:
  0.0 1.1 %constant_dynamic-slice_fusion.8 = (bf16[128,384]{1,0:T(8,128)(2,1)S(1)}, bf16[128,384]{1,0:T(8,128)(2,1)S(1)}, bf16[128,384]{1,0:T(8,128)(2,1)S(1)}, bf16[128,384]{1,0:T(8,128)(2,1)S(1)}) fusion(bf16[128,1536]{1,0:T(8,128)(2,1)} %param.9, s32[]{:T(128)S(6)} %select_n.11, s32[]{:T(128)S(6)} %select_n.9, s32[]{:T(128)S(6)} %select_n.8, s32[]{:T(128)S(6)} %select_n.10), kind=kLoop, calls=%fused_computation.44 | loop fusion | bytes 786448 | tf_op jit(solution)/shard_map/dynamic_slice | solution.py:51
  1.1 1.3 %constant_dynamic-slice_fusion = (bf16[128,384]{1,0:T(8,128)(2,1)S(1)}, bf16[128,384]{1,0:T(8,128)(2,1)S(1)}, bf16[128,384]{1,0:T(8,128)(2,1)S(1)}, bf16[128,384...) fusion(bf16[128,1536]{1,0:T(8,128)(2,1)} %param.11, ...), kind=kLoop, calls=%fused_computation.36 | loop fusion | bytes 1572880 | tf_op jit(solution)/shard_map/dynamic_slice | solution.py:51
  2.4 0.0 copy-start
  2.4 0.1 pad_add_fusion.where_ref
  2.5 0.8 shard_map.91
  3.3 2.2 %collective-permute-start.9 = (bf16[384,128]{1,0:T(8,128)(2,1)S(1)}, bf16[384,128]{1,0:T(8,128)(2,1)S(1)}, u32[]{:S(2)}, u32[]{:S(2)}) collective-permute-start(bf16[384,128]{1,0:T(8,128)(2,1)S(1)} %get-tuple-element.30), channel_id=1, source_target_pairs={{0,4},{4,0},{8,12},{12,8},{1,5},{5,1},{9,13},{13,9},{2,6},{6,2},{1... | collective-permute-start | bytes 294920 | tf_op jit(solution)/shard_map/ppermute | solution.py:23
  5.5 2.3 %collective-permute-start.12 = (bf16[384,128]{1,0:T(8,128)(2,1)S(1)}, bf16[384,128]{1,0:T(8,128)(2,1)S(1)}, u32[]{:S(2)}, u32[]{:S(2)}) collective-permute-start(bf16[384,128]{1,0:T(8,128)(2,1)S(1)} %get-tuple-element.31), channel_id=1, source_target_pairs={{0,8},{4,12},{8,0},{12,4},{1,9},{5,13},{9,1},{13,5},{2,10},{6,14},... | collective-permute-start | bytes 294920 | tf_op jit(solution)/shard_map/ppermute | solution.py:23
  7.8 0.0 collective-permute-start.15
  7.8 0.3 collective-permute-start.1
  8.2 1.3 %collective-permute-start.8 = (bf16[320,128]{1,0:T(8,128)(2,1)S(1)}, bf16[320,128]{1,0:T(8,128)(2,1)S(1)}, u32[]{:S(2)}, u32[]{:S(2)}) collective-permute-start(bf16[320,128]{1,0:T(8,128)(2,1)S(1)} %pad_maximum_fusion.8), channel_id=1, source_target_pairs={{0,2},{1,3},{2,0},{3,1},{4,6},{5,7},{6,4},{7,5},{8,10},{9,11},{10,... | collective-permute-start | bytes 245768 | tf_op jit(solution)/shard_map/ppermute | solution.py:23
  9.5 2.3 %collective-permute-done.8 = bf16[320,128]{1,0:T(8,128)(2,1)S(1)} collective-permute-done((bf16[320,128]{1,0:T(8,128)(2,1)S(1)}, bf16[320,128]{1,0:T(8,128)(2,1)S(1)}, u32[]{:S(2)}, u32[]{:S(2)}) %collective-permute-start.8) | collective-permute-done | bytes 81952 | tf_op jit(solution)/shard_map/ppermute | solution.py:23
  11.9 3.2 %collective-permute-start.4 = (bf16[384,256]{1,0:T(8,128)(2,1)S(1)}, bf16[384,256]{1,0:T(8,128)(2,1)S(1)}, u32[]{:S(2)}, u32[]{:S(2)}) collective-permute-start(bf16[384,256]{1,0:T(8,128)(2,1)S(1)} %get-tuple-element.27), channel_id=1, source_target_pairs={{0,8},{4,12},{8,0},{12,4},{1,9},{5,13},{9,1},{13,5},{2,10},{6,14},... | collective-permute-start | bytes 589832 | tf_op jit(solution)/shard_map/ppermute | solution.py:23
  15.0 0.0 collective-permute-done.12
  15.0 0.1 collective-permute-start.7
  15.2 0.0 collective-permute-done.15
  15.2 1.3 %collective-permute-start = (bf16[320,256]{1,0:T(8,128)(2,1)S(1)}, bf16[320,256]{1,0:T(8,128)(2,1)S(1)}, u32[]{:S(2)}, u32[]{:S(2)}) collective-permute-start(bf16[320,256]{1,0:T(8,128)(2,1)S(1)} %pad_maximum_fusion.2), channel_id=1, source_target_pairs={{0,2},{1,3},{2,0},{3,1},{4,6},{5,7},{6,4},{7,5},{8,10},{9,11},{10,... | collective-permute-start | bytes 491528 | tf_op jit(solution)/shard_map/ppermute | solution.py:23
  16.5 0.0 collective-permute-done.9
  16.5 0.3 collective-permute-start.13
  16.9 2.8 %collective-permute-done = bf16[320,256]{1,0:T(8,128)(2,1)S(1)} collective-permute-done((bf16[320,256]{1,0:T(8,128)(2,1)S(1)}, bf16[320,256]{1,0:T(8,128)(2,1)S(1)}, u32[]{:S(2)}, u32[]{:S(2)}) %collective-permute-start) | collective-permute-done | bytes 163872 | tf_op jit(solution)/shard_map/ppermute | solution.py:23
  19.7 1.2 %collective-permute-start.16 = (bf16[320,128]{1,0:T(8,128)(2,1)S(1)}, bf16[320,128]{1,0:T(8,128)(2,1)S(1)}, u32[]{:S(2)}, u32[]{:S(2)}) collective-permute-start(bf16[320,128]{1,0:T(8,128)(2,1)S(1)} %pad_maximum_fusion.11), channel_id=1, source_target_pairs={{0,2},{1,3},{2,0},{3,1},{4,6},{5,7},{6,4},{7,5},{8,10},{9,11},{10,... | collective-permute-start | bytes 245768 | tf_op jit(solution)/shard_map/ppermute | solution.py:23
  20.9 2.9 %collective-permute-done.16 = bf16[320,128]{1,0:T(8,128)(2,1)S(1)} collective-permute-done((bf16[320,128]{1,0:T(8,128)(2,1)S(1)}, bf16[320,128]{1,0:T(8,128)(2,1)S(1)}, u32[]{:S(2)}, u32[]{:S(2)}) %collective-permute-start.16) | collective-permute-done | bytes 81952 | tf_op jit(solution)/shard_map/ppermute | solution.py:23
  23.8 1.3 %collective-permute-start.10 = (bf16[320,128]{1,0:T(8,128)(2,1)S(1)}, bf16[320,128]{1,0:T(8,128)(2,1)S(1)}, u32[]{:S(2)}, u32[]{:S(2)}) collective-permute-start(bf16[320,128]{1,0:T(8,128)(2,1)S(1)} %pad_maximum_fusion.9), channel_id=1, source_target_pairs={{0,2},{1,3},{2,0},{3,1},{4,6},{5,7},{6,4},{7,5},{8,10},{9,11},{10,... | collective-permute-start | bytes 245768 | tf_op jit(solution)/shard_map/ppermute | solution.py:23
  25.2 0.0 collective-permute-done.13
  25.2 6.3 %collective-permute-start.17 = (bf16[576,128]{1,0:T(8,128)(2,1)S(1)}, bf16[576,128]{1,0:T(8,128)(2,1)S(1)}, u32[]{:S(2)}, u32[]{:S(2)}) collective-permute-start(bf16[576,128]{1,0:T(8,128)(2,1)S(1)} %pad_maximum_fusion.7.refs_8_), channel_id=1, source_target_pairs={{0,1},{1,0},{2,3},{3,2},{4,5},{5,4},{6,7},{7,6},{8,9},{9,8},{10,11... | collective-permute-start | bytes 442376 | tf_op jit(solution)/shard_map/ppermute | solution.py:23
  31.5 2.8 %collective-permute-start.14 = (bf16[576,128]{1,0:T(8,128)(2,1)S(1)}, bf16[576,128]{1,0:T(8,128)(2,1)S(1)}, u32[]{:S(2)}, u32[]{:S(2)}) collective-permute-start(bf16[576,128]{1,0:T(8,128)(2,1)S(1)} %pad_maximum_fusion.6.refs_6_), channel_id=1, source_target_pairs={{0,1},{1,0},{2,3},{3,2},{4,5},{5,4},{6,7},{7,6},{8,9},{9,8},{10,11... | collective-permute-start | bytes 442376 | tf_op jit(solution)/shard_map/ppermute | solution.py:23
  34.4 0.0 collective-permute-done.4
  34.4 0.1 collective-permute-start.11
  34.6 1.3 %collective-permute-start.5 = (bf16[320,256]{1,0:T(8,128)(2,1)S(1)}, bf16[320,256]{1,0:T(8,128)(2,1)S(1)}, u32[]{:S(2)}, u32[]{:S(2)}) collective-permute-start(bf16[320,256]{1,0:T(8,128)(2,1)S(1)} %pad_maximum_fusion.4), channel_id=1, source_target_pairs={{0,2},{1,3},{2,0},{3,1},{4,6},{5,7},{6,4},{7,5},{8,10},{9,11},{10,... | collective-permute-start | bytes 491528 | tf_op jit(solution)/shard_map/ppermute | solution.py:23
  35.9 0.3 collective-permute-start.2
  36.3 0.0 collective-permute-done.14.refs_7_
  36.3 3.6 %collective-permute-done.5 = bf16[320,256]{1,0:T(8,128)(2,1)S(1)} collective-permute-done((bf16[320,256]{1,0:T(8,128)(2,1)S(1)}, bf16[320,256]{1,0:T(8,128)(2,1)S(1)}, u32[]{:S(2)}, u32[]{:S(2)}) %collective-permute-start.5) | collective-permute-done | bytes 163872 | tf_op jit(solution)/shard_map/ppermute | solution.py:23
  40.0 2.3 %collective-permute-start.6 = (bf16[576,256]{1,0:T(8,128)(2,1)S(1)}, bf16[576,256]{1,0:T(8,128)(2,1)S(1)}, u32[]{:S(2)}, u32[]{:S(2)}) collective-permute-start(bf16[576,256]{1,0:T(8,128)(2,1)S(1)} %pad_maximum_fusion.refs_6_), channel_id=1, source_target_pairs={{0,1},{1,0},{2,3},{3,2},{4,5},{5,4},{6,7},{7,6},{8,9},{9,8},{10,11... | collective-permute-start | bytes 884744 | tf_op jit(solution)/shard_map/ppermute | solution.py:23
  42.3 1.1 %collective-permute-done.2 = bf16[320,256]{1,0:T(8,128)(2,1)S(1)} collective-permute-done((bf16[320,256]{1,0:T(8,128)(2,1)S(1)}, bf16[320,256]{1,0:T(8,128)(2,1)S(1)}, u32[]{:S(2)}, u32[]{:S(2)}) %collective-permute-start.2) | collective-permute-done | bytes 163872 | tf_op jit(solution)/shard_map/ppermute | solution.py:23
  43.5 0.0 collective-permute-done.11.refs_5_
  43.5 1.5 %shard_map.93 = (bf16[4,32,128]{2,1,0:T(8,128)(2,1)S(1)}, bf16[4,32,128]{2,1,0:T(8,128)(2,1)S(1)}) custom-call(bf16[128,128]{1,0:T(8,128)(2,1)S(1)} %pad_maximum_fusion.16.refs_0_, bf16[128,128]{1,0:T(8,128)(2,1)S(1)} %pad_maximum_fusion.17.refs_1_, bf16[128,128]{1,0:T(8,128)(2,1)S(1)} %pad_maximum_fusion.18.refs_2_, ...), custom_call_target="tpu_custom_call" | custom-call | tf_op jit(solution)/shard_map/pallas_call | solution.py:143
  45.0 1.5 %shard_map.92 = (bf16[4,32,128]{2,1,0:T(8,128)(2,1)S(1)}, bf16[4,32,128]{2,1,0:T(8,128)(2,1)S(1)}) custom-call(bf16[128,128]{1,0:T(8,128)(2,1)S(1)} %pad_maximum_fusion.16.refs_0_, bf16[128,128]{1,0:T(8,128)(2,1)S(1)} %pad_maximum_fusion.17.refs_1_, bf16[128,128]{1,0:T(8,128)(2,1)S(1)} %pad_maximum_fusion.18.refs_2_, ...), custom_call_target="tpu_custom_call" | custom-call | tf_op jit(solution)/shard_map/pallas_call | solution.py:143
  46.6 1.3 %collective-permute-start.18 = (bf16[320,256]{1,0:T(8,128)(2,1)S(1)}, bf16[320,256]{1,0:T(8,128)(2,1)S(1)}, u32[]{:S(2)}, u32[]{:S(2)}) collective-permute-start(bf16[320,256]{1,0:T(8,128)(2,1)S(1)} %pad_maximum_fusion.5), channel_id=1, source_target_pairs={{0,2},{1,3},{2,0},{3,1},{4,6},{5,7},{6,4},{7,5},{8,10},{9,11},{10,... | collective-permute-start | bytes 491528 | tf_op jit(solution)/shard_map/ppermute | solution.py:23
  47.9 1.6 %collective-permute-start.3 = (bf16[1152,256]{1,0:T(8,128)(2,1)S(1)}, bf16[1152,256]{1,0:T(8,128)(2,1)S(1)}, u32[]{:S(2)}, u32[]{:S(2)}) collective-permute-start(bf16[1152,256]{1,0:T(8,128)(2,1)S(1)} %get-tuple-element.78.refs_4_), channel_id=1, source_target_pairs={{0,1},{1,0},{2,3},{3,2},{4,5},{5,4},{6,7},{7,6},{8,9},{9,8},{10,11... | collective-permute-start | bytes 1769480 | tf_op jit(solution)/shard_map/ppermute | solution.py:23
  49.5 0.6 collective-permute-start.19
  50.1 9.3 %collective-permute-start.21 = (bf16[4,32,128]{2,1,0:T(8,128)(2,1)S(1)}, bf16[4,32,128]{2,1,0:T(8,128)(2,1)S(1)}, u32[]{:S(2)}, u32[]{:S(2)}) collective-permute-start(bf16[4,32,128]{2,1,0:T(8,128)(2,1)S(1)} %get-tuple-element.33), channel_id=1, source_target_pairs={{0,12},{4,8},{8,4},{12,0},{1,13},{5,9},{9,5},{13,1},{2,14},{6,10},... | collective-permute-start | bytes 98312 | tf_op jit(solution)/shard_map/ppermute | solution.py:23
  59.4 0.0 collective-permute-done.18
  59.4 0.2 collective-permute-start.20
  59.6 0.0 collective-permute-done.19.refs_1_
  59.6 1.7 %collective-permute-done.21.refs_3_ = bf16[4,32,128]{2,1,0:T(8,128)(2,1)S(1)} collective-permute-done((bf16[4,32,128]{2,1,0:T(8,128)(2,1)S(1)}, bf16[4,32,128]{2,1,0:T(8,128)(2,1)S(1)}, u32[]{:S(2)}, u32[]{:S(2)}) %collective-permute-start.21) | collective-permute-done | bytes 32800 | tf_op jit(solution)/shard_map/ppermute | solution.py:23
  61.3 1.7 %collective-permute-done.20.refs_2_ = bf16[4,32,128]{2,1,0:T(8,128)(2,1)S(1)} collective-permute-done((bf16[4,32,128]{2,1,0:T(8,128)(2,1)S(1)}, bf16[4,32,128]{2,1,0:T(8,128)(2,1)S(1)}, u32[]{:S(2)}, u32[]{:S(2)}) %collective-permute-start.20) | collective-permute-done | bytes 32800 | tf_op jit(solution)/shard_map/ppermute | solution.py:23
  63.0 1.7 %collective-permute-start.22 = (bf16[576,256]{1,0:T(8,128)(2,1)S(1)}, bf16[576,256]{1,0:T(8,128)(2,1)S(1)}, u32[]{:S(2)}, u32[]{:S(2)}) collective-permute-start(bf16[576,256]{1,0:T(8,128)(2,1)S(1)} %pad_maximum_fusion.1.refs_8_), channel_id=1, source_target_pairs={{0,1},{1,0},{2,3},{3,2},{4,5},{5,4},{6,7},{7,6},{8,9},{9,8},{10,11... | collective-permute-start | bytes 884744 | tf_op jit(solution)/shard_map/ppermute | solution.py:23
  64.7 0.0 collective-permute-done.6.refs_7_
  64.8 1.2 %collective-permute-done.22.refs_9_ = bf16[576,256]{1,0:T(8,128)(2,1)S(1)} collective-permute-done((bf16[576,256]{1,0:T(8,128)(2,1)S(1)}, bf16[576,256]{1,0:T(8,128)(2,1)S(1)}, u32[]{:S(2)}, u32[]{:S(2)}) %collective-permute-start.22) | collective-permute-done | bytes 294944 | tf_op jit(solution)/shard_map/ppermute | solution.py:23
  66.0 0.0 collective-permute-done.3.refs_5_
  66.0 1.6 %shard_map.94 = (bf16[4,32,256]{2,1,0:T(8,128)(2,1)S(1)}, bf16[4,32,256]{2,1,0:T(8,128)(2,1)S(1)}) custom-call(bf16[128,256]{1,0:T(8,128)(2,1)S(1)} %pad_maximum_fusion.12.refs_0_, bf16[128,256]{1,0:T(8,128)(2,1)S(1)} %pad_maximum_fusion.13.refs_1_, bf16[128,256]{1,0:T(8,128)(2,1)S(1)} %pad_maximum_fusion.14.refs_2_, ...), custom_call_target="tpu_custom_call" | custom-call | tf_op jit(solution)/shard_map/pallas_call | solution.py:143
  67.6 0.9 collective-permute-start.25
  68.5 1.6 %shard_map.95 = (bf16[4,32,256]{2,1,0:T(8,128)(2,1)S(1)}, bf16[4,32,256]{2,1,0:T(8,128)(2,1)S(1)}) custom-call(bf16[128,256]{1,0:T(8,128)(2,1)S(1)} %pad_maximum_fusion.12.refs_0_, bf16[128,256]{1,0:T(8,128)(2,1)S(1)} %pad_maximum_fusion.13.refs_1_, bf16[128,256]{1,0:T(8,128)(2,1)S(1)} %pad_maximum_fusion.14.refs_2_, ...), custom_call_target="tpu_custom_call" | custom-call | tf_op jit(solution)/shard_map/pallas_call | solution.py:143
  70.1 1.6 %collective-permute-start.24 = (bf16[4,32,256]{2,1,0:T(8,128)(2,1)S(1)}, bf16[4,32,256]{2,1,0:T(8,128)(2,1)S(1)}, u32[]{:S(2)}, u32[]{:S(2)}) collective-permute-start(bf16[4,32,256]{2,1,0:T(8,128)(2,1)S(1)} %get-tuple-element.40), channel_id=1, source_target_pairs={{0,4},{4,0},{8,12},{12,8},{1,5},{5,1},{9,13},{13,9},{2,6},{6,2},{1... | collective-permute-start | bytes 196616 | tf_op jit(solution)/shard_map/ppermute | solution.py:23
  71.8 1.2 %collective-permute-start.23 = (bf16[4,32,256]{2,1,0:T(8,128)(2,1)S(1)}, bf16[4,32,256]{2,1,0:T(8,128)(2,1)S(1)}, u32[]{:S(2)}, u32[]{:S(2)}) collective-permute-start(bf16[4,32,256]{2,1,0:T(8,128)(2,1)S(1)} %get-tuple-element.39), channel_id=1, source_target_pairs={{0,8},{4,12},{8,0},{12,4},{1,9},{5,13},{9,1},{13,5},{2,10},{6,14},... | collective-permute-start | bytes 196616 | tf_op jit(solution)/shard_map/ppermute | solution.py:23
  73.0 0.0 copy-start.4
  73.0 3.5 %shard_map.96.refs_6_ = f32[6,128,512]{2,1,0:T(8,128)S(1)} custom-call(s32[4]{0:T(128)S(1)} %pad_add_fusion.where_ref, bf16[4,32,128]{2,1,0:T(8,128)(2,1)S(1)} %get-tuple-element.36.refs_0_, bf16[4,32,128]{2,1,0:T(8,128)(2,1)S(1)} %collective-permute-done.19.refs_1_, bf16[4,32,128]{2,1,0:T(8,128)(2,1)S(1)} %collective-permute-done.20.refs_2_, ...), custom_call_target="tpu_custom_call" | custom-call | tf_op jit(solution)/shard_map/pallas_call | solution.py:208
  76.5 1.0 %collective-permute-done.23.refs_0_ = bf16[4,32,256]{2,1,0:T(8,128)(2,1)S(1)} collective-permute-done((bf16[4,32,256]{2,1,0:T(8,128)(2,1)S(1)}, bf16[4,32,256]{2,1,0:T(8,128)(2,1)S(1)}, u32[]{:S(2)}, u32[]{:S(2)}) %collective-permute-start.23) | collective-permute-done | bytes 65568 | tf_op jit(solution)/shard_map/ppermute | solution.py:23
  77.6 0.0 copy-start.1
  77.6 0.0 copy-start.5
  77.6 3.5 %shard_map.97 = (bf16[128,32]{1,0:T(8,128)(2,1)S(1)}, bf16[128,32]{1,0:T(8,128)(2,1)S(1)}) custom-call(s32[4]{0:T(128)S(1)} %pad_add_fusion.where_ref, bf16[4,32,256]{2,1,0:T(8,128)(2,1)S(1)} %collective-permute-done.23.refs_0_, bf16[4,32,256]{2,1,0:T(8,128)(2,1)S(1)} %collective-permute-done.24.refs_1_, bf16[1536,3072]{1,0:T(8,128)(2,1)S(1)} %copy-done, ...), custom_call_target="tpu_custom_call" | custom-call | tf_op jit(solution)/shard_map/pallas_call | solution.py:282
  81.1 2.8 %collective-permute-start.27 = (bf16[128,32]{1,0:T(8,128)(2,1)S(1)}, bf16[128,32]{1,0:T(8,128)(2,1)S(1)}, u32[]{:S(2)}, u32[]{:S(2)}) collective-permute-start(bf16[128,32]{1,0:T(8,128)(2,1)S(1)} %get-tuple-element.43.even_ref), channel_id=1, source_target_pairs={{1,0},{2,1},{3,2},{4,3},{5,4},{6,5},{7,6},{8,7},{9,8},{10,9},{11,1... | collective-permute-start | bytes 24584 | tf_op jit(solution)/shard_map/ppermute | solution.py:428
  83.9 3.0 %collective-permute-start.26 = (bf16[128,32]{1,0:T(8,128)(2,1)S(1)}, bf16[128,32]{1,0:T(8,128)(2,1)S(1)}, u32[]{:S(2)}, u32[]{:S(2)}) collective-permute-start(bf16[128,32]{1,0:T(8,128)(2,1)S(1)} %get-tuple-element.44.odd_ref), channel_id=1, source_target_pairs={{0,1},{1,2},{2,3},{3,4},{4,5},{5,6},{6,7},{7,8},{8,9},{9,10},{10,1... | collective-permute-start | bytes 24584 | tf_op jit(solution)/shard_map/ppermute | solution.py:427
  87.0 1.0 %collective-permute-done.26.left_ref = bf16[128,32]{1,0:T(8,128)(2,1)S(1)} collective-permute-done((bf16[128,32]{1,0:T(8,128)(2,1)S(1)}, bf16[128,32]{1,0:T(8,128)(2,1)S(1)}, u32[]{:S(2)}, u32[]{:S(2)}) %collective-permute-start.26) | collective-permute-done | bytes 8224 | tf_op jit(solution)/shard_map/ppermute | solution.py:427
  88.0 2.2 %shard_map.98 = bf16[4,2,64,512]{3,2,1,0:T(8,128)(2,1)} custom-call(s32[4]{0:T(128)S(1)} %pad_add_fusion.where_ref, bf16[128,32]{1,0:T(8,128)(2,1)S(1)} %get-tuple-element.43.even_ref, bf16[128,32]{1,0:T(8,128)(2,1)S(1)} %get-tuple-element.44.odd_ref, bf16[128,32]{1,0:T(8,128)(2,1)S(1)} %collective-permute-done.26.left_ref, ...), custom_call_target="tpu_custom_call" | custom-call | tf_op jit(solution)/shard_map/pallas_call | solution.py:351
  (81 shorter events, 0.5 us)
Async XLA Ops:
  2.4 70.5 %copy-start = (bf16[1536,3072]{1,0:T(8,128)(2,1)S(1)}, bf16[1536,3072]{1,0:T(8,128)(2,1)}, u32[]{:S(2)}) copy-start(bf16[1536,3072]{1,0:T(8,128)(2,1)} %refs_5_.1) | copy-start | bytes 28311556
  3.3 13.2 %collective-permute-start.9 = (bf16[384,128]{1,0:T(8,128)(2,1)S(1)}, bf16[384,128]{1,0:T(8,128)(2,1)S(1)}, u32[]{:S(2)}, u32[]{:S(2)}) collective-permute-start(bf16[384,128]{1,0:T(8,128)(2,1)S(1)} %get-tuple-element.30), channel_id=1, source_target_pairs={{0,4},{4,0},{8,12},{12,8},{1,5},{5,1},{9,13},{13,9},{2,6},{6,2},{1... | collective-permute-start | bytes 294920 | tf_op jit(solution)/shard_map/ppermute | solution.py:23
  5.5 9.5 %collective-permute-start.12 = (bf16[384,128]{1,0:T(8,128)(2,1)S(1)}, bf16[384,128]{1,0:T(8,128)(2,1)S(1)}, u32[]{:S(2)}, u32[]{:S(2)}) collective-permute-start(bf16[384,128]{1,0:T(8,128)(2,1)S(1)} %get-tuple-element.31), channel_id=1, source_target_pairs={{0,8},{4,12},{8,0},{12,4},{1,9},{5,13},{9,1},{13,5},{2,10},{6,14},... | collective-permute-start | bytes 294920 | tf_op jit(solution)/shard_map/ppermute | solution.py:23
  7.8 7.3 %collective-permute-start.15 = (bf16[384,128]{1,0:T(8,128)(2,1)S(1)}, bf16[384,128]{1,0:T(8,128)(2,1)S(1)}, u32[]{:S(2)}, u32[]{:S(2)}) collective-permute-start(bf16[384,128]{1,0:T(8,128)(2,1)S(1)} %get-tuple-element.32), channel_id=1, source_target_pairs={{0,12},{4,8},{8,4},{12,0},{1,13},{5,9},{9,5},{13,1},{2,14},{6,10},... | collective-permute-start | bytes 294920 | tf_op jit(solution)/shard_map/ppermute | solution.py:23
  7.8 26.7 %collective-permute-start.1 = (bf16[384,256]{1,0:T(8,128)(2,1)S(1)}, bf16[384,256]{1,0:T(8,128)(2,1)S(1)}, u32[]{:S(2)}, u32[]{:S(2)}) collective-permute-start(bf16[384,256]{1,0:T(8,128)(2,1)S(1)} %get-tuple-element.26), channel_id=1, source_target_pairs={{0,4},{4,0},{8,12},{12,8},{1,5},{5,1},{9,13},{13,9},{2,6},{6,2},{1... | collective-permute-start | bytes 589832 | tf_op jit(solution)/shard_map/ppermute | solution.py:23
  8.2 3.7 %collective-permute-start.8 = (bf16[320,128]{1,0:T(8,128)(2,1)S(1)}, bf16[320,128]{1,0:T(8,128)(2,1)S(1)}, u32[]{:S(2)}, u32[]{:S(2)}) collective-permute-start(bf16[320,128]{1,0:T(8,128)(2,1)S(1)} %pad_maximum_fusion.8), channel_id=1, source_target_pairs={{0,2},{1,3},{2,0},{3,1},{4,6},{5,7},{6,4},{7,5},{8,10},{9,11},{10,... | collective-permute-start | bytes 245768 | tf_op jit(solution)/shard_map/ppermute | solution.py:23
  11.9 22.5 %collective-permute-start.4 = (bf16[384,256]{1,0:T(8,128)(2,1)S(1)}, bf16[384,256]{1,0:T(8,128)(2,1)S(1)}, u32[]{:S(2)}, u32[]{:S(2)}) collective-permute-start(bf16[384,256]{1,0:T(8,128)(2,1)S(1)} %get-tuple-element.27), channel_id=1, source_target_pairs={{0,8},{4,12},{8,0},{12,4},{1,9},{5,13},{9,1},{13,5},{2,10},{6,14},... | collective-permute-start | bytes 589832 | tf_op jit(solution)/shard_map/ppermute | solution.py:23
  15.0 20.8 %collective-permute-start.7 = (bf16[384,256]{1,0:T(8,128)(2,1)S(1)}, bf16[384,256]{1,0:T(8,128)(2,1)S(1)}, u32[]{:S(2)}, u32[]{:S(2)}) collective-permute-start(bf16[384,256]{1,0:T(8,128)(2,1)S(1)} %get-tuple-element.28), channel_id=1, source_target_pairs={{0,12},{4,8},{8,4},{12,0},{1,13},{5,9},{9,5},{13,1},{2,14},{6,10},... | collective-permute-start | bytes 589832 | tf_op jit(solution)/shard_map/ppermute | solution.py:23
  15.2 4.5 %collective-permute-start = (bf16[320,256]{1,0:T(8,128)(2,1)S(1)}, bf16[320,256]{1,0:T(8,128)(2,1)S(1)}, u32[]{:S(2)}, u32[]{:S(2)}) collective-permute-start(bf16[320,256]{1,0:T(8,128)(2,1)S(1)} %pad_maximum_fusion.2), channel_id=1, source_target_pairs={{0,2},{1,3},{2,0},{3,1},{4,6},{5,7},{6,4},{7,5},{8,10},{9,11},{10,... | collective-permute-start | bytes 491528 | tf_op jit(solution)/shard_map/ppermute | solution.py:23
  16.5 8.7 %collective-permute-start.13 = (bf16[320,128]{1,0:T(8,128)(2,1)S(1)}, bf16[320,128]{1,0:T(8,128)(2,1)S(1)}, u32[]{:S(2)}, u32[]{:S(2)}) collective-permute-start(bf16[320,128]{1,0:T(8,128)(2,1)S(1)} %pad_maximum_fusion.10), channel_id=1, source_target_pairs={{0,2},{1,3},{2,0},{3,1},{4,6},{5,7},{6,4},{7,5},{8,10},{9,11},{10,... | collective-permute-start | bytes 245768 | tf_op jit(solution)/shard_map/ppermute | solution.py:23
  19.7 4.1 %collective-permute-start.16 = (bf16[320,128]{1,0:T(8,128)(2,1)S(1)}, bf16[320,128]{1,0:T(8,128)(2,1)S(1)}, u32[]{:S(2)}, u32[]{:S(2)}) collective-permute-start(bf16[320,128]{1,0:T(8,128)(2,1)S(1)} %pad_maximum_fusion.11), channel_id=1, source_target_pairs={{0,2},{1,3},{2,0},{3,1},{4,6},{5,7},{6,4},{7,5},{8,10},{9,11},{10,... | collective-permute-start | bytes 245768 | tf_op jit(solution)/shard_map/ppermute | solution.py:23
  23.8 7.7 %collective-permute-start.10 = (bf16[320,128]{1,0:T(8,128)(2,1)S(1)}, bf16[320,128]{1,0:T(8,128)(2,1)S(1)}, u32[]{:S(2)}, u32[]{:S(2)}) collective-permute-start(bf16[320,128]{1,0:T(8,128)(2,1)S(1)} %pad_maximum_fusion.9), channel_id=1, source_target_pairs={{0,2},{1,3},{2,0},{3,1},{4,6},{5,7},{6,4},{7,5},{8,10},{9,11},{10,... | collective-permute-start | bytes 245768 | tf_op jit(solution)/shard_map/ppermute | solution.py:23
  25.2 11.1 %collective-permute-start.17 = (bf16[576,128]{1,0:T(8,128)(2,1)S(1)}, bf16[576,128]{1,0:T(8,128)(2,1)S(1)}, u32[]{:S(2)}, u32[]{:S(2)}) collective-permute-start(bf16[576,128]{1,0:T(8,128)(2,1)S(1)} %pad_maximum_fusion.7.refs_8_), channel_id=1, source_target_pairs={{0,1},{1,0},{2,3},{3,2},{4,5},{5,4},{6,7},{7,6},{8,9},{9,8},{10,11... | collective-permute-start | bytes 442376 | tf_op jit(solution)/shard_map/ppermute | solution.py:23
  31.5 4.8 %collective-permute-start.14 = (bf16[576,128]{1,0:T(8,128)(2,1)S(1)}, bf16[576,128]{1,0:T(8,128)(2,1)S(1)}, u32[]{:S(2)}, u32[]{:S(2)}) collective-permute-start(bf16[576,128]{1,0:T(8,128)(2,1)S(1)} %pad_maximum_fusion.6.refs_6_), channel_id=1, source_target_pairs={{0,1},{1,0},{2,3},{3,2},{4,5},{5,4},{6,7},{7,6},{8,9},{9,8},{10,11... | collective-permute-start | bytes 442376 | tf_op jit(solution)/shard_map/ppermute | solution.py:23
  34.4 9.1 %collective-permute-start.11 = (bf16[1152,128]{1,0:T(8,128)(2,1)S(1)}, bf16[1152,128]{1,0:T(8,128)(2,1)S(1)}, u32[]{:S(2)}, u32[]{:S(2)}) collective-permute-start(bf16[1152,128]{1,0:T(8,128)(2,1)S(1)} %get-tuple-element.98.refs_4_), channel_id=1, source_target_pairs={{0,1},{1,0},{2,3},{3,2},{4,5},{5,4},{6,7},{7,6},{8,9},{9,8},{10,11... | collective-permute-start | bytes 884744 | tf_op jit(solution)/shard_map/ppermute | solution.py:23
  34.6 5.4 %collective-permute-start.5 = (bf16[320,256]{1,0:T(8,128)(2,1)S(1)}, bf16[320,256]{1,0:T(8,128)(2,1)S(1)}, u32[]{:S(2)}, u32[]{:S(2)}) collective-permute-start(bf16[320,256]{1,0:T(8,128)(2,1)S(1)} %pad_maximum_fusion.4), channel_id=1, source_target_pairs={{0,2},{1,3},{2,0},{3,1},{4,6},{5,7},{6,4},{7,5},{8,10},{9,11},{10,... | collective-permute-start | bytes 491528 | tf_op jit(solution)/shard_map/ppermute | solution.py:23
  35.9 7.5 %collective-permute-start.2 = (bf16[320,256]{1,0:T(8,128)(2,1)S(1)}, bf16[320,256]{1,0:T(8,128)(2,1)S(1)}, u32[]{:S(2)}, u32[]{:S(2)}) collective-permute-start(bf16[320,256]{1,0:T(8,128)(2,1)S(1)} %pad_maximum_fusion.3), channel_id=1, source_target_pairs={{0,2},{1,3},{2,0},{3,1},{4,6},{5,7},{6,4},{7,5},{8,10},{9,11},{10,... | collective-permute-start | bytes 491528 | tf_op jit(solution)/shard_map/ppermute | solution.py:23
  40.0 24.8 %collective-permute-start.6 = (bf16[576,256]{1,0:T(8,128)(2,1)S(1)}, bf16[576,256]{1,0:T(8,128)(2,1)S(1)}, u32[]{:S(2)}, u32[]{:S(2)}) collective-permute-start(bf16[576,256]{1,0:T(8,128)(2,1)S(1)} %pad_maximum_fusion.refs_6_), channel_id=1, source_target_pairs={{0,1},{1,0},{2,3},{3,2},{4,5},{5,4},{6,7},{7,6},{8,9},{9,8},{10,11... | collective-permute-start | bytes 884744 | tf_op jit(solution)/shard_map/ppermute | solution.py:23
  46.6 12.8 %collective-permute-start.18 = (bf16[320,256]{1,0:T(8,128)(2,1)S(1)}, bf16[320,256]{1,0:T(8,128)(2,1)S(1)}, u32[]{:S(2)}, u32[]{:S(2)}) collective-permute-start(bf16[320,256]{1,0:T(8,128)(2,1)S(1)} %pad_maximum_fusion.5), channel_id=1, source_target_pairs={{0,2},{1,3},{2,0},{3,1},{4,6},{5,7},{6,4},{7,5},{8,10},{9,11},{10,... | collective-permute-start | bytes 491528 | tf_op jit(solution)/shard_map/ppermute | solution.py:23
  47.9 18.1 %collective-permute-start.3 = (bf16[1152,256]{1,0:T(8,128)(2,1)S(1)}, bf16[1152,256]{1,0:T(8,128)(2,1)S(1)}, u32[]{:S(2)}, u32[]{:S(2)}) collective-permute-start(bf16[1152,256]{1,0:T(8,128)(2,1)S(1)} %get-tuple-element.78.refs_4_), channel_id=1, source_target_pairs={{0,1},{1,0},{2,3},{3,2},{4,5},{5,4},{6,7},{7,6},{8,9},{9,8},{10,11... | collective-permute-start | bytes 1769480 | tf_op jit(solution)/shard_map/ppermute | solution.py:23
  49.5 10.1 %collective-permute-start.19 = (bf16[4,32,128]{2,1,0:T(8,128)(2,1)S(1)}, bf16[4,32,128]{2,1,0:T(8,128)(2,1)S(1)}, u32[]{:S(2)}, u32[]{:S(2)}) collective-permute-start(bf16[4,32,128]{2,1,0:T(8,128)(2,1)S(1)} %get-tuple-element.35), channel_id=1, source_target_pairs={{0,4},{4,0},{8,12},{12,8},{1,5},{5,1},{9,13},{13,9},{2,6},{6,2},{1... | collective-permute-start | bytes 98312 | tf_op jit(solution)/shard_map/ppermute | solution.py:23
  50.1 11.2 %collective-permute-start.21 = (bf16[4,32,128]{2,1,0:T(8,128)(2,1)S(1)}, bf16[4,32,128]{2,1,0:T(8,128)(2,1)S(1)}, u32[]{:S(2)}, u32[]{:S(2)}) collective-permute-start(bf16[4,32,128]{2,1,0:T(8,128)(2,1)S(1)} %get-tuple-element.33), channel_id=1, source_target_pairs={{0,12},{4,8},{8,4},{12,0},{1,13},{5,9},{9,5},{13,1},{2,14},{6,10},... | collective-permute-start | bytes 98312 | tf_op jit(solution)/shard_map/ppermute | solution.py:23
  59.4 3.7 %collective-permute-start.20 = (bf16[4,32,128]{2,1,0:T(8,128)(2,1)S(1)}, bf16[4,32,128]{2,1,0:T(8,128)(2,1)S(1)}, u32[]{:S(2)}, u32[]{:S(2)}) collective-permute-start(bf16[4,32,128]{2,1,0:T(8,128)(2,1)S(1)} %get-tuple-element.34), channel_id=1, source_target_pairs={{0,8},{4,12},{8,0},{12,4},{1,9},{5,13},{9,1},{13,5},{2,10},{6,14},... | collective-permute-start | bytes 98312 | tf_op jit(solution)/shard_map/ppermute | solution.py:23
  63.0 2.9 %collective-permute-start.22 = (bf16[576,256]{1,0:T(8,128)(2,1)S(1)}, bf16[576,256]{1,0:T(8,128)(2,1)S(1)}, u32[]{:S(2)}, u32[]{:S(2)}) collective-permute-start(bf16[576,256]{1,0:T(8,128)(2,1)S(1)} %pad_maximum_fusion.1.refs_8_), channel_id=1, source_target_pairs={{0,1},{1,0},{2,3},{3,2},{4,5},{5,4},{6,7},{7,6},{8,9},{9,8},{10,11... | collective-permute-start | bytes 884744 | tf_op jit(solution)/shard_map/ppermute | solution.py:23
  67.6 5.3 %collective-permute-start.25 = (bf16[4,32,256]{2,1,0:T(8,128)(2,1)S(1)}, bf16[4,32,256]{2,1,0:T(8,128)(2,1)S(1)}, u32[]{:S(2)}, u32[]{:S(2)}) collective-permute-start(bf16[4,32,256]{2,1,0:T(8,128)(2,1)S(1)} %get-tuple-element.42), channel_id=1, source_target_pairs={{0,12},{4,8},{8,4},{12,0},{1,13},{5,9},{9,5},{13,1},{2,14},{6,10},... | collective-permute-start | bytes 196616 | tf_op jit(solution)/shard_map/ppermute | solution.py:23
  70.1 6.4 %collective-permute-start.24 = (bf16[4,32,256]{2,1,0:T(8,128)(2,1)S(1)}, bf16[4,32,256]{2,1,0:T(8,128)(2,1)S(1)}, u32[]{:S(2)}, u32[]{:S(2)}) collective-permute-start(bf16[4,32,256]{2,1,0:T(8,128)(2,1)S(1)} %get-tuple-element.40), channel_id=1, source_target_pairs={{0,4},{4,0},{8,12},{12,8},{1,5},{5,1},{9,13},{13,9},{2,6},{6,2},{1... | collective-permute-start | bytes 196616 | tf_op jit(solution)/shard_map/ppermute | solution.py:23
  71.8 5.8 %collective-permute-start.23 = (bf16[4,32,256]{2,1,0:T(8,128)(2,1)S(1)}, bf16[4,32,256]{2,1,0:T(8,128)(2,1)S(1)}, u32[]{:S(2)}, u32[]{:S(2)}) collective-permute-start(bf16[4,32,256]{2,1,0:T(8,128)(2,1)S(1)} %get-tuple-element.39), channel_id=1, source_target_pairs={{0,8},{4,12},{8,0},{12,4},{1,9},{5,13},{9,1},{13,5},{2,10},{6,14},... | collective-permute-start | bytes 196616 | tf_op jit(solution)/shard_map/ppermute | solution.py:23
  72.9 4.6 %copy-start.2 = (bf16[3072,64]{0,1:T(8,128)(2,1)S(1)}, bf16[3072,64]{0,1:T(8,128)(2,1)}, u32[]{:S(2)}) copy-start(bf16[3072,64]{0,1:T(8,128)(2,1)} %param.15) | copy-start | bytes 1179652
  72.9 4.6 %copy-start.3 = (f32[3072]{0:T(1024)S(1)}, f32[3072]{0:T(1024)}, u32[]{:S(2)}) copy-start(f32[3072]{0:T(1024)} %param.14) | copy-start | bytes 36868
  73.0 4.6 %copy-start.4 = (f32[3072]{0:T(1024)S(1)}, f32[3072]{0:T(1024)}, u32[]{:S(2)}) copy-start(f32[3072]{0:T(1024)} %param.13) | copy-start | bytes 36868
  77.6 10.4 %copy-start.1 = (bf16[432,512]{1,0:T(8,128)(2,1)S(1)}, bf16[432,512]{1,0:T(8,128)(2,1)}, u32[]{:S(2)}) copy-start(bf16[432,512]{1,0:T(8,128)(2,1)} %w_ref.1) | copy-start | bytes 1327108
  77.6 10.4 %copy-start.5 = (f32[512]{0:T(512)S(1)}, f32[512]{0:T(512)}, u32[]{:S(2)}) copy-start(f32[512]{0:T(512)} %param.17) | copy-start | bytes 6148
  81.1 5.8 %collective-permute-start.27 = (bf16[128,32]{1,0:T(8,128)(2,1)S(1)}, bf16[128,32]{1,0:T(8,128)(2,1)S(1)}, u32[]{:S(2)}, u32[]{:S(2)}) collective-permute-start(bf16[128,32]{1,0:T(8,128)(2,1)S(1)} %get-tuple-element.43.even_ref), channel_id=1, source_target_pairs={{1,0},{2,1},{3,2},{4,3},{5,4},{6,5},{7,6},{8,7},{9,8},{10,9},{11,1... | collective-permute-start | bytes 24584 | tf_op jit(solution)/shard_map/ppermute | solution.py:428
  83.9 4.0 %collective-permute-start.26 = (bf16[128,32]{1,0:T(8,128)(2,1)S(1)}, bf16[128,32]{1,0:T(8,128)(2,1)S(1)}, u32[]{:S(2)}, u32[]{:S(2)}) collective-permute-start(bf16[128,32]{1,0:T(8,128)(2,1)S(1)} %get-tuple-element.44.odd_ref), channel_id=1, source_target_pairs={{0,1},{1,2},{2,3},{3,4},{4,5},{5,6},{6,7},{7,8},{8,9},{9,10},{10,1... | collective-permute-start | bytes 24584 | tf_op jit(solution)/shard_map/ppermute | solution.py:427

commit v13 on v10

--- a/solution.py
+++ b/solution.py
@@ -22,39 +22,38 @@
     return lax.ppermute(source, axis, [(i, i ^ distance) for i in range(count)])
 
 
-def bundle_kernel(where_ref, *refs, groups, planes, distances):
-    tokens = refs[0].shape[0]
+def bundle_kernel(where_ref, qkv_ref, *out_refs, groups, planes, distances):
+    tokens, width = qkv_ref.shape[0] // 3, qkv_ref.shape[1]
+    group_width = width // groups
     rows_dev = tokens // (groups * planes)
     to = lax.broadcasted_iota(jnp.int32, (tokens, tokens), 0)
     at = lax.broadcasted_iota(jnp.int32, (tokens, tokens), 1)
     j, t, row = to // (groups * rows_dev), (to // rows_dev) % groups, to % rows_dev
-    count = len(distances)
-    cut = [refs[n * count : (n + 1) * count] for n in range(4)]
-    for r, q_ref, k_ref, v_ref, out_ref in zip(distances, *cut):
+    for r, out_ref in zip(distances, out_refs):
         group = where_ref[0] ^ r
+        lanes = pl.ds(pl.multiple_of(group * group_width, 128), group_width)
         place = row * (groups * planes) + (t ^ group) * planes + (j ^ where_ref[1])
         order = (at == place).astype(jnp.bfloat16)
-        out_ref[:tokens] = k_ref[...]
-        out_ref[tokens : 2 * tokens] = v_ref[...]
-        mixed = jnp.dot(order, q_ref[...], preferred_element_type=jnp.float32)
+        out_ref[: 2 * tokens] = qkv_ref[tokens:, lanes]
+        mixed = jnp.dot(order, qkv_ref[:tokens, lanes], preferred_element_type=jnp.float32)
         out_ref[2 * tokens :] = mixed.astype(jnp.bfloat16)
 
 
 def bundles(where, queries, keys, values, groups, planes, distances):
-    def cut(source, r):
-        width = source.shape[1] // groups
-        return lax.dynamic_slice_in_dim(source, (lax.axis_index("heads") ^ r) * width, width, axis=1)
-
     tokens, width = queries.shape
     vmem = pl.BlockSpec(memory_space=pltpu.VMEM)
     result = jax.ShapeDtypeStruct((3 * tokens, width // groups), jnp.bfloat16)
     return pl.pallas_call(
         functools.partial(bundle_kernel, groups=groups, planes=planes, distances=distances),
-        in_specs=[pl.BlockSpec(memory_space=pltpu.SMEM)] + [vmem] * (3 * len(distances)),
+        in_specs=[pl.BlockSpec(memory_space=pltpu.SMEM), vmem],
         out_specs=[vmem] * len(distances),
         out_shape=[result] * len(distances),
         compiler_params=pltpu.CompilerParams(vmem_limit_bytes=VMEM_LIMIT),
-    )(where, *[cut(source, r) for source in (queries, keys, values) for r in distances])
+    )(where, jnp.concatenate([queries, keys, values], axis=0))
+
+
+def after(value, *others):
+    return lax.optimization_barrier((value,) + others)[0]
 
 
 def attend_kernel(*refs, sources, planes, blocks, part, targets, rows_step):
@@ -363,10 +362,9 @@
             )
     asked = [asked[r] for r in range(groups)]
 
-    first, second = (3, 2), (1, 0)
     near, far = (0, 3), (2, 1)
     results = {}
-    for targets in (first, second):
+    for targets in ((3,), (2,), (1, 0)):
         for t, o in zip(targets, attend(asked, keys_values, targets, planes)):
             results[t] = o if t == 0 else swap(o, "heads", t)
     partial = project(where, [results[t] for t in near], near, w_out, 512)

time: 72.1 us -> 70.7 us (0.981)
  local copies, waits for them, and re-layouts: 2.79 us -> 0.41 us
  other arithmetic: 0.33 us -> 1.64 us
  waiting for transfers between devices: 25.8 us -> 24.7 us
    dynamic_slice x2 -> x0, local copies, waits for them, and re-layouts: 2.39 us -> none  [cut(): lax.dynamic_slice_in_dim(source, (lax.axis_index('heads') ^ r) * width, w...]
    concatenate x0 -> x1, other arithmetic: none -> 1.31 us  [bundles(): jnp.concatenate([queries, keys, values], axis=0)]
    ppermute x13, waiting for transfers between devices: 22.5 us -> 21.4 us  [swap(): return lax.ppermute(source, axis, [(i, i ^ distance) for i in range(count)])]
    ppermute x1, starting transfers between devices: 2.61 us -> 3.34 us  [shards(): left = lax.ppermute(odd, both, [(i, i + 1) for i in range(devices - 1)])]
    pallas_call x2 -> x3, Pallas kernels: 4.53 us -> 5.12 us  [attend(): pl.pallas_call(functools.partial(attend_kernel, sources=sources, planes=p...]
  transfers between devices with their start and end apart: 15 -> 15, of which waited for: 6 -> 7; matrix products, arithmetic and copies ran while one was open for 1% -> 1% of each run, Pallas kernels for 7% -> 9%
where the time goes in v13:
time: 70.7 us; the launch traced here: 70.5 us
  starting transfers between devices  28.8 us (41%)
  waiting for transfers between devices  24.7 us (35%)
  Pallas kernels  14.6 us (21%)
  other arithmetic  1.64 us (2%)
    ppermute x13, starting transfers between devices, swap(): return lax.ppermute(source, axis, [(i, i ^ distance) for i in range(count)])  23.6 us
    ppermute x13, waiting for transfers between devices, swap(): return lax.ppermute(source, axis, [(i, i ^ distance) for i in range(count)])  21.4 us
    pallas_call x3, Pallas kernels, attend(): pl.pallas_call(functools.partial(attend_kernel, sources=sources, planes=p...  5.12 us
    pallas_call x1, Pallas kernels, final_layer(): pl.pallas_call(functools.partial(final_kernel, targets=targets, planes=pl...  3.78 us
    ppermute x1, starting transfers between devices, shards(): left = lax.ppermute(odd, both, [(i, i + 1) for i in range(devices - 1)])  3.34 us
    ppermute x1, waiting for transfers between devices, shards(): right = lax.ppermute(even, both, [(i + 1, i) for i in range(devices - 1)])  3.29 us
    pallas_call x1, Pallas kernels, project(): pl.pallas_call(functools.partial(project_kernel, targets=targets), grid_s...  2.66 us
    pallas_call x1, Pallas kernels, convolve(): pl.pallas_call(convolve_kernel, in_specs=[smem] + [vmem] * 6, out_specs=v...  2.16 us
  transfers between devices with their start and end apart: 15, of which 7 were waited for; matrix products, arithmetic and copies ran while one was open for 1% of the time, Pallas kernels for 9%

profile of v13, /device:TPU:1, one launch (start us, length us, event | category | flops | bytes accessed | tf_op | source)
XLA Modules:
  0.0 70.5 jit_solution(17438061059860033550)
XLA Ops:
  0.0 1.3 %pad_maximum_fusion.qkv_ref = bf16[384,1536]{1,0:T(8,128)(2,1)S(1)} fusion(bf16[128,1536]{1,0:T(8,128)(2,1)} %param.11, bf16[128,1536]{1,0:T(8,128)(2,1)} %param.10, bf16[128,1536]{1,0:T(8,128)(2,1)} %param.9), kind=kLoop, calls=%fused_computation | loop fusion | flops 3538944 | bytes 2359296 | tf_op jit(solution)/shard_map/concatenate | solution.py:52
  1.3 0.1 pad_add_fusion.where_ref
  1.4 0.0 slice-start
  1.4 0.8 %shard_map.91 = (bf16[384,384]{1,0:T(8,128)(2,1)S(1)}, bf16[384,384]{1,0:T(8,128)(2,1)S(1)}, bf16[384,384]{1,0:T(8,128)(2,1)S(1)}, bf16[384,384]{1,0:T(8,128)(2,1)S(1)}) custom-call(s32[4]{0:T(128)S(1)} %pad_add_fusion.where_ref, bf16[384,1536]{1,0:T(8,128)(2,1)S(1)} %pad_maximum_fusion.qkv_ref), custom_call_target="tpu_custom_call" | custom-call | tf_op jit(solution)/shard_map/pallas_call | solution.py:46
  2.3 2.1 %collective-permute-start = (bf16[320,384]{1,0:T(8,128)(2,1)S(1)}, bf16[320,384]{1,0:T(8,128)(2,1)S(1)}, u32[]{:S(2)}, u32[]{:S(2)}) collective-permute-start(bf16[320,384]{1,0:T(8,128)(2,1)S(1)} %pad_maximum_fusion.3), channel_id=1, source_target_pairs={{0,2},{1,3},{2,0},{3,1},{4,6},{5,7},{6,4},{7,5},{8,10},{9,11},{10,... | collective-permute-start | bytes 737288 | tf_op jit(solution)/shard_map/ppermute | solution.py:22
  4.4 1.3 %collective-permute-start.1 = (bf16[384,384]{1,0:T(8,128)(2,1)S(1)}, bf16[384,384]{1,0:T(8,128)(2,1)S(1)}, u32[]{:S(2)}, u32[]{:S(2)}) collective-permute-start(bf16[384,384]{1,0:T(8,128)(2,1)S(1)} %get-tuple-element.14), channel_id=1, source_target_pairs={{0,4},{4,0},{8,12},{12,8},{1,5},{5,1},{9,13},{13,9},{2,6},{6,2},{1... | collective-permute-start | bytes 884744 | tf_op jit(solution)/shard_map/ppermute | solution.py:22
  5.7 2.3 %collective-permute-start.4 = (bf16[384,384]{1,0:T(8,128)(2,1)S(1)}, bf16[384,384]{1,0:T(8,128)(2,1)S(1)}, u32[]{:S(2)}, u32[]{:S(2)}) collective-permute-start(bf16[384,384]{1,0:T(8,128)(2,1)S(1)} %get-tuple-element.15), channel_id=1, source_target_pairs={{0,8},{4,12},{8,0},{12,4},{1,9},{5,13},{9,1},{13,5},{2,10},{6,14},... | collective-permute-start | bytes 884744 | tf_op jit(solution)/shard_map/ppermute | solution.py:22
  8.0 0.0 collective-permute-start.7
  8.1 2.1 %collective-permute-done = bf16[320,384]{1,0:T(8,128)(2,1)S(1)} collective-permute-done((bf16[320,384]{1,0:T(8,128)(2,1)S(1)}, bf16[320,384]{1,0:T(8,128)(2,1)S(1)}, u32[]{:S(2)}, u32[]{:S(2)}) %collective-permute-start) | collective-permute-done | bytes 245792 | tf_op jit(solution)/shard_map/ppermute | solution.py:22
  10.2 7.2 %collective-permute-done.1 = bf16[384,384]{1,0:T(8,128)(2,1)S(1)} collective-permute-done((bf16[384,384]{1,0:T(8,128)(2,1)S(1)}, bf16[384,384]{1,0:T(8,128)(2,1)S(1)}, u32[]{:S(2)}, u32[]{:S(2)}) %collective-permute-start.1) | collective-permute-done | bytes 294944 | tf_op jit(solution)/shard_map/ppermute | solution.py:22
  17.4 0.1 fusion.5
  17.5 0.5 collective-permute-start.2
  18.0 0.0 collective-permute-done.4
  18.0 1.1 %collective-permute-start.5 = (bf16[320,384]{1,0:T(8,128)(2,1)S(1)}, bf16[320,384]{1,0:T(8,128)(2,1)S(1)}, u32[]{:S(2)}, u32[]{:S(2)}) collective-permute-start(bf16[320,384]{1,0:T(8,128)(2,1)S(1)} %pad_maximum_fusion.5), channel_id=1, source_target_pairs={{0,2},{1,3},{2,0},{3,1},{4,6},{5,7},{6,4},{7,5},{8,10},{9,11},{10,... | collective-permute-start | bytes 737288 | tf_op jit(solution)/shard_map/ppermute | solution.py:22
  19.2 7.5 %collective-permute-done.7 = bf16[384,384]{1,0:T(8,128)(2,1)S(1)} collective-permute-done((bf16[384,384]{1,0:T(8,128)(2,1)S(1)}, bf16[384,384]{1,0:T(8,128)(2,1)S(1)}, u32[]{:S(2)}, u32[]{:S(2)}) %collective-permute-start.7) | collective-permute-done | bytes 294944 | tf_op jit(solution)/shard_map/ppermute | solution.py:22
  26.8 0.3 collective-permute-start.8
  27.1 0.0 collective-permute-done.2
  27.2 5.7 %collective-permute-start.3 = (bf16[1152,384]{1,0:T(8,128)(2,1)S(1)}, bf16[1152,384]{1,0:T(8,128)(2,1)S(1)}, u32[]{:S(2)}, u32[]{:S(2)}) collective-permute-start(bf16[1152,384]{1,0:T(8,128)(2,1)S(1)} %get-tuple-element.40.refs_4_), channel_id=1, source_target_pairs={{0,1},{1,0},{2,3},{3,2},{4,5},{5,4},{6,7},{7,6},{8,9},{9,8},{10,11... | collective-permute-start | bytes 2654216 | tf_op jit(solution)/shard_map/ppermute | solution.py:22
  33.0 0.0 collective-permute-done.5
  33.0 0.0 slice-start.1
  33.1 3.9 %collective-permute-start.6 = (bf16[576,384]{1,0:T(8,128)(2,1)S(1)}, bf16[576,384]{1,0:T(8,128)(2,1)S(1)}, u32[]{:S(2)}, u32[]{:S(2)}) collective-permute-start(bf16[576,384]{1,0:T(8,128)(2,1)S(1)} %pad_maximum_fusion.1.refs_6_), channel_id=1, source_target_pairs={{0,1},{1,0},{2,3},{3,2},{4,5},{5,4},{6,7},{7,6},{8,9},{9,8},{10,11... | collective-permute-start | bytes 1327112 | tf_op jit(solution)/shard_map/ppermute | solution.py:22
  37.0 0.0 collective-permute-done.8
  37.1 2.5 %collective-permute-start.9 = (bf16[576,384]{1,0:T(8,128)(2,1)S(1)}, bf16[576,384]{1,0:T(8,128)(2,1)S(1)}, u32[]{:S(2)}, u32[]{:S(2)}) collective-permute-start(bf16[576,384]{1,0:T(8,128)(2,1)S(1)} %pad_maximum_fusion.2.refs_8_), channel_id=1, source_target_pairs={{0,1},{1,0},{2,3},{3,2},{4,5},{5,4},{6,7},{7,6},{8,9},{9,8},{10,11... | collective-permute-start | bytes 1327112 | tf_op jit(solution)/shard_map/ppermute | solution.py:22
  39.6 0.0 collective-permute-done.6.refs_7_
  39.6 1.4 %collective-permute-done.9.refs_9_ = bf16[576,384]{1,0:T(8,128)(2,1)S(1)} collective-permute-done((bf16[576,384]{1,0:T(8,128)(2,1)S(1)}, bf16[576,384]{1,0:T(8,128)(2,1)S(1)}, u32[]{:S(2)}, u32[]{:S(2)}) %collective-permute-start.9) | collective-permute-done | bytes 442400 | tf_op jit(solution)/shard_map/ppermute | solution.py:22
  41.0 0.0 collective-permute-done.3.refs_5_
  41.1 1.4 %shard_map.94 = bf16[4,32,384]{2,1,0:T(8,128)(2,1)S(1)} custom-call(bf16[128,384]{1,0:T(8,128)(2,1)S(1)} %get-tuple-element.43.refs_0_, bf16[128,384]{1,0:T(8,128)(2,1)S(1)} %get-tuple-element.44.refs_1_, bf16[128,384]{1,0:T(8,128)(2,1)S(1)} %pad_maximum_fusion.9.refs_2_, bf16[128,384]{1,0:T(8,128)(2,1)S(1)} %pad_maximum_fusion.10.refs_3_, ...), custom_call_target="tpu_custom_call" | custom-call | tf_op jit(solution)/shard_map/pallas_call | solution.py:134
  42.5 0.0 slice-start.2
  42.6 2.3 %collective-permute-start.12 = (bf16[4,32,384]{2,1,0:T(8,128)(2,1)S(1)}, bf16[4,32,384]{2,1,0:T(8,128)(2,1)S(1)}, u32[]{:S(2)}, u32[]{:S(2)}) collective-permute-start(bf16[4,32,384]{2,1,0:T(8,128)(2,1)S(1)} %shard_map.94), channel_id=1, source_target_pairs={{0,12},{4,8},{8,4},{12,0},{1,13},{5,9},{9,5},{13,1},{2,14},{6,10},... | collective-permute-start | bytes 294920 | tf_op jit(solution)/shard_map/ppermute | solution.py:22
  44.8 1.4 %shard_map.92 = bf16[4,32,384]{2,1,0:T(8,128)(2,1)S(1)} custom-call(bf16[128,384]{1,0:T(8,128)(2,1)S(1)} %get-tuple-element.43.refs_0_, bf16[128,384]{1,0:T(8,128)(2,1)S(1)} %get-tuple-element.44.refs_1_, bf16[128,384]{1,0:T(8,128)(2,1)S(1)} %pad_maximum_fusion.9.refs_2_, bf16[128,384]{1,0:T(8,128)(2,1)S(1)} %pad_maximum_fusion.10.refs_3_, ...), custom_call_target="tpu_custom_call" | custom-call | tf_op jit(solution)/shard_map/pallas_call | solution.py:134
  46.3 1.4 %collective-permute-start.10 = (bf16[4,32,384]{2,1,0:T(8,128)(2,1)S(1)}, bf16[4,32,384]{2,1,0:T(8,128)(2,1)S(1)}, u32[]{:S(2)}, u32[]{:S(2)}) collective-permute-start(bf16[4,32,384]{2,1,0:T(8,128)(2,1)S(1)} %shard_map.92), channel_id=1, source_target_pairs={{0,8},{4,12},{8,0},{12,4},{1,9},{5,13},{9,1},{13,5},{2,10},{6,14},... | collective-permute-start | bytes 294920 | tf_op jit(solution)/shard_map/ppermute | solution.py:22
  47.6 2.3 %shard_map.93 = (bf16[4,32,384]{2,1,0:T(8,128)(2,1)S(1)}, bf16[4,32,384]{2,1,0:T(8,128)(2,1)S(1)}) custom-call(bf16[128,384]{1,0:T(8,128)(2,1)S(1)} %get-tuple-element.43.refs_0_, bf16[128,384]{1,0:T(8,128)(2,1)S(1)} %get-tuple-element.44.refs_1_, bf16[128,384]{1,0:T(8,128)(2,1)S(1)} %pad_maximum_fusion.9.refs_2_, ...), custom_call_target="tpu_custom_call" | custom-call | tf_op jit(solution)/shard_map/pallas_call | solution.py:134
  49.9 0.2 collective-permute-start.11
  50.1 0.0 collective-permute-done.12.refs_1_
  50.1 0.0 slice-done
  50.1 0.0 slice-done.1
  50.1 0.0 slice-done.2
  50.1 0.0 copy-start.1
  50.1 0.0 copy-start.2
  50.1 0.0 copy-start.3
  50.1 2.7 %shard_map.95.refs_4_ = f32[6,128,512]{2,1,0:T(8,128)S(1)} custom-call(s32[4]{0:T(128)S(1)} %pad_add_fusion.where_ref, bf16[4,32,384]{2,1,0:T(8,128)(2,1)S(1)} %get-tuple-element.18.refs_0_, bf16[4,32,384]{2,1,0:T(8,128)(2,1)S(1)} %collective-permute-done.12.refs_1_, bf16[1536,3072]{1,0:T(8,128)(2,1)S(1)} %bitcast.8, bf16[1536,3072]{1,0:T(8,128)(2,1)S(1)} %bitcast.8), custom_call_target="tpu_custom_call" | custom-call | tf_op jit(solution)/shard_map/pallas_call | solution.py:179
  52.8 2.7 %collective-permute-done.10.refs_0_ = bf16[4,32,384]{2,1,0:T(8,128)(2,1)S(1)} collective-permute-done((bf16[4,32,384]{2,1,0:T(8,128)(2,1)S(1)}, bf16[4,32,384]{2,1,0:T(8,128)(2,1)S(1)}, u32[]{:S(2)}, u32[]{:S(2)}) %collective-permute-start.10) | collective-permute-done | bytes 98336 | tf_op jit(solution)/shard_map/ppermute | solution.py:22
  55.5 0.4 collective-permute-done.11.refs_1_
  55.9 0.0 copy-done.1
  55.9 0.0 copy-done.2
  55.9 0.0 copy-done.3
  56.0 0.0 copy-start
  56.0 0.0 copy-start.4
  56.0 3.8 %shard_map.96 = (bf16[128,32]{1,0:T(8,128)(2,1)S(1)}, bf16[128,32]{1,0:T(8,128)(2,1)S(1)}) custom-call(s32[4]{0:T(128)S(1)} %pad_add_fusion.where_ref, bf16[4,32,384]{2,1,0:T(8,128)(2,1)S(1)} %collective-permute-done.10.refs_0_, bf16[4,32,384]{2,1,0:T(8,128)(2,1)S(1)} %collective-permute-done.11.refs_1_, bf16[1536,3072]{1,0:T(8,128)(2,1)S(1)} %bitcast.8, ...), custom_call_target="tpu_custom_call" | custom-call | tf_op jit(solution)/shard_map/pallas_call | solution.py:254
  59.8 3.3 %collective-permute-start.13 = (bf16[128,32]{1,0:T(8,128)(2,1)S(1)}, bf16[128,32]{1,0:T(8,128)(2,1)S(1)}, u32[]{:S(2)}, u32[]{:S(2)}) collective-permute-start(bf16[128,32]{1,0:T(8,128)(2,1)S(1)} %get-tuple-element.20.odd_ref), channel_id=1, source_target_pairs={{0,1},{1,2},{2,3},{3,4},{4,5},{5,6},{6,7},{7,8},{8,9},{9,10},{10,1... | collective-permute-start | bytes 24584 | tf_op jit(solution)/shard_map/ppermute | solution.py:376
  63.1 1.9 %collective-permute-start.14 = (bf16[128,32]{1,0:T(8,128)(2,1)S(1)}, bf16[128,32]{1,0:T(8,128)(2,1)S(1)}, u32[]{:S(2)}, u32[]{:S(2)}) collective-permute-start(bf16[128,32]{1,0:T(8,128)(2,1)S(1)} %get-tuple-element.19.even_ref), channel_id=1, source_target_pairs={{1,0},{2,1},{3,2},{4,3},{5,4},{6,5},{7,6},{8,7},{9,8},{10,9},{11,1... | collective-permute-start | bytes 24584 | tf_op jit(solution)/shard_map/ppermute | solution.py:377
  65.0 0.0 collective-permute-done.13.left_ref
  65.1 3.3 %collective-permute-done.14.right_ref = bf16[128,32]{1,0:T(8,128)(2,1)S(1)} collective-permute-done((bf16[128,32]{1,0:T(8,128)(2,1)S(1)}, bf16[128,32]{1,0:T(8,128)(2,1)S(1)}, u32[]{:S(2)}, u32[]{:S(2)}) %collective-permute-start.14) | collective-permute-done | bytes 8224 | tf_op jit(solution)/shard_map/ppermute | solution.py:377
  68.3 0.0 copy-done
  68.3 0.0 copy-done.4
  68.4 2.2 %shard_map.97 = bf16[4,2,64,512]{3,2,1,0:T(8,128)(2,1)} custom-call(s32[4]{0:T(128)S(1)} %pad_add_fusion.where_ref, bf16[128,32]{1,0:T(8,128)(2,1)S(1)} %get-tuple-element.19.even_ref, bf16[128,32]{1,0:T(8,128)(2,1)S(1)} %get-tuple-element.20.odd_ref, bf16[128,32]{1,0:T(8,128)(2,1)S(1)} %collective-permute-done.13.left_ref, ...), custom_call_target="tpu_custom_call" | custom-call | tf_op jit(solution)/shard_map/pallas_call | solution.py:315
  (32 shorter events, 0.6 us)
Async XLA Ops:
  1.4 48.7 %slice-start = ((s8[9437184]{0:T(1024)(128)(4,1)}), s8[4194304]{0:T(1024)(128)(4,1)S(1)}, s32[]{:S(2)}) async-start(s8[9437184]{0:T(1024)(128)(4,1)} %bitcast.7), calls=%async_computation | async-start | bytes 8388608
  2.3 7.8 %collective-permute-start = (bf16[320,384]{1,0:T(8,128)(2,1)S(1)}, bf16[320,384]{1,0:T(8,128)(2,1)S(1)}, u32[]{:S(2)}, u32[]{:S(2)}) collective-permute-start(bf16[320,384]{1,0:T(8,128)(2,1)S(1)} %pad_maximum_fusion.3), channel_id=1, source_target_pairs={{0,2},{1,3},{2,0},{3,1},{4,6},{5,7},{6,4},{7,5},{8,10},{9,11},{10,... | collective-permute-start | bytes 737288 | tf_op jit(solution)/shard_map/ppermute | solution.py:22
  4.4 13.0 %collective-permute-start.1 = (bf16[384,384]{1,0:T(8,128)(2,1)S(1)}, bf16[384,384]{1,0:T(8,128)(2,1)S(1)}, u32[]{:S(2)}, u32[]{:S(2)}) collective-permute-start(bf16[384,384]{1,0:T(8,128)(2,1)S(1)} %get-tuple-element.14), channel_id=1, source_target_pairs={{0,4},{4,0},{8,12},{12,8},{1,5},{5,1},{9,13},{13,9},{2,6},{6,2},{1... | collective-permute-start | bytes 884744 | tf_op jit(solution)/shard_map/ppermute | solution.py:22
  5.7 12.2 %collective-permute-start.4 = (bf16[384,384]{1,0:T(8,128)(2,1)S(1)}, bf16[384,384]{1,0:T(8,128)(2,1)S(1)}, u32[]{:S(2)}, u32[]{:S(2)}) collective-permute-start(bf16[384,384]{1,0:T(8,128)(2,1)S(1)} %get-tuple-element.15), channel_id=1, source_target_pairs={{0,8},{4,12},{8,0},{12,4},{1,9},{5,13},{9,1},{13,5},{2,10},{6,14},... | collective-permute-start | bytes 884744 | tf_op jit(solution)/shard_map/ppermute | solution.py:22
  8.0 18.7 %collective-permute-start.7 = (bf16[384,384]{1,0:T(8,128)(2,1)S(1)}, bf16[384,384]{1,0:T(8,128)(2,1)S(1)}, u32[]{:S(2)}, u32[]{:S(2)}) collective-permute-start(bf16[384,384]{1,0:T(8,128)(2,1)S(1)} %get-tuple-element.16), channel_id=1, source_target_pairs={{0,12},{4,8},{8,4},{12,0},{1,13},{5,9},{9,5},{13,1},{2,14},{6,10},... | collective-permute-start | bytes 884744 | tf_op jit(solution)/shard_map/ppermute | solution.py:22
  17.5 9.6 %collective-permute-start.2 = (bf16[320,384]{1,0:T(8,128)(2,1)S(1)}, bf16[320,384]{1,0:T(8,128)(2,1)S(1)}, u32[]{:S(2)}, u32[]{:S(2)}) collective-permute-start(bf16[320,384]{1,0:T(8,128)(2,1)S(1)} %pad_maximum_fusion.4), channel_id=1, source_target_pairs={{0,2},{1,3},{2,0},{3,1},{4,6},{5,7},{6,4},{7,5},{8,10},{9,11},{10,... | collective-permute-start | bytes 737288 | tf_op jit(solution)/shard_map/ppermute | solution.py:22
  18.0 14.9 %collective-permute-start.5 = (bf16[320,384]{1,0:T(8,128)(2,1)S(1)}, bf16[320,384]{1,0:T(8,128)(2,1)S(1)}, u32[]{:S(2)}, u32[]{:S(2)}) collective-permute-start(bf16[320,384]{1,0:T(8,128)(2,1)S(1)} %pad_maximum_fusion.5), channel_id=1, source_target_pairs={{0,2},{1,3},{2,0},{3,1},{4,6},{5,7},{6,4},{7,5},{8,10},{9,11},{10,... | collective-permute-start | bytes 737288 | tf_op jit(solution)/shard_map/ppermute | solution.py:22
  26.8 10.2 %collective-permute-start.8 = (bf16[320,384]{1,0:T(8,128)(2,1)S(1)}, bf16[320,384]{1,0:T(8,128)(2,1)S(1)}, u32[]{:S(2)}, u32[]{:S(2)}) collective-permute-start(bf16[320,384]{1,0:T(8,128)(2,1)S(1)} %pad_maximum_fusion.6), channel_id=1, source_target_pairs={{0,2},{1,3},{2,0},{3,1},{4,6},{5,7},{6,4},{7,5},{8,10},{9,11},{10,... | collective-permute-start | bytes 737288 | tf_op jit(solution)/shard_map/ppermute | solution.py:22
  27.2 13.8 %collective-permute-start.3 = (bf16[1152,384]{1,0:T(8,128)(2,1)S(1)}, bf16[1152,384]{1,0:T(8,128)(2,1)S(1)}, u32[]{:S(2)}, u32[]{:S(2)}) collective-permute-start(bf16[1152,384]{1,0:T(8,128)(2,1)S(1)} %get-tuple-element.40.refs_4_), channel_id=1, source_target_pairs={{0,1},{1,0},{2,3},{3,2},{4,5},{5,4},{6,7},{7,6},{8,9},{9,8},{10,11... | collective-permute-start | bytes 2654216 | tf_op jit(solution)/shard_map/ppermute | solution.py:22
  33.0 17.1 %slice-start.1 = ((s8[9437184]{0:T(1024)(128)(4,1)}), s8[4194304]{0:T(1024)(128)(4,1)S(1)}, s32[]{:S(2)}) async-start(s8[9437184]{0:T(1024)(128)(4,1)} %bitcast.7), calls=%async_computation.1 | async-start | bytes 8388608
  33.1 6.5 %collective-permute-start.6 = (bf16[576,384]{1,0:T(8,128)(2,1)S(1)}, bf16[576,384]{1,0:T(8,128)(2,1)S(1)}, u32[]{:S(2)}, u32[]{:S(2)}) collective-permute-start(bf16[576,384]{1,0:T(8,128)(2,1)S(1)} %pad_maximum_fusion.1.refs_6_), channel_id=1, source_target_pairs={{0,1},{1,0},{2,3},{3,2},{4,5},{5,4},{6,7},{7,6},{8,9},{9,8},{10,11... | collective-permute-start | bytes 1327112 | tf_op jit(solution)/shard_map/ppermute | solution.py:22
  37.1 3.9 %collective-permute-start.9 = (bf16[576,384]{1,0:T(8,128)(2,1)S(1)}, bf16[576,384]{1,0:T(8,128)(2,1)S(1)}, u32[]{:S(2)}, u32[]{:S(2)}) collective-permute-start(bf16[576,384]{1,0:T(8,128)(2,1)S(1)} %pad_maximum_fusion.2.refs_8_), channel_id=1, source_target_pairs={{0,1},{1,0},{2,3},{3,2},{4,5},{5,4},{6,7},{7,6},{8,9},{9,8},{10,11... | collective-permute-start | bytes 1327112 | tf_op jit(solution)/shard_map/ppermute | solution.py:22
  42.5 7.6 %slice-start.2 = ((s8[9437184]{0:T(1024)(128)(4,1)}), s8[1048576]{0:T(1024)(128)(4,1)S(1)}, s32[]{:S(2)}) async-start(s8[9437184]{0:T(1024)(128)(4,1)} %bitcast.7), calls=%async_computation.2 | async-start | bytes 2097152
  42.6 7.5 %collective-permute-start.12 = (bf16[4,32,384]{2,1,0:T(8,128)(2,1)S(1)}, bf16[4,32,384]{2,1,0:T(8,128)(2,1)S(1)}, u32[]{:S(2)}, u32[]{:S(2)}) collective-permute-start(bf16[4,32,384]{2,1,0:T(8,128)(2,1)S(1)} %shard_map.94), channel_id=1, source_target_pairs={{0,12},{4,8},{8,4},{12,0},{1,13},{5,9},{9,5},{13,1},{2,14},{6,10},... | collective-permute-start | bytes 294920 | tf_op jit(solution)/shard_map/ppermute | solution.py:22
  46.3 9.3 %collective-permute-start.10 = (bf16[4,32,384]{2,1,0:T(8,128)(2,1)S(1)}, bf16[4,32,384]{2,1,0:T(8,128)(2,1)S(1)}, u32[]{:S(2)}, u32[]{:S(2)}) collective-permute-start(bf16[4,32,384]{2,1,0:T(8,128)(2,1)S(1)} %shard_map.92), channel_id=1, source_target_pairs={{0,8},{4,12},{8,0},{12,4},{1,9},{5,13},{9,1},{13,5},{2,10},{6,14},... | collective-permute-start | bytes 294920 | tf_op jit(solution)/shard_map/ppermute | solution.py:22
  49.9 6.1 %collective-permute-start.11 = (bf16[4,32,384]{2,1,0:T(8,128)(2,1)S(1)}, bf16[4,32,384]{2,1,0:T(8,128)(2,1)S(1)}, u32[]{:S(2)}, u32[]{:S(2)}) collective-permute-start(bf16[4,32,384]{2,1,0:T(8,128)(2,1)S(1)} %get-tuple-element.17), channel_id=1, source_target_pairs={{0,4},{4,0},{8,12},{12,8},{1,5},{5,1},{9,13},{13,9},{2,6},{6,2},{1... | collective-permute-start | bytes 294920 | tf_op jit(solution)/shard_map/ppermute | solution.py:22
  50.1 5.8 %copy-start.1 = (bf16[3072,64]{0,1:T(8,128)(2,1)S(1)}, bf16[3072,64]{0,1:T(8,128)(2,1)}, u32[]{:S(2)}) copy-start(bf16[3072,64]{0,1:T(8,128)(2,1)} %param.15) | copy-start | bytes 1179652
  50.1 5.8 %copy-start.2 = (f32[3072]{0:T(1024)S(1)}, f32[3072]{0:T(1024)}, u32[]{:S(2)}) copy-start(f32[3072]{0:T(1024)} %param.14) | copy-start | bytes 36868
  50.1 5.8 %copy-start.3 = (f32[3072]{0:T(1024)S(1)}, f32[3072]{0:T(1024)}, u32[]{:S(2)}) copy-start(f32[3072]{0:T(1024)} %param.13) | copy-start | bytes 36868
  56.0 12.4 %copy-start = (bf16[432,512]{1,0:T(8,128)(2,1)S(1)}, bf16[432,512]{1,0:T(8,128)(2,1)}, u32[]{:S(2)}) copy-start(bf16[432,512]{1,0:T(8,128)(2,1)} %w_ref.1) | copy-start | bytes 1327108
  56.0 12.4 %copy-start.4 = (f32[512]{0:T(512)S(1)}, f32[512]{0:T(512)}, u32[]{:S(2)}) copy-start(f32[512]{0:T(512)} %param.17) | copy-start | bytes 6148
  59.8 5.3 %collective-permute-start.13 = (bf16[128,32]{1,0:T(8,128)(2,1)S(1)}, bf16[128,32]{1,0:T(8,128)(2,1)S(1)}, u32[]{:S(2)}, u32[]{:S(2)}) collective-permute-start(bf16[128,32]{1,0:T(8,128)(2,1)S(1)} %get-tuple-element.20.odd_ref), channel_id=1, source_target_pairs={{0,1},{1,2},{2,3},{3,4},{4,5},{5,6},{6,7},{7,8},{8,9},{9,10},{10,1... | collective-permute-start | bytes 24584 | tf_op jit(solution)/shard_map/ppermute | solution.py:376
  63.1 5.2 %collective-permute-start.14 = (bf16[128,32]{1,0:T(8,128)(2,1)S(1)}, bf16[128,32]{1,0:T(8,128)(2,1)S(1)}, u32[]{:S(2)}, u32[]{:S(2)}) collective-permute-start(bf16[128,32]{1,0:T(8,128)(2,1)S(1)} %get-tuple-element.19.even_ref), channel_id=1, source_target_pairs={{1,0},{2,1},{3,2},{4,3},{5,4},{6,5},{7,6},{8,7},{9,8},{10,9},{11,1... | collective-permute-start | bytes 24584 | tf_op jit(solution)/shard_map/ppermute | solution.py:377

commit v14 on v13

--- a/solution.py
+++ b/solution.py
@@ -192,7 +192,7 @@
 
 def final_kernel(where_ref, *refs, targets, planes, rows_dev):
     count = len(targets)
-    partial_ref, scale_ref, shift_ref, w_final_ref, even_ref, odd_ref, lined, projected = refs[2 * count :]
+    partial_ref, scale_ref, shift_ref, w_final_ref, inner_ref, outer_ref, lined, projected = refs[2 * count :]
     step = pl.program_id(0)
     heads_at, plane_at = where_ref[0], where_ref[1]
     tokens = lined.shape[0]
@@ -239,9 +239,9 @@
         row_order = (at == place).astype(jnp.bfloat16)
         cells = jnp.dot(patches, lane_order, preferred_element_type=jnp.float32)
         cells = jnp.dot(row_order, cells.astype(jnp.bfloat16), preferred_element_type=jnp.float32)
-        cells = cells.astype(jnp.bfloat16)
-        even_ref[...] = cells[:, :half]
-        odd_ref[...] = cells[:, half:]
+        first = plane_at % 2 == 0
+        inner_ref[...] = jnp.where(first, cells[:, half:], cells[:, :half]).astype(jnp.bfloat16)
+        outer_ref[...] = jnp.where(first, cells[:, :half], cells[:, half:]).astype(jnp.bfloat16)
 
 
 def final_layer(where, attended, targets, partial, w_out, scale_mod, shift_mod, w_final, rows_dev, planes):
@@ -274,14 +274,19 @@
     )(where, *attended, *[w_out] * len(targets), partial, scale_mod[None], shift_mod[None], w_final.T)
 
 
-def convolve_kernel(where_ref, even_ref, odd_ref, left_ref, right_ref, w_ref, bias_ref, out_ref, latent):
+def convolve_kernel(
+    where_ref, inner_ref, outer_ref, inner_got_ref, outer_got_ref, w_ref, bias_ref, out_ref, latent
+):
     frames, cols, _, ch = latent.shape
-    rows = even_ref.shape[0] // frames
+    rows = inner_ref.shape[0] // frames
     height = 2 * rows
-    even = even_ref[...].astype(jnp.float32)
-    odd = odd_ref[...].astype(jnp.float32)
-    left = jnp.where(where_ref[2] == 0, even, left_ref[...].astype(jnp.float32))
-    right = jnp.where(where_ref[2] == where_ref[3] - 1, odd, right_ref[...].astype(jnp.float32))
+    inner, outer, inner_got, outer_got = [
+        ref[...].astype(jnp.float32) for ref in (inner_ref, outer_ref, inner_got_ref, outer_got_ref)
+    ]
+    first = where_ref[2] % 2 == 0
+    even, odd = jnp.where(first, outer, inner), jnp.where(first, inner, outer)
+    left = jnp.where(where_ref[2] == 0, even, jnp.where(first, outer_got, inner_got))
+    right = jnp.where(where_ref[2] == where_ref[3] - 1, odd, jnp.where(first, inner_got, outer_got))
     for x, cells in enumerate((left, even, odd, right)):
         for f in range(frames):
             own = cells[f * rows : (f + 1) * rows]
@@ -307,8 +312,8 @@
         out_ref[:, x] = acc.reshape(frames, height, acc.shape[1])
 
 
-def convolve(where, even, odd, left, right, conv_weight, conv_bias):
-    rows = even.shape[0] // FRAMES
+def convolve(where, inner, outer, inner_got, outer_got, conv_weight, conv_bias):
+    rows = inner.shape[0] // FRAMES
     channels = conv_weight.shape[1]
     smem = pl.BlockSpec(memory_space=pltpu.SMEM)
     vmem = pl.BlockSpec(memory_space=pltpu.VMEM)
@@ -319,7 +324,7 @@
         out_shape=jax.ShapeDtypeStruct((FRAMES, 2, 2 * rows, channels), jnp.bfloat16),
         scratch_shapes=[pltpu.VMEM((FRAMES, 4, 2 * rows + 16, LATENT_CH), jnp.float32)],
         compiler_params=pltpu.CompilerParams(vmem_limit_bytes=VMEM_LIMIT),
-    )(where, even, odd, left, right, conv_weight, conv_bias[None])
+    )(where, inner, outer, inner_got, outer_got, conv_weight, conv_bias[None])
 
 
 def shards(queries, keys, values, w_out, shift_mod, scale_mod, w_final, conv_weight, conv_bias):
@@ -364,18 +369,18 @@
 
     near, far = (0, 3), (2, 1)
     results = {}
-    for targets in ((3,), (2,), (1, 0)):
+    for targets in ((3,), (2,), (1,), (0,)):
         for t, o in zip(targets, attend(asked, keys_values, targets, planes)):
             results[t] = o if t == 0 else swap(o, "heads", t)
-    partial = project(where, [results[t] for t in near], near, w_out, 512)
+    partial = project(where, [results[t] for t in near], near, w_out, 1024)
     sent = [results[t] for t in far]
-    even, odd = final_layer(
+    inner, outer = final_layer(
         where, sent, far, partial, w_out, scale_mod, shift_mod, w_final, rows_dev, planes
     )
-    both = ("heads", "plane")
-    left = lax.ppermute(odd, both, [(i, i + 1) for i in range(devices - 1)])
-    right = lax.ppermute(even, both, [(i + 1, i) for i in range(devices - 1)])
-    return convolve(where, even, odd, left, right, conv_weight, conv_bias)
+    pairs = [(i, i + 1) for i in range(1, devices - 1, 2)]
+    inner_got = swap(inner, "plane", 1)
+    outer_got = lax.ppermute(outer, ("heads", "plane"), pairs + [(j, i) for i, j in pairs])
+    return convolve(where, inner, outer, inner_got, outer_got, conv_weight, conv_bias)
 
 
 def solution(mesh):

time: 70.7 us -> 67.5 us (0.955)
  starting transfers between devices: 28.8 us -> 26.8 us
    ppermute x2 -> x1, starting transfers between devices: 5.26 us -> 2.07 us  [shards(): lax.ppermute(outer, ('heads', 'plane'), pairs + [(j, i) for i, j in pairs])]
    ppermute x13 -> x14, starting transfers between devices: 23.6 us -> 24.7 us  [swap(): return lax.ppermute(source, axis, [(i, i ^ distance) for i in range(count)])]
    pallas_call x3 -> x4, Pallas kernels: 5.12 us -> 5.68 us  [attend(): pl.pallas_call(functools.partial(attend_kernel, sources=sources, planes=p...]
    ppermute x13 -> x14, waiting for transfers between devices: 21.4 us -> 21 us  [swap(): return lax.ppermute(source, axis, [(i, i ^ distance) for i in range(count)])]
    ppermute x2 -> x1, waiting for transfers between devices: 3.3 us -> 3.13 us  [shards(): lax.ppermute(outer, ('heads', 'plane'), pairs + [(j, i) for i, j in pairs])]
  transfers between devices with their start and end apart: 15 -> 15, of which waited for: 7 -> 6; matrix products, arithmetic and copies ran while one was open for 1% -> 1% of each run, Pallas kernels for 9% -> 9%
where the time goes in v14:
time: 67.5 us; the launch traced here: 67.3 us
  starting transfers between devices  26.8 us (40%)
  waiting for transfers between devices  24.1 us (36%)
  Pallas kernels  14 us (21%)
  other arithmetic  1.64 us (2%)
    ppermute x14, starting transfers between devices, swap(): return lax.ppermute(source, axis, [(i, i ^ distance) for i in range(count)])  24.7 us
    ppermute x14, waiting for transfers between devices, swap(): return lax.ppermute(source, axis, [(i, i ^ distance) for i in range(count)])  21 us
    pallas_call x4, Pallas kernels, attend(): pl.pallas_call(functools.partial(attend_kernel, sources=sources, planes=p...  5.68 us
    pallas_call x1, Pallas kernels, final_layer(): pl.pallas_call(functools.partial(final_kernel, targets=targets, planes=pl...  3.21 us
    ppermute x1, waiting for transfers between devices, shards(): lax.ppermute(outer, ('heads', 'plane'), pairs + [(j, i) for i, j in pairs])  3.13 us
    pallas_call x1, Pallas kernels, convolve(): pl.pallas_call(convolve_kernel, in_specs=[smem] + [vmem] * 6, out_specs=v...  2.17 us
    pallas_call x1, Pallas kernels, project(): pl.pallas_call(functools.partial(project_kernel, targets=targets), grid_s...  2.07 us
    ppermute x1, starting transfers between devices, shards(): lax.ppermute(outer, ('heads', 'plane'), pairs + [(j, i) for i, j in pairs])  2.07 us
  transfers between devices with their start and end apart: 15, of which 6 were waited for; matrix products, arithmetic and copies ran while one was open for 1% of the time, Pallas kernels for 9%

profile of v14, /device:TPU:1, one launch (start us, length us, event | category | flops | bytes accessed | tf_op | source)
XLA Modules:
  0.0 67.3 jit_solution(14364454874894673178)
XLA Ops:
  0.0 1.3 %pad_maximum_fusion.qkv_ref = bf16[384,1536]{1,0:T(8,128)(2,1)S(1)} fusion(bf16[128,1536]{1,0:T(8,128)(2,1)} %param.11, bf16[128,1536]{1,0:T(8,128)(2,1)} %param.10, bf16[128,1536]{1,0:T(8,128)(2,1)} %param.9), kind=kLoop, calls=%fused_computation | loop fusion | flops 3538944 | bytes 2359296 | tf_op jit(solution)/shard_map/concatenate | solution.py:52
  1.3 0.1 pad_add_fusion.where_ref
  1.4 0.8 %shard_map.91 = (bf16[384,384]{1,0:T(8,128)(2,1)S(1)}, bf16[384,384]{1,0:T(8,128)(2,1)S(1)}, bf16[384,384]{1,0:T(8,128)(2,1)S(1)}, bf16[384,384]{1,0:T(8,128)(2,1)S(1)}) custom-call(s32[4]{0:T(128)S(1)} %pad_add_fusion.where_ref, bf16[384,1536]{1,0:T(8,128)(2,1)S(1)} %pad_maximum_fusion.qkv_ref), custom_call_target="tpu_custom_call" | custom-call | tf_op jit(solution)/shard_map/pallas_call | solution.py:46
  2.3 2.1 %collective-permute-start = (bf16[320,384]{1,0:T(8,128)(2,1)S(1)}, bf16[320,384]{1,0:T(8,128)(2,1)S(1)}, u32[]{:S(2)}, u32[]{:S(2)}) collective-permute-start(bf16[320,384]{1,0:T(8,128)(2,1)S(1)} %pad_maximum_fusion.3), channel_id=1, source_target_pairs={{0,2},{1,3},{2,0},{3,1},{4,6},{5,7},{6,4},{7,5},{8,10},{9,11},{10,... | collective-permute-start | bytes 737288 | tf_op jit(solution)/shard_map/ppermute | solution.py:22
  4.4 1.3 %collective-permute-start.1 = (bf16[384,384]{1,0:T(8,128)(2,1)S(1)}, bf16[384,384]{1,0:T(8,128)(2,1)S(1)}, u32[]{:S(2)}, u32[]{:S(2)}) collective-permute-start(bf16[384,384]{1,0:T(8,128)(2,1)S(1)} %get-tuple-element.12), channel_id=1, source_target_pairs={{0,4},{4,0},{8,12},{12,8},{1,5},{5,1},{9,13},{13,9},{2,6},{6,2},{1... | collective-permute-start | bytes 884744 | tf_op jit(solution)/shard_map/ppermute | solution.py:22
  5.7 2.3 %collective-permute-start.4 = (bf16[384,384]{1,0:T(8,128)(2,1)S(1)}, bf16[384,384]{1,0:T(8,128)(2,1)S(1)}, u32[]{:S(2)}, u32[]{:S(2)}) collective-permute-start(bf16[384,384]{1,0:T(8,128)(2,1)S(1)} %get-tuple-element.13), channel_id=1, source_target_pairs={{0,8},{4,12},{8,0},{12,4},{1,9},{5,13},{9,1},{13,5},{2,10},{6,14},... | collective-permute-start | bytes 884744 | tf_op jit(solution)/shard_map/ppermute | solution.py:22
  8.0 0.0 collective-permute-start.7
  8.1 2.1 %collective-permute-done = bf16[320,384]{1,0:T(8,128)(2,1)S(1)} collective-permute-done((bf16[320,384]{1,0:T(8,128)(2,1)S(1)}, bf16[320,384]{1,0:T(8,128)(2,1)S(1)}, u32[]{:S(2)}, u32[]{:S(2)}) %collective-permute-start) | collective-permute-done | bytes 245792 | tf_op jit(solution)/shard_map/ppermute | solution.py:22
  10.1 7.2 %collective-permute-done.1 = bf16[384,384]{1,0:T(8,128)(2,1)S(1)} collective-permute-done((bf16[384,384]{1,0:T(8,128)(2,1)S(1)}, bf16[384,384]{1,0:T(8,128)(2,1)S(1)}, u32[]{:S(2)}, u32[]{:S(2)}) %collective-permute-start.1) | collective-permute-done | bytes 294944 | tf_op jit(solution)/shard_map/ppermute | solution.py:22
  17.4 0.1 fusion.5
  17.5 0.5 collective-permute-start.2
  18.0 0.0 collective-permute-done.4
  18.1 1.1 %collective-permute-start.5 = (bf16[320,384]{1,0:T(8,128)(2,1)S(1)}, bf16[320,384]{1,0:T(8,128)(2,1)S(1)}, u32[]{:S(2)}, u32[]{:S(2)}) collective-permute-start(bf16[320,384]{1,0:T(8,128)(2,1)S(1)} %pad_maximum_fusion.5), channel_id=1, source_target_pairs={{0,2},{1,3},{2,0},{3,1},{4,6},{5,7},{6,4},{7,5},{8,10},{9,11},{10,... | collective-permute-start | bytes 737288 | tf_op jit(solution)/shard_map/ppermute | solution.py:22
  19.2 7.5 %collective-permute-done.7 = bf16[384,384]{1,0:T(8,128)(2,1)S(1)} collective-permute-done((bf16[384,384]{1,0:T(8,128)(2,1)S(1)}, bf16[384,384]{1,0:T(8,128)(2,1)S(1)}, u32[]{:S(2)}, u32[]{:S(2)}) %collective-permute-start.7) | collective-permute-done | bytes 294944 | tf_op jit(solution)/shard_map/ppermute | solution.py:22
  26.8 0.3 collective-permute-start.8
  27.1 0.0 collective-permute-done.2
  27.2 5.7 %collective-permute-start.3 = (bf16[1152,384]{1,0:T(8,128)(2,1)S(1)}, bf16[1152,384]{1,0:T(8,128)(2,1)S(1)}, u32[]{:S(2)}, u32[]{:S(2)}) collective-permute-start(bf16[1152,384]{1,0:T(8,128)(2,1)S(1)} %get-tuple-element.36.refs_4_), channel_id=1, source_target_pairs={{0,1},{1,0},{2,3},{3,2},{4,5},{5,4},{6,7},{7,6},{8,9},{9,8},{10,11... | collective-permute-start | bytes 2654216 | tf_op jit(solution)/shard_map/ppermute | solution.py:22
  33.0 0.0 collective-permute-done.5
  33.1 3.9 %collective-permute-start.6 = (bf16[576,384]{1,0:T(8,128)(2,1)S(1)}, bf16[576,384]{1,0:T(8,128)(2,1)S(1)}, u32[]{:S(2)}, u32[]{:S(2)}) collective-permute-start(bf16[576,384]{1,0:T(8,128)(2,1)S(1)} %pad_maximum_fusion.1.refs_6_), channel_id=1, source_target_pairs={{0,1},{1,0},{2,3},{3,2},{4,5},{5,4},{6,7},{7,6},{8,9},{9,8},{10,11... | collective-permute-start | bytes 1327112 | tf_op jit(solution)/shard_map/ppermute | solution.py:22
  36.9 0.0 collective-permute-done.8
  37.0 0.0 slice-start
  37.1 2.5 %collective-permute-start.9 = (bf16[576,384]{1,0:T(8,128)(2,1)S(1)}, bf16[576,384]{1,0:T(8,128)(2,1)S(1)}, u32[]{:S(2)}, u32[]{:S(2)}) collective-permute-start(bf16[576,384]{1,0:T(8,128)(2,1)S(1)} %pad_maximum_fusion.2.refs_8_), channel_id=1, source_target_pairs={{0,1},{1,0},{2,3},{3,2},{4,5},{5,4},{6,7},{7,6},{8,9},{9,8},{10,11... | collective-permute-start | bytes 1327112 | tf_op jit(solution)/shard_map/ppermute | solution.py:22
  39.6 0.0 collective-permute-done.6.refs_7_
  39.6 1.4 %collective-permute-done.9.refs_9_ = bf16[576,384]{1,0:T(8,128)(2,1)S(1)} collective-permute-done((bf16[576,384]{1,0:T(8,128)(2,1)S(1)}, bf16[576,384]{1,0:T(8,128)(2,1)S(1)}, u32[]{:S(2)}, u32[]{:S(2)}) %collective-permute-start.9) | collective-permute-done | bytes 442400 | tf_op jit(solution)/shard_map/ppermute | solution.py:22
  41.0 0.0 collective-permute-done.3.refs_5_
  41.1 0.0 slice-start.1
  41.1 1.4 %shard_map.95 = bf16[4,32,384]{2,1,0:T(8,128)(2,1)S(1)} custom-call(bf16[128,384]{1,0:T(8,128)(2,1)S(1)} %get-tuple-element.39.refs_0_, bf16[128,384]{1,0:T(8,128)(2,1)S(1)} %get-tuple-element.40.refs_1_, bf16[128,384]{1,0:T(8,128)(2,1)S(1)} %pad_maximum_fusion.9.refs_2_, bf16[128,384]{1,0:T(8,128)(2,1)S(1)} %pad_maximum_fusion.10.refs_3_, ...), custom_call_target="tpu_custom_call" | custom-call | tf_op jit(solution)/shard_map/pallas_call | solution.py:134
  42.6 2.3 %collective-permute-start.12 = (bf16[4,32,384]{2,1,0:T(8,128)(2,1)S(1)}, bf16[4,32,384]{2,1,0:T(8,128)(2,1)S(1)}, u32[]{:S(2)}, u32[]{:S(2)}) collective-permute-start(bf16[4,32,384]{2,1,0:T(8,128)(2,1)S(1)} %shard_map.95), channel_id=1, source_target_pairs={{0,12},{4,8},{8,4},{12,0},{1,13},{5,9},{9,5},{13,1},{2,14},{6,10},... | collective-permute-start | bytes 294920 | tf_op jit(solution)/shard_map/ppermute | solution.py:22
  44.8 1.4 %shard_map.92 = bf16[4,32,384]{2,1,0:T(8,128)(2,1)S(1)} custom-call(bf16[128,384]{1,0:T(8,128)(2,1)S(1)} %get-tuple-element.39.refs_0_, bf16[128,384]{1,0:T(8,128)(2,1)S(1)} %get-tuple-element.40.refs_1_, bf16[128,384]{1,0:T(8,128)(2,1)S(1)} %pad_maximum_fusion.9.refs_2_, bf16[128,384]{1,0:T(8,128)(2,1)S(1)} %pad_maximum_fusion.10.refs_3_, ...), custom_call_target="tpu_custom_call" | custom-call | tf_op jit(solution)/shard_map/pallas_call | solution.py:134
  46.3 0.0 slice-start.2
  46.3 1.3 %collective-permute-start.10 = (bf16[4,32,384]{2,1,0:T(8,128)(2,1)S(1)}, bf16[4,32,384]{2,1,0:T(8,128)(2,1)S(1)}, u32[]{:S(2)}, u32[]{:S(2)}) collective-permute-start(bf16[4,32,384]{2,1,0:T(8,128)(2,1)S(1)} %shard_map.92), channel_id=1, source_target_pairs={{0,8},{4,12},{8,0},{12,4},{1,9},{5,13},{9,1},{13,5},{2,10},{6,14},... | collective-permute-start | bytes 294920 | tf_op jit(solution)/shard_map/ppermute | solution.py:22
  47.6 1.4 %shard_map.93 = bf16[4,32,384]{2,1,0:T(8,128)(2,1)S(1)} custom-call(bf16[128,384]{1,0:T(8,128)(2,1)S(1)} %get-tuple-element.39.refs_0_, bf16[128,384]{1,0:T(8,128)(2,1)S(1)} %get-tuple-element.40.refs_1_, bf16[128,384]{1,0:T(8,128)(2,1)S(1)} %pad_maximum_fusion.9.refs_2_, bf16[128,384]{1,0:T(8,128)(2,1)S(1)} %pad_maximum_fusion.10.refs_3_, ...), custom_call_target="tpu_custom_call" | custom-call | tf_op jit(solution)/shard_map/pallas_call | solution.py:134
  49.0 0.2 collective-permute-start.11
  49.3 1.4 %shard_map.94.refs_0_ = bf16[4,32,384]{2,1,0:T(8,128)(2,1)S(1)} custom-call(bf16[128,384]{1,0:T(8,128)(2,1)S(1)} %get-tuple-element.39.refs_0_, bf16[128,384]{1,0:T(8,128)(2,1)S(1)} %get-tuple-element.40.refs_1_, bf16[128,384]{1,0:T(8,128)(2,1)S(1)} %pad_maximum_fusion.9.refs_2_, bf16[128,384]{1,0:T(8,128)(2,1)S(1)} %pad_maximum_fusion.10.refs_3_, ...), custom_call_target="tpu_custom_call" | custom-call | tf_op jit(solution)/shard_map/pallas_call | solution.py:134
  50.7 0.0 copy-start.1
  50.7 0.0 copy-start.2
  50.7 0.0 copy-start.3
  50.7 0.0 collective-permute-done.12.refs_1_
  50.7 0.0 slice-done
  50.7 0.0 slice-done.1
  50.7 0.0 slice-done.2
  50.8 2.1 %shard_map.96.refs_4_ = f32[3,128,1024]{2,1,0:T(8,128)S(1)} custom-call(s32[4]{0:T(128)S(1)} %pad_add_fusion.where_ref, bf16[4,32,384]{2,1,0:T(8,128)(2,1)S(1)} %shard_map.94.refs_0_, bf16[4,32,384]{2,1,0:T(8,128)(2,1)S(1)} %collective-permute-done.12.refs_1_, bf16[1536,3072]{1,0:T(8,128)(2,1)S(1)} %bitcast.8, bf16[1536,3072]{1,0:T(8,128)(2,1)S(1)} %bitcast.8), custom_call_target="tpu_custom_call" | custom-call | tf_op jit(solution)/shard_map/pallas_call | solution.py:179
  52.8 2.7 %collective-permute-done.10.refs_0_ = bf16[4,32,384]{2,1,0:T(8,128)(2,1)S(1)} collective-permute-done((bf16[4,32,384]{2,1,0:T(8,128)(2,1)S(1)}, bf16[4,32,384]{2,1,0:T(8,128)(2,1)S(1)}, u32[]{:S(2)}, u32[]{:S(2)}) %collective-permute-start.10) | collective-permute-done | bytes 98336 | tf_op jit(solution)/shard_map/ppermute | solution.py:22
  55.5 0.0 collective-permute-done.11.refs_1_
  55.5 0.0 copy-done.1
  55.5 0.0 copy-done.2
  55.5 0.0 copy-done.3
  55.6 0.0 copy-start
  55.6 0.0 copy-start.4
  55.6 3.2 %shard_map.97 = (bf16[128,32]{1,0:T(8,128)(2,1)S(1)}, bf16[128,32]{1,0:T(8,128)(2,1)S(1)}) custom-call(s32[4]{0:T(128)S(1)} %pad_add_fusion.where_ref, bf16[4,32,384]{2,1,0:T(8,128)(2,1)S(1)} %collective-permute-done.10.refs_0_, bf16[4,32,384]{2,1,0:T(8,128)(2,1)S(1)} %collective-permute-done.11.refs_1_, bf16[1536,3072]{1,0:T(8,128)(2,1)S(1)} %bitcast.8, ...), custom_call_target="tpu_custom_call" | custom-call | tf_op jit(solution)/shard_map/pallas_call | solution.py:254
  58.8 1.1 %collective-permute-start.13 = (bf16[128,32]{1,0:T(8,128)(2,1)S(1)}, bf16[128,32]{1,0:T(8,128)(2,1)S(1)}, u32[]{:S(2)}, u32[]{:S(2)}) collective-permute-start(bf16[128,32]{1,0:T(8,128)(2,1)S(1)} %get-tuple-element.15.inner_ref), channel_id=1, source_target_pairs={{0,1},{1,0},{2,3},{3,2},{4,5},{5,4},{6,7},{7,6},{8,9},{9,8},{10,11... | collective-permute-start | bytes 24584 | tf_op jit(solution)/shard_map/ppermute | solution.py:22
  59.9 2.1 %collective-permute-start.14 = (bf16[128,32]{1,0:T(8,128)(2,1)S(1)}, bf16[128,32]{1,0:T(8,128)(2,1)S(1)}, u32[]{:S(2)}, u32[]{:S(2)}) collective-permute-start(bf16[128,32]{1,0:T(8,128)(2,1)S(1)} %get-tuple-element.16.outer_ref), channel_id=1, source_target_pairs={{1,2},{3,4},{5,6},{7,8},{9,10},{11,12},{13,14},{2,1},{4,3},{6,5},{... | collective-permute-start | bytes 24584 | tf_op jit(solution)/shard_map/ppermute | solution.py:382
  62.0 0.0 collective-permute-done.13.inner_got_ref
  62.0 3.1 %collective-permute-done.14.outer_got_ref = bf16[128,32]{1,0:T(8,128)(2,1)S(1)} collective-permute-done((bf16[128,32]{1,0:T(8,128)(2,1)S(1)}, bf16[128,32]{1,0:T(8,128)(2,1)S(1)}, u32[]{:S(2)}, u32[]{:S(2)}) %collective-permute-start.14) | collective-permute-done | bytes 8224 | tf_op jit(solution)/shard_map/ppermute | solution.py:382
  65.1 0.0 copy-done
  65.1 0.0 copy-done.4
  65.1 2.2 %shard_map.98 = bf16[4,2,64,512]{3,2,1,0:T(8,128)(2,1)} custom-call(s32[4]{0:T(128)S(1)} %pad_add_fusion.where_ref, bf16[128,32]{1,0:T(8,128)(2,1)S(1)} %get-tuple-element.15.inner_ref, bf16[128,32]{1,0:T(8,128)(2,1)S(1)} %get-tuple-element.16.outer_ref, bf16[128,32]{1,0:T(8,128)(2,1)S(1)} %collective-permute-done.13.inner_got_ref, ...), custom_call_target="tpu_custom_call" | custom-call | tf_op jit(solution)/shard_map/pallas_call | solution.py:320
  (32 shorter events, 0.6 us)
Async XLA Ops:
  2.3 7.8 %collective-permute-start = (bf16[320,384]{1,0:T(8,128)(2,1)S(1)}, bf16[320,384]{1,0:T(8,128)(2,1)S(1)}, u32[]{:S(2)}, u32[]{:S(2)}) collective-permute-start(bf16[320,384]{1,0:T(8,128)(2,1)S(1)} %pad_maximum_fusion.3), channel_id=1, source_target_pairs={{0,2},{1,3},{2,0},{3,1},{4,6},{5,7},{6,4},{7,5},{8,10},{9,11},{10,... | collective-permute-start | bytes 737288 | tf_op jit(solution)/shard_map/ppermute | solution.py:22
  4.4 13.0 %collective-permute-start.1 = (bf16[384,384]{1,0:T(8,128)(2,1)S(1)}, bf16[384,384]{1,0:T(8,128)(2,1)S(1)}, u32[]{:S(2)}, u32[]{:S(2)}) collective-permute-start(bf16[384,384]{1,0:T(8,128)(2,1)S(1)} %get-tuple-element.12), channel_id=1, source_target_pairs={{0,4},{4,0},{8,12},{12,8},{1,5},{5,1},{9,13},{13,9},{2,6},{6,2},{1... | collective-permute-start | bytes 884744 | tf_op jit(solution)/shard_map/ppermute | solution.py:22
  5.7 12.2 %collective-permute-start.4 = (bf16[384,384]{1,0:T(8,128)(2,1)S(1)}, bf16[384,384]{1,0:T(8,128)(2,1)S(1)}, u32[]{:S(2)}, u32[]{:S(2)}) collective-permute-start(bf16[384,384]{1,0:T(8,128)(2,1)S(1)} %get-tuple-element.13), channel_id=1, source_target_pairs={{0,8},{4,12},{8,0},{12,4},{1,9},{5,13},{9,1},{13,5},{2,10},{6,14},... | collective-permute-start | bytes 884744 | tf_op jit(solution)/shard_map/ppermute | solution.py:22
  8.0 18.7 %collective-permute-start.7 = (bf16[384,384]{1,0:T(8,128)(2,1)S(1)}, bf16[384,384]{1,0:T(8,128)(2,1)S(1)}, u32[]{:S(2)}, u32[]{:S(2)}) collective-permute-start(bf16[384,384]{1,0:T(8,128)(2,1)S(1)} %get-tuple-element.14), channel_id=1, source_target_pairs={{0,12},{4,8},{8,4},{12,0},{1,13},{5,9},{9,5},{13,1},{2,14},{6,10},... | collective-permute-start | bytes 884744 | tf_op jit(solution)/shard_map/ppermute | solution.py:22
  17.5 9.6 %collective-permute-start.2 = (bf16[320,384]{1,0:T(8,128)(2,1)S(1)}, bf16[320,384]{1,0:T(8,128)(2,1)S(1)}, u32[]{:S(2)}, u32[]{:S(2)}) collective-permute-start(bf16[320,384]{1,0:T(8,128)(2,1)S(1)} %pad_maximum_fusion.4), channel_id=1, source_target_pairs={{0,2},{1,3},{2,0},{3,1},{4,6},{5,7},{6,4},{7,5},{8,10},{9,11},{10,... | collective-permute-start | bytes 737288 | tf_op jit(solution)/shard_map/ppermute | solution.py:22
  18.1 14.9 %collective-permute-start.5 = (bf16[320,384]{1,0:T(8,128)(2,1)S(1)}, bf16[320,384]{1,0:T(8,128)(2,1)S(1)}, u32[]{:S(2)}, u32[]{:S(2)}) collective-permute-start(bf16[320,384]{1,0:T(8,128)(2,1)S(1)} %pad_maximum_fusion.5), channel_id=1, source_target_pairs={{0,2},{1,3},{2,0},{3,1},{4,6},{5,7},{6,4},{7,5},{8,10},{9,11},{10,... | collective-permute-start | bytes 737288 | tf_op jit(solution)/shard_map/ppermute | solution.py:22
  26.8 10.2 %collective-permute-start.8 = (bf16[320,384]{1,0:T(8,128)(2,1)S(1)}, bf16[320,384]{1,0:T(8,128)(2,1)S(1)}, u32[]{:S(2)}, u32[]{:S(2)}) collective-permute-start(bf16[320,384]{1,0:T(8,128)(2,1)S(1)} %pad_maximum_fusion.6), channel_id=1, source_target_pairs={{0,2},{1,3},{2,0},{3,1},{4,6},{5,7},{6,4},{7,5},{8,10},{9,11},{10,... | collective-permute-start | bytes 737288 | tf_op jit(solution)/shard_map/ppermute | solution.py:22
  27.2 13.8 %collective-permute-start.3 = (bf16[1152,384]{1,0:T(8,128)(2,1)S(1)}, bf16[1152,384]{1,0:T(8,128)(2,1)S(1)}, u32[]{:S(2)}, u32[]{:S(2)}) collective-permute-start(bf16[1152,384]{1,0:T(8,128)(2,1)S(1)} %get-tuple-element.36.refs_4_), channel_id=1, source_target_pairs={{0,1},{1,0},{2,3},{3,2},{4,5},{5,4},{6,7},{7,6},{8,9},{9,8},{10,11... | collective-permute-start | bytes 2654216 | tf_op jit(solution)/shard_map/ppermute | solution.py:22
  33.1 6.5 %collective-permute-start.6 = (bf16[576,384]{1,0:T(8,128)(2,1)S(1)}, bf16[576,384]{1,0:T(8,128)(2,1)S(1)}, u32[]{:S(2)}, u32[]{:S(2)}) collective-permute-start(bf16[576,384]{1,0:T(8,128)(2,1)S(1)} %pad_maximum_fusion.1.refs_6_), channel_id=1, source_target_pairs={{0,1},{1,0},{2,3},{3,2},{4,5},{5,4},{6,7},{7,6},{8,9},{9,8},{10,11... | collective-permute-start | bytes 1327112 | tf_op jit(solution)/shard_map/ppermute | solution.py:22
  37.0 13.7 %slice-start = ((s8[9437184]{0:T(1024)(128)(4,1)}), s8[4194304]{0:T(1024)(128)(4,1)S(1)}, s32[]{:S(2)}) async-start(s8[9437184]{0:T(1024)(128)(4,1)} %bitcast.7), calls=%async_computation | async-start | bytes 8388608
  37.1 3.9 %collective-permute-start.9 = (bf16[576,384]{1,0:T(8,128)(2,1)S(1)}, bf16[576,384]{1,0:T(8,128)(2,1)S(1)}, u32[]{:S(2)}, u32[]{:S(2)}) collective-permute-start(bf16[576,384]{1,0:T(8,128)(2,1)S(1)} %pad_maximum_fusion.2.refs_8_), channel_id=1, source_target_pairs={{0,1},{1,0},{2,3},{3,2},{4,5},{5,4},{6,7},{7,6},{8,9},{9,8},{10,11... | collective-permute-start | bytes 1327112 | tf_op jit(solution)/shard_map/ppermute | solution.py:22
  41.1 9.6 %slice-start.1 = ((s8[9437184]{0:T(1024)(128)(4,1)}), s8[4194304]{0:T(1024)(128)(4,1)S(1)}, s32[]{:S(2)}) async-start(s8[9437184]{0:T(1024)(128)(4,1)} %bitcast.7), calls=%async_computation.1 | async-start | bytes 8388608
  42.6 8.1 %collective-permute-start.12 = (bf16[4,32,384]{2,1,0:T(8,128)(2,1)S(1)}, bf16[4,32,384]{2,1,0:T(8,128)(2,1)S(1)}, u32[]{:S(2)}, u32[]{:S(2)}) collective-permute-start(bf16[4,32,384]{2,1,0:T(8,128)(2,1)S(1)} %shard_map.95), channel_id=1, source_target_pairs={{0,12},{4,8},{8,4},{12,0},{1,13},{5,9},{9,5},{13,1},{2,14},{6,10},... | collective-permute-start | bytes 294920 | tf_op jit(solution)/shard_map/ppermute | solution.py:22
  46.3 4.5 %slice-start.2 = ((s8[9437184]{0:T(1024)(128)(4,1)}), s8[1048576]{0:T(1024)(128)(4,1)S(1)}, s32[]{:S(2)}) async-start(s8[9437184]{0:T(1024)(128)(4,1)} %bitcast.7), calls=%async_computation.2 | async-start | bytes 2097152
  46.3 9.3 %collective-permute-start.10 = (bf16[4,32,384]{2,1,0:T(8,128)(2,1)S(1)}, bf16[4,32,384]{2,1,0:T(8,128)(2,1)S(1)}, u32[]{:S(2)}, u32[]{:S(2)}) collective-permute-start(bf16[4,32,384]{2,1,0:T(8,128)(2,1)S(1)} %shard_map.92), channel_id=1, source_target_pairs={{0,8},{4,12},{8,0},{12,4},{1,9},{5,13},{9,1},{13,5},{2,10},{6,14},... | collective-permute-start | bytes 294920 | tf_op jit(solution)/shard_map/ppermute | solution.py:22
  49.0 6.5 %collective-permute-start.11 = (bf16[4,32,384]{2,1,0:T(8,128)(2,1)S(1)}, bf16[4,32,384]{2,1,0:T(8,128)(2,1)S(1)}, u32[]{:S(2)}, u32[]{:S(2)}) collective-permute-start(bf16[4,32,384]{2,1,0:T(8,128)(2,1)S(1)} %shard_map.93), channel_id=1, source_target_pairs={{0,4},{4,0},{8,12},{12,8},{1,5},{5,1},{9,13},{13,9},{2,6},{6,2},{1... | collective-permute-start | bytes 294920 | tf_op jit(solution)/shard_map/ppermute | solution.py:22
  50.7 4.9 %copy-start.1 = (bf16[3072,64]{0,1:T(8,128)(2,1)S(1)}, bf16[3072,64]{0,1:T(8,128)(2,1)}, u32[]{:S(2)}) copy-start(bf16[3072,64]{0,1:T(8,128)(2,1)} %param.15) | copy-start | bytes 1179652
  50.7 4.9 %copy-start.2 = (f32[3072]{0:T(1024)S(1)}, f32[3072]{0:T(1024)}, u32[]{:S(2)}) copy-start(f32[3072]{0:T(1024)} %param.14) | copy-start | bytes 36868
  50.7 4.9 %copy-start.3 = (f32[3072]{0:T(1024)S(1)}, f32[3072]{0:T(1024)}, u32[]{:S(2)}) copy-start(f32[3072]{0:T(1024)} %param.13) | copy-start | bytes 36868
  55.6 9.6 %copy-start = (bf16[432,512]{1,0:T(8,128)(2,1)S(1)}, bf16[432,512]{1,0:T(8,128)(2,1)}, u32[]{:S(2)}) copy-start(bf16[432,512]{1,0:T(8,128)(2,1)} %w_ref.1) | copy-start | bytes 1327108
  55.6 9.6 %copy-start.4 = (f32[512]{0:T(512)S(1)}, f32[512]{0:T(512)}, u32[]{:S(2)}) copy-start(f32[512]{0:T(512)} %param.17) | copy-start | bytes 6148
  58.8 3.2 %collective-permute-start.13 = (bf16[128,32]{1,0:T(8,128)(2,1)S(1)}, bf16[128,32]{1,0:T(8,128)(2,1)S(1)}, u32[]{:S(2)}, u32[]{:S(2)}) collective-permute-start(bf16[128,32]{1,0:T(8,128)(2,1)S(1)} %get-tuple-element.15.inner_ref), channel_id=1, source_target_pairs={{0,1},{1,0},{2,3},{3,2},{4,5},{5,4},{6,7},{7,6},{8,9},{9,8},{10,11... | collective-permute-start | bytes 24584 | tf_op jit(solution)/shard_map/ppermute | solution.py:22
  59.9 5.2 %collective-permute-start.14 = (bf16[128,32]{1,0:T(8,128)(2,1)S(1)}, bf16[128,32]{1,0:T(8,128)(2,1)S(1)}, u32[]{:S(2)}, u32[]{:S(2)}) collective-permute-start(bf16[128,32]{1,0:T(8,128)(2,1)S(1)} %get-tuple-element.16.outer_ref), channel_id=1, source_target_pairs={{1,2},{3,4},{5,6},{7,8},{9,10},{11,12},{13,14},{2,1},{4,3},{6,5},{... | collective-permute-start | bytes 24584 | tf_op jit(solution)/shard_map/ppermute | solution.py:382

commit v15 on v14

--- a/solution.py
+++ b/solution.py
@@ -274,57 +274,95 @@
     )(where, *attended, *[w_out] * len(targets), partial, scale_mod[None], shift_mod[None], w_final.T)
 
 
-def convolve_kernel(
-    where_ref, inner_ref, outer_ref, inner_got_ref, outer_got_ref, w_ref, bias_ref, out_ref, latent
-):
-    frames, cols, _, ch = latent.shape
-    rows = inner_ref.shape[0] // frames
-    height = 2 * rows
-    inner, outer, inner_got, outer_got = [
-        ref[...].astype(jnp.float32) for ref in (inner_ref, outer_ref, inner_got_ref, outer_got_ref)
-    ]
-    first = where_ref[2] % 2 == 0
-    even, odd = jnp.where(first, outer, inner), jnp.where(first, inner, outer)
-    left = jnp.where(where_ref[2] == 0, even, jnp.where(first, outer_got, inner_got))
-    right = jnp.where(where_ref[2] == where_ref[3] - 1, odd, jnp.where(first, inner_got, outer_got))
-    for x, cells in enumerate((left, even, odd, right)):
+def lay_out(latent, columns):
+    frames, _, extent, ch = latent.shape
+    height = extent - 16
+    rows = height // 2
+    for x, cells in enumerate(columns):
         for f in range(frames):
             own = cells[f * rows : (f + 1) * rows]
             for p in range(2):
                 latent[f, x, pl.ds(8 + p, rows, stride=2), :] = own[:, p * ch : (p + 1) * ch]
             latent[f, x, 7:8, :] = own[:1, :ch]
             latent[f, x, 8 + height : 9 + height, :] = own[rows - 1 :, ch:]
-    depth = 9 * ch
-    for x in range(cols - 2):
-        stacked = []
-        for f in range(frames):
-            taps = [latent[f, x + b, 7 + e : 7 + e + height, :] for b in range(3) for e in range(3)]
-            stacked.append(jnp.concatenate(taps, axis=1).astype(jnp.bfloat16))
-        stacked = [stacked[0]] * 2 + stacked
-        acc = None
-        for a in range(3):
-            flat = jnp.concatenate(stacked[a : a + frames], axis=0)
-            part = jnp.dot(
-                flat, w_ref[a * depth : (a + 1) * depth, :], preferred_element_type=jnp.float32
-            )
-            acc = part if acc is None else acc + part
-        acc = (acc + bias_ref[...]).astype(jnp.bfloat16)
-        out_ref[:, x] = acc.reshape(frames, height, acc.shape[1])
-
-
-def convolve(where, inner, outer, inner_got, outer_got, conv_weight, conv_bias):
+
+
+def tap_sum(latent, w_ref, columns, shift):
+    frames, _, extent, ch = latent.shape
+    height = extent - 16
+    stacked = []
+    for f in range(frames):
+        taps = [latent[f, x, 7 + e : 7 + e + height, :] for x in columns for e in range(3)]
+        stacked.append(jnp.concatenate(taps, axis=1).astype(jnp.bfloat16))
+    stacked = [stacked[0]] * 2 + stacked
+    depth = 3 * len(columns) * ch
+    total = None
+    for a in range(3):
+        flat = jnp.concatenate(stacked[a : a + frames], axis=0)
+        first = (9 * a + 3 * shift) * ch
+        part = jnp.dot(flat, w_ref[first : first + depth, :], preferred_element_type=jnp.float32)
+        total = part if total is None else total + part
+    return total
+
+
+def own_columns(where_ref, inner_ref, outer_ref):
+    inner, outer = inner_ref[...].astype(jnp.float32), outer_ref[...].astype(jnp.float32)
+    first = where_ref[2] % 2 == 0
+    return jnp.where(first, outer, inner), jnp.where(first, inner, outer)
+
+
+def own_taps_kernel(where_ref, inner_ref, outer_ref, w_ref, out_ref, latent):
+    lay_out(latent, own_columns(where_ref, inner_ref, outer_ref))
+    out_ref[0] = tap_sum(latent, w_ref, (0, 1), 1)
+    out_ref[1] = tap_sum(latent, w_ref, (0, 1), 0)
+
+
+def halo_taps_kernel(
+    where_ref, inner_ref, outer_ref, inner_got_ref, outer_got_ref, own_ref, w_ref, bias_ref, out_ref, latent
+):
+    even, odd = own_columns(where_ref, inner_ref, outer_ref)
+    right, left = own_columns(where_ref, outer_got_ref, inner_got_ref)
+    left = jnp.where(where_ref[2] == 0, even, left)
+    right = jnp.where(where_ref[2] == where_ref[3] - 1, odd, right)
+    lay_out(latent, (left, right))
+    frames, _, height, channels = out_ref.shape
+    for x in range(2):
+        total = own_ref[x] + tap_sum(latent, w_ref, (x,), 2 * x) + bias_ref[...]
+        out_ref[:, x] = total.astype(jnp.bfloat16).reshape(frames, height, channels)
+
+
+def latent_scratch(rows):
+    return [pltpu.VMEM((FRAMES, 2, 2 * rows + 16, LATENT_CH), jnp.float32)]
+
+
+def convolve_own(where, inner, outer, conv_weight):
     rows = inner.shape[0] // FRAMES
     channels = conv_weight.shape[1]
     smem = pl.BlockSpec(memory_space=pltpu.SMEM)
     vmem = pl.BlockSpec(memory_space=pltpu.VMEM)
     return pl.pallas_call(
-        convolve_kernel,
-        in_specs=[smem] + [vmem] * 6,
+        own_taps_kernel,
+        in_specs=[smem] + [vmem] * 3,
+        out_specs=vmem,
+        out_shape=jax.ShapeDtypeStruct((2, FRAMES * 2 * rows, channels), jnp.float32),
+        scratch_shapes=latent_scratch(rows),
+        compiler_params=pltpu.CompilerParams(vmem_limit_bytes=VMEM_LIMIT),
+    )(where, inner, outer, conv_weight)
+
+
+def convolve_halo(where, inner, outer, inner_got, outer_got, own, conv_weight, conv_bias):
+    rows = inner.shape[0] // FRAMES
+    channels = conv_weight.shape[1]
+    smem = pl.BlockSpec(memory_space=pltpu.SMEM)
+    vmem = pl.BlockSpec(memory_space=pltpu.VMEM)
+    return pl.pallas_call(
+        halo_taps_kernel,
+        in_specs=[smem] + [vmem] * 7,
         out_specs=vmem,
         out_shape=jax.ShapeDtypeStruct((FRAMES, 2, 2 * rows, channels), jnp.bfloat16),
-        scratch_shapes=[pltpu.VMEM((FRAMES, 4, 2 * rows + 16, LATENT_CH), jnp.float32)],
+        scratch_shapes=latent_scratch(rows),
         compiler_params=pltpu.CompilerParams(vmem_limit_bytes=VMEM_LIMIT),
-    )(where, inner, outer, inner_got, outer_got, conv_weight, conv_bias[None])
+    )(where, inner, outer, inner_got, outer_got, own, conv_weight, conv_bias[None])
 
 
 def shards(queries, keys, values, w_out, shift_mod, scale_mod, w_final, conv_weight, conv_bias):
@@ -372,7 +410,7 @@
     for targets in ((3,), (2,), (1,), (0,)):
         for t, o in zip(targets, attend(asked, keys_values, targets, planes)):
             results[t] = o if t == 0 else swap(o, "heads", t)
-    partial = project(where, [results[t] for t in near], near, w_out, 1024)
+    partial = project(where, [results[t] for t in near], near, w_out, 1536)
     sent = [results[t] for t in far]
     inner, outer = final_layer(
         where, sent, far, partial, w_out, scale_mod, shift_mod, w_final, rows_dev, planes
@@ -380,7 +418,8 @@
     pairs = [(i, i + 1) for i in range(1, devices - 1, 2)]
     inner_got = swap(inner, "plane", 1)
     outer_got = lax.ppermute(outer, ("heads", "plane"), pairs + [(j, i) for i, j in pairs])
-    return convolve(where, inner, outer, inner_got, outer_got, conv_weight, conv_bias)
+    own = convolve_own(where, inner, outer, conv_weight)
+    return convolve_halo(where, inner, outer, inner_got, outer_got, own, conv_weight, conv_bias)
 
 
 def solution(mesh):

time: 67.5 us -> 67.2 us (level)
  waiting for transfers between devices: 24.1 us -> 23 us
  Pallas kernels: 14 us -> 14.8 us
    ppermute x1, waiting for transfers between devices: 3.13 us -> 1.78 us  [shards(): lax.ppermute(outer, ('heads', 'plane'), pairs + [(j, i) for i, j in pairs])]
    pallas_call x1 -> x2, Pallas kernels: 2.17 us -> 3.41 us  [the longest x1 2.09 us: convolve_halo(): pl.pallas_call(halo_taps_kernel, in_specs=[smem] + [vmem] * 7, out_specs=...]
  transfers between devices with their start and end apart: 15 -> 15, of which waited for: 6 -> 6; matrix products, arithmetic and copies ran while one was open for 1% -> 1% of each run, Pallas kernels for 9% -> 11%
where the time goes in v15:
time: 67.2 us; the launch traced here: 67 us
  starting transfers between devices  26.8 us (40%)
  waiting for transfers between devices  23 us (34%)
  Pallas kernels  14.8 us (22%)
  other arithmetic  1.64 us (2%)
    ppermute x14, starting transfers between devices, swap(): return lax.ppermute(source, axis, [(i, i ^ distance) for i in range(count)])  24.8 us
    ppermute x14, waiting for transfers between devices, swap(): return lax.ppermute(source, axis, [(i, i ^ distance) for i in range(count)])  21.2 us
    pallas_call x4, Pallas kernels, attend(): pl.pallas_call(functools.partial(attend_kernel, sources=sources, planes=p...  5.68 us
    pallas_call x1, Pallas kernels, final_layer(): pl.pallas_call(functools.partial(final_kernel, targets=targets, planes=pl...  3 us
    pallas_call x1, Pallas kernels, convolve_halo(): pl.pallas_call(halo_taps_kernel, in_specs=[smem] + [vmem] * 7, out_specs=...  2.09 us
    ppermute x1, starting transfers between devices, shards(): lax.ppermute(outer, ('heads', 'plane'), pairs + [(j, i) for i, j in pairs])  2.08 us
    pallas_call x1, Pallas kernels, project(): pl.pallas_call(functools.partial(project_kernel, targets=targets), grid_s...  1.87 us
    ppermute x1, waiting for transfers between devices, shards(): lax.ppermute(outer, ('heads', 'plane'), pairs + [(j, i) for i, j in pairs])  1.78 us
  transfers between devices with their start and end apart: 15, of which 6 were waited for; matrix products, arithmetic and copies ran while one was open for 1% of the time, Pallas kernels for 11%

profile of v15, /device:TPU:1, one launch (start us, length us, event | category | flops | bytes accessed | tf_op | source)
XLA Modules:
  0.0 67.0 jit_solution(13987536804348136339)
XLA Ops:
  0.0 1.3 %pad_maximum_fusion.qkv_ref = bf16[384,1536]{1,0:T(8,128)(2,1)S(1)} fusion(bf16[128,1536]{1,0:T(8,128)(2,1)} %param.11, bf16[128,1536]{1,0:T(8,128)(2,1)} %param.10, bf16[128,1536]{1,0:T(8,128)(2,1)} %param.9), kind=kLoop, calls=%fused_computation | loop fusion | flops 3538944 | bytes 2359296 | tf_op jit(solution)/shard_map/concatenate | solution.py:52
  1.3 0.1 pad_add_fusion.where_ref
  1.4 0.8 %shard_map.91 = (bf16[384,384]{1,0:T(8,128)(2,1)S(1)}, bf16[384,384]{1,0:T(8,128)(2,1)S(1)}, bf16[384,384]{1,0:T(8,128)(2,1)S(1)}, bf16[384,384]{1,0:T(8,128)(2,1)S(1)}) custom-call(s32[4]{0:T(128)S(1)} %pad_add_fusion.where_ref, bf16[384,1536]{1,0:T(8,128)(2,1)S(1)} %pad_maximum_fusion.qkv_ref), custom_call_target="tpu_custom_call" | custom-call | tf_op jit(solution)/shard_map/pallas_call | solution.py:46
  2.3 2.1 %collective-permute-start = (bf16[320,384]{1,0:T(8,128)(2,1)S(1)}, bf16[320,384]{1,0:T(8,128)(2,1)S(1)}, u32[]{:S(2)}, u32[]{:S(2)}) collective-permute-start(bf16[320,384]{1,0:T(8,128)(2,1)S(1)} %pad_maximum_fusion.3), channel_id=1, source_target_pairs={{0,2},{1,3},{2,0},{3,1},{4,6},{5,7},{6,4},{7,5},{8,10},{9,11},{10,... | collective-permute-start | bytes 737288 | tf_op jit(solution)/shard_map/ppermute | solution.py:22
  4.4 1.3 %collective-permute-start.1 = (bf16[384,384]{1,0:T(8,128)(2,1)S(1)}, bf16[384,384]{1,0:T(8,128)(2,1)S(1)}, u32[]{:S(2)}, u32[]{:S(2)}) collective-permute-start(bf16[384,384]{1,0:T(8,128)(2,1)S(1)} %get-tuple-element.12), channel_id=1, source_target_pairs={{0,4},{4,0},{8,12},{12,8},{1,5},{5,1},{9,13},{13,9},{2,6},{6,2},{1... | collective-permute-start | bytes 884744 | tf_op jit(solution)/shard_map/ppermute | solution.py:22
  5.7 2.3 %collective-permute-start.4 = (bf16[384,384]{1,0:T(8,128)(2,1)S(1)}, bf16[384,384]{1,0:T(8,128)(2,1)S(1)}, u32[]{:S(2)}, u32[]{:S(2)}) collective-permute-start(bf16[384,384]{1,0:T(8,128)(2,1)S(1)} %get-tuple-element.13), channel_id=1, source_target_pairs={{0,8},{4,12},{8,0},{12,4},{1,9},{5,13},{9,1},{13,5},{2,10},{6,14},... | collective-permute-start | bytes 884744 | tf_op jit(solution)/shard_map/ppermute | solution.py:22
  8.0 0.0 collective-permute-start.7
  8.1 2.1 %collective-permute-done = bf16[320,384]{1,0:T(8,128)(2,1)S(1)} collective-permute-done((bf16[320,384]{1,0:T(8,128)(2,1)S(1)}, bf16[320,384]{1,0:T(8,128)(2,1)S(1)}, u32[]{:S(2)}, u32[]{:S(2)}) %collective-permute-start) | collective-permute-done | bytes 245792 | tf_op jit(solution)/shard_map/ppermute | solution.py:22
  10.1 7.2 %collective-permute-done.1 = bf16[384,384]{1,0:T(8,128)(2,1)S(1)} collective-permute-done((bf16[384,384]{1,0:T(8,128)(2,1)S(1)}, bf16[384,384]{1,0:T(8,128)(2,1)S(1)}, u32[]{:S(2)}, u32[]{:S(2)}) %collective-permute-start.1) | collective-permute-done | bytes 294944 | tf_op jit(solution)/shard_map/ppermute | solution.py:22
  17.4 0.1 fusion.5
  17.5 0.5 collective-permute-start.2
  18.0 0.0 collective-permute-done.4
  18.1 1.1 %collective-permute-start.5 = (bf16[320,384]{1,0:T(8,128)(2,1)S(1)}, bf16[320,384]{1,0:T(8,128)(2,1)S(1)}, u32[]{:S(2)}, u32[]{:S(2)}) collective-permute-start(bf16[320,384]{1,0:T(8,128)(2,1)S(1)} %pad_maximum_fusion.5), channel_id=1, source_target_pairs={{0,2},{1,3},{2,0},{3,1},{4,6},{5,7},{6,4},{7,5},{8,10},{9,11},{10,... | collective-permute-start | bytes 737288 | tf_op jit(solution)/shard_map/ppermute | solution.py:22
  19.2 7.5 %collective-permute-done.7 = bf16[384,384]{1,0:T(8,128)(2,1)S(1)} collective-permute-done((bf16[384,384]{1,0:T(8,128)(2,1)S(1)}, bf16[384,384]{1,0:T(8,128)(2,1)S(1)}, u32[]{:S(2)}, u32[]{:S(2)}) %collective-permute-start.7) | collective-permute-done | bytes 294944 | tf_op jit(solution)/shard_map/ppermute | solution.py:22
  26.8 0.3 collective-permute-start.8
  27.1 0.0 collective-permute-done.2
  27.2 5.7 %collective-permute-start.3 = (bf16[1152,384]{1,0:T(8,128)(2,1)S(1)}, bf16[1152,384]{1,0:T(8,128)(2,1)S(1)}, u32[]{:S(2)}, u32[]{:S(2)}) collective-permute-start(bf16[1152,384]{1,0:T(8,128)(2,1)S(1)} %get-tuple-element.36.refs_4_), channel_id=1, source_target_pairs={{0,1},{1,0},{2,3},{3,2},{4,5},{5,4},{6,7},{7,6},{8,9},{9,8},{10,11... | collective-permute-start | bytes 2654216 | tf_op jit(solution)/shard_map/ppermute | solution.py:22
  33.0 0.0 collective-permute-done.5
  33.1 3.9 %collective-permute-start.6 = (bf16[576,384]{1,0:T(8,128)(2,1)S(1)}, bf16[576,384]{1,0:T(8,128)(2,1)S(1)}, u32[]{:S(2)}, u32[]{:S(2)}) collective-permute-start(bf16[576,384]{1,0:T(8,128)(2,1)S(1)} %pad_maximum_fusion.1.refs_6_), channel_id=1, source_target_pairs={{0,1},{1,0},{2,3},{3,2},{4,5},{5,4},{6,7},{7,6},{8,9},{9,8},{10,11... | collective-permute-start | bytes 1327112 | tf_op jit(solution)/shard_map/ppermute | solution.py:22
  36.9 0.0 collective-permute-done.8
  37.0 0.0 slice-start
  37.1 2.5 %collective-permute-start.9 = (bf16[576,384]{1,0:T(8,128)(2,1)S(1)}, bf16[576,384]{1,0:T(8,128)(2,1)S(1)}, u32[]{:S(2)}, u32[]{:S(2)}) collective-permute-start(bf16[576,384]{1,0:T(8,128)(2,1)S(1)} %pad_maximum_fusion.2.refs_8_), channel_id=1, source_target_pairs={{0,1},{1,0},{2,3},{3,2},{4,5},{5,4},{6,7},{7,6},{8,9},{9,8},{10,11... | collective-permute-start | bytes 1327112 | tf_op jit(solution)/shard_map/ppermute | solution.py:22
  39.6 0.0 collective-permute-done.6.refs_7_
  39.6 1.4 %collective-permute-done.9.refs_9_ = bf16[576,384]{1,0:T(8,128)(2,1)S(1)} collective-permute-done((bf16[576,384]{1,0:T(8,128)(2,1)S(1)}, bf16[576,384]{1,0:T(8,128)(2,1)S(1)}, u32[]{:S(2)}, u32[]{:S(2)}) %collective-permute-start.9) | collective-permute-done | bytes 442400 | tf_op jit(solution)/shard_map/ppermute | solution.py:22
  41.0 0.0 collective-permute-done.3.refs_5_
  41.1 0.0 slice-start.1
  41.1 1.4 %shard_map.95 = bf16[4,32,384]{2,1,0:T(8,128)(2,1)S(1)} custom-call(bf16[128,384]{1,0:T(8,128)(2,1)S(1)} %get-tuple-element.39.refs_0_, bf16[128,384]{1,0:T(8,128)(2,1)S(1)} %get-tuple-element.40.refs_1_, bf16[128,384]{1,0:T(8,128)(2,1)S(1)} %pad_maximum_fusion.9.refs_2_, bf16[128,384]{1,0:T(8,128)(2,1)S(1)} %pad_maximum_fusion.10.refs_3_, ...), custom_call_target="tpu_custom_call" | custom-call | tf_op jit(solution)/shard_map/pallas_call | solution.py:134
  42.6 2.3 %collective-permute-start.12 = (bf16[4,32,384]{2,1,0:T(8,128)(2,1)S(1)}, bf16[4,32,384]{2,1,0:T(8,128)(2,1)S(1)}, u32[]{:S(2)}, u32[]{:S(2)}) collective-permute-start(bf16[4,32,384]{2,1,0:T(8,128)(2,1)S(1)} %shard_map.95), channel_id=1, source_target_pairs={{0,12},{4,8},{8,4},{12,0},{1,13},{5,9},{9,5},{13,1},{2,14},{6,10},... | collective-permute-start | bytes 294920 | tf_op jit(solution)/shard_map/ppermute | solution.py:22
  44.8 1.4 %shard_map.92 = bf16[4,32,384]{2,1,0:T(8,128)(2,1)S(1)} custom-call(bf16[128,384]{1,0:T(8,128)(2,1)S(1)} %get-tuple-element.39.refs_0_, bf16[128,384]{1,0:T(8,128)(2,1)S(1)} %get-tuple-element.40.refs_1_, bf16[128,384]{1,0:T(8,128)(2,1)S(1)} %pad_maximum_fusion.9.refs_2_, bf16[128,384]{1,0:T(8,128)(2,1)S(1)} %pad_maximum_fusion.10.refs_3_, ...), custom_call_target="tpu_custom_call" | custom-call | tf_op jit(solution)/shard_map/pallas_call | solution.py:134
  46.3 0.0 slice-start.2
  46.3 1.3 %collective-permute-start.10 = (bf16[4,32,384]{2,1,0:T(8,128)(2,1)S(1)}, bf16[4,32,384]{2,1,0:T(8,128)(2,1)S(1)}, u32[]{:S(2)}, u32[]{:S(2)}) collective-permute-start(bf16[4,32,384]{2,1,0:T(8,128)(2,1)S(1)} %shard_map.92), channel_id=1, source_target_pairs={{0,8},{4,12},{8,0},{12,4},{1,9},{5,13},{9,1},{13,5},{2,10},{6,14},... | collective-permute-start | bytes 294920 | tf_op jit(solution)/shard_map/ppermute | solution.py:22
  47.6 1.4 %shard_map.93 = bf16[4,32,384]{2,1,0:T(8,128)(2,1)S(1)} custom-call(bf16[128,384]{1,0:T(8,128)(2,1)S(1)} %get-tuple-element.39.refs_0_, bf16[128,384]{1,0:T(8,128)(2,1)S(1)} %get-tuple-element.40.refs_1_, bf16[128,384]{1,0:T(8,128)(2,1)S(1)} %pad_maximum_fusion.9.refs_2_, bf16[128,384]{1,0:T(8,128)(2,1)S(1)} %pad_maximum_fusion.10.refs_3_, ...), custom_call_target="tpu_custom_call" | custom-call | tf_op jit(solution)/shard_map/pallas_call | solution.py:134
  49.0 0.2 collective-permute-start.11
  49.3 1.4 %shard_map.94.refs_0_ = bf16[4,32,384]{2,1,0:T(8,128)(2,1)S(1)} custom-call(bf16[128,384]{1,0:T(8,128)(2,1)S(1)} %get-tuple-element.39.refs_0_, bf16[128,384]{1,0:T(8,128)(2,1)S(1)} %get-tuple-element.40.refs_1_, bf16[128,384]{1,0:T(8,128)(2,1)S(1)} %pad_maximum_fusion.9.refs_2_, bf16[128,384]{1,0:T(8,128)(2,1)S(1)} %pad_maximum_fusion.10.refs_3_, ...), custom_call_target="tpu_custom_call" | custom-call | tf_op jit(solution)/shard_map/pallas_call | solution.py:134
  50.7 0.0 copy-start.1
  50.7 0.0 copy-start.2
  50.7 0.0 copy-start.3
  50.7 0.0 collective-permute-done.12.refs_1_
  50.7 0.0 slice-done
  50.7 0.0 slice-done.1
  50.7 0.0 slice-done.2
  50.8 1.9 %shard_map.96.refs_4_ = f32[2,128,1536]{2,1,0:T(8,128)S(1)} custom-call(s32[4]{0:T(128)S(1)} %pad_add_fusion.where_ref, bf16[4,32,384]{2,1,0:T(8,128)(2,1)S(1)} %shard_map.94.refs_0_, bf16[4,32,384]{2,1,0:T(8,128)(2,1)S(1)} %collective-permute-done.12.refs_1_, bf16[1536,3072]{1,0:T(8,128)(2,1)S(1)} %bitcast.8, bf16[1536,3072]{1,0:T(8,128)(2,1)S(1)} %bitcast.8), custom_call_target="tpu_custom_call" | custom-call | tf_op jit(solution)/shard_map/pallas_call | solution.py:179
  52.6 2.9 %collective-permute-done.10.refs_0_ = bf16[4,32,384]{2,1,0:T(8,128)(2,1)S(1)} collective-permute-done((bf16[4,32,384]{2,1,0:T(8,128)(2,1)S(1)}, bf16[4,32,384]{2,1,0:T(8,128)(2,1)S(1)}, u32[]{:S(2)}, u32[]{:S(2)}) %collective-permute-start.10) | collective-permute-done | bytes 98336 | tf_op jit(solution)/shard_map/ppermute | solution.py:22
  55.5 0.0 collective-permute-done.11.refs_1_
  55.5 0.0 copy-done.1
  55.5 0.0 copy-done.2
  55.5 0.0 copy-done.3
  55.6 0.0 copy-start
  55.6 0.0 copy-start.4
  55.6 3.0 %shard_map.97 = (bf16[128,32]{1,0:T(8,128)(2,1)S(1)}, bf16[128,32]{1,0:T(8,128)(2,1)S(1)}) custom-call(s32[4]{0:T(128)S(1)} %pad_add_fusion.where_ref, bf16[4,32,384]{2,1,0:T(8,128)(2,1)S(1)} %collective-permute-done.10.refs_0_, bf16[4,32,384]{2,1,0:T(8,128)(2,1)S(1)} %collective-permute-done.11.refs_1_, bf16[1536,3072]{1,0:T(8,128)(2,1)S(1)} %bitcast.8, ...), custom_call_target="tpu_custom_call" | custom-call | tf_op jit(solution)/shard_map/pallas_call | solution.py:254
  58.6 1.1 %collective-permute-start.13 = (bf16[128,32]{1,0:T(8,128)(2,1)S(1)}, bf16[128,32]{1,0:T(8,128)(2,1)S(1)}, u32[]{:S(2)}, u32[]{:S(2)}) collective-permute-start(bf16[128,32]{1,0:T(8,128)(2,1)S(1)} %get-tuple-element.15.inner_ref), channel_id=1, source_target_pairs={{0,1},{1,0},{2,3},{3,2},{4,5},{5,4},{6,7},{7,6},{8,9},{9,8},{10,11... | collective-permute-start | bytes 24584 | tf_op jit(solution)/shard_map/ppermute | solution.py:22
  59.7 2.1 %collective-permute-start.14 = (bf16[128,32]{1,0:T(8,128)(2,1)S(1)}, bf16[128,32]{1,0:T(8,128)(2,1)S(1)}, u32[]{:S(2)}, u32[]{:S(2)}) collective-permute-start(bf16[128,32]{1,0:T(8,128)(2,1)S(1)} %get-tuple-element.16.outer_ref), channel_id=1, source_target_pairs={{1,2},{3,4},{5,6},{7,8},{9,10},{11,12},{13,14},{2,1},{4,3},{6,5},{... | collective-permute-start | bytes 24584 | tf_op jit(solution)/shard_map/ppermute | solution.py:420
  61.8 0.0 copy-done
  61.8 1.3 %shard_map.98.own_ref = f32[2,256,512]{2,1,0:T(8,128)S(1)} custom-call(s32[4]{0:T(128)S(1)} %pad_add_fusion.where_ref, bf16[128,32]{1,0:T(8,128)(2,1)S(1)} %get-tuple-element.15.inner_ref, bf16[128,32]{1,0:T(8,128)(2,1)S(1)} %get-tuple-element.16.outer_ref, bf16[432,512]{1,0:T(8,128)(2,1)S(1)} %copy-done), custom_call_target="tpu_custom_call" | custom-call | tf_op jit(solution)/shard_map/pallas_call | solution.py:343
  63.1 0.0 collective-permute-done.13.inner_got_ref
  63.2 1.8 %collective-permute-done.14.outer_got_ref = bf16[128,32]{1,0:T(8,128)(2,1)S(1)} collective-permute-done((bf16[128,32]{1,0:T(8,128)(2,1)S(1)}, bf16[128,32]{1,0:T(8,128)(2,1)S(1)}, u32[]{:S(2)}, u32[]{:S(2)}) %collective-permute-start.14) | collective-permute-done | bytes 8224 | tf_op jit(solution)/shard_map/ppermute | solution.py:420
  64.9 0.0 copy-done.4
  64.9 2.1 %shard_map.99 = bf16[4,2,64,512]{3,2,1,0:T(8,128)(2,1)} custom-call(s32[4]{0:T(128)S(1)} %pad_add_fusion.where_ref, bf16[128,32]{1,0:T(8,128)(2,1)S(1)} %get-tuple-element.15.inner_ref, bf16[128,32]{1,0:T(8,128)(2,1)S(1)} %get-tuple-element.16.outer_ref, bf16[128,32]{1,0:T(8,128)(2,1)S(1)} %collective-permute-done.13.inner_got_ref, ...), custom_call_target="tpu_custom_call" | custom-call | tf_op jit(solution)/shard_map/pallas_call | solution.py:358
  (32 shorter events, 0.6 us)
Async XLA Ops:
  2.3 7.8 %collective-permute-start = (bf16[320,384]{1,0:T(8,128)(2,1)S(1)}, bf16[320,384]{1,0:T(8,128)(2,1)S(1)}, u32[]{:S(2)}, u32[]{:S(2)}) collective-permute-start(bf16[320,384]{1,0:T(8,128)(2,1)S(1)} %pad_maximum_fusion.3), channel_id=1, source_target_pairs={{0,2},{1,3},{2,0},{3,1},{4,6},{5,7},{6,4},{7,5},{8,10},{9,11},{10,... | collective-permute-start | bytes 737288 | tf_op jit(solution)/shard_map/ppermute | solution.py:22
  4.4 13.0 %collective-permute-start.1 = (bf16[384,384]{1,0:T(8,128)(2,1)S(1)}, bf16[384,384]{1,0:T(8,128)(2,1)S(1)}, u32[]{:S(2)}, u32[]{:S(2)}) collective-permute-start(bf16[384,384]{1,0:T(8,128)(2,1)S(1)} %get-tuple-element.12), channel_id=1, source_target_pairs={{0,4},{4,0},{8,12},{12,8},{1,5},{5,1},{9,13},{13,9},{2,6},{6,2},{1... | collective-permute-start | bytes 884744 | tf_op jit(solution)/shard_map/ppermute | solution.py:22
  5.7 12.2 %collective-permute-start.4 = (bf16[384,384]{1,0:T(8,128)(2,1)S(1)}, bf16[384,384]{1,0:T(8,128)(2,1)S(1)}, u32[]{:S(2)}, u32[]{:S(2)}) collective-permute-start(bf16[384,384]{1,0:T(8,128)(2,1)S(1)} %get-tuple-element.13), channel_id=1, source_target_pairs={{0,8},{4,12},{8,0},{12,4},{1,9},{5,13},{9,1},{13,5},{2,10},{6,14},... | collective-permute-start | bytes 884744 | tf_op jit(solution)/shard_map/ppermute | solution.py:22
  8.0 18.7 %collective-permute-start.7 = (bf16[384,384]{1,0:T(8,128)(2,1)S(1)}, bf16[384,384]{1,0:T(8,128)(2,1)S(1)}, u32[]{:S(2)}, u32[]{:S(2)}) collective-permute-start(bf16[384,384]{1,0:T(8,128)(2,1)S(1)} %get-tuple-element.14), channel_id=1, source_target_pairs={{0,12},{4,8},{8,4},{12,0},{1,13},{5,9},{9,5},{13,1},{2,14},{6,10},... | collective-permute-start | bytes 884744 | tf_op jit(solution)/shard_map/ppermute | solution.py:22
  17.5 9.6 %collective-permute-start.2 = (bf16[320,384]{1,0:T(8,128)(2,1)S(1)}, bf16[320,384]{1,0:T(8,128)(2,1)S(1)}, u32[]{:S(2)}, u32[]{:S(2)}) collective-permute-start(bf16[320,384]{1,0:T(8,128)(2,1)S(1)} %pad_maximum_fusion.4), channel_id=1, source_target_pairs={{0,2},{1,3},{2,0},{3,1},{4,6},{5,7},{6,4},{7,5},{8,10},{9,11},{10,... | collective-permute-start | bytes 737288 | tf_op jit(solution)/shard_map/ppermute | solution.py:22
  18.1 14.9 %collective-permute-start.5 = (bf16[320,384]{1,0:T(8,128)(2,1)S(1)}, bf16[320,384]{1,0:T(8,128)(2,1)S(1)}, u32[]{:S(2)}, u32[]{:S(2)}) collective-permute-start(bf16[320,384]{1,0:T(8,128)(2,1)S(1)} %pad_maximum_fusion.5), channel_id=1, source_target_pairs={{0,2},{1,3},{2,0},{3,1},{4,6},{5,7},{6,4},{7,5},{8,10},{9,11},{10,... | collective-permute-start | bytes 737288 | tf_op jit(solution)/shard_map/ppermute | solution.py:22
  26.8 10.2 %collective-permute-start.8 = (bf16[320,384]{1,0:T(8,128)(2,1)S(1)}, bf16[320,384]{1,0:T(8,128)(2,1)S(1)}, u32[]{:S(2)}, u32[]{:S(2)}) collective-permute-start(bf16[320,384]{1,0:T(8,128)(2,1)S(1)} %pad_maximum_fusion.6), channel_id=1, source_target_pairs={{0,2},{1,3},{2,0},{3,1},{4,6},{5,7},{6,4},{7,5},{8,10},{9,11},{10,... | collective-permute-start | bytes 737288 | tf_op jit(solution)/shard_map/ppermute | solution.py:22
  27.2 13.8 %collective-permute-start.3 = (bf16[1152,384]{1,0:T(8,128)(2,1)S(1)}, bf16[1152,384]{1,0:T(8,128)(2,1)S(1)}, u32[]{:S(2)}, u32[]{:S(2)}) collective-permute-start(bf16[1152,384]{1,0:T(8,128)(2,1)S(1)} %get-tuple-element.36.refs_4_), channel_id=1, source_target_pairs={{0,1},{1,0},{2,3},{3,2},{4,5},{5,4},{6,7},{7,6},{8,9},{9,8},{10,11... | collective-permute-start | bytes 2654216 | tf_op jit(solution)/shard_map/ppermute | solution.py:22
  33.1 6.5 %collective-permute-start.6 = (bf16[576,384]{1,0:T(8,128)(2,1)S(1)}, bf16[576,384]{1,0:T(8,128)(2,1)S(1)}, u32[]{:S(2)}, u32[]{:S(2)}) collective-permute-start(bf16[576,384]{1,0:T(8,128)(2,1)S(1)} %pad_maximum_fusion.1.refs_6_), channel_id=1, source_target_pairs={{0,1},{1,0},{2,3},{3,2},{4,5},{5,4},{6,7},{7,6},{8,9},{9,8},{10,11... | collective-permute-start | bytes 1327112 | tf_op jit(solution)/shard_map/ppermute | solution.py:22
  37.0 13.7 %slice-start = ((s8[9437184]{0:T(1024)(128)(4,1)}), s8[4194304]{0:T(1024)(128)(4,1)S(1)}, s32[]{:S(2)}) async-start(s8[9437184]{0:T(1024)(128)(4,1)} %bitcast.7), calls=%async_computation | async-start | bytes 8388608
  37.1 3.9 %collective-permute-start.9 = (bf16[576,384]{1,0:T(8,128)(2,1)S(1)}, bf16[576,384]{1,0:T(8,128)(2,1)S(1)}, u32[]{:S(2)}, u32[]{:S(2)}) collective-permute-start(bf16[576,384]{1,0:T(8,128)(2,1)S(1)} %pad_maximum_fusion.2.refs_8_), channel_id=1, source_target_pairs={{0,1},{1,0},{2,3},{3,2},{4,5},{5,4},{6,7},{7,6},{8,9},{9,8},{10,11... | collective-permute-start | bytes 1327112 | tf_op jit(solution)/shard_map/ppermute | solution.py:22
  41.1 9.6 %slice-start.1 = ((s8[9437184]{0:T(1024)(128)(4,1)}), s8[4194304]{0:T(1024)(128)(4,1)S(1)}, s32[]{:S(2)}) async-start(s8[9437184]{0:T(1024)(128)(4,1)} %bitcast.7), calls=%async_computation.1 | async-start | bytes 8388608
  42.6 8.1 %collective-permute-start.12 = (bf16[4,32,384]{2,1,0:T(8,128)(2,1)S(1)}, bf16[4,32,384]{2,1,0:T(8,128)(2,1)S(1)}, u32[]{:S(2)}, u32[]{:S(2)}) collective-permute-start(bf16[4,32,384]{2,1,0:T(8,128)(2,1)S(1)} %shard_map.95), channel_id=1, source_target_pairs={{0,12},{4,8},{8,4},{12,0},{1,13},{5,9},{9,5},{13,1},{2,14},{6,10},... | collective-permute-start | bytes 294920 | tf_op jit(solution)/shard_map/ppermute | solution.py:22
  46.3 4.5 %slice-start.2 = ((s8[9437184]{0:T(1024)(128)(4,1)}), s8[1048576]{0:T(1024)(128)(4,1)S(1)}, s32[]{:S(2)}) async-start(s8[9437184]{0:T(1024)(128)(4,1)} %bitcast.7), calls=%async_computation.2 | async-start | bytes 2097152
  46.3 9.3 %collective-permute-start.10 = (bf16[4,32,384]{2,1,0:T(8,128)(2,1)S(1)}, bf16[4,32,384]{2,1,0:T(8,128)(2,1)S(1)}, u32[]{:S(2)}, u32[]{:S(2)}) collective-permute-start(bf16[4,32,384]{2,1,0:T(8,128)(2,1)S(1)} %shard_map.92), channel_id=1, source_target_pairs={{0,8},{4,12},{8,0},{12,4},{1,9},{5,13},{9,1},{13,5},{2,10},{6,14},... | collective-permute-start | bytes 294920 | tf_op jit(solution)/shard_map/ppermute | solution.py:22
  49.0 6.5 %collective-permute-start.11 = (bf16[4,32,384]{2,1,0:T(8,128)(2,1)S(1)}, bf16[4,32,384]{2,1,0:T(8,128)(2,1)S(1)}, u32[]{:S(2)}, u32[]{:S(2)}) collective-permute-start(bf16[4,32,384]{2,1,0:T(8,128)(2,1)S(1)} %shard_map.93), channel_id=1, source_target_pairs={{0,4},{4,0},{8,12},{12,8},{1,5},{5,1},{9,13},{13,9},{2,6},{6,2},{1... | collective-permute-start | bytes 294920 | tf_op jit(solution)/shard_map/ppermute | solution.py:22
  50.7 4.9 %copy-start.1 = (bf16[3072,64]{0,1:T(8,128)(2,1)S(1)}, bf16[3072,64]{0,1:T(8,128)(2,1)}, u32[]{:S(2)}) copy-start(bf16[3072,64]{0,1:T(8,128)(2,1)} %param.15) | copy-start | bytes 1179652
  50.7 4.9 %copy-start.2 = (f32[3072]{0:T(1024)S(1)}, f32[3072]{0:T(1024)}, u32[]{:S(2)}) copy-start(f32[3072]{0:T(1024)} %param.14) | copy-start | bytes 36868
  50.7 4.9 %copy-start.3 = (f32[3072]{0:T(1024)S(1)}, f32[3072]{0:T(1024)}, u32[]{:S(2)}) copy-start(f32[3072]{0:T(1024)} %param.13) | copy-start | bytes 36868
  55.6 6.3 %copy-start = (bf16[432,512]{1,0:T(8,128)(2,1)S(1)}, bf16[432,512]{1,0:T(8,128)(2,1)}, u32[]{:S(2)}) copy-start(bf16[432,512]{1,0:T(8,128)(2,1)} %w_ref.3) | copy-start | bytes 1327108
  55.6 9.4 %copy-start.4 = (f32[512]{0:T(512)S(1)}, f32[512]{0:T(512)}, u32[]{:S(2)}) copy-start(f32[512]{0:T(512)} %param.17) | copy-start | bytes 6148
  58.6 4.6 %collective-permute-start.13 = (bf16[128,32]{1,0:T(8,128)(2,1)S(1)}, bf16[128,32]{1,0:T(8,128)(2,1)S(1)}, u32[]{:S(2)}, u32[]{:S(2)}) collective-permute-start(bf16[128,32]{1,0:T(8,128)(2,1)S(1)} %get-tuple-element.15.inner_ref), channel_id=1, source_target_pairs={{0,1},{1,0},{2,3},{3,2},{4,5},{5,4},{6,7},{7,6},{8,9},{9,8},{10,11... | collective-permute-start | bytes 24584 | tf_op jit(solution)/shard_map/ppermute | solution.py:22
  59.7 5.2 %collective-permute-start.14 = (bf16[128,32]{1,0:T(8,128)(2,1)S(1)}, bf16[128,32]{1,0:T(8,128)(2,1)S(1)}, u32[]{:S(2)}, u32[]{:S(2)}) collective-permute-start(bf16[128,32]{1,0:T(8,128)(2,1)S(1)} %get-tuple-element.16.outer_ref), channel_id=1, source_target_pairs={{1,2},{3,4},{5,6},{7,8},{9,10},{11,12},{13,14},{2,1},{4,3},{6,5},{... | collective-permute-start | bytes 24584 | tf_op jit(solution)/shard_map/ppermute | solution.py:420

commit v16 on v14

--- a/solution.py
+++ b/solution.py
@@ -344,10 +344,15 @@
 
     both_parts, share = 2 * tokens, tokens // planes
     held = {r: [got[r]] for r in range(groups)}
-    for r in (0, 1, 2, 3):
+    for batch in ((0, 1), (2,), (3,)):
         for d in range(2, planes, 2):
-            asked = got[r][both_parts + d * share : both_parts + (d + 2) * share]
-            held[r].append(swap(jnp.concatenate([got[r][:both_parts], asked], axis=0), "plane", d))
+            sent = []
+            for r in batch:
+                sent += [got[r][:both_parts], got[r][both_parts + d * share : both_parts + (d + 2) * share]]
+            crossed = swap(jnp.concatenate(sent, axis=0), "plane", d)
+            extent = both_parts + 2 * share
+            for n, r in enumerate(batch):
+                held[r].append(crossed[n * extent : (n + 1) * extent])
 
     keys_values, asked = [], {}
     for distances in ((0, 1), (2,), (3,)):
@@ -372,7 +377,7 @@
     for targets in ((3,), (2,), (1,), (0,)):
         for t, o in zip(targets, attend(asked, keys_values, targets, planes)):
             results[t] = o if t == 0 else swap(o, "heads", t)
-    partial = project(where, [results[t] for t in near], near, w_out, 1024)
+    partial = project(where, [results[t] for t in near], near, w_out, 1536)
     sent = [results[t] for t in far]
     inner, outer = final_layer(
         where, sent, far, partial, w_out, scale_mod, shift_mod, w_final, rows_dev, planes

time: 67.5 us -> 67.8 us (level)
  waiting for transfers between devices: 24.1 us -> 29.2 us
  starting transfers between devices: 26.8 us -> 22.4 us
    ppermute x14 -> x13, waiting for transfers between devices: 21 us -> 27 us  [swap(): return lax.ppermute(source, axis, [(i, i ^ distance) for i in range(count)])]
    ppermute x14 -> x13, starting transfers between devices: 24.7 us -> 19.4 us  [swap(): return lax.ppermute(source, axis, [(i, i ^ distance) for i in range(count)])]
    ppermute x1, starting transfers between devices: 2.07 us -> 3.01 us  [shards(): lax.ppermute(outer, ('heads', 'plane'), pairs + [(j, i) for i, j in pairs])]
    ppermute x1, waiting for transfers between devices: 3.13 us -> 2.2 us  [shards(): lax.ppermute(outer, ('heads', 'plane'), pairs + [(j, i) for i, j in pairs])]
  transfers between devices with their start and end apart: 15 -> 14, of which waited for: 6 -> 8; matrix products, arithmetic and copies ran while one was open for 1% -> 1% of each run, Pallas kernels for 9% -> 9%
where the time goes in v16:
time: 67.8 us; the launch traced here: 67.6 us
  waiting for transfers between devices  29.2 us (43%)
  starting transfers between devices  22.4 us (33%)
  Pallas kernels  13.6 us (20%)
  other arithmetic  1.64 us (2%)
    ppermute x13, waiting for transfers between devices, swap(): return lax.ppermute(source, axis, [(i, i ^ distance) for i in range(count)])  27 us
    ppermute x13, starting transfers between devices, swap(): return lax.ppermute(source, axis, [(i, i ^ distance) for i in range(count)])  19.4 us
    pallas_call x4, Pallas kernels, attend(): pl.pallas_call(functools.partial(attend_kernel, sources=sources, planes=p...  5.69 us
    pallas_call x1, Pallas kernels, final_layer(): pl.pallas_call(functools.partial(final_kernel, targets=targets, planes=pl...  3.01 us
    ppermute x1, starting transfers between devices, shards(): lax.ppermute(outer, ('heads', 'plane'), pairs + [(j, i) for i, j in pairs])  3.01 us
    ppermute x1, waiting for transfers between devices, shards(): lax.ppermute(outer, ('heads', 'plane'), pairs + [(j, i) for i, j in pairs])  2.2 us
    pallas_call x1, Pallas kernels, convolve(): pl.pallas_call(convolve_kernel, in_specs=[smem] + [vmem] * 6, out_specs=v...  2.17 us
    pallas_call x1, Pallas kernels, project(): pl.pallas_call(functools.partial(project_kernel, targets=targets), grid_s...  1.87 us
  transfers between devices with their start and end apart: 14, of which 8 were waited for; matrix products, arithmetic and copies ran while one was open for 1% of the time, Pallas kernels for 9%

profile of v16, /device:TPU:1, one launch (start us, length us, event | category | flops | bytes accessed | tf_op | source)
XLA Modules:
  0.0 67.6 jit_solution(6676312856778764003)
XLA Ops:
  0.0 1.3 %pad_maximum_fusion.qkv_ref = bf16[384,1536]{1,0:T(8,128)(2,1)S(1)} fusion(bf16[128,1536]{1,0:T(8,128)(2,1)} %param.11, bf16[128,1536]{1,0:T(8,128)(2,1)} %param.10, bf16[128,1536]{1,0:T(8,128)(2,1)} %param.9), kind=kLoop, calls=%fused_computation | loop fusion | flops 3538944 | bytes 2359296 | tf_op jit(solution)/shard_map/concatenate | solution.py:52
  1.3 0.1 pad_add_fusion.where_ref
  1.4 0.8 %shard_map.91 = (bf16[384,384]{1,0:T(8,128)(2,1)S(1)}, bf16[384,384]{1,0:T(8,128)(2,1)S(1)}, bf16[384,384]{1,0:T(8,128)(2,1)S(1)}, bf16[384,384]{1,0:T(8,128)(2,1)S(1)}) custom-call(s32[4]{0:T(128)S(1)} %pad_add_fusion.where_ref, bf16[384,1536]{1,0:T(8,128)(2,1)S(1)} %pad_maximum_fusion.qkv_ref), custom_call_target="tpu_custom_call" | custom-call | tf_op jit(solution)/shard_map/pallas_call | solution.py:46
  2.2 2.2 %collective-permute-start = (bf16[384,384]{1,0:T(8,128)(2,1)S(1)}, bf16[384,384]{1,0:T(8,128)(2,1)S(1)}, u32[]{:S(2)}, u32[]{:S(2)}) collective-permute-start(bf16[384,384]{1,0:T(8,128)(2,1)S(1)} %get-tuple-element.12), channel_id=1, source_target_pairs={{0,4},{4,0},{8,12},{12,8},{1,5},{5,1},{9,13},{13,9},{2,6},{6,2},{1... | collective-permute-start | bytes 884744 | tf_op jit(solution)/shard_map/ppermute | solution.py:22
  4.4 2.3 %collective-permute-start.3 = (bf16[384,384]{1,0:T(8,128)(2,1)S(1)}, bf16[384,384]{1,0:T(8,128)(2,1)S(1)}, u32[]{:S(2)}, u32[]{:S(2)}) collective-permute-start(bf16[384,384]{1,0:T(8,128)(2,1)S(1)} %get-tuple-element.13), channel_id=1, source_target_pairs={{0,8},{4,12},{8,0},{12,4},{1,9},{5,13},{9,1},{13,5},{2,10},{6,14},... | collective-permute-start | bytes 884744 | tf_op jit(solution)/shard_map/ppermute | solution.py:22
  6.7 0.0 collective-permute-start.6
  6.8 9.9 %collective-permute-done = bf16[384,384]{1,0:T(8,128)(2,1)S(1)} collective-permute-done((bf16[384,384]{1,0:T(8,128)(2,1)S(1)}, bf16[384,384]{1,0:T(8,128)(2,1)S(1)}, u32[]{:S(2)}, u32[]{:S(2)}) %collective-permute-start) | collective-permute-done | bytes 294944 | tf_op jit(solution)/shard_map/ppermute | solution.py:22
  16.7 0.1 pad_maximum_fusion.1
  16.8 1.1 %collective-permute-start.1 = (bf16[640,384]{1,0:T(8,128)(2,1)S(1)}, bf16[640,384]{1,0:T(8,128)(2,1)S(1)}, u32[]{:S(2)}, u32[]{:S(2)}) collective-permute-start(bf16[640,384]{1,0:T(8,128)(2,1)S(1)} %pad_maximum_fusion.1), channel_id=1, source_target_pairs={{0,2},{1,3},{2,0},{3,1},{4,6},{5,7},{6,4},{7,5},{8,10},{9,11},{10,... | collective-permute-start | bytes 1474568 | tf_op jit(solution)/shard_map/ppermute | solution.py:22
  17.9 0.0 collective-permute-done.3
  18.0 0.5 collective-permute-start.4
  18.5 7.2 %collective-permute-done.6 = bf16[384,384]{1,0:T(8,128)(2,1)S(1)} collective-permute-done((bf16[384,384]{1,0:T(8,128)(2,1)S(1)}, bf16[384,384]{1,0:T(8,128)(2,1)S(1)}, u32[]{:S(2)}, u32[]{:S(2)}) %collective-permute-start.6) | collective-permute-done | bytes 294944 | tf_op jit(solution)/shard_map/ppermute | solution.py:22
  25.8 1.3 %collective-permute-start.7 = (bf16[320,384]{1,0:T(8,128)(2,1)S(1)}, bf16[320,384]{1,0:T(8,128)(2,1)S(1)}, u32[]{:S(2)}, u32[]{:S(2)}) collective-permute-start(bf16[320,384]{1,0:T(8,128)(2,1)S(1)} %pad_maximum_fusion.5), channel_id=1, source_target_pairs={{0,2},{1,3},{2,0},{3,1},{4,6},{5,7},{6,4},{7,5},{8,10},{9,11},{10,... | collective-permute-start | bytes 737288 | tf_op jit(solution)/shard_map/ppermute | solution.py:22
  27.1 6.2 %collective-permute-done.4 = bf16[320,384]{1,0:T(8,128)(2,1)S(1)} collective-permute-done((bf16[320,384]{1,0:T(8,128)(2,1)S(1)}, bf16[320,384]{1,0:T(8,128)(2,1)S(1)}, u32[]{:S(2)}, u32[]{:S(2)}) %collective-permute-start.4) | collective-permute-done | bytes 245792 | tf_op jit(solution)/shard_map/ppermute | solution.py:22
  33.4 4.7 %collective-permute-start.5 = (bf16[576,384]{1,0:T(8,128)(2,1)S(1)}, bf16[576,384]{1,0:T(8,128)(2,1)S(1)}, u32[]{:S(2)}, u32[]{:S(2)}) collective-permute-start(bf16[576,384]{1,0:T(8,128)(2,1)S(1)} %pad_maximum_fusion.2.refs_6_), channel_id=1, source_target_pairs={{0,1},{1,0},{2,3},{3,2},{4,5},{5,4},{6,7},{7,6},{8,9},{9,8},{10,11... | collective-permute-start | bytes 1327112 | tf_op jit(solution)/shard_map/ppermute | solution.py:22
  38.0 0.0 collective-permute-done.1
  38.2 0.1 collective-permute-start.2
  38.3 0.2 collective-permute-done.7
  38.6 0.0 slice-start
  38.6 2.6 %collective-permute-start.8 = (bf16[576,384]{1,0:T(8,128)(2,1)S(1)}, bf16[576,384]{1,0:T(8,128)(2,1)S(1)}, u32[]{:S(2)}, u32[]{:S(2)}) collective-permute-start(bf16[576,384]{1,0:T(8,128)(2,1)S(1)} %pad_maximum_fusion.3.refs_8_), channel_id=1, source_target_pairs={{0,1},{1,0},{2,3},{3,2},{4,5},{5,4},{6,7},{7,6},{8,9},{9,8},{10,11... | collective-permute-start | bytes 1327112 | tf_op jit(solution)/shard_map/ppermute | solution.py:22
  41.2 0.0 collective-permute-done.5.refs_7_
  41.2 1.4 %collective-permute-done.8.refs_9_ = bf16[576,384]{1,0:T(8,128)(2,1)S(1)} collective-permute-done((bf16[576,384]{1,0:T(8,128)(2,1)S(1)}, bf16[576,384]{1,0:T(8,128)(2,1)S(1)}, u32[]{:S(2)}, u32[]{:S(2)}) %collective-permute-start.8) | collective-permute-done | bytes 442400 | tf_op jit(solution)/shard_map/ppermute | solution.py:22
  42.7 0.0 collective-permute-done.2.refs_5_
  42.7 0.0 slice-start.1
  42.7 1.4 %shard_map.95 = bf16[4,32,384]{2,1,0:T(8,128)(2,1)S(1)} custom-call(bf16[128,384]{1,0:T(8,128)(2,1)S(1)} %get-tuple-element.36.refs_0_, bf16[128,384]{1,0:T(8,128)(2,1)S(1)} %get-tuple-element.37.refs_1_, bf16[128,384]{1,0:T(8,128)(2,1)S(1)} %pad_maximum_fusion.8.refs_2_, bf16[128,384]{1,0:T(8,128)(2,1)S(1)} %pad_maximum_fusion.9.refs_3_, ...), custom_call_target="tpu_custom_call" | custom-call | tf_op jit(solution)/shard_map/pallas_call | solution.py:134
  44.2 2.7 %collective-permute-start.11 = (bf16[4,32,384]{2,1,0:T(8,128)(2,1)S(1)}, bf16[4,32,384]{2,1,0:T(8,128)(2,1)S(1)}, u32[]{:S(2)}, u32[]{:S(2)}) collective-permute-start(bf16[4,32,384]{2,1,0:T(8,128)(2,1)S(1)} %shard_map.95), channel_id=1, source_target_pairs={{0,12},{4,8},{8,4},{12,0},{1,13},{5,9},{9,5},{13,1},{2,14},{6,10},... | collective-permute-start | bytes 294920 | tf_op jit(solution)/shard_map/ppermute | solution.py:22
  46.9 1.4 %shard_map.92 = bf16[4,32,384]{2,1,0:T(8,128)(2,1)S(1)} custom-call(bf16[128,384]{1,0:T(8,128)(2,1)S(1)} %get-tuple-element.36.refs_0_, bf16[128,384]{1,0:T(8,128)(2,1)S(1)} %get-tuple-element.37.refs_1_, bf16[128,384]{1,0:T(8,128)(2,1)S(1)} %pad_maximum_fusion.8.refs_2_, bf16[128,384]{1,0:T(8,128)(2,1)S(1)} %pad_maximum_fusion.9.refs_3_, ...), custom_call_target="tpu_custom_call" | custom-call | tf_op jit(solution)/shard_map/pallas_call | solution.py:134
  48.3 0.0 slice-start.2
  48.3 0.1 collective-permute-start.9
  48.4 1.4 %shard_map.93 = bf16[4,32,384]{2,1,0:T(8,128)(2,1)S(1)} custom-call(bf16[128,384]{1,0:T(8,128)(2,1)S(1)} %get-tuple-element.36.refs_0_, bf16[128,384]{1,0:T(8,128)(2,1)S(1)} %get-tuple-element.37.refs_1_, bf16[128,384]{1,0:T(8,128)(2,1)S(1)} %pad_maximum_fusion.8.refs_2_, bf16[128,384]{1,0:T(8,128)(2,1)S(1)} %pad_maximum_fusion.9.refs_3_, ...), custom_call_target="tpu_custom_call" | custom-call | tf_op jit(solution)/shard_map/pallas_call | solution.py:134
  49.8 1.0 %collective-permute-start.10 = (bf16[4,32,384]{2,1,0:T(8,128)(2,1)S(1)}, bf16[4,32,384]{2,1,0:T(8,128)(2,1)S(1)}, u32[]{:S(2)}, u32[]{:S(2)}) collective-permute-start(bf16[4,32,384]{2,1,0:T(8,128)(2,1)S(1)} %shard_map.93), channel_id=1, source_target_pairs={{0,4},{4,0},{8,12},{12,8},{1,5},{5,1},{9,13},{13,9},{2,6},{6,2},{1... | collective-permute-start | bytes 294920 | tf_op jit(solution)/shard_map/ppermute | solution.py:22
  50.8 1.4 %shard_map.94.refs_0_ = bf16[4,32,384]{2,1,0:T(8,128)(2,1)S(1)} custom-call(bf16[128,384]{1,0:T(8,128)(2,1)S(1)} %get-tuple-element.36.refs_0_, bf16[128,384]{1,0:T(8,128)(2,1)S(1)} %get-tuple-element.37.refs_1_, bf16[128,384]{1,0:T(8,128)(2,1)S(1)} %pad_maximum_fusion.8.refs_2_, bf16[128,384]{1,0:T(8,128)(2,1)S(1)} %pad_maximum_fusion.9.refs_3_, ...), custom_call_target="tpu_custom_call" | custom-call | tf_op jit(solution)/shard_map/pallas_call | solution.py:134
  52.2 0.0 copy-start.1
  52.2 0.0 copy-start.2
  52.2 0.0 copy-start.3
  52.2 0.0 collective-permute-done.11.refs_1_
  52.3 0.0 slice-done
  52.3 0.0 slice-done.1
  52.3 0.0 slice-done.2
  52.3 1.9 %shard_map.96.refs_4_ = f32[2,128,1536]{2,1,0:T(8,128)S(1)} custom-call(s32[4]{0:T(128)S(1)} %pad_add_fusion.where_ref, bf16[4,32,384]{2,1,0:T(8,128)(2,1)S(1)} %shard_map.94.refs_0_, bf16[4,32,384]{2,1,0:T(8,128)(2,1)S(1)} %collective-permute-done.11.refs_1_, bf16[1536,3072]{1,0:T(8,128)(2,1)S(1)} %bitcast.8, bf16[1536,3072]{1,0:T(8,128)(2,1)S(1)} %bitcast.8), custom_call_target="tpu_custom_call" | custom-call | tf_op jit(solution)/shard_map/pallas_call | solution.py:179
  54.2 0.8 %collective-permute-done.9.refs_0_ = bf16[4,32,384]{2,1,0:T(8,128)(2,1)S(1)} collective-permute-done((bf16[4,32,384]{2,1,0:T(8,128)(2,1)S(1)}, bf16[4,32,384]{2,1,0:T(8,128)(2,1)S(1)}, u32[]{:S(2)}, u32[]{:S(2)}) %collective-permute-start.9) | collective-permute-done | bytes 98336 | tf_op jit(solution)/shard_map/ppermute | solution.py:22
  55.0 1.2 %collective-permute-done.10.refs_1_ = bf16[4,32,384]{2,1,0:T(8,128)(2,1)S(1)} collective-permute-done((bf16[4,32,384]{2,1,0:T(8,128)(2,1)S(1)}, bf16[4,32,384]{2,1,0:T(8,128)(2,1)S(1)}, u32[]{:S(2)}, u32[]{:S(2)}) %collective-permute-start.10) | collective-permute-done | bytes 98336 | tf_op jit(solution)/shard_map/ppermute | solution.py:22
  56.2 0.0 copy-done.1
  56.2 0.0 copy-done.2
  56.2 0.0 copy-done.3
  56.2 0.0 copy-start
  56.2 0.0 copy-start.4
  56.2 3.0 %shard_map.97 = (bf16[128,32]{1,0:T(8,128)(2,1)S(1)}, bf16[128,32]{1,0:T(8,128)(2,1)S(1)}) custom-call(s32[4]{0:T(128)S(1)} %pad_add_fusion.where_ref, bf16[4,32,384]{2,1,0:T(8,128)(2,1)S(1)} %collective-permute-done.9.refs_0_, bf16[4,32,384]{2,1,0:T(8,128)(2,1)S(1)} %collective-permute-done.10.refs_1_, bf16[1536,3072]{1,0:T(8,128)(2,1)S(1)} %bitcast.8, ...), custom_call_target="tpu_custom_call" | custom-call | tf_op jit(solution)/shard_map/pallas_call | solution.py:254
  59.2 1.0 %collective-permute-start.12 = (bf16[128,32]{1,0:T(8,128)(2,1)S(1)}, bf16[128,32]{1,0:T(8,128)(2,1)S(1)}, u32[]{:S(2)}, u32[]{:S(2)}) collective-permute-start(bf16[128,32]{1,0:T(8,128)(2,1)S(1)} %get-tuple-element.15.inner_ref), channel_id=1, source_target_pairs={{0,1},{1,0},{2,3},{3,2},{4,5},{5,4},{6,7},{7,6},{8,9},{9,8},{10,11... | collective-permute-start | bytes 24584 | tf_op jit(solution)/shard_map/ppermute | solution.py:22
  60.2 3.0 %collective-permute-start.13 = (bf16[128,32]{1,0:T(8,128)(2,1)S(1)}, bf16[128,32]{1,0:T(8,128)(2,1)S(1)}, u32[]{:S(2)}, u32[]{:S(2)}) collective-permute-start(bf16[128,32]{1,0:T(8,128)(2,1)S(1)} %get-tuple-element.16.outer_ref), channel_id=1, source_target_pairs={{1,2},{3,4},{5,6},{7,8},{9,10},{11,12},{13,14},{2,1},{4,3},{6,5},{... | collective-permute-start | bytes 24584 | tf_op jit(solution)/shard_map/ppermute | solution.py:387
  63.3 0.0 collective-permute-done.12.inner_got_ref
  63.3 2.2 %collective-permute-done.13.outer_got_ref = bf16[128,32]{1,0:T(8,128)(2,1)S(1)} collective-permute-done((bf16[128,32]{1,0:T(8,128)(2,1)S(1)}, bf16[128,32]{1,0:T(8,128)(2,1)S(1)}, u32[]{:S(2)}, u32[]{:S(2)}) %collective-permute-start.13) | collective-permute-done | bytes 8224 | tf_op jit(solution)/shard_map/ppermute | solution.py:387
  65.5 0.0 copy-done
  65.5 0.0 copy-done.4
  65.5 2.2 %shard_map.98 = bf16[4,2,64,512]{3,2,1,0:T(8,128)(2,1)} custom-call(s32[4]{0:T(128)S(1)} %pad_add_fusion.where_ref, bf16[128,32]{1,0:T(8,128)(2,1)S(1)} %get-tuple-element.15.inner_ref, bf16[128,32]{1,0:T(8,128)(2,1)S(1)} %get-tuple-element.16.outer_ref, bf16[128,32]{1,0:T(8,128)(2,1)S(1)} %collective-permute-done.12.inner_got_ref, ...), custom_call_target="tpu_custom_call" | custom-call | tf_op jit(solution)/shard_map/pallas_call | solution.py:320
  (32 shorter events, 0.6 us)
Async XLA Ops:
  2.2 14.5 %collective-permute-start = (bf16[384,384]{1,0:T(8,128)(2,1)S(1)}, bf16[384,384]{1,0:T(8,128)(2,1)S(1)}, u32[]{:S(2)}, u32[]{:S(2)}) collective-permute-start(bf16[384,384]{1,0:T(8,128)(2,1)S(1)} %get-tuple-element.12), channel_id=1, source_target_pairs={{0,4},{4,0},{8,12},{12,8},{1,5},{5,1},{9,13},{13,9},{2,6},{6,2},{1... | collective-permute-start | bytes 884744 | tf_op jit(solution)/shard_map/ppermute | solution.py:22
  4.4 13.5 %collective-permute-start.3 = (bf16[384,384]{1,0:T(8,128)(2,1)S(1)}, bf16[384,384]{1,0:T(8,128)(2,1)S(1)}, u32[]{:S(2)}, u32[]{:S(2)}) collective-permute-start(bf16[384,384]{1,0:T(8,128)(2,1)S(1)} %get-tuple-element.13), channel_id=1, source_target_pairs={{0,8},{4,12},{8,0},{12,4},{1,9},{5,13},{9,1},{13,5},{2,10},{6,14},... | collective-permute-start | bytes 884744 | tf_op jit(solution)/shard_map/ppermute | solution.py:22
  6.7 19.0 %collective-permute-start.6 = (bf16[384,384]{1,0:T(8,128)(2,1)S(1)}, bf16[384,384]{1,0:T(8,128)(2,1)S(1)}, u32[]{:S(2)}, u32[]{:S(2)}) collective-permute-start(bf16[384,384]{1,0:T(8,128)(2,1)S(1)} %get-tuple-element.14), channel_id=1, source_target_pairs={{0,12},{4,8},{8,4},{12,0},{1,13},{5,9},{9,5},{13,1},{2,14},{6,10},... | collective-permute-start | bytes 884744 | tf_op jit(solution)/shard_map/ppermute | solution.py:22
  16.8 21.2 %collective-permute-start.1 = (bf16[640,384]{1,0:T(8,128)(2,1)S(1)}, bf16[640,384]{1,0:T(8,128)(2,1)S(1)}, u32[]{:S(2)}, u32[]{:S(2)}) collective-permute-start(bf16[640,384]{1,0:T(8,128)(2,1)S(1)} %pad_maximum_fusion.1), channel_id=1, source_target_pairs={{0,2},{1,3},{2,0},{3,1},{4,6},{5,7},{6,4},{7,5},{8,10},{9,11},{10,... | collective-permute-start | bytes 1474568 | tf_op jit(solution)/shard_map/ppermute | solution.py:22
  18.0 15.3 %collective-permute-start.4 = (bf16[320,384]{1,0:T(8,128)(2,1)S(1)}, bf16[320,384]{1,0:T(8,128)(2,1)S(1)}, u32[]{:S(2)}, u32[]{:S(2)}) collective-permute-start(bf16[320,384]{1,0:T(8,128)(2,1)S(1)} %pad_maximum_fusion.4), channel_id=1, source_target_pairs={{0,2},{1,3},{2,0},{3,1},{4,6},{5,7},{6,4},{7,5},{8,10},{9,11},{10,... | collective-permute-start | bytes 737288 | tf_op jit(solution)/shard_map/ppermute | solution.py:22
  25.8 12.7 %collective-permute-start.7 = (bf16[320,384]{1,0:T(8,128)(2,1)S(1)}, bf16[320,384]{1,0:T(8,128)(2,1)S(1)}, u32[]{:S(2)}, u32[]{:S(2)}) collective-permute-start(bf16[320,384]{1,0:T(8,128)(2,1)S(1)} %pad_maximum_fusion.5), channel_id=1, source_target_pairs={{0,2},{1,3},{2,0},{3,1},{4,6},{5,7},{6,4},{7,5},{8,10},{9,11},{10,... | collective-permute-start | bytes 737288 | tf_op jit(solution)/shard_map/ppermute | solution.py:22
  33.4 7.8 %collective-permute-start.5 = (bf16[576,384]{1,0:T(8,128)(2,1)S(1)}, bf16[576,384]{1,0:T(8,128)(2,1)S(1)}, u32[]{:S(2)}, u32[]{:S(2)}) collective-permute-start(bf16[576,384]{1,0:T(8,128)(2,1)S(1)} %pad_maximum_fusion.2.refs_6_), channel_id=1, source_target_pairs={{0,1},{1,0},{2,3},{3,2},{4,5},{5,4},{6,7},{7,6},{8,9},{9,8},{10,11... | collective-permute-start | bytes 1327112 | tf_op jit(solution)/shard_map/ppermute | solution.py:22
  38.2 4.4 %collective-permute-start.2 = (bf16[1152,384]{1,0:T(8,128)(2,1)S(1)}, bf16[1152,384]{1,0:T(8,128)(2,1)S(1)}, u32[]{:S(2)}, u32[]{:S(2)}) collective-permute-start(bf16[1152,384]{1,0:T(8,128)(2,1)S(1)} %get-tuple-element.20.refs_4_), channel_id=1, source_target_pairs={{0,1},{1,0},{2,3},{3,2},{4,5},{5,4},{6,7},{7,6},{8,9},{9,8},{10,11... | collective-permute-start | bytes 2654216 | tf_op jit(solution)/shard_map/ppermute | solution.py:22
  38.6 13.7 %slice-start = ((s8[9437184]{0:T(1024)(128)(4,1)}), s8[4194304]{0:T(1024)(128)(4,1)S(1)}, s32[]{:S(2)}) async-start(s8[9437184]{0:T(1024)(128)(4,1)} %bitcast.7), calls=%async_computation | async-start | bytes 8388608
  38.6 4.0 %collective-permute-start.8 = (bf16[576,384]{1,0:T(8,128)(2,1)S(1)}, bf16[576,384]{1,0:T(8,128)(2,1)S(1)}, u32[]{:S(2)}, u32[]{:S(2)}) collective-permute-start(bf16[576,384]{1,0:T(8,128)(2,1)S(1)} %pad_maximum_fusion.3.refs_8_), channel_id=1, source_target_pairs={{0,1},{1,0},{2,3},{3,2},{4,5},{5,4},{6,7},{7,6},{8,9},{9,8},{10,11... | collective-permute-start | bytes 1327112 | tf_op jit(solution)/shard_map/ppermute | solution.py:22
  42.7 9.5 %slice-start.1 = ((s8[9437184]{0:T(1024)(128)(4,1)}), s8[4194304]{0:T(1024)(128)(4,1)S(1)}, s32[]{:S(2)}) async-start(s8[9437184]{0:T(1024)(128)(4,1)} %bitcast.7), calls=%async_computation.1 | async-start | bytes 8388608
  44.2 8.1 %collective-permute-start.11 = (bf16[4,32,384]{2,1,0:T(8,128)(2,1)S(1)}, bf16[4,32,384]{2,1,0:T(8,128)(2,1)S(1)}, u32[]{:S(2)}, u32[]{:S(2)}) collective-permute-start(bf16[4,32,384]{2,1,0:T(8,128)(2,1)S(1)} %shard_map.95), channel_id=1, source_target_pairs={{0,12},{4,8},{8,4},{12,0},{1,13},{5,9},{9,5},{13,1},{2,14},{6,10},... | collective-permute-start | bytes 294920 | tf_op jit(solution)/shard_map/ppermute | solution.py:22
  48.3 4.0 %slice-start.2 = ((s8[9437184]{0:T(1024)(128)(4,1)}), s8[1048576]{0:T(1024)(128)(4,1)S(1)}, s32[]{:S(2)}) async-start(s8[9437184]{0:T(1024)(128)(4,1)} %bitcast.7), calls=%async_computation.2 | async-start | bytes 2097152
  48.3 6.7 %collective-permute-start.9 = (bf16[4,32,384]{2,1,0:T(8,128)(2,1)S(1)}, bf16[4,32,384]{2,1,0:T(8,128)(2,1)S(1)}, u32[]{:S(2)}, u32[]{:S(2)}) collective-permute-start(bf16[4,32,384]{2,1,0:T(8,128)(2,1)S(1)} %shard_map.92), channel_id=1, source_target_pairs={{0,8},{4,12},{8,0},{12,4},{1,9},{5,13},{9,1},{13,5},{2,10},{6,14},... | collective-permute-start | bytes 294920 | tf_op jit(solution)/shard_map/ppermute | solution.py:22
  49.8 6.4 %collective-permute-start.10 = (bf16[4,32,384]{2,1,0:T(8,128)(2,1)S(1)}, bf16[4,32,384]{2,1,0:T(8,128)(2,1)S(1)}, u32[]{:S(2)}, u32[]{:S(2)}) collective-permute-start(bf16[4,32,384]{2,1,0:T(8,128)(2,1)S(1)} %shard_map.93), channel_id=1, source_target_pairs={{0,4},{4,0},{8,12},{12,8},{1,5},{5,1},{9,13},{13,9},{2,6},{6,2},{1... | collective-permute-start | bytes 294920 | tf_op jit(solution)/shard_map/ppermute | solution.py:22
  52.2 4.0 %copy-start.1 = (bf16[3072,64]{0,1:T(8,128)(2,1)S(1)}, bf16[3072,64]{0,1:T(8,128)(2,1)}, u32[]{:S(2)}) copy-start(bf16[3072,64]{0,1:T(8,128)(2,1)} %param.15) | copy-start | bytes 1179652
  52.2 4.0 %copy-start.2 = (f32[3072]{0:T(1024)S(1)}, f32[3072]{0:T(1024)}, u32[]{:S(2)}) copy-start(f32[3072]{0:T(1024)} %param.14) | copy-start | bytes 36868
  52.2 4.0 %copy-start.3 = (f32[3072]{0:T(1024)S(1)}, f32[3072]{0:T(1024)}, u32[]{:S(2)}) copy-start(f32[3072]{0:T(1024)} %param.13) | copy-start | bytes 36868
  56.2 9.3 %copy-start = (bf16[432,512]{1,0:T(8,128)(2,1)S(1)}, bf16[432,512]{1,0:T(8,128)(2,1)}, u32[]{:S(2)}) copy-start(bf16[432,512]{1,0:T(8,128)(2,1)} %w_ref.1) | copy-start | bytes 1327108
  56.2 9.2 %copy-start.4 = (f32[512]{0:T(512)S(1)}, f32[512]{0:T(512)}, u32[]{:S(2)}) copy-start(f32[512]{0:T(512)} %param.17) | copy-start | bytes 6148
  59.2 4.0 %collective-permute-start.12 = (bf16[128,32]{1,0:T(8,128)(2,1)S(1)}, bf16[128,32]{1,0:T(8,128)(2,1)S(1)}, u32[]{:S(2)}, u32[]{:S(2)}) collective-permute-start(bf16[128,32]{1,0:T(8,128)(2,1)S(1)} %get-tuple-element.15.inner_ref), channel_id=1, source_target_pairs={{0,1},{1,0},{2,3},{3,2},{4,5},{5,4},{6,7},{7,6},{8,9},{9,8},{10,11... | collective-permute-start | bytes 24584 | tf_op jit(solution)/shard_map/ppermute | solution.py:22
  60.2 5.2 %collective-permute-start.13 = (bf16[128,32]{1,0:T(8,128)(2,1)S(1)}, bf16[128,32]{1,0:T(8,128)(2,1)S(1)}, u32[]{:S(2)}, u32[]{:S(2)}) collective-permute-start(bf16[128,32]{1,0:T(8,128)(2,1)S(1)} %get-tuple-element.16.outer_ref), channel_id=1, source_target_pairs={{1,2},{3,4},{5,6},{7,8},{9,10},{11,12},{13,14},{2,1},{4,3},{6,5},{... | collective-permute-start | bytes 24584 | tf_op jit(solution)/shard_map/ppermute | solution.py:387

commit v17 on v14

--- a/solution.py
+++ b/solution.py
@@ -295,11 +295,17 @@
             latent[f, x, 7:8, :] = own[:1, :ch]
             latent[f, x, 8 + height : 9 + height, :] = own[rows - 1 :, ch:]
     depth = 9 * ch
+    row_taps = [
+        [
+            jnp.concatenate([latent[f, x, 7 + e : 7 + e + height, :] for e in range(3)], axis=1).astype(
+                jnp.bfloat16
+            )
+            for x in range(cols)
+        ]
+        for f in range(frames)
+    ]
     for x in range(cols - 2):
-        stacked = []
-        for f in range(frames):
-            taps = [latent[f, x + b, 7 + e : 7 + e + height, :] for b in range(3) for e in range(3)]
-            stacked.append(jnp.concatenate(taps, axis=1).astype(jnp.bfloat16))
+        stacked = [jnp.concatenate(row_taps[f][x : x + 3], axis=1) for f in range(frames)]
         stacked = [stacked[0]] * 2 + stacked
         acc = None
         for a in range(3):
@@ -372,7 +378,7 @@
     for targets in ((3,), (2,), (1,), (0,)):
         for t, o in zip(targets, attend(asked, keys_values, targets, planes)):
             results[t] = o if t == 0 else swap(o, "heads", t)
-    partial = project(where, [results[t] for t in near], near, w_out, 1024)
+    partial = project(where, [results[t] for t in near], near, w_out, 1536)
     sent = [results[t] for t in far]
     inner, outer = final_layer(
         where, sent, far, partial, w_out, scale_mod, shift_mod, w_final, rows_dev, planes

time: 67.5 us -> 67.4 us (level)
  no operation moved by 1% of the time
where the time goes in v17:
time: 67.4 us; the launch traced here: 67.3 us
  starting transfers between devices  26.8 us (40%)
  waiting for transfers between devices  24.3 us (36%)
  Pallas kernels  13.7 us (20%)
  other arithmetic  1.64 us (2%)
    ppermute x14, starting transfers between devices, swap(): return lax.ppermute(source, axis, [(i, i ^ distance) for i in range(count)])  24.8 us
    ppermute x14, waiting for transfers between devices, swap(): return lax.ppermute(source, axis, [(i, i ^ distance) for i in range(count)])  21.2 us
    pallas_call x4, Pallas kernels, attend(): pl.pallas_call(functools.partial(attend_kernel, sources=sources, planes=p...  5.68 us
    ppermute x1, waiting for transfers between devices, shards(): lax.ppermute(outer, ('heads', 'plane'), pairs + [(j, i) for i, j in pairs])  3.12 us
    pallas_call x1, Pallas kernels, final_layer(): pl.pallas_call(functools.partial(final_kernel, targets=targets, planes=pl...  3 us
    pallas_call x1, Pallas kernels, convolve(): pl.pallas_call(convolve_kernel, in_specs=[smem] + [vmem] * 6, out_specs=v...  2.31 us
    ppermute x1, starting transfers between devices, shards(): lax.ppermute(outer, ('heads', 'plane'), pairs + [(j, i) for i, j in pairs])  2.08 us
    pallas_call x1, Pallas kernels, project(): pl.pallas_call(functools.partial(project_kernel, targets=targets), grid_s...  1.87 us
  transfers between devices with their start and end apart: 15, of which 6 were waited for; matrix products, arithmetic and copies ran while one was open for 1% of the time, Pallas kernels for 9%

profile of v17, /device:TPU:1, one launch (start us, length us, event | category | flops | bytes accessed | tf_op | source)
XLA Modules:
  0.0 67.3 jit_solution(3362219937684418660)
XLA Ops:
  0.0 1.3 %pad_maximum_fusion.qkv_ref = bf16[384,1536]{1,0:T(8,128)(2,1)S(1)} fusion(bf16[128,1536]{1,0:T(8,128)(2,1)} %param.11, bf16[128,1536]{1,0:T(8,128)(2,1)} %param.10, bf16[128,1536]{1,0:T(8,128)(2,1)} %param.9), kind=kLoop, calls=%fused_computation | loop fusion | flops 3538944 | bytes 2359296 | tf_op jit(solution)/shard_map/concatenate | solution.py:52
  1.3 0.1 pad_add_fusion.where_ref
  1.4 0.8 %shard_map.91 = (bf16[384,384]{1,0:T(8,128)(2,1)S(1)}, bf16[384,384]{1,0:T(8,128)(2,1)S(1)}, bf16[384,384]{1,0:T(8,128)(2,1)S(1)}, bf16[384,384]{1,0:T(8,128)(2,1)S(1)}) custom-call(s32[4]{0:T(128)S(1)} %pad_add_fusion.where_ref, bf16[384,1536]{1,0:T(8,128)(2,1)S(1)} %pad_maximum_fusion.qkv_ref), custom_call_target="tpu_custom_call" | custom-call | tf_op jit(solution)/shard_map/pallas_call | solution.py:46
  2.3 2.1 %collective-permute-start = (bf16[320,384]{1,0:T(8,128)(2,1)S(1)}, bf16[320,384]{1,0:T(8,128)(2,1)S(1)}, u32[]{:S(2)}, u32[]{:S(2)}) collective-permute-start(bf16[320,384]{1,0:T(8,128)(2,1)S(1)} %pad_maximum_fusion.3), channel_id=1, source_target_pairs={{0,2},{1,3},{2,0},{3,1},{4,6},{5,7},{6,4},{7,5},{8,10},{9,11},{10,... | collective-permute-start | bytes 737288 | tf_op jit(solution)/shard_map/ppermute | solution.py:22
  4.4 1.3 %collective-permute-start.1 = (bf16[384,384]{1,0:T(8,128)(2,1)S(1)}, bf16[384,384]{1,0:T(8,128)(2,1)S(1)}, u32[]{:S(2)}, u32[]{:S(2)}) collective-permute-start(bf16[384,384]{1,0:T(8,128)(2,1)S(1)} %get-tuple-element.12), channel_id=1, source_target_pairs={{0,4},{4,0},{8,12},{12,8},{1,5},{5,1},{9,13},{13,9},{2,6},{6,2},{1... | collective-permute-start | bytes 884744 | tf_op jit(solution)/shard_map/ppermute | solution.py:22
  5.7 2.3 %collective-permute-start.4 = (bf16[384,384]{1,0:T(8,128)(2,1)S(1)}, bf16[384,384]{1,0:T(8,128)(2,1)S(1)}, u32[]{:S(2)}, u32[]{:S(2)}) collective-permute-start(bf16[384,384]{1,0:T(8,128)(2,1)S(1)} %get-tuple-element.13), channel_id=1, source_target_pairs={{0,8},{4,12},{8,0},{12,4},{1,9},{5,13},{9,1},{13,5},{2,10},{6,14},... | collective-permute-start | bytes 884744 | tf_op jit(solution)/shard_map/ppermute | solution.py:22
  8.0 0.0 collective-permute-start.7
  8.1 2.1 %collective-permute-done = bf16[320,384]{1,0:T(8,128)(2,1)S(1)} collective-permute-done((bf16[320,384]{1,0:T(8,128)(2,1)S(1)}, bf16[320,384]{1,0:T(8,128)(2,1)S(1)}, u32[]{:S(2)}, u32[]{:S(2)}) %collective-permute-start) | collective-permute-done | bytes 245792 | tf_op jit(solution)/shard_map/ppermute | solution.py:22
  10.1 7.2 %collective-permute-done.1 = bf16[384,384]{1,0:T(8,128)(2,1)S(1)} collective-permute-done((bf16[384,384]{1,0:T(8,128)(2,1)S(1)}, bf16[384,384]{1,0:T(8,128)(2,1)S(1)}, u32[]{:S(2)}, u32[]{:S(2)}) %collective-permute-start.1) | collective-permute-done | bytes 294944 | tf_op jit(solution)/shard_map/ppermute | solution.py:22
  17.4 0.1 fusion.5
  17.5 0.5 collective-permute-start.2
  18.0 0.0 collective-permute-done.4
  18.1 1.1 %collective-permute-start.5 = (bf16[320,384]{1,0:T(8,128)(2,1)S(1)}, bf16[320,384]{1,0:T(8,128)(2,1)S(1)}, u32[]{:S(2)}, u32[]{:S(2)}) collective-permute-start(bf16[320,384]{1,0:T(8,128)(2,1)S(1)} %pad_maximum_fusion.5), channel_id=1, source_target_pairs={{0,2},{1,3},{2,0},{3,1},{4,6},{5,7},{6,4},{7,5},{8,10},{9,11},{10,... | collective-permute-start | bytes 737288 | tf_op jit(solution)/shard_map/ppermute | solution.py:22
  19.2 7.5 %collective-permute-done.7 = bf16[384,384]{1,0:T(8,128)(2,1)S(1)} collective-permute-done((bf16[384,384]{1,0:T(8,128)(2,1)S(1)}, bf16[384,384]{1,0:T(8,128)(2,1)S(1)}, u32[]{:S(2)}, u32[]{:S(2)}) %collective-permute-start.7) | collective-permute-done | bytes 294944 | tf_op jit(solution)/shard_map/ppermute | solution.py:22
  26.8 0.3 collective-permute-start.8
  27.1 0.0 collective-permute-done.2
  27.2 5.7 %collective-permute-start.3 = (bf16[1152,384]{1,0:T(8,128)(2,1)S(1)}, bf16[1152,384]{1,0:T(8,128)(2,1)S(1)}, u32[]{:S(2)}, u32[]{:S(2)}) collective-permute-start(bf16[1152,384]{1,0:T(8,128)(2,1)S(1)} %get-tuple-element.36.refs_4_), channel_id=1, source_target_pairs={{0,1},{1,0},{2,3},{3,2},{4,5},{5,4},{6,7},{7,6},{8,9},{9,8},{10,11... | collective-permute-start | bytes 2654216 | tf_op jit(solution)/shard_map/ppermute | solution.py:22
  33.0 0.0 collective-permute-done.5
  33.1 3.9 %collective-permute-start.6 = (bf16[576,384]{1,0:T(8,128)(2,1)S(1)}, bf16[576,384]{1,0:T(8,128)(2,1)S(1)}, u32[]{:S(2)}, u32[]{:S(2)}) collective-permute-start(bf16[576,384]{1,0:T(8,128)(2,1)S(1)} %pad_maximum_fusion.1.refs_6_), channel_id=1, source_target_pairs={{0,1},{1,0},{2,3},{3,2},{4,5},{5,4},{6,7},{7,6},{8,9},{9,8},{10,11... | collective-permute-start | bytes 1327112 | tf_op jit(solution)/shard_map/ppermute | solution.py:22
  36.9 0.0 collective-permute-done.8
  37.0 0.0 slice-start
  37.1 2.5 %collective-permute-start.9 = (bf16[576,384]{1,0:T(8,128)(2,1)S(1)}, bf16[576,384]{1,0:T(8,128)(2,1)S(1)}, u32[]{:S(2)}, u32[]{:S(2)}) collective-permute-start(bf16[576,384]{1,0:T(8,128)(2,1)S(1)} %pad_maximum_fusion.2.refs_8_), channel_id=1, source_target_pairs={{0,1},{1,0},{2,3},{3,2},{4,5},{5,4},{6,7},{7,6},{8,9},{9,8},{10,11... | collective-permute-start | bytes 1327112 | tf_op jit(solution)/shard_map/ppermute | solution.py:22
  39.6 0.0 collective-permute-done.6.refs_7_
  39.6 1.4 %collective-permute-done.9.refs_9_ = bf16[576,384]{1,0:T(8,128)(2,1)S(1)} collective-permute-done((bf16[576,384]{1,0:T(8,128)(2,1)S(1)}, bf16[576,384]{1,0:T(8,128)(2,1)S(1)}, u32[]{:S(2)}, u32[]{:S(2)}) %collective-permute-start.9) | collective-permute-done | bytes 442400 | tf_op jit(solution)/shard_map/ppermute | solution.py:22
  41.0 0.0 collective-permute-done.3.refs_5_
  41.1 0.0 slice-start.1
  41.1 1.4 %shard_map.95 = bf16[4,32,384]{2,1,0:T(8,128)(2,1)S(1)} custom-call(bf16[128,384]{1,0:T(8,128)(2,1)S(1)} %get-tuple-element.39.refs_0_, bf16[128,384]{1,0:T(8,128)(2,1)S(1)} %get-tuple-element.40.refs_1_, bf16[128,384]{1,0:T(8,128)(2,1)S(1)} %pad_maximum_fusion.9.refs_2_, bf16[128,384]{1,0:T(8,128)(2,1)S(1)} %pad_maximum_fusion.10.refs_3_, ...), custom_call_target="tpu_custom_call" | custom-call | tf_op jit(solution)/shard_map/pallas_call | solution.py:134
  42.6 2.3 %collective-permute-start.12 = (bf16[4,32,384]{2,1,0:T(8,128)(2,1)S(1)}, bf16[4,32,384]{2,1,0:T(8,128)(2,1)S(1)}, u32[]{:S(2)}, u32[]{:S(2)}) collective-permute-start(bf16[4,32,384]{2,1,0:T(8,128)(2,1)S(1)} %shard_map.95), channel_id=1, source_target_pairs={{0,12},{4,8},{8,4},{12,0},{1,13},{5,9},{9,5},{13,1},{2,14},{6,10},... | collective-permute-start | bytes 294920 | tf_op jit(solution)/shard_map/ppermute | solution.py:22
  44.8 1.4 %shard_map.92 = bf16[4,32,384]{2,1,0:T(8,128)(2,1)S(1)} custom-call(bf16[128,384]{1,0:T(8,128)(2,1)S(1)} %get-tuple-element.39.refs_0_, bf16[128,384]{1,0:T(8,128)(2,1)S(1)} %get-tuple-element.40.refs_1_, bf16[128,384]{1,0:T(8,128)(2,1)S(1)} %pad_maximum_fusion.9.refs_2_, bf16[128,384]{1,0:T(8,128)(2,1)S(1)} %pad_maximum_fusion.10.refs_3_, ...), custom_call_target="tpu_custom_call" | custom-call | tf_op jit(solution)/shard_map/pallas_call | solution.py:134
  46.3 0.0 slice-start.2
  46.3 1.3 %collective-permute-start.10 = (bf16[4,32,384]{2,1,0:T(8,128)(2,1)S(1)}, bf16[4,32,384]{2,1,0:T(8,128)(2,1)S(1)}, u32[]{:S(2)}, u32[]{:S(2)}) collective-permute-start(bf16[4,32,384]{2,1,0:T(8,128)(2,1)S(1)} %shard_map.92), channel_id=1, source_target_pairs={{0,8},{4,12},{8,0},{12,4},{1,9},{5,13},{9,1},{13,5},{2,10},{6,14},... | collective-permute-start | bytes 294920 | tf_op jit(solution)/shard_map/ppermute | solution.py:22
  47.6 1.4 %shard_map.93 = bf16[4,32,384]{2,1,0:T(8,128)(2,1)S(1)} custom-call(bf16[128,384]{1,0:T(8,128)(2,1)S(1)} %get-tuple-element.39.refs_0_, bf16[128,384]{1,0:T(8,128)(2,1)S(1)} %get-tuple-element.40.refs_1_, bf16[128,384]{1,0:T(8,128)(2,1)S(1)} %pad_maximum_fusion.9.refs_2_, bf16[128,384]{1,0:T(8,128)(2,1)S(1)} %pad_maximum_fusion.10.refs_3_, ...), custom_call_target="tpu_custom_call" | custom-call | tf_op jit(solution)/shard_map/pallas_call | solution.py:134
  49.0 0.2 collective-permute-start.11
  49.3 1.4 %shard_map.94.refs_0_ = bf16[4,32,384]{2,1,0:T(8,128)(2,1)S(1)} custom-call(bf16[128,384]{1,0:T(8,128)(2,1)S(1)} %get-tuple-element.39.refs_0_, bf16[128,384]{1,0:T(8,128)(2,1)S(1)} %get-tuple-element.40.refs_1_, bf16[128,384]{1,0:T(8,128)(2,1)S(1)} %pad_maximum_fusion.9.refs_2_, bf16[128,384]{1,0:T(8,128)(2,1)S(1)} %pad_maximum_fusion.10.refs_3_, ...), custom_call_target="tpu_custom_call" | custom-call | tf_op jit(solution)/shard_map/pallas_call | solution.py:134
  50.7 0.0 copy-start.1
  50.7 0.0 copy-start.2
  50.7 0.0 copy-start.3
  50.7 0.0 collective-permute-done.12.refs_1_
  50.7 0.0 slice-done
  50.7 0.0 slice-done.1
  50.7 0.0 slice-done.2
  50.8 1.9 %shard_map.96.refs_4_ = f32[2,128,1536]{2,1,0:T(8,128)S(1)} custom-call(s32[4]{0:T(128)S(1)} %pad_add_fusion.where_ref, bf16[4,32,384]{2,1,0:T(8,128)(2,1)S(1)} %shard_map.94.refs_0_, bf16[4,32,384]{2,1,0:T(8,128)(2,1)S(1)} %collective-permute-done.12.refs_1_, bf16[1536,3072]{1,0:T(8,128)(2,1)S(1)} %bitcast.8, bf16[1536,3072]{1,0:T(8,128)(2,1)S(1)} %bitcast.8), custom_call_target="tpu_custom_call" | custom-call | tf_op jit(solution)/shard_map/pallas_call | solution.py:179
  52.6 2.9 %collective-permute-done.10.refs_0_ = bf16[4,32,384]{2,1,0:T(8,128)(2,1)S(1)} collective-permute-done((bf16[4,32,384]{2,1,0:T(8,128)(2,1)S(1)}, bf16[4,32,384]{2,1,0:T(8,128)(2,1)S(1)}, u32[]{:S(2)}, u32[]{:S(2)}) %collective-permute-start.10) | collective-permute-done | bytes 98336 | tf_op jit(solution)/shard_map/ppermute | solution.py:22
  55.5 0.0 collective-permute-done.11.refs_1_
  55.5 0.0 copy-done.1
  55.5 0.0 copy-done.2
  55.5 0.0 copy-done.3
  55.6 0.0 copy-start
  55.6 0.0 copy-start.4
  55.6 3.0 %shard_map.97 = (bf16[128,32]{1,0:T(8,128)(2,1)S(1)}, bf16[128,32]{1,0:T(8,128)(2,1)S(1)}) custom-call(s32[4]{0:T(128)S(1)} %pad_add_fusion.where_ref, bf16[4,32,384]{2,1,0:T(8,128)(2,1)S(1)} %collective-permute-done.10.refs_0_, bf16[4,32,384]{2,1,0:T(8,128)(2,1)S(1)} %collective-permute-done.11.refs_1_, bf16[1536,3072]{1,0:T(8,128)(2,1)S(1)} %bitcast.8, ...), custom_call_target="tpu_custom_call" | custom-call | tf_op jit(solution)/shard_map/pallas_call | solution.py:254
  58.6 1.1 %collective-permute-start.13 = (bf16[128,32]{1,0:T(8,128)(2,1)S(1)}, bf16[128,32]{1,0:T(8,128)(2,1)S(1)}, u32[]{:S(2)}, u32[]{:S(2)}) collective-permute-start(bf16[128,32]{1,0:T(8,128)(2,1)S(1)} %get-tuple-element.15.inner_ref), channel_id=1, source_target_pairs={{0,1},{1,0},{2,3},{3,2},{4,5},{5,4},{6,7},{7,6},{8,9},{9,8},{10,11... | collective-permute-start | bytes 24584 | tf_op jit(solution)/shard_map/ppermute | solution.py:22
  59.7 2.1 %collective-permute-start.14 = (bf16[128,32]{1,0:T(8,128)(2,1)S(1)}, bf16[128,32]{1,0:T(8,128)(2,1)S(1)}, u32[]{:S(2)}, u32[]{:S(2)}) collective-permute-start(bf16[128,32]{1,0:T(8,128)(2,1)S(1)} %get-tuple-element.16.outer_ref), channel_id=1, source_target_pairs={{1,2},{3,4},{5,6},{7,8},{9,10},{11,12},{13,14},{2,1},{4,3},{6,5},{... | collective-permute-start | bytes 24584 | tf_op jit(solution)/shard_map/ppermute | solution.py:388
  61.8 0.0 collective-permute-done.13.inner_got_ref
  61.8 3.1 %collective-permute-done.14.outer_got_ref = bf16[128,32]{1,0:T(8,128)(2,1)S(1)} collective-permute-done((bf16[128,32]{1,0:T(8,128)(2,1)S(1)}, bf16[128,32]{1,0:T(8,128)(2,1)S(1)}, u32[]{:S(2)}, u32[]{:S(2)}) %collective-permute-start.14) | collective-permute-done | bytes 8224 | tf_op jit(solution)/shard_map/ppermute | solution.py:388
  64.9 0.0 copy-done
  64.9 0.0 copy-done.4
  64.9 2.3 %shard_map.98 = bf16[4,2,64,512]{3,2,1,0:T(8,128)(2,1)} custom-call(s32[4]{0:T(128)S(1)} %pad_add_fusion.where_ref, bf16[128,32]{1,0:T(8,128)(2,1)S(1)} %get-tuple-element.15.inner_ref, bf16[128,32]{1,0:T(8,128)(2,1)S(1)} %get-tuple-element.16.outer_ref, bf16[128,32]{1,0:T(8,128)(2,1)S(1)} %collective-permute-done.13.inner_got_ref, ...), custom_call_target="tpu_custom_call" | custom-call | tf_op jit(solution)/shard_map/pallas_call | solution.py:326
  (32 shorter events, 0.6 us)
Async XLA Ops:
  2.3 7.8 %collective-permute-start = (bf16[320,384]{1,0:T(8,128)(2,1)S(1)}, bf16[320,384]{1,0:T(8,128)(2,1)S(1)}, u32[]{:S(2)}, u32[]{:S(2)}) collective-permute-start(bf16[320,384]{1,0:T(8,128)(2,1)S(1)} %pad_maximum_fusion.3), channel_id=1, source_target_pairs={{0,2},{1,3},{2,0},{3,1},{4,6},{5,7},{6,4},{7,5},{8,10},{9,11},{10,... | collective-permute-start | bytes 737288 | tf_op jit(solution)/shard_map/ppermute | solution.py:22
  4.4 13.0 %collective-permute-start.1 = (bf16[384,384]{1,0:T(8,128)(2,1)S(1)}, bf16[384,384]{1,0:T(8,128)(2,1)S(1)}, u32[]{:S(2)}, u32[]{:S(2)}) collective-permute-start(bf16[384,384]{1,0:T(8,128)(2,1)S(1)} %get-tuple-element.12), channel_id=1, source_target_pairs={{0,4},{4,0},{8,12},{12,8},{1,5},{5,1},{9,13},{13,9},{2,6},{6,2},{1... | collective-permute-start | bytes 884744 | tf_op jit(solution)/shard_map/ppermute | solution.py:22
  5.7 12.2 %collective-permute-start.4 = (bf16[384,384]{1,0:T(8,128)(2,1)S(1)}, bf16[384,384]{1,0:T(8,128)(2,1)S(1)}, u32[]{:S(2)}, u32[]{:S(2)}) collective-permute-start(bf16[384,384]{1,0:T(8,128)(2,1)S(1)} %get-tuple-element.13), channel_id=1, source_target_pairs={{0,8},{4,12},{8,0},{12,4},{1,9},{5,13},{9,1},{13,5},{2,10},{6,14},... | collective-permute-start | bytes 884744 | tf_op jit(solution)/shard_map/ppermute | solution.py:22
  8.0 18.7 %collective-permute-start.7 = (bf16[384,384]{1,0:T(8,128)(2,1)S(1)}, bf16[384,384]{1,0:T(8,128)(2,1)S(1)}, u32[]{:S(2)}, u32[]{:S(2)}) collective-permute-start(bf16[384,384]{1,0:T(8,128)(2,1)S(1)} %get-tuple-element.14), channel_id=1, source_target_pairs={{0,12},{4,8},{8,4},{12,0},{1,13},{5,9},{9,5},{13,1},{2,14},{6,10},... | collective-permute-start | bytes 884744 | tf_op jit(solution)/shard_map/ppermute | solution.py:22
  17.5 9.6 %collective-permute-start.2 = (bf16[320,384]{1,0:T(8,128)(2,1)S(1)}, bf16[320,384]{1,0:T(8,128)(2,1)S(1)}, u32[]{:S(2)}, u32[]{:S(2)}) collective-permute-start(bf16[320,384]{1,0:T(8,128)(2,1)S(1)} %pad_maximum_fusion.4), channel_id=1, source_target_pairs={{0,2},{1,3},{2,0},{3,1},{4,6},{5,7},{6,4},{7,5},{8,10},{9,11},{10,... | collective-permute-start | bytes 737288 | tf_op jit(solution)/shard_map/ppermute | solution.py:22
  18.1 14.9 %collective-permute-start.5 = (bf16[320,384]{1,0:T(8,128)(2,1)S(1)}, bf16[320,384]{1,0:T(8,128)(2,1)S(1)}, u32[]{:S(2)}, u32[]{:S(2)}) collective-permute-start(bf16[320,384]{1,0:T(8,128)(2,1)S(1)} %pad_maximum_fusion.5), channel_id=1, source_target_pairs={{0,2},{1,3},{2,0},{3,1},{4,6},{5,7},{6,4},{7,5},{8,10},{9,11},{10,... | collective-permute-start | bytes 737288 | tf_op jit(solution)/shard_map/ppermute | solution.py:22
  26.8 10.2 %collective-permute-start.8 = (bf16[320,384]{1,0:T(8,128)(2,1)S(1)}, bf16[320,384]{1,0:T(8,128)(2,1)S(1)}, u32[]{:S(2)}, u32[]{:S(2)}) collective-permute-start(bf16[320,384]{1,0:T(8,128)(2,1)S(1)} %pad_maximum_fusion.6), channel_id=1, source_target_pairs={{0,2},{1,3},{2,0},{3,1},{4,6},{5,7},{6,4},{7,5},{8,10},{9,11},{10,... | collective-permute-start | bytes 737288 | tf_op jit(solution)/shard_map/ppermute | solution.py:22
  27.2 13.8 %collective-permute-start.3 = (bf16[1152,384]{1,0:T(8,128)(2,1)S(1)}, bf16[1152,384]{1,0:T(8,128)(2,1)S(1)}, u32[]{:S(2)}, u32[]{:S(2)}) collective-permute-start(bf16[1152,384]{1,0:T(8,128)(2,1)S(1)} %get-tuple-element.36.refs_4_), channel_id=1, source_target_pairs={{0,1},{1,0},{2,3},{3,2},{4,5},{5,4},{6,7},{7,6},{8,9},{9,8},{10,11... | collective-permute-start | bytes 2654216 | tf_op jit(solution)/shard_map/ppermute | solution.py:22
  33.1 6.5 %collective-permute-start.6 = (bf16[576,384]{1,0:T(8,128)(2,1)S(1)}, bf16[576,384]{1,0:T(8,128)(2,1)S(1)}, u32[]{:S(2)}, u32[]{:S(2)}) collective-permute-start(bf16[576,384]{1,0:T(8,128)(2,1)S(1)} %pad_maximum_fusion.1.refs_6_), channel_id=1, source_target_pairs={{0,1},{1,0},{2,3},{3,2},{4,5},{5,4},{6,7},{7,6},{8,9},{9,8},{10,11... | collective-permute-start | bytes 1327112 | tf_op jit(solution)/shard_map/ppermute | solution.py:22
  37.0 13.7 %slice-start = ((s8[9437184]{0:T(1024)(128)(4,1)}), s8[4194304]{0:T(1024)(128)(4,1)S(1)}, s32[]{:S(2)}) async-start(s8[9437184]{0:T(1024)(128)(4,1)} %bitcast.7), calls=%async_computation | async-start | bytes 8388608
  37.1 3.9 %collective-permute-start.9 = (bf16[576,384]{1,0:T(8,128)(2,1)S(1)}, bf16[576,384]{1,0:T(8,128)(2,1)S(1)}, u32[]{:S(2)}, u32[]{:S(2)}) collective-permute-start(bf16[576,384]{1,0:T(8,128)(2,1)S(1)} %pad_maximum_fusion.2.refs_8_), channel_id=1, source_target_pairs={{0,1},{1,0},{2,3},{3,2},{4,5},{5,4},{6,7},{7,6},{8,9},{9,8},{10,11... | collective-permute-start | bytes 1327112 | tf_op jit(solution)/shard_map/ppermute | solution.py:22
  41.1 9.6 %slice-start.1 = ((s8[9437184]{0:T(1024)(128)(4,1)}), s8[4194304]{0:T(1024)(128)(4,1)S(1)}, s32[]{:S(2)}) async-start(s8[9437184]{0:T(1024)(128)(4,1)} %bitcast.7), calls=%async_computation.1 | async-start | bytes 8388608
  42.6 8.1 %collective-permute-start.12 = (bf16[4,32,384]{2,1,0:T(8,128)(2,1)S(1)}, bf16[4,32,384]{2,1,0:T(8,128)(2,1)S(1)}, u32[]{:S(2)}, u32[]{:S(2)}) collective-permute-start(bf16[4,32,384]{2,1,0:T(8,128)(2,1)S(1)} %shard_map.95), channel_id=1, source_target_pairs={{0,12},{4,8},{8,4},{12,0},{1,13},{5,9},{9,5},{13,1},{2,14},{6,10},... | collective-permute-start | bytes 294920 | tf_op jit(solution)/shard_map/ppermute | solution.py:22
  46.3 4.5 %slice-start.2 = ((s8[9437184]{0:T(1024)(128)(4,1)}), s8[1048576]{0:T(1024)(128)(4,1)S(1)}, s32[]{:S(2)}) async-start(s8[9437184]{0:T(1024)(128)(4,1)} %bitcast.7), calls=%async_computation.2 | async-start | bytes 2097152
  46.3 9.3 %collective-permute-start.10 = (bf16[4,32,384]{2,1,0:T(8,128)(2,1)S(1)}, bf16[4,32,384]{2,1,0:T(8,128)(2,1)S(1)}, u32[]{:S(2)}, u32[]{:S(2)}) collective-permute-start(bf16[4,32,384]{2,1,0:T(8,128)(2,1)S(1)} %shard_map.92), channel_id=1, source_target_pairs={{0,8},{4,12},{8,0},{12,4},{1,9},{5,13},{9,1},{13,5},{2,10},{6,14},... | collective-permute-start | bytes 294920 | tf_op jit(solution)/shard_map/ppermute | solution.py:22
  49.0 6.5 %collective-permute-start.11 = (bf16[4,32,384]{2,1,0:T(8,128)(2,1)S(1)}, bf16[4,32,384]{2,1,0:T(8,128)(2,1)S(1)}, u32[]{:S(2)}, u32[]{:S(2)}) collective-permute-start(bf16[4,32,384]{2,1,0:T(8,128)(2,1)S(1)} %shard_map.93), channel_id=1, source_target_pairs={{0,4},{4,0},{8,12},{12,8},{1,5},{5,1},{9,13},{13,9},{2,6},{6,2},{1... | collective-permute-start | bytes 294920 | tf_op jit(solution)/shard_map/ppermute | solution.py:22
  50.7 4.9 %copy-start.1 = (bf16[3072,64]{0,1:T(8,128)(2,1)S(1)}, bf16[3072,64]{0,1:T(8,128)(2,1)}, u32[]{:S(2)}) copy-start(bf16[3072,64]{0,1:T(8,128)(2,1)} %param.15) | copy-start | bytes 1179652
  50.7 4.9 %copy-start.2 = (f32[3072]{0:T(1024)S(1)}, f32[3072]{0:T(1024)}, u32[]{:S(2)}) copy-start(f32[3072]{0:T(1024)} %param.14) | copy-start | bytes 36868
  50.7 4.9 %copy-start.3 = (f32[3072]{0:T(1024)S(1)}, f32[3072]{0:T(1024)}, u32[]{:S(2)}) copy-start(f32[3072]{0:T(1024)} %param.13) | copy-start | bytes 36868
  55.6 9.4 %copy-start = (bf16[432,512]{1,0:T(8,128)(2,1)S(1)}, bf16[432,512]{1,0:T(8,128)(2,1)}, u32[]{:S(2)}) copy-start(bf16[432,512]{1,0:T(8,128)(2,1)} %w_ref.1) | copy-start | bytes 1327108
  55.6 9.4 %copy-start.4 = (f32[512]{0:T(512)S(1)}, f32[512]{0:T(512)}, u32[]{:S(2)}) copy-start(f32[512]{0:T(512)} %param.17) | copy-start | bytes 6148
  58.6 3.2 %collective-permute-start.13 = (bf16[128,32]{1,0:T(8,128)(2,1)S(1)}, bf16[128,32]{1,0:T(8,128)(2,1)S(1)}, u32[]{:S(2)}, u32[]{:S(2)}) collective-permute-start(bf16[128,32]{1,0:T(8,128)(2,1)S(1)} %get-tuple-element.15.inner_ref), channel_id=1, source_target_pairs={{0,1},{1,0},{2,3},{3,2},{4,5},{5,4},{6,7},{7,6},{8,9},{9,8},{10,11... | collective-permute-start | bytes 24584 | tf_op jit(solution)/shard_map/ppermute | solution.py:22
  59.7 5.2 %collective-permute-start.14 = (bf16[128,32]{1,0:T(8,128)(2,1)S(1)}, bf16[128,32]{1,0:T(8,128)(2,1)S(1)}, u32[]{:S(2)}, u32[]{:S(2)}) collective-permute-start(bf16[128,32]{1,0:T(8,128)(2,1)S(1)} %get-tuple-element.16.outer_ref), channel_id=1, source_target_pairs={{1,2},{3,4},{5,6},{7,8},{9,10},{11,12},{13,14},{2,1},{4,3},{6,5},{... | collective-permute-start | bytes 24584 | tf_op jit(solution)/shard_map/ppermute | solution.py:388

commit v18 on v14

--- a/solution.py
+++ b/solution.py
@@ -275,7 +275,7 @@
 
 
 def convolve_kernel(
-    where_ref, inner_ref, outer_ref, inner_got_ref, outer_got_ref, w_ref, bias_ref, out_ref, latent
+    where_ref, inner_ref, outer_ref, outer_got_ref, inner_got_ref, w_ref, bias_ref, out_ref, latent
 ):
     frames, cols, _, ch = latent.shape
     rows = inner_ref.shape[0] // frames
@@ -324,7 +324,7 @@
         out_shape=jax.ShapeDtypeStruct((FRAMES, 2, 2 * rows, channels), jnp.bfloat16),
         scratch_shapes=[pltpu.VMEM((FRAMES, 4, 2 * rows + 16, LATENT_CH), jnp.float32)],
         compiler_params=pltpu.CompilerParams(vmem_limit_bytes=VMEM_LIMIT),
-    )(where, inner, outer, inner_got, outer_got, conv_weight, conv_bias[None])
+    )(where, inner, outer, outer_got, inner_got, conv_weight, conv_bias[None])
 
 
 def shards(queries, keys, values, w_out, shift_mod, scale_mod, w_final, conv_weight, conv_bias):
@@ -372,7 +372,7 @@
     for targets in ((3,), (2,), (1,), (0,)):
         for t, o in zip(targets, attend(asked, keys_values, targets, planes)):
             results[t] = o if t == 0 else swap(o, "heads", t)
-    partial = project(where, [results[t] for t in near], near, w_out, 1024)
+    partial = project(where, [results[t] for t in near], near, w_out, 1536)
     sent = [results[t] for t in far]
     inner, outer = final_layer(
         where, sent, far, partial, w_out, scale_mod, shift_mod, w_final, rows_dev, planes

time: 67.5 us -> 66.1 us (0.979)
  waiting for transfers between devices: 24.1 us -> 23.2 us
    ppermute x1, waiting for transfers between devices: 3.13 us -> 1.99 us  [shards(): lax.ppermute(outer, ('heads', 'plane'), pairs + [(j, i) for i, j in pairs])]
    ppermute x1, starting transfers between devices: 2.07 us -> 3.15 us  [shards(): lax.ppermute(outer, ('heads', 'plane'), pairs + [(j, i) for i, j in pairs])]
    ppermute x14, starting transfers between devices: 24.7 us -> 23.7 us  [swap(): return lax.ppermute(source, axis, [(i, i ^ distance) for i in range(count)])]
where the time goes in v18:
time: 66.1 us; the launch traced here: 66 us
  starting transfers between devices  26.8 us (41%)
  waiting for transfers between devices  23.2 us (35%)
  Pallas kernels  13.6 us (21%)
  other arithmetic  1.64 us (2%)
    ppermute x14, starting transfers between devices, swap(): return lax.ppermute(source, axis, [(i, i ^ distance) for i in range(count)])  23.7 us
    ppermute x14, waiting for transfers between devices, swap(): return lax.ppermute(source, axis, [(i, i ^ distance) for i in range(count)])  21.2 us
    pallas_call x4, Pallas kernels, attend(): pl.pallas_call(functools.partial(attend_kernel, sources=sources, planes=p...  5.68 us
    ppermute x1, starting transfers between devices, shards(): lax.ppermute(outer, ('heads', 'plane'), pairs + [(j, i) for i, j in pairs])  3.15 us
    pallas_call x1, Pallas kernels, final_layer(): pl.pallas_call(functools.partial(final_kernel, targets=targets, planes=pl...  3 us
    pallas_call x1, Pallas kernels, convolve(): pl.pallas_call(convolve_kernel, in_specs=[smem] + [vmem] * 6, out_specs=v...  2.17 us
    ppermute x1, waiting for transfers between devices, shards(): lax.ppermute(outer, ('heads', 'plane'), pairs + [(j, i) for i, j in pairs])  1.99 us
    pallas_call x1, Pallas kernels, project(): pl.pallas_call(functools.partial(project_kernel, targets=targets), grid_s...  1.87 us
  transfers between devices with their start and end apart: 15, of which 6 were waited for; matrix products, arithmetic and copies ran while one was open for 1% of the time, Pallas kernels for 9%

profile of v18, /device:TPU:1, one launch (start us, length us, event | category | flops | bytes accessed | tf_op | source)
XLA Modules:
  0.0 66.0 jit_solution(13998442289269624341)
XLA Ops:
  0.0 1.3 %pad_maximum_fusion.qkv_ref = bf16[384,1536]{1,0:T(8,128)(2,1)S(1)} fusion(bf16[128,1536]{1,0:T(8,128)(2,1)} %param.11, bf16[128,1536]{1,0:T(8,128)(2,1)} %param.10, bf16[128,1536]{1,0:T(8,128)(2,1)} %param.9), kind=kLoop, calls=%fused_computation | loop fusion | flops 3538944 | bytes 2359296 | tf_op jit(solution)/shard_map/concatenate | solution.py:52
  1.3 0.1 pad_add_fusion.where_ref
  1.4 0.8 %shard_map.91 = (bf16[384,384]{1,0:T(8,128)(2,1)S(1)}, bf16[384,384]{1,0:T(8,128)(2,1)S(1)}, bf16[384,384]{1,0:T(8,128)(2,1)S(1)}, bf16[384,384]{1,0:T(8,128)(2,1)S(1)}) custom-call(s32[4]{0:T(128)S(1)} %pad_add_fusion.where_ref, bf16[384,1536]{1,0:T(8,128)(2,1)S(1)} %pad_maximum_fusion.qkv_ref), custom_call_target="tpu_custom_call" | custom-call | tf_op jit(solution)/shard_map/pallas_call | solution.py:46
  2.3 2.1 %collective-permute-start = (bf16[320,384]{1,0:T(8,128)(2,1)S(1)}, bf16[320,384]{1,0:T(8,128)(2,1)S(1)}, u32[]{:S(2)}, u32[]{:S(2)}) collective-permute-start(bf16[320,384]{1,0:T(8,128)(2,1)S(1)} %pad_maximum_fusion.3), channel_id=1, source_target_pairs={{0,2},{1,3},{2,0},{3,1},{4,6},{5,7},{6,4},{7,5},{8,10},{9,11},{10,... | collective-permute-start | bytes 737288 | tf_op jit(solution)/shard_map/ppermute | solution.py:22
  4.4 1.3 %collective-permute-start.1 = (bf16[384,384]{1,0:T(8,128)(2,1)S(1)}, bf16[384,384]{1,0:T(8,128)(2,1)S(1)}, u32[]{:S(2)}, u32[]{:S(2)}) collective-permute-start(bf16[384,384]{1,0:T(8,128)(2,1)S(1)} %get-tuple-element.12), channel_id=1, source_target_pairs={{0,4},{4,0},{8,12},{12,8},{1,5},{5,1},{9,13},{13,9},{2,6},{6,2},{1... | collective-permute-start | bytes 884744 | tf_op jit(solution)/shard_map/ppermute | solution.py:22
  5.7 2.3 %collective-permute-start.4 = (bf16[384,384]{1,0:T(8,128)(2,1)S(1)}, bf16[384,384]{1,0:T(8,128)(2,1)S(1)}, u32[]{:S(2)}, u32[]{:S(2)}) collective-permute-start(bf16[384,384]{1,0:T(8,128)(2,1)S(1)} %get-tuple-element.13), channel_id=1, source_target_pairs={{0,8},{4,12},{8,0},{12,4},{1,9},{5,13},{9,1},{13,5},{2,10},{6,14},... | collective-permute-start | bytes 884744 | tf_op jit(solution)/shard_map/ppermute | solution.py:22
  8.0 0.0 collective-permute-start.7
  8.1 2.1 %collective-permute-done = bf16[320,384]{1,0:T(8,128)(2,1)S(1)} collective-permute-done((bf16[320,384]{1,0:T(8,128)(2,1)S(1)}, bf16[320,384]{1,0:T(8,128)(2,1)S(1)}, u32[]{:S(2)}, u32[]{:S(2)}) %collective-permute-start) | collective-permute-done | bytes 245792 | tf_op jit(solution)/shard_map/ppermute | solution.py:22
  10.1 7.2 %collective-permute-done.1 = bf16[384,384]{1,0:T(8,128)(2,1)S(1)} collective-permute-done((bf16[384,384]{1,0:T(8,128)(2,1)S(1)}, bf16[384,384]{1,0:T(8,128)(2,1)S(1)}, u32[]{:S(2)}, u32[]{:S(2)}) %collective-permute-start.1) | collective-permute-done | bytes 294944 | tf_op jit(solution)/shard_map/ppermute | solution.py:22
  17.4 0.1 fusion.5
  17.5 0.5 collective-permute-start.2
  18.0 0.0 collective-permute-done.4
  18.1 1.1 %collective-permute-start.5 = (bf16[320,384]{1,0:T(8,128)(2,1)S(1)}, bf16[320,384]{1,0:T(8,128)(2,1)S(1)}, u32[]{:S(2)}, u32[]{:S(2)}) collective-permute-start(bf16[320,384]{1,0:T(8,128)(2,1)S(1)} %pad_maximum_fusion.5), channel_id=1, source_target_pairs={{0,2},{1,3},{2,0},{3,1},{4,6},{5,7},{6,4},{7,5},{8,10},{9,11},{10,... | collective-permute-start | bytes 737288 | tf_op jit(solution)/shard_map/ppermute | solution.py:22
  19.2 7.5 %collective-permute-done.7 = bf16[384,384]{1,0:T(8,128)(2,1)S(1)} collective-permute-done((bf16[384,384]{1,0:T(8,128)(2,1)S(1)}, bf16[384,384]{1,0:T(8,128)(2,1)S(1)}, u32[]{:S(2)}, u32[]{:S(2)}) %collective-permute-start.7) | collective-permute-done | bytes 294944 | tf_op jit(solution)/shard_map/ppermute | solution.py:22
  26.8 0.3 collective-permute-start.8
  27.1 0.0 collective-permute-done.2
  27.2 5.7 %collective-permute-start.3 = (bf16[1152,384]{1,0:T(8,128)(2,1)S(1)}, bf16[1152,384]{1,0:T(8,128)(2,1)S(1)}, u32[]{:S(2)}, u32[]{:S(2)}) collective-permute-start(bf16[1152,384]{1,0:T(8,128)(2,1)S(1)} %get-tuple-element.36.refs_4_), channel_id=1, source_target_pairs={{0,1},{1,0},{2,3},{3,2},{4,5},{5,4},{6,7},{7,6},{8,9},{9,8},{10,11... | collective-permute-start | bytes 2654216 | tf_op jit(solution)/shard_map/ppermute | solution.py:22
  33.0 0.0 collective-permute-done.5
  33.1 3.9 %collective-permute-start.6 = (bf16[576,384]{1,0:T(8,128)(2,1)S(1)}, bf16[576,384]{1,0:T(8,128)(2,1)S(1)}, u32[]{:S(2)}, u32[]{:S(2)}) collective-permute-start(bf16[576,384]{1,0:T(8,128)(2,1)S(1)} %pad_maximum_fusion.1.refs_6_), channel_id=1, source_target_pairs={{0,1},{1,0},{2,3},{3,2},{4,5},{5,4},{6,7},{7,6},{8,9},{9,8},{10,11... | collective-permute-start | bytes 1327112 | tf_op jit(solution)/shard_map/ppermute | solution.py:22
  36.9 0.0 collective-permute-done.8
  37.0 0.0 slice-start
  37.1 2.5 %collective-permute-start.9 = (bf16[576,384]{1,0:T(8,128)(2,1)S(1)}, bf16[576,384]{1,0:T(8,128)(2,1)S(1)}, u32[]{:S(2)}, u32[]{:S(2)}) collective-permute-start(bf16[576,384]{1,0:T(8,128)(2,1)S(1)} %pad_maximum_fusion.2.refs_8_), channel_id=1, source_target_pairs={{0,1},{1,0},{2,3},{3,2},{4,5},{5,4},{6,7},{7,6},{8,9},{9,8},{10,11... | collective-permute-start | bytes 1327112 | tf_op jit(solution)/shard_map/ppermute | solution.py:22
  39.6 0.0 collective-permute-done.6.refs_7_
  39.6 1.4 %collective-permute-done.9.refs_9_ = bf16[576,384]{1,0:T(8,128)(2,1)S(1)} collective-permute-done((bf16[576,384]{1,0:T(8,128)(2,1)S(1)}, bf16[576,384]{1,0:T(8,128)(2,1)S(1)}, u32[]{:S(2)}, u32[]{:S(2)}) %collective-permute-start.9) | collective-permute-done | bytes 442400 | tf_op jit(solution)/shard_map/ppermute | solution.py:22
  41.0 0.0 collective-permute-done.3.refs_5_
  41.1 0.0 slice-start.1
  41.1 1.4 %shard_map.95 = bf16[4,32,384]{2,1,0:T(8,128)(2,1)S(1)} custom-call(bf16[128,384]{1,0:T(8,128)(2,1)S(1)} %get-tuple-element.39.refs_0_, bf16[128,384]{1,0:T(8,128)(2,1)S(1)} %get-tuple-element.40.refs_1_, bf16[128,384]{1,0:T(8,128)(2,1)S(1)} %pad_maximum_fusion.9.refs_2_, bf16[128,384]{1,0:T(8,128)(2,1)S(1)} %pad_maximum_fusion.10.refs_3_, ...), custom_call_target="tpu_custom_call" | custom-call | tf_op jit(solution)/shard_map/pallas_call | solution.py:134
  42.6 2.3 %collective-permute-start.12 = (bf16[4,32,384]{2,1,0:T(8,128)(2,1)S(1)}, bf16[4,32,384]{2,1,0:T(8,128)(2,1)S(1)}, u32[]{:S(2)}, u32[]{:S(2)}) collective-permute-start(bf16[4,32,384]{2,1,0:T(8,128)(2,1)S(1)} %shard_map.95), channel_id=1, source_target_pairs={{0,12},{4,8},{8,4},{12,0},{1,13},{5,9},{9,5},{13,1},{2,14},{6,10},... | collective-permute-start | bytes 294920 | tf_op jit(solution)/shard_map/ppermute | solution.py:22
  44.8 1.4 %shard_map.92 = bf16[4,32,384]{2,1,0:T(8,128)(2,1)S(1)} custom-call(bf16[128,384]{1,0:T(8,128)(2,1)S(1)} %get-tuple-element.39.refs_0_, bf16[128,384]{1,0:T(8,128)(2,1)S(1)} %get-tuple-element.40.refs_1_, bf16[128,384]{1,0:T(8,128)(2,1)S(1)} %pad_maximum_fusion.9.refs_2_, bf16[128,384]{1,0:T(8,128)(2,1)S(1)} %pad_maximum_fusion.10.refs_3_, ...), custom_call_target="tpu_custom_call" | custom-call | tf_op jit(solution)/shard_map/pallas_call | solution.py:134
  46.3 0.0 slice-start.2
  46.3 1.3 %collective-permute-start.10 = (bf16[4,32,384]{2,1,0:T(8,128)(2,1)S(1)}, bf16[4,32,384]{2,1,0:T(8,128)(2,1)S(1)}, u32[]{:S(2)}, u32[]{:S(2)}) collective-permute-start(bf16[4,32,384]{2,1,0:T(8,128)(2,1)S(1)} %shard_map.92), channel_id=1, source_target_pairs={{0,8},{4,12},{8,0},{12,4},{1,9},{5,13},{9,1},{13,5},{2,10},{6,14},... | collective-permute-start | bytes 294920 | tf_op jit(solution)/shard_map/ppermute | solution.py:22
  47.6 1.4 %shard_map.93 = bf16[4,32,384]{2,1,0:T(8,128)(2,1)S(1)} custom-call(bf16[128,384]{1,0:T(8,128)(2,1)S(1)} %get-tuple-element.39.refs_0_, bf16[128,384]{1,0:T(8,128)(2,1)S(1)} %get-tuple-element.40.refs_1_, bf16[128,384]{1,0:T(8,128)(2,1)S(1)} %pad_maximum_fusion.9.refs_2_, bf16[128,384]{1,0:T(8,128)(2,1)S(1)} %pad_maximum_fusion.10.refs_3_, ...), custom_call_target="tpu_custom_call" | custom-call | tf_op jit(solution)/shard_map/pallas_call | solution.py:134
  49.0 0.2 collective-permute-start.11
  49.3 1.4 %shard_map.94.refs_0_ = bf16[4,32,384]{2,1,0:T(8,128)(2,1)S(1)} custom-call(bf16[128,384]{1,0:T(8,128)(2,1)S(1)} %get-tuple-element.39.refs_0_, bf16[128,384]{1,0:T(8,128)(2,1)S(1)} %get-tuple-element.40.refs_1_, bf16[128,384]{1,0:T(8,128)(2,1)S(1)} %pad_maximum_fusion.9.refs_2_, bf16[128,384]{1,0:T(8,128)(2,1)S(1)} %pad_maximum_fusion.10.refs_3_, ...), custom_call_target="tpu_custom_call" | custom-call | tf_op jit(solution)/shard_map/pallas_call | solution.py:134
  50.7 0.0 copy-start.1
  50.7 0.0 copy-start.2
  50.7 0.0 copy-start.3
  50.7 0.0 collective-permute-done.12.refs_1_
  50.7 0.0 slice-done
  50.7 0.0 slice-done.1
  50.7 0.0 slice-done.2
  50.8 1.9 %shard_map.96.refs_4_ = f32[2,128,1536]{2,1,0:T(8,128)S(1)} custom-call(s32[4]{0:T(128)S(1)} %pad_add_fusion.where_ref, bf16[4,32,384]{2,1,0:T(8,128)(2,1)S(1)} %shard_map.94.refs_0_, bf16[4,32,384]{2,1,0:T(8,128)(2,1)S(1)} %collective-permute-done.12.refs_1_, bf16[1536,3072]{1,0:T(8,128)(2,1)S(1)} %bitcast.8, bf16[1536,3072]{1,0:T(8,128)(2,1)S(1)} %bitcast.8), custom_call_target="tpu_custom_call" | custom-call | tf_op jit(solution)/shard_map/pallas_call | solution.py:179
  52.6 2.9 %collective-permute-done.10.refs_0_ = bf16[4,32,384]{2,1,0:T(8,128)(2,1)S(1)} collective-permute-done((bf16[4,32,384]{2,1,0:T(8,128)(2,1)S(1)}, bf16[4,32,384]{2,1,0:T(8,128)(2,1)S(1)}, u32[]{:S(2)}, u32[]{:S(2)}) %collective-permute-start.10) | collective-permute-done | bytes 98336 | tf_op jit(solution)/shard_map/ppermute | solution.py:22
  55.5 0.0 collective-permute-done.11.refs_1_
  55.5 0.0 copy-done.1
  55.5 0.0 copy-done.2
  55.5 0.0 copy-done.3
  55.6 0.0 copy-start
  55.6 0.0 copy-start.4
  55.6 3.0 %shard_map.97 = (bf16[128,32]{1,0:T(8,128)(2,1)S(1)}, bf16[128,32]{1,0:T(8,128)(2,1)S(1)}) custom-call(s32[4]{0:T(128)S(1)} %pad_add_fusion.where_ref, bf16[4,32,384]{2,1,0:T(8,128)(2,1)S(1)} %collective-permute-done.10.refs_0_, bf16[4,32,384]{2,1,0:T(8,128)(2,1)S(1)} %collective-permute-done.11.refs_1_, bf16[1536,3072]{1,0:T(8,128)(2,1)S(1)} %bitcast.8, ...), custom_call_target="tpu_custom_call" | custom-call | tf_op jit(solution)/shard_map/pallas_call | solution.py:254
  58.6 3.1 %collective-permute-start.13 = (bf16[128,32]{1,0:T(8,128)(2,1)S(1)}, bf16[128,32]{1,0:T(8,128)(2,1)S(1)}, u32[]{:S(2)}, u32[]{:S(2)}) collective-permute-start(bf16[128,32]{1,0:T(8,128)(2,1)S(1)} %get-tuple-element.16.outer_ref), channel_id=1, source_target_pairs={{1,2},{3,4},{5,6},{7,8},{9,10},{11,12},{13,14},{2,1},{4,3},{6,5},{... | collective-permute-start | bytes 24584 | tf_op jit(solution)/shard_map/ppermute | solution.py:382
  61.7 0.1 collective-permute-start.14
  61.8 2.0 %collective-permute-done.13.outer_got_ref = bf16[128,32]{1,0:T(8,128)(2,1)S(1)} collective-permute-done((bf16[128,32]{1,0:T(8,128)(2,1)S(1)}, bf16[128,32]{1,0:T(8,128)(2,1)S(1)}, u32[]{:S(2)}, u32[]{:S(2)}) %collective-permute-start.13) | collective-permute-done | bytes 8224 | tf_op jit(solution)/shard_map/ppermute | solution.py:382
  63.8 0.0 collective-permute-done.14.inner_got_ref
  63.8 0.0 copy-done
  63.8 0.0 copy-done.4
  63.8 2.2 %shard_map.98 = bf16[4,2,64,512]{3,2,1,0:T(8,128)(2,1)} custom-call(s32[4]{0:T(128)S(1)} %pad_add_fusion.where_ref, bf16[128,32]{1,0:T(8,128)(2,1)S(1)} %get-tuple-element.15.inner_ref, bf16[128,32]{1,0:T(8,128)(2,1)S(1)} %get-tuple-element.16.outer_ref, bf16[128,32]{1,0:T(8,128)(2,1)S(1)} %collective-permute-done.13.outer_got_ref, ...), custom_call_target="tpu_custom_call" | custom-call | tf_op jit(solution)/shard_map/pallas_call | solution.py:320
  (32 shorter events, 0.6 us)
Async XLA Ops:
  2.3 7.8 %collective-permute-start = (bf16[320,384]{1,0:T(8,128)(2,1)S(1)}, bf16[320,384]{1,0:T(8,128)(2,1)S(1)}, u32[]{:S(2)}, u32[]{:S(2)}) collective-permute-start(bf16[320,384]{1,0:T(8,128)(2,1)S(1)} %pad_maximum_fusion.3), channel_id=1, source_target_pairs={{0,2},{1,3},{2,0},{3,1},{4,6},{5,7},{6,4},{7,5},{8,10},{9,11},{10,... | collective-permute-start | bytes 737288 | tf_op jit(solution)/shard_map/ppermute | solution.py:22
  4.4 13.0 %collective-permute-start.1 = (bf16[384,384]{1,0:T(8,128)(2,1)S(1)}, bf16[384,384]{1,0:T(8,128)(2,1)S(1)}, u32[]{:S(2)}, u32[]{:S(2)}) collective-permute-start(bf16[384,384]{1,0:T(8,128)(2,1)S(1)} %get-tuple-element.12), channel_id=1, source_target_pairs={{0,4},{4,0},{8,12},{12,8},{1,5},{5,1},{9,13},{13,9},{2,6},{6,2},{1... | collective-permute-start | bytes 884744 | tf_op jit(solution)/shard_map/ppermute | solution.py:22
  5.7 12.2 %collective-permute-start.4 = (bf16[384,384]{1,0:T(8,128)(2,1)S(1)}, bf16[384,384]{1,0:T(8,128)(2,1)S(1)}, u32[]{:S(2)}, u32[]{:S(2)}) collective-permute-start(bf16[384,384]{1,0:T(8,128)(2,1)S(1)} %get-tuple-element.13), channel_id=1, source_target_pairs={{0,8},{4,12},{8,0},{12,4},{1,9},{5,13},{9,1},{13,5},{2,10},{6,14},... | collective-permute-start | bytes 884744 | tf_op jit(solution)/shard_map/ppermute | solution.py:22
  8.0 18.7 %collective-permute-start.7 = (bf16[384,384]{1,0:T(8,128)(2,1)S(1)}, bf16[384,384]{1,0:T(8,128)(2,1)S(1)}, u32[]{:S(2)}, u32[]{:S(2)}) collective-permute-start(bf16[384,384]{1,0:T(8,128)(2,1)S(1)} %get-tuple-element.14), channel_id=1, source_target_pairs={{0,12},{4,8},{8,4},{12,0},{1,13},{5,9},{9,5},{13,1},{2,14},{6,10},... | collective-permute-start | bytes 884744 | tf_op jit(solution)/shard_map/ppermute | solution.py:22
  17.5 9.6 %collective-permute-start.2 = (bf16[320,384]{1,0:T(8,128)(2,1)S(1)}, bf16[320,384]{1,0:T(8,128)(2,1)S(1)}, u32[]{:S(2)}, u32[]{:S(2)}) collective-permute-start(bf16[320,384]{1,0:T(8,128)(2,1)S(1)} %pad_maximum_fusion.4), channel_id=1, source_target_pairs={{0,2},{1,3},{2,0},{3,1},{4,6},{5,7},{6,4},{7,5},{8,10},{9,11},{10,... | collective-permute-start | bytes 737288 | tf_op jit(solution)/shard_map/ppermute | solution.py:22
  18.1 14.9 %collective-permute-start.5 = (bf16[320,384]{1,0:T(8,128)(2,1)S(1)}, bf16[320,384]{1,0:T(8,128)(2,1)S(1)}, u32[]{:S(2)}, u32[]{:S(2)}) collective-permute-start(bf16[320,384]{1,0:T(8,128)(2,1)S(1)} %pad_maximum_fusion.5), channel_id=1, source_target_pairs={{0,2},{1,3},{2,0},{3,1},{4,6},{5,7},{6,4},{7,5},{8,10},{9,11},{10,... | collective-permute-start | bytes 737288 | tf_op jit(solution)/shard_map/ppermute | solution.py:22
  26.8 10.2 %collective-permute-start.8 = (bf16[320,384]{1,0:T(8,128)(2,1)S(1)}, bf16[320,384]{1,0:T(8,128)(2,1)S(1)}, u32[]{:S(2)}, u32[]{:S(2)}) collective-permute-start(bf16[320,384]{1,0:T(8,128)(2,1)S(1)} %pad_maximum_fusion.6), channel_id=1, source_target_pairs={{0,2},{1,3},{2,0},{3,1},{4,6},{5,7},{6,4},{7,5},{8,10},{9,11},{10,... | collective-permute-start | bytes 737288 | tf_op jit(solution)/shard_map/ppermute | solution.py:22
  27.2 13.8 %collective-permute-start.3 = (bf16[1152,384]{1,0:T(8,128)(2,1)S(1)}, bf16[1152,384]{1,0:T(8,128)(2,1)S(1)}, u32[]{:S(2)}, u32[]{:S(2)}) collective-permute-start(bf16[1152,384]{1,0:T(8,128)(2,1)S(1)} %get-tuple-element.36.refs_4_), channel_id=1, source_target_pairs={{0,1},{1,0},{2,3},{3,2},{4,5},{5,4},{6,7},{7,6},{8,9},{9,8},{10,11... | collective-permute-start | bytes 2654216 | tf_op jit(solution)/shard_map/ppermute | solution.py:22
  33.1 6.5 %collective-permute-start.6 = (bf16[576,384]{1,0:T(8,128)(2,1)S(1)}, bf16[576,384]{1,0:T(8,128)(2,1)S(1)}, u32[]{:S(2)}, u32[]{:S(2)}) collective-permute-start(bf16[576,384]{1,0:T(8,128)(2,1)S(1)} %pad_maximum_fusion.1.refs_6_), channel_id=1, source_target_pairs={{0,1},{1,0},{2,3},{3,2},{4,5},{5,4},{6,7},{7,6},{8,9},{9,8},{10,11... | collective-permute-start | bytes 1327112 | tf_op jit(solution)/shard_map/ppermute | solution.py:22
  37.0 13.7 %slice-start = ((s8[9437184]{0:T(1024)(128)(4,1)}), s8[4194304]{0:T(1024)(128)(4,1)S(1)}, s32[]{:S(2)}) async-start(s8[9437184]{0:T(1024)(128)(4,1)} %bitcast.7), calls=%async_computation | async-start | bytes 8388608
  37.1 3.9 %collective-permute-start.9 = (bf16[576,384]{1,0:T(8,128)(2,1)S(1)}, bf16[576,384]{1,0:T(8,128)(2,1)S(1)}, u32[]{:S(2)}, u32[]{:S(2)}) collective-permute-start(bf16[576,384]{1,0:T(8,128)(2,1)S(1)} %pad_maximum_fusion.2.refs_8_), channel_id=1, source_target_pairs={{0,1},{1,0},{2,3},{3,2},{4,5},{5,4},{6,7},{7,6},{8,9},{9,8},{10,11... | collective-permute-start | bytes 1327112 | tf_op jit(solution)/shard_map/ppermute | solution.py:22
  41.1 9.6 %slice-start.1 = ((s8[9437184]{0:T(1024)(128)(4,1)}), s8[4194304]{0:T(1024)(128)(4,1)S(1)}, s32[]{:S(2)}) async-start(s8[9437184]{0:T(1024)(128)(4,1)} %bitcast.7), calls=%async_computation.1 | async-start | bytes 8388608
  42.6 8.1 %collective-permute-start.12 = (bf16[4,32,384]{2,1,0:T(8,128)(2,1)S(1)}, bf16[4,32,384]{2,1,0:T(8,128)(2,1)S(1)}, u32[]{:S(2)}, u32[]{:S(2)}) collective-permute-start(bf16[4,32,384]{2,1,0:T(8,128)(2,1)S(1)} %shard_map.95), channel_id=1, source_target_pairs={{0,12},{4,8},{8,4},{12,0},{1,13},{5,9},{9,5},{13,1},{2,14},{6,10},... | collective-permute-start | bytes 294920 | tf_op jit(solution)/shard_map/ppermute | solution.py:22
  46.3 4.5 %slice-start.2 = ((s8[9437184]{0:T(1024)(128)(4,1)}), s8[1048576]{0:T(1024)(128)(4,1)S(1)}, s32[]{:S(2)}) async-start(s8[9437184]{0:T(1024)(128)(4,1)} %bitcast.7), calls=%async_computation.2 | async-start | bytes 2097152
  46.3 9.3 %collective-permute-start.10 = (bf16[4,32,384]{2,1,0:T(8,128)(2,1)S(1)}, bf16[4,32,384]{2,1,0:T(8,128)(2,1)S(1)}, u32[]{:S(2)}, u32[]{:S(2)}) collective-permute-start(bf16[4,32,384]{2,1,0:T(8,128)(2,1)S(1)} %shard_map.92), channel_id=1, source_target_pairs={{0,8},{4,12},{8,0},{12,4},{1,9},{5,13},{9,1},{13,5},{2,10},{6,14},... | collective-permute-start | bytes 294920 | tf_op jit(solution)/shard_map/ppermute | solution.py:22
  49.0 6.5 %collective-permute-start.11 = (bf16[4,32,384]{2,1,0:T(8,128)(2,1)S(1)}, bf16[4,32,384]{2,1,0:T(8,128)(2,1)S(1)}, u32[]{:S(2)}, u32[]{:S(2)}) collective-permute-start(bf16[4,32,384]{2,1,0:T(8,128)(2,1)S(1)} %shard_map.93), channel_id=1, source_target_pairs={{0,4},{4,0},{8,12},{12,8},{1,5},{5,1},{9,13},{13,9},{2,6},{6,2},{1... | collective-permute-start | bytes 294920 | tf_op jit(solution)/shard_map/ppermute | solution.py:22
  50.7 4.9 %copy-start.1 = (bf16[3072,64]{0,1:T(8,128)(2,1)S(1)}, bf16[3072,64]{0,1:T(8,128)(2,1)}, u32[]{:S(2)}) copy-start(bf16[3072,64]{0,1:T(8,128)(2,1)} %param.15) | copy-start | bytes 1179652
  50.7 4.9 %copy-start.2 = (f32[3072]{0:T(1024)S(1)}, f32[3072]{0:T(1024)}, u32[]{:S(2)}) copy-start(f32[3072]{0:T(1024)} %param.14) | copy-start | bytes 36868
  50.7 4.9 %copy-start.3 = (f32[3072]{0:T(1024)S(1)}, f32[3072]{0:T(1024)}, u32[]{:S(2)}) copy-start(f32[3072]{0:T(1024)} %param.13) | copy-start | bytes 36868
  55.6 8.3 %copy-start = (bf16[432,512]{1,0:T(8,128)(2,1)S(1)}, bf16[432,512]{1,0:T(8,128)(2,1)}, u32[]{:S(2)}) copy-start(bf16[432,512]{1,0:T(8,128)(2,1)} %w_ref.1) | copy-start | bytes 1327108
  55.6 8.2 %copy-start.4 = (f32[512]{0:T(512)S(1)}, f32[512]{0:T(512)}, u32[]{:S(2)}) copy-start(f32[512]{0:T(512)} %param.17) | copy-start | bytes 6148
  58.6 5.2 %collective-permute-start.13 = (bf16[128,32]{1,0:T(8,128)(2,1)S(1)}, bf16[128,32]{1,0:T(8,128)(2,1)S(1)}, u32[]{:S(2)}, u32[]{:S(2)}) collective-permute-start(bf16[128,32]{1,0:T(8,128)(2,1)S(1)} %get-tuple-element.16.outer_ref), channel_id=1, source_target_pairs={{1,2},{3,4},{5,6},{7,8},{9,10},{11,12},{13,14},{2,1},{4,3},{6,5},{... | collective-permute-start | bytes 24584 | tf_op jit(solution)/shard_map/ppermute | solution.py:382
  61.7 2.1 %collective-permute-start.14 = (bf16[128,32]{1,0:T(8,128)(2,1)S(1)}, bf16[128,32]{1,0:T(8,128)(2,1)S(1)}, u32[]{:S(2)}, u32[]{:S(2)}) collective-permute-start(bf16[128,32]{1,0:T(8,128)(2,1)S(1)} %get-tuple-element.15.inner_ref), channel_id=1, source_target_pairs={{0,1},{1,0},{2,3},{3,2},{4,5},{5,4},{6,7},{7,6},{8,9},{9,8},{10,11... | collective-permute-start | bytes 24584 | tf_op jit(solution)/shard_map/ppermute | solution.py:22
